TPU v7x, 32 devices: a whole 2x2x4 slice. The times are simulated.
32 devices in a mesh: rows: 16 (over z, x, core), cols: 2 (over y).
Axes of the slice: x: 2, y: 2, z: 4, core: 2. Of those that a mesh axis runs over, the one named last changes fastest.
Arguments:
- right_sides: float32 [4, 16, 128, 256], P(None, 'rows'), may hold values from -6 to 6
- factor_blocks: bfloat16 [3, 16, 2, 8, 256, 256], P(None, 'rows', 'cols'), may hold values from -0.125 to 0.125
- diag_inverses: bfloat16 [4, 16, 256, 256], P(None, 'rows')
- source_ids: int32 [3, 16, 2, 8], P(None, 'rows', 'cols'), may hold values from 0 to 47, as said below
- block_counts: int32 [3, 16, 2], P(None, 'rows', 'cols'), may hold values from 1 to 8, as said below
Outputs:
- solution: float32 [4, 16, 128, 256], P(None, 'rows', 'cols')
Inputs may be any that keep to these rules, and one draw needn't show every extreme that they name: source_ids[l, t, c, k] = m * 16 + s names a supernode of a level m <= l with s % 2 == c. block_counts[l, t, c] slots of target t on group c hold blocks of the factor; slots at and past it are not part of the factor. In every level some target and group has all 8 slots live.
All inputs are finite; a program needn't handle non-finite values.
Results may differ from a plain program's by a relative error of at most 0.007.
Values may be sent and summed in bfloat16 or wider, within the bound.
No kernel may reach another device: no remote copies, remote signals or barrier semaphores. Data moves between devices by JAX's collectives and lax.ppermute only.
A program may use at most 128 MiB of HBM per device.

v0:
```python
import jax
import jax.numpy as jnp
from jax import lax
from jax.sharding import PartitionSpec as P


def locate(source, row_count, col_count):
    return source // row_count * (row_count // col_count) + source % row_count // col_count


def slot_sum(running, blocks, chosen_ids, live_count, solved_store, row_count, col_count):

    def add_block(slot_index, partial_value):
        source = chosen_ids[slot_index]
        solved_piece = lax.dynamic_index_in_dim(
            solved_store, locate(source, row_count, col_count), 0, keepdims=False
        )
        factor_piece = lax.dynamic_index_in_dim(blocks, slot_index, 0, keepdims=False)
        return partial_value + jnp.dot(
            solved_piece, factor_piece, preferred_element_type=jnp.float32
        )

    return lax.fori_loop(0, live_count, add_block, running)


def shards(right_sides, factor_blocks, diag_inverses, source_ids, block_counts):
    row_count = lax.axis_size("rows")
    col_count = lax.axis_size("cols")
    level_count = right_sides.shape[0]
    rhs_count = right_sides.shape[2]
    block_width = right_sides.shape[3]
    share_rows = rhs_count // col_count
    col_index = lax.axis_index("cols")
    per_level = row_count // col_count
    solved_store = jnp.zeros(((level_count - 1) * per_level, rhs_count, block_width), jnp.bfloat16)
    partials = [jnp.zeros((rhs_count, block_width), jnp.float32)] * level_count
    solutions = []
    for level_index in range(level_count):
        if level_index > 0:
            partials[level_index] = slot_sum(
                partials[level_index],
                factor_blocks[level_index - 1, 0, 0],
                source_ids[level_index - 1, 0, 0],
                block_counts[level_index - 1, 0, 0],
                solved_store,
                row_count,
                col_count,
            )
        own_rhs = lax.dynamic_slice_in_dim(
            right_sides[level_index, 0], col_index * share_rows, share_rows, 0
        )
        if level_index > 0:
            own_rhs = own_rhs - lax.psum_scatter(
                partials[level_index], "cols", scatter_dimension=0, tiled=True
            )
        own_solution = jnp.dot(
            own_rhs.astype(jnp.bfloat16),
            diag_inverses[level_index, 0],
            preferred_element_type=jnp.float32,
        )
        solutions.append(own_solution)
        if level_index < level_count - 1:
            pieces = lax.all_gather(
                own_solution.astype(jnp.bfloat16)[None], "rows", axis=0, tiled=True
            )
            grouped = pieces.reshape(per_level, col_count, share_rows, block_width)
            regrouped = lax.all_to_all(grouped, "cols", split_axis=1, concat_axis=2, tiled=True)
            solved_store = solved_store.at[
                level_index * per_level : (level_index + 1) * per_level
            ].set(regrouped[:, 0])
    return jnp.stack(solutions)[:, None]


def solution(mesh):
    return jax.shard_map(
        shards,
        mesh=mesh,
        in_specs=(
            P(None, "rows", None, None),
            P(None, "rows", "cols", None, None, None),
            P(None, "rows", None, None),
            P(None, "rows", "cols", None),
            P(None, "rows", "cols"),
        ),
        out_specs=P(None, "rows", "cols", None),
        check_vma=False,
    )
```

profile of v0, /device:TPU:0, one launch (start us, length us, event | category | flops | bytes accessed | tf_op | source)
XLA Modules:
  0.0 260.7 jit_solution(2217184039318313030)
XLA Ops:
  6.5 0.9 slice.116
  7.4 1.7 fusion.40
  9.1 24.6 %all-gather = bf16[1024,256]{1,0:T(8,128)(2,1)S(1)} all-gather(bf16[64,256]{1,0:T(8,128)(2,1)S(1)} %get-tuple-element.425), channel_id=2, replica_groups=mesh['rows'=16,'cols'=2] {'rows'}, dimensions={0}, use_global_device_ids=true | all-gather | bytes 557056 | tf_op jit(solution)/shard_map/all_gather | solution.py:63
  33.7 0.8 copy.11
  34.5 3.5 %all-to-all-start = ((bf16[8,2,64,256]{3,2,0,1:T(8,128)(2,1)}), bf16[8,2,64,256]{3,2,0,1:T(8,128)(2,1)S(1)}, u32[]{:S(2)}, u32[]{:S(2)}) async-start(bf16[8,2,64,256]{3,2,0,1:T(8,128)(2,1)} %copy.11), calls=%async_computation | async-start | bytes 1048576 | tf_op jit(solution)/shard_map/all_to_all | solution.py:67
  38.0 0.0 reduce-scatter.4.cloned.1.call-start
  38.1 3.5 %slice_bitcast_fusion = (bf16[8,256,256]{2,1,0:T(8,128)(2,1)S(1)}, bf16[8,256,256]{2,1,0:T(8,128)(2,1)}, bf16[8,256,256]{2,1,0:T(8,128)(2,1)}) fusion(bf16[3,1,1,8,256,256]{5,4,3,2,1,0:T(8,128)(2,1)} %param.18), kind=kLoop, calls=%fused_computation.19 | loop fusion | bytes 6291456 | tf_op jit(solution)/shard_map/squeeze | solution.py:42
  41.6 0.7 fusion.39
  42.3 4.5 %all-to-all-done = bf16[8,2,64,256]{3,2,0,1:T(8,128)(2,1)S(1)} async-done(((bf16[8,2,64,256]{3,2,0,1:T(8,128)(2,1)}), bf16[8,2,64,256]{3,2,0,1:T(8,128)(2,1)S(1)}, u32[]{:S(2)}, u32[]{:S(2)}) %all-to-all-start) | async-done | bytes 524320 | tf_op jit(solution)/shard_map/all_to_all | solution.py:67
  46.8 0.1 scatter.10
  47.0 5.7 %while.42 = (s32[]{:T(128)}, f32[128,256]{1,0:T(8,128)S(1)}, s32[]{:T(128)}, s32[8]{0:T(128)S(1)}, bf16[24,128,256]{2,1,0:T(8,128)(2,1)S(1)}, /*index=5*/bf16[8,...) while((s32[]{:T(128)}, f32[128,256]{1,0:T(8,128)S(1)}, ...), condition=%wide.region_1.2_spmd, body=%wide.region_0.0_spmd.sunk | while | flops 16810028 | bytes 459334 | solution.py:23
  47.7 0.6 dynamic_slice.141
  50.9 1.1 convolution_add_fusion.6
  52.7 0.6 copy-done.1
  53.3 0.0 reduce-scatter.4.cloned.1.call-update
  53.4 41.0 %reduce-scatter.4.cloned.1.call-done = f32[64,256]{1,0:T(8,128)} async-done(((f32[128,256]{1,0:T(8,128)}), f32[64,256]{1,0:T(8,128)}) %reduce-scatter.4.cloned.1.call-update) | async-done | bytes 65552 | tf_op jit(solution)/shard_map/reduce_scatter | solution.py:53
  94.4 1.1 fusion.41
  95.5 22.9 %all-gather.1 = bf16[1024,256]{1,0:T(8,128)(2,1)S(1)} all-gather(bf16[64,256]{1,0:T(8,128)(2,1)S(1)} %get-tuple-element.427), channel_id=3, replica_groups=mesh['rows'=16,'cols'=2] {'rows'}, dimensions={0}, use_global_device_ids=true | all-gather | bytes 557056 | tf_op jit(solution)/shard_map/all_gather | solution.py:63
  118.4 0.8 copy.13
  119.2 3.5 %all-to-all-start.1 = ((bf16[8,2,64,256]{3,2,0,1:T(8,128)(2,1)}), bf16[8,2,64,256]{3,2,0,1:T(8,128)(2,1)S(1)}, u32[]{:S(2)}, u32[]{:S(2)}) async-start(bf16[8,2,64,256]{3,2,0,1:T(8,128)(2,1)} %copy.13), calls=%async_computation.2 | async-start | bytes 1048576 | tf_op jit(solution)/shard_map/all_to_all | solution.py:67
  122.7 0.0 reduce-scatter.6.cloned.1.call-start
  122.7 8.7 %all-to-all-done.1 = bf16[8,2,64,256]{3,2,0,1:T(8,128)(2,1)S(1)} async-done(((bf16[8,2,64,256]{3,2,0,1:T(8,128)(2,1)}), bf16[8,2,64,256]{3,2,0,1:T(8,128)(2,1)S(1)}, u32[]{:S(2)}, u32[]{:S(2)}) %all-to-all-start.1) | async-done | bytes 524320 | tf_op jit(solution)/shard_map/all_to_all | solution.py:67
  131.6 20.6 %while.43 = (s32[]{:T(128)}, f32[128,256]{1,0:T(8,128)S(1)}, s32[]{:T(128)}, s32[8]{0:T(128)S(1)}, bf16[24,128,256]{2,1,0:T(8,128)(2,1)S(1)}, /*index=5*/bf16[8,...) while((s32[]{:T(128)}, f32[128,256]{1,0:T(8,128)S(1)}, ...), condition=%wide.region_4.5_spmd, body=%wide.region_3.4_spmd.sunk | while | flops 16810028 | bytes 459334 | solution.py:23
  132.2 0.6 dynamic_slice.144
  135.4 1.1 convolution_add_fusion.7
  137.2 0.6 dynamic_slice.144
  140.4 1.1 convolution_add_fusion.7
  142.2 0.6 dynamic_slice.144
  145.4 1.1 convolution_add_fusion.7
  147.2 0.6 dynamic_slice.144
  150.4 1.1 convolution_add_fusion.7
  152.2 0.6 copy-done.2
  152.8 0.0 reduce-scatter.6.cloned.1.call-update
  152.8 24.8 %reduce-scatter.6.cloned.1.call-done = f32[64,256]{1,0:T(8,128)} async-done(((f32[128,256]{1,0:T(8,128)}), f32[64,256]{1,0:T(8,128)}) %reduce-scatter.6.cloned.1.call-update) | async-done | bytes 65552 | tf_op jit(solution)/shard_map/reduce_scatter | solution.py:53
  177.6 1.1 fusion.42
  178.7 22.8 %all-gather.2 = bf16[1024,256]{1,0:T(8,128)(2,1)S(1)} all-gather(bf16[64,256]{1,0:T(8,128)(2,1)S(1)} %get-tuple-element.429), channel_id=4, replica_groups=mesh['rows'=16,'cols'=2] {'rows'}, dimensions={0}, use_global_device_ids=true | all-gather | bytes 557056 | tf_op jit(solution)/shard_map/all_gather | solution.py:63
  201.5 0.8 copy.15
  202.4 3.5 %all-to-all-start.2 = ((bf16[8,2,64,256]{3,2,0,1:T(8,128)(2,1)}), bf16[8,2,64,256]{3,2,0,1:T(8,128)(2,1)S(1)}, u32[]{:S(2)}, u32[]{:S(2)}) async-start(bf16[8,2,64,256]{3,2,0,1:T(8,128)(2,1)} %copy.15), calls=%async_computation.4 | async-start | bytes 1048576 | tf_op jit(solution)/shard_map/all_to_all | solution.py:67
  205.8 0.0 reduce-scatter.8.cloned.1.call-start
  205.9 8.7 %all-to-all-done.2 = bf16[8,2,64,256]{3,2,0,1:T(8,128)(2,1)S(1)} async-done(((bf16[8,2,64,256]{3,2,0,1:T(8,128)(2,1)}), bf16[8,2,64,256]{3,2,0,1:T(8,128)(2,1)S(1)}, u32[]{:S(2)}, u32[]{:S(2)}) %all-to-all-start.2) | async-done | bytes 524320 | tf_op jit(solution)/shard_map/all_to_all | solution.py:67
  214.7 4.6 %while.44 = (s32[]{:T(128)}, f32[128,256]{1,0:T(8,128)S(1)}, s32[]{:T(128)}, s32[8]{0:T(128)S(1)}, bf16[24,128,256]{2,1,0:T(8,128)(2,1)S(1)}, /*index=5*/bf16[8,...) while((s32[]{:T(128)}, f32[128,256]{1,0:T(8,128)S(1)}, ...), condition=%wide.region_7.8_spmd, body=%wide.region_6.7_spmd.sunk | while | flops 16810028 | bytes 459334 | solution.py:23
  215.3 0.7 dynamic_slice.147
  218.5 0.2 convolution_add_fusion.8
  219.3 0.6 copy-done
  220.0 0.0 reduce-scatter.8.cloned.1.call-update
  220.0 32.3 %reduce-scatter.8.cloned.1.call-done = f32[64,256]{1,0:T(8,128)} async-done(((f32[128,256]{1,0:T(8,128)}), f32[64,256]{1,0:T(8,128)}) %reduce-scatter.8.cloned.1.call-update) | async-done | bytes 65552 | tf_op jit(solution)/shard_map/reduce_scatter | solution.py:53
  252.3 1.1 convolution_bitcast_fusion
  253.4 0.7 maximum_bitcast_fusion
  (21 shorter events, 0.3 us)
Async XLA Ops:
  34.5 12.2 %all-to-all-start = ((bf16[8,2,64,256]{3,2,0,1:T(8,128)(2,1)}), bf16[8,2,64,256]{3,2,0,1:T(8,128)(2,1)S(1)}, u32[]{:S(2)}, u32[]{:S(2)}) async-start(bf16[8,2,64,256]{3,2,0,1:T(8,128)(2,1)} %copy.11), calls=%async_computation | async-start | bytes 1048576 | tf_op jit(solution)/shard_map/all_to_all | solution.py:67
  38.0 3.6 %copy-start.5 = (s32[3,1,1]{0,2,1:T(1,128)S(1)}, s32[3,1,1]{0,2,1:T(1,128)}, u32[]{:S(2)}) copy-start(s32[3,1,1]{0,2,1:T(1,128)} %param.21) | copy-start | bytes 40
  38.0 4.2 %copy-start.6 = (s32[3,1,1,8]{3,2,1,0:T(1,128)S(1)}, s32[3,1,1,8]{3,2,1,0:T(1,128)}, u32[]{:S(2)}) copy-start(s32[3,1,1,8]{3,2,1,0:T(1,128)} %param.20) | copy-start | bytes 292
  38.0 56.4 %reduce-scatter.4.cloned.1.call-start = ((), (), s32[]{:S(2)}) async-start(), calls=%async_computation.6 | async-start | bytes 196608 | tf_op jit(solution)/shard_map/reduce_scatter | solution.py:53
  47.0 6.4 %copy-start.3 = (f32[4,1,128,256]{3,2,1,0:T(8,128)S(1)}, f32[4,1,128,256]{3,2,1,0:T(8,128)}, u32[]{:S(2)}) copy-start(f32[4,1,128,256]{3,2,1,0:T(8,128)} %param.17) | copy-start | bytes 1572868
  52.7 0.7 copy-start.1
  119.2 12.2 %all-to-all-start.1 = ((bf16[8,2,64,256]{3,2,0,1:T(8,128)(2,1)}), bf16[8,2,64,256]{3,2,0,1:T(8,128)(2,1)S(1)}, u32[]{:S(2)}, u32[]{:S(2)}) async-start(bf16[8,2,64,256]{3,2,0,1:T(8,128)(2,1)} %copy.13), calls=%async_computation.2 | async-start | bytes 1048576 | tf_op jit(solution)/shard_map/all_to_all | solution.py:67
  122.7 54.9 %reduce-scatter.6.cloned.1.call-start = ((), (), s32[]{:S(2)}) async-start(), calls=%async_computation.7 | async-start | bytes 196608 | tf_op jit(solution)/shard_map/reduce_scatter | solution.py:53
  152.1 0.7 copy-start.2
  202.4 12.2 %all-to-all-start.2 = ((bf16[8,2,64,256]{3,2,0,1:T(8,128)(2,1)}), bf16[8,2,64,256]{3,2,0,1:T(8,128)(2,1)S(1)}, u32[]{:S(2)}, u32[]{:S(2)}) async-start(bf16[8,2,64,256]{3,2,0,1:T(8,128)(2,1)} %copy.15), calls=%async_computation.4 | async-start | bytes 1048576 | tf_op jit(solution)/shard_map/all_to_all | solution.py:67
  205.8 46.5 %reduce-scatter.8.cloned.1.call-start = ((), (), s32[]{:S(2)}) async-start(), calls=%async_computation.8 | async-start | bytes 196608 | tf_op jit(solution)/shard_map/reduce_scatter | solution.py:53
  214.7 38.7 %copy-start.4 = (f32[64,256]{1,0:T(8,128)S(1)}, f32[64,256]{1,0:T(8,128)}, u32[]{:S(2)}) copy-start(f32[64,256]{1,0:T(8,128)} %get-tuple-element.426) | copy-start | bytes 196612
  219.3 0.7 copy-start
Sparse Core Ops, SparseCore 0:
  53.5 40.8 reduce-scatter.3
  152.9 24.6 reduce-scatter.5
  220.1 32.1 reduce-scatter.7
where the time goes:
time: 262 us; the launch traced here: 261 us
  waiting for transfers between devices  120 us (46%)
  blocking collectives  70.3 us (27%)
  loops' own time  21.5 us (8%)
  local copies, waits for them, and re-layouts  13.6 us (5%)
  between operations  13.3 us (5%)
  starting transfers between devices  10.6 us (4%)
  matrix products  10.5 us (4%)
    reduce_scatter x3, waiting for transfers between devices, shards(): lax.psum_scatter(partials[level_index], 'cols', scatter_dimension=0, tile...  98.1 us
    all_gather x3, blocking collectives, shards(): lax.all_gather(own_solution.astype(jnp.bfloat16)[None], 'rows', axis=0, t...  70.3 us
    all_to_all x3, waiting for transfers between devices, shards(): lax.all_to_all(grouped, 'cols', split_axis=1, concat_axis=2, tiled=True)  21.9 us
    another operation x3, loops' own time, slot_sum(): return lax.fori_loop(0, live_count, add_block, running)  21.5 us
    all_to_all x3, starting transfers between devices, shards(): lax.all_to_all(grouped, 'cols', split_axis=1, concat_axis=2, tiled=True)  10.5 us
    dot_general x6, matrix products, add_block(): jnp.dot(solved_piece, factor_piece, preferred_element_type=jnp.float32)  5.58 us
  transfers between devices with their start and end apart: 6, of which 6 were waited for; matrix products, arithmetic and copies ran while one was open for 2% of the time, Pallas kernels for 0%

commit v1 on v0

v1 whole, which is shorter than its diff:
```python
import functools

import jax
import jax.numpy as jnp
from jax import lax
from jax.experimental import pallas as pl
from jax.experimental.pallas import tpu as pltpu
from jax.sharding import PartitionSpec as P


def level_kernel(groups, ids_ref, counts_ref, store_ref, *refs):
    factor_refs = refs[:groups]
    rhs_ref, inverse_ref, out_ref, rounded_ref, gathered = refs[groups:]
    slots, width = factor_refs[0].shape[0], factor_refs[0].shape[1]
    update = None
    for g in range(groups):
        for k in range(slots):
            piece = store_ref[ids_ref[g, k]]
            live = jnp.where(k < counts_ref[g], 1.0, 0.0).astype(piece.dtype)
            gathered[:, k * width:(k + 1) * width] = piece * live
        term = jnp.dot(
            gathered[...],
            factor_refs[g][...].reshape(slots * width, width),
            preferred_element_type=jnp.float32,
        )
        update = term if update is None else update + term
    reduced = (rhs_ref[...] - update).astype(jnp.bfloat16)
    solved = jnp.dot(reduced, inverse_ref[...], preferred_element_type=jnp.float32)
    out_ref[...] = solved
    rounded_ref[...] = solved.astype(jnp.bfloat16)


def solve_level(ids, counts, store, factors, rhs, inverse):
    groups = len(factors)
    rows, width = rhs.shape
    slots = factors[0].shape[0]
    vmem = pl.BlockSpec(memory_space=pltpu.VMEM)
    smem = pl.BlockSpec(memory_space=pltpu.SMEM)
    return pl.pallas_call(
        functools.partial(level_kernel, groups),
        out_shape=(
            jax.ShapeDtypeStruct((rows, width), jnp.float32),
            jax.ShapeDtypeStruct((rows, width), jnp.bfloat16),
        ),
        in_specs=[smem, smem, vmem] + [vmem] * groups + [vmem, vmem],
        out_specs=(vmem, vmem),
        scratch_shapes=[pltpu.VMEM((rows, slots * width), jnp.bfloat16)],
        compiler_params=pltpu.CompilerParams(vmem_limit_bytes=32 * 1024 * 1024),
        cost_estimate=pl.CostEstimate(
            flops=2 * rows * width * width * (groups * slots + 1),
            bytes_accessed=groups * slots * width * width * 2,
            transcendentals=0,
        ),
    )(ids, counts, store, *factors, rhs, inverse)


def shards(right_sides, factor_blocks, diag_inverses, source_ids, block_counts):
    col_count = lax.axis_size("cols")
    level_count, _, rhs_count, width = right_sides.shape
    share_rows = rhs_count // col_count
    col_index = lax.axis_index("cols")

    described = jnp.concatenate([source_ids[:, 0, 0], block_counts[:, 0, 0][:, None]], axis=1)
    factors = [[factor_blocks[l, 0, 0]] for l in range(level_count - 1)]
    descriptions = [described]
    for shift in range(1, col_count):
        pairs = [(i, (i + shift) % col_count) for i in range(col_count)]
        descriptions.append(lax.ppermute(described, "cols", pairs))
    for l in range(level_count - 1):
        for shift in range(1, col_count):
            pairs = [(i, (i + shift) % col_count) for i in range(col_count)]
            factors[l].append(lax.ppermute(factor_blocks[l, 0, 0], "cols", pairs))
    descriptions = jnp.stack(descriptions)

    rhs = lax.dynamic_slice_in_dim(right_sides[:, 0], col_index * share_rows, share_rows, 1)
    solutions = []
    stores = []
    for l in range(level_count):
        if l == 0:
            own = jnp.dot(
                rhs[0].astype(jnp.bfloat16), diag_inverses[0, 0], preferred_element_type=jnp.float32
            )
            rounded = own.astype(jnp.bfloat16)
        else:
            ids = descriptions[:, l - 1, :-1]
            counts = descriptions[:, l - 1, -1]
            store = stores[0] if l == 1 else jnp.concatenate(stores, axis=0)
            own, rounded = solve_level(ids, counts, store, factors[l - 1], rhs[l], diag_inverses[l, 0])
        solutions.append(own)
        if l < level_count - 1:
            stores.append(lax.all_gather(rounded, "rows", axis=0))
    return jnp.stack(solutions)[:, None]


def solution(mesh):
    return jax.shard_map(
        shards,
        mesh=mesh,
        in_specs=(
            P(None, "rows", None, None),
            P(None, "rows", "cols", None, None, None),
            P(None, "rows", None, None),
            P(None, "rows", "cols", None),
            P(None, "rows", "cols"),
        ),
        out_specs=P(None, "rows", "cols", None),
        check_vma=False,
    )
```

time: 262 us -> 84 us (0.32)
  waiting for transfers between devices: 120 us -> 0.01 us
  loops' own time: 21.5 us -> 0 us
  between operations: 13.3 us -> 0.08 us
  matrix products: 10.5 us -> 1.74 us
  local copies, waits for them, and re-layouts: 13.6 us -> 5.46 us
  blocking collectives: 70.3 us -> 63.6 us
  Pallas kernels: 0 us -> 6.3 us
  starting transfers between devices: 10.6 us -> 5.13 us
    reduce_scatter x3 -> x0, waiting for transfers between devices: 98.1 us -> none  [shards(): lax.psum_scatter(partials[level_index], 'cols', scatter_dimension=0, tile...]
    all_to_all x3 -> x0, waiting for transfers between devices: 21.9 us -> none  [shards(): lax.all_to_all(grouped, 'cols', split_axis=1, concat_axis=2, tiled=True)]
    another operation x3 -> x0, loops' own time: 21.5 us -> none  [slot_sum(): return lax.fori_loop(0, live_count, add_block, running)]
    all_to_all x3 -> x0, starting transfers between devices: 10.5 us -> none  [shards(): lax.all_to_all(grouped, 'cols', split_axis=1, concat_axis=2, tiled=True)]
    dot_general x10 -> x1, matrix products: 10.5 us -> 1.74 us  [shards(): jnp.dot(rhs[0].astype(jnp.bfloat16), diag_inverses[0, 0], preferred_eleme...]
    all_gather x3, blocking collectives: 70.3 us -> 63.6 us  [shards(): stores.append(lax.all_gather(rounded, 'rows', axis=0))]
    pallas_call x0 -> x3, Pallas kernels: none -> 6.3 us  [solve_level(): pl.pallas_call(functools.partial(level_kernel, groups), out_shape=(jax.Sh...]
    ppermute x0 -> x4, starting transfers between devices: none -> 5.13 us  [the longest x1 2.97 us: shards(): descriptions.append(lax.ppermute(described, 'cols', pairs))]
  transfers between devices with their start and end apart: 6 -> 4, of which waited for: 6 -> 0; matrix products, arithmetic and copies ran while one was open for 2% -> 8% of each run, Pallas kernels for 0% -> 5%
where the time goes in v1:
time: 84 us; the launch traced here: 83.7 us
  blocking collectives  63.6 us (76%)
  Pallas kernels  6.3 us (8%)
  local copies, waits for them, and re-layouts  5.46 us (6%)
  starting transfers between devices  5.13 us (6%)
  matrix products  1.74 us (2%)
  other arithmetic  1.4 us (2%)
    all_gather x3, blocking collectives, shards(): stores.append(lax.all_gather(rounded, 'rows', axis=0))  63.6 us
    pallas_call x3, Pallas kernels, solve_level(): pl.pallas_call(functools.partial(level_kernel, groups), out_shape=(jax.Sh...  6.3 us
    ppermute x1, starting transfers between devices, shards(): descriptions.append(lax.ppermute(described, 'cols', pairs))  2.97 us
    ppermute x3, starting transfers between devices, shards(): factors[l].append(lax.ppermute(factor_blocks[l, 0, 0], 'cols', pairs))  2.17 us
    squeeze x1, local copies, waits for them, and re-layouts, shards(): factors = [[factor_blocks[l, 0, 0]] for l in range(level_count - 1)]  2.06 us
    dot_general x1, matrix products, shards(): jnp.dot(rhs[0].astype(jnp.bfloat16), diag_inverses[0, 0], preferred_eleme...  1.74 us
  transfers between devices with their start and end apart: 4, of which 0 were waited for; matrix products, arithmetic and copies ran while one was open for 8% of the time, Pallas kernels for 5%

profile of v1, /device:TPU:0, one launch (start us, length us, event | category | flops | bytes accessed | tf_op | source)
XLA Modules:
  0.0 83.7 jit_solution(7863578600086801090)
XLA Ops:
  0.0 0.7 copy.8
  0.7 0.7 copy.12
  1.4 0.1 pad_add_fusion
  1.5 3.0 %collective-permute-start = (s32[3,9]{1,0:T(4,128)S(1)}, s32[3,9]{1,0:T(4,128)S(1)}, u32[]{:S(2)}, u32[]{:S(2)}) collective-permute-start(s32[3,9]{1,0:T(4,128)S(1)} %pad_add_fusion), channel_id=1, source_target_pairs={{0,1},{1,0},{2,3},{3,2},{4,5},{5,4},{6,7},{7,6},{8,9},{9,8},{10,11... | collective-permute-start | bytes 332 | tf_op jit(solution)/shard_map/ppermute | solution.py:68
  4.5 2.1 %slice_bitcast_fusion = (bf16[8,256,256]{2,1,0:T(8,128)(2,1)S(1)}, bf16[8,256,256]{2,1,0:T(8,128)(2,1)S(1)}, bf16[8,256,256]{2,1,0:T(8,128)(2,1)S(1)}) fusion(bf16[3,1,1,8,256,256]{5,4,3,2,1,0:T(8,128)(2,1)} %param.6), kind=kLoop, calls=%fused_computation.2 | loop fusion | bytes 6291456 | tf_op jit(solution)/shard_map/squeeze | solution.py:64
  6.5 0.1 collective-permute-start.1
  6.6 2.0 %collective-permute-start.2 = (bf16[8,256,256]{2,1,0:T(8,128)(2,1)S(1)}, bf16[8,256,256]{2,1,0:T(8,128)(2,1)}, u32[]{:S(2)}, u32[]{:S(2)}) collective-permute-start(bf16[8,256,256]{2,1,0:T(8,128)(2,1)S(1)} %get-tuple-element.20.refs_0_), channel_id=1, source_target_pairs={{0,1},{1,0},{2,3},{3,2},{4,5},{5,4},{6,7},{7,6},{8,9},{9,8},{10,11... | collective-permute-start | bytes 3145736 | tf_op jit(solution)/shard_map/ppermute | solution.py:72
  8.6 0.1 collective-permute-start.3
  8.7 1.1 %slice_bitcast_fusion.3 = (bf16[256,256]{1,0:T(8,128)(2,1)S(1)}, bf16[256,256]{1,0:T(8,128)(2,1)S(1)}, bf16[256,256]{1,0:T(8,128)(2,1)S(1)}) fusion(bf16[4,1,256,256]{3,2,1,0:T(8,128)(2,1)} %param.7), kind=kLoop, calls=%fused_computation.8 | loop fusion | bytes 786432 | tf_op jit(solution)/shard_map/squeeze | solution.py:88
  9.8 1.7 %fusion.14 = (bf16[64,256]{1,0:T(8,128)(2,1)}, f32[64,256]{1,0:T(8,128)}) fusion(bf16[4,1,256,256]{3,2,1,0:T(8,128)(2,1)} %param.7, f32[4,1,128,256]{3,2,1,0:T(8,128)} %param.5, s32[]{:T(128)S(6)} %select_n.3), kind=kOutput, calls=%fused_computation.39 | convolution fusion | flops 8404992 | bytes 262148 | tf_op jit(solution)/shard_map/dot_general | solution.py:80
  11.5 23.9 %all-gather = bf16[1024,256]{1,0:T(8,128)(2,1)S(1)} all-gather(bf16[64,256]{1,0:T(8,128)(2,1)} %get-tuple-element.30), channel_id=2, replica_groups=mesh['rows'=16,'cols'=2] {'rows'}, dimensions={0}, use_global_device_ids=true | all-gather | bytes 557056 | tf_op jit(solution)/shard_map/all_gather | solution.py:91
  35.4 0.9 %dynamic-slice_bitcast_fusion = (f32[64,256]{1,0:T(8,128)S(1)}, f32[64,256]{1,0:T(8,128)S(1)}, f32[64,256]{1,0:T(8,128)S(1)}) fusion(f32[4,1,128,256]{3,2,1,0:T(8,128)} %param.5, s32[]{:T(128)S(6)} %add.16, s32[]{:T(128)S(6)} %select_n.3, s32[]{:T(128)S(6)} %add.14, s32[]{:T(128)S(6)} %add.11), kind=kLoop, calls=%fused_computation.12 | loop fusion | bytes 393232 | tf_op jit(solution)/shard_map/squeeze | solution.py:88
  36.3 0.1 fusion.15
  36.4 0.0 collective-permute-done
  36.4 0.3 fusion.13
  36.6 0.0 collective-permute-done.1.refs_1_
  36.6 1.9 %shard_map.55 = (f32[64,256]{1,0:T(8,128)S(1)}, bf16[64,256]{1,0:T(8,128)(2,1)S(1)}) custom-call(s32[2,8]{1,0:T(2,128)S(1)} %bitcast.57, s32[2]{0:T(128)S(1)} %get-tuple-element.15.counts_ref, bf16[16,64,256]{2,1,0:T(8,128)(2,1)S(1)} %bitcast.49, bf16[8,256,256]{2,1,0:T(8,128)(2,1)S(1)} %get-tuple-element.19.refs_0_, ...), custom_call_target="tpu_custom_call" | custom-call | flops 142606336 | bytes 2097152 | tf_op jit(solution)/shard_map/pallas_call | solution.py:39
  38.5 19.2 %all-gather.1 = bf16[1024,256]{1,0:T(8,128)(2,1)S(1)} all-gather(bf16[64,256]{1,0:T(8,128)(2,1)S(1)} %get-tuple-element.11), channel_id=3, replica_groups=mesh['rows'=16,'cols'=2] {'rows'}, dimensions={0}, use_global_device_ids=true | all-gather | bytes 557056 | tf_op jit(solution)/shard_map/all_gather | solution.py:91
  57.7 0.1 pad_maximum_fusion.1.store_ref
  57.8 0.0 collective-permute-done.2.refs_1_
  57.8 1.9 %shard_map.56 = (f32[64,256]{1,0:T(8,128)S(1)}, bf16[64,256]{1,0:T(8,128)(2,1)S(1)}) custom-call(s32[2,8]{1,0:T(2,128)S(1)} %bitcast.56, s32[2]{0:T(128)S(1)} %get-tuple-element.16.counts_ref, bf16[32,64,256]{2,1,0:T(8,128)(2,1)S(1)} %pad_maximum_fusion.1.store_ref, bf16[8,256,256]{2,1,0:T(8,128)(2,1)S(1)} %get-tuple-element.20.refs_0_, ...), custom_call_target="tpu_custom_call" | custom-call | flops 142606336 | bytes 2097152 | tf_op jit(solution)/shard_map/pallas_call | solution.py:39
  59.7 20.5 %all-gather.2 = bf16[1024,256]{1,0:T(8,128)(2,1)S(1)} all-gather(bf16[64,256]{1,0:T(8,128)(2,1)S(1)} %get-tuple-element.13), channel_id=4, replica_groups=mesh['rows'=16,'cols'=2] {'rows'}, dimensions={0}, use_global_device_ids=true | all-gather | bytes 557056 | tf_op jit(solution)/shard_map/all_gather | solution.py:91
  80.2 0.2 pad_maximum_fusion.store_ref
  80.4 0.0 collective-permute-done.3.refs_1_
  80.4 0.0 copy-start
  80.4 2.5 %shard_map.57 = (f32[64,256]{1,0:T(8,128)S(1)}, bf16[64,256]{1,0:T(8,128)(2,1)}) custom-call(s32[2,8]{1,0:T(2,128)S(1)} %bitcast.55, s32[2]{0:T(128)S(1)} %get-tuple-element.17.counts_ref, bf16[48,64,256]{2,1,0:T(8,128)(2,1)S(1)} %pad_maximum_fusion.store_ref, bf16[8,256,256]{2,1,0:T(8,128)(2,1)S(1)} %get-tuple-element.18.refs_0_, ...), custom_call_target="tpu_custom_call" | custom-call | flops 142606336 | bytes 2097152 | tf_op jit(solution)/shard_map/pallas_call | solution.py:39
  82.9 0.0 copy-done
  83.0 0.7 maximum_bitcast_fusion
  (1 shorter events, 0.0 us)
Async XLA Ops:
  1.5 34.9 %collective-permute-start = (s32[3,9]{1,0:T(4,128)S(1)}, s32[3,9]{1,0:T(4,128)S(1)}, u32[]{:S(2)}, u32[]{:S(2)}) collective-permute-start(s32[3,9]{1,0:T(4,128)S(1)} %pad_add_fusion), channel_id=1, source_target_pairs={{0,1},{1,0},{2,3},{3,2},{4,5},{5,4},{6,7},{7,6},{8,9},{9,8},{10,11... | collective-permute-start | bytes 332 | tf_op jit(solution)/shard_map/ppermute | solution.py:68
  6.5 30.1 %collective-permute-start.1 = (bf16[8,256,256]{2,1,0:T(8,128)(2,1)S(1)}, bf16[8,256,256]{2,1,0:T(8,128)(2,1)}, u32[]{:S(2)}, u32[]{:S(2)}) collective-permute-start(bf16[8,256,256]{2,1,0:T(8,128)(2,1)S(1)} %get-tuple-element.19.refs_0_), channel_id=1, source_target_pairs={{0,1},{1,0},{2,3},{3,2},{4,5},{5,4},{6,7},{7,6},{8,9},{9,8},{10,11... | collective-permute-start | bytes 3145736 | tf_op jit(solution)/shard_map/ppermute | solution.py:72
  6.6 51.2 %collective-permute-start.2 = (bf16[8,256,256]{2,1,0:T(8,128)(2,1)S(1)}, bf16[8,256,256]{2,1,0:T(8,128)(2,1)}, u32[]{:S(2)}, u32[]{:S(2)}) collective-permute-start(bf16[8,256,256]{2,1,0:T(8,128)(2,1)S(1)} %get-tuple-element.20.refs_0_), channel_id=1, source_target_pairs={{0,1},{1,0},{2,3},{3,2},{4,5},{5,4},{6,7},{7,6},{8,9},{9,8},{10,11... | collective-permute-start | bytes 3145736 | tf_op jit(solution)/shard_map/ppermute | solution.py:72
  8.6 71.8 %collective-permute-start.3 = (bf16[8,256,256]{2,1,0:T(8,128)(2,1)S(1)}, bf16[8,256,256]{2,1,0:T(8,128)(2,1)}, u32[]{:S(2)}, u32[]{:S(2)}) collective-permute-start(bf16[8,256,256]{2,1,0:T(8,128)(2,1)S(1)} %get-tuple-element.18.refs_0_), channel_id=1, source_target_pairs={{0,1},{1,0},{2,3},{3,2},{4,5},{5,4},{6,7},{7,6},{8,9},{9,8},{10,11... | collective-permute-start | bytes 3145736 | tf_op jit(solution)/shard_map/ppermute | solution.py:72
  80.4 2.5 %copy-start = (f32[64,256]{1,0:T(8,128)S(1)}, f32[64,256]{1,0:T(8,128)}, u32[]{:S(2)}) copy-start(f32[64,256]{1,0:T(8,128)} %get-tuple-element.31) | copy-start | bytes 196612

commit v2 on v1

--- a/solution.py
+++ b/solution.py
@@ -7,6 +7,128 @@
 from jax.experimental.pallas import tpu as pltpu
 from jax.sharding import PartitionSpec as P
 
+VMEM_LIMIT = 32 * 1024 * 1024
+
+
+def gather_slots(ids_ref, counts_ref, place, group, store_ref, gathered, slots, width):
+    for k in range(slots):
+        piece = store_ref[place(ids_ref[group, k])]
+        live = jnp.where(k < counts_ref[group], 1.0, 0.0).astype(piece.dtype)
+        gathered[:, k * width:(k + 1) * width] = piece * live
+
+
+def flat_dot(gathered, factor_ref):
+    slots, width = factor_ref.shape[0], factor_ref.shape[1]
+    return jnp.dot(
+        gathered[...],
+        factor_ref[...].reshape(slots * width, width),
+        preferred_element_type=jnp.float32,
+    )
+
+
+def pair_kernel(levels, chips, own_ref, ids_ref, counts_ref, *refs):
+    pieces = refs[:levels * chips]
+    factor_refs = refs[levels * chips:levels * chips + 2]
+    first_ref, second_ref, store, gathered = refs[levels * chips + 2:]
+    slots, width = factor_refs[0].shape[0], factor_refs[0].shape[1]
+    chip, flipped = own_ref[0], own_ref[1]
+    for i, piece in enumerate(pieces):
+        store[i] = piece[...]
+
+    def place(source):
+        level, rest = source // (2 * chips), source % (2 * chips)
+        return level * chips + jnp.bitwise_xor(rest // 2, chip)
+
+    sums = []
+    for g in range(2):
+        gather_slots(ids_ref, counts_ref, place, g, store, gathered, slots, width)
+        sums.append(flat_dot(gathered, factor_refs[g]))
+    first_ref[...] = jnp.where(flipped == 0, sums[0], sums[1])
+    second_ref[...] = jnp.where(flipped == 0, sums[1], sums[0])
+
+
+def pair_sums(own, ids, counts, pieces, factors, chips):
+    rows, width = pieces[0].shape
+    levels = len(pieces) // chips
+    slots = factors[0].shape[0]
+    vmem = pl.BlockSpec(memory_space=pltpu.VMEM)
+    smem = pl.BlockSpec(memory_space=pltpu.SMEM)
+    part = jax.ShapeDtypeStruct((rows, width), jnp.float32)
+    return pl.pallas_call(
+        functools.partial(pair_kernel, levels, chips),
+        out_shape=(part, part),
+        in_specs=[smem] * 3 + [vmem] * (len(pieces) + 2),
+        out_specs=(vmem, vmem),
+        scratch_shapes=[
+            pltpu.VMEM((len(pieces), rows, width), jnp.bfloat16),
+            pltpu.VMEM((rows, slots * width), jnp.bfloat16),
+        ],
+        compiler_params=pltpu.CompilerParams(vmem_limit_bytes=VMEM_LIMIT),
+        cost_estimate=pl.CostEstimate(
+            flops=4 * rows * width * width * slots,
+            bytes_accessed=2 * slots * width * width * 2,
+            transcendentals=0,
+        ),
+    )(own, ids, counts, *pieces, *factors)
+
+
+def paired_shards(row_count, right_sides, factor_blocks, diag_inverses, source_ids, block_counts):
+    level_count, _, rhs_count, width = right_sides.shape
+    share_rows = rhs_count // 2
+    chips = row_count // 2
+    row, col = lax.axis_index("rows"), lax.axis_index("cols")
+    chip, core = row // 2, row % 2
+
+    def over_both(move):
+        pairs = []
+        for j in range(chips):
+            for k in range(2):
+                for c in range(2):
+                    tj, tk, tc = move(j, k, c)
+                    pairs.append(((2 * j + k) * 2 + c, (2 * tj + tk) * 2 + tc))
+        return pairs
+
+    def swap_core(x):
+        return lax.ppermute(x, "rows", [(i, i ^ 1) for i in range(row_count)])
+
+    def spread(x):
+        return [
+            lax.ppermute(x, ("rows", "cols"), over_both(lambda j, k, c, d=d: (j ^ d, c, k)))
+            for d in range(chips)
+        ]
+
+    def collect(first, second):
+        return [
+            lax.ppermute(x, ("rows", "cols"), over_both(lambda j, k, c, e=e: (j, c ^ e, k)))
+            for e, x in enumerate((first, second))
+        ]
+
+    described = jnp.concatenate([source_ids[:, 0, 0], block_counts[:, 0, 0][:, None]], axis=1)
+    descriptions = jnp.stack([described, swap_core(described)])
+    factors = [
+        (factor_blocks[l, 0, 0], swap_core(factor_blocks[l, 0, 0])) for l in range(level_count - 1)
+    ]
+    own = jnp.stack([chip, jnp.bitwise_xor(core, col)]).astype(jnp.int32)
+
+    rhs = lax.dynamic_slice_in_dim(right_sides[:, 0], col * share_rows, share_rows, 1)
+    solutions = []
+    pieces = []
+    for l in range(level_count):
+        reduced = rhs[l]
+        if l > 0:
+            ids = descriptions[:, l - 1, :-1]
+            counts = descriptions[:, l - 1, -1]
+            first, second = pair_sums(own, ids, counts, pieces, factors[l - 1], chips)
+            arrived = collect(first, second)
+            reduced = reduced - (arrived[0] + arrived[1])
+        solved = jnp.dot(
+            reduced.astype(jnp.bfloat16), diag_inverses[l, 0], preferred_element_type=jnp.float32
+        )
+        solutions.append(solved)
+        if l < level_count - 1:
+            pieces += spread(solved.astype(jnp.bfloat16))
+    return jnp.stack(solutions)[:, None]
+
 
 def level_kernel(groups, ids_ref, counts_ref, store_ref, *refs):
     factor_refs = refs[:groups]
@@ -14,15 +136,8 @@
     slots, width = factor_refs[0].shape[0], factor_refs[0].shape[1]
     update = None
     for g in range(groups):
-        for k in range(slots):
-            piece = store_ref[ids_ref[g, k]]
-            live = jnp.where(k < counts_ref[g], 1.0, 0.0).astype(piece.dtype)
-            gathered[:, k * width:(k + 1) * width] = piece * live
-        term = jnp.dot(
-            gathered[...],
-            factor_refs[g][...].reshape(slots * width, width),
-            preferred_element_type=jnp.float32,
-        )
+        gather_slots(ids_ref, counts_ref, lambda s: s, g, store_ref, gathered, slots, width)
+        term = flat_dot(gathered, factor_refs[g])
         update = term if update is None else update + term
     reduced = (rhs_ref[...] - update).astype(jnp.bfloat16)
     solved = jnp.dot(reduced, inverse_ref[...], preferred_element_type=jnp.float32)
@@ -45,7 +160,7 @@
         in_specs=[smem, smem, vmem] + [vmem] * groups + [vmem, vmem],
         out_specs=(vmem, vmem),
         scratch_shapes=[pltpu.VMEM((rows, slots * width), jnp.bfloat16)],
-        compiler_params=pltpu.CompilerParams(vmem_limit_bytes=32 * 1024 * 1024),
+        compiler_params=pltpu.CompilerParams(vmem_limit_bytes=VMEM_LIMIT),
         cost_estimate=pl.CostEstimate(
             flops=2 * rows * width * width * (groups * slots + 1),
             bytes_accessed=groups * slots * width * width * 2,
@@ -54,8 +169,7 @@
     )(ids, counts, store, *factors, rhs, inverse)
 
 
-def shards(right_sides, factor_blocks, diag_inverses, source_ids, block_counts):
-    col_count = lax.axis_size("cols")
+def rotated_shards(col_count, right_sides, factor_blocks, diag_inverses, source_ids, block_counts):
     level_count, _, rhs_count, width = right_sides.shape
     share_rows = rhs_count // col_count
     col_index = lax.axis_index("cols")
@@ -93,6 +207,12 @@
 
 
 def solution(mesh):
+    row_count, col_count = mesh.shape["rows"], mesh.shape["cols"]
+    chips = row_count // 2
+    if col_count == 2 and row_count == 2 * chips and chips & (chips - 1) == 0:
+        shards = functools.partial(paired_shards, row_count)
+    else:
+        shards = functools.partial(rotated_shards, col_count)
     return jax.shard_map(
         shards,
         mesh=mesh,

time: 84 us -> 102 us (1.21)
  blocking collectives: 63.6 us -> 0 us
  starting transfers between devices: 5.13 us -> 61.4 us
  waiting for transfers between devices: 0.01 us -> 25.9 us
  matrix products: 1.74 us -> 5 us
  local copies, waits for them, and re-layouts: 5.46 us -> 2.26 us
    all_gather x3 -> x0, blocking collectives: 63.6 us -> none  [shards(): stores.append(lax.all_gather(rounded, 'rows', axis=0))]
    ppermute x4 -> x34, starting transfers between devices: 5.13 us -> 61.4 us  [the longest x24 40 us: spread(): lax.ppermute(x, ('rows', 'cols'), over_both(lambda j, k, c, d=d: (j ^ d,...]
    ppermute x4 -> x34, waiting for transfers between devices: 0.01 us -> 25.9 us  [the longest x24 13.1 us: spread(): lax.ppermute(x, ('rows', 'cols'), over_both(lambda j, k, c, d=d: (j ^ d,...]
    dot_general x1 -> x4, matrix products: 1.74 us -> 5 us  [paired_shards(): jnp.dot(reduced.astype(jnp.bfloat16), diag_inverses[l, 0], preferred_elem...]
    squeeze x3 -> x1, local copies, waits for them, and re-layouts: 4.03 us -> 2.16 us  [paired_shards(): factor_blocks[l, 0, 0]]
  transfers between devices with their start and end apart: 4 -> 34, of which waited for: 0 -> 10; matrix products, arithmetic and copies ran while one was open for 8% -> 4% of each run, Pallas kernels for 5% -> 4%
where the time goes in v2:
time: 102 us
  starting transfers between devices  61.4 us (60%)
  waiting for transfers between devices  25.9 us (25%)
  Pallas kernels  5.87 us (6%)
  matrix products  5 us (5%)
  local copies, waits for them, and re-layouts  2.26 us (2%)
  other arithmetic  1.22 us (1%)
    ppermute x24, starting transfers between devices, spread(): lax.ppermute(x, ('rows', 'cols'), over_both(lambda j, k, c, d=d: (j ^ d,...  40 us
    ppermute x6, starting transfers between devices, collect(): lax.ppermute(x, ('rows', 'cols'), over_both(lambda j, k, c, e=e: (j, c ^...  17.1 us
    ppermute x24, waiting for transfers between devices, spread(): lax.ppermute(x, ('rows', 'cols'), over_both(lambda j, k, c, d=d: (j ^ d,...  13.1 us
    ppermute x6, waiting for transfers between devices, collect(): lax.ppermute(x, ('rows', 'cols'), over_both(lambda j, k, c, e=e: (j, c ^...  12 us
    pallas_call x3, Pallas kernels, pair_sums(): pl.pallas_call(functools.partial(pair_kernel, levels, chips), out_shape=(...  5.87 us
    dot_general x4, matrix products, paired_shards(): jnp.dot(reduced.astype(jnp.bfloat16), diag_inverses[l, 0], preferred_elem...  5 us
    ppermute x4, starting transfers between devices, swap_core(): return lax.ppermute(x, 'rows', [(i, i ^ 1) for i in range(row_count)])  4.3 us
    squeeze x1, local copies, waits for them, and re-layouts, paired_shards(): factor_blocks[l, 0, 0]  2.16 us
  transfers between devices with their start and end apart: 34, of which 10 were waited for; matrix products, arithmetic and copies ran while one was open for 4% of the time, Pallas kernels for 4%

profile of v2, /device:TPU:0, one launch (start us, length us, event | category | flops | bytes accessed | tf_op | source)
XLA Modules:
  0.0 101.8 jit_solution(2778812947462865828)
XLA Ops:
  0.0 2.2 %slice_bitcast_fusion = (bf16[8,256,256]{2,1,0:T(8,128)(2,1)S(1)}, bf16[8,256,256]{2,1,0:T(8,128)(2,1)S(1)}, bf16[8,256,256]{2,1,0:T(8,128)(2,1)S(1)}) fusion(bf16[3,1,1,8,256,256]{5,4,3,2,1,0:T(8,128)(2,1)} %param.6), kind=kLoop, calls=%fused_computation.1 | loop fusion | bytes 6291456 | tf_op jit(solution)/shard_map/squeeze | solution.py:109
  2.2 0.5 collective-permute-start.9
  2.8 1.7 %fusion.34 = (bf16[64,256]{1,0:T(8,128)(2,1)S(1)}, f32[64,256]{1,0:T(8,128)}) fusion(bf16[4,1,256,256]{3,2,1,0:T(8,128)(2,1)} %param.7, f32[4,1,128,256]{3,2,1,0:T(8,128)} %param.5, s32[]{:T(128)S(6)} %select_n.14), kind=kOutput, calls=%fused_computation.53 | convolution fusion | flops 8404992 | bytes 262148 | tf_op jit(solution)/shard_map/dot_general | solution.py:124
  4.5 0.7 collective-permute-start.1
  5.2 3.0 %collective-permute-start.2 = (bf16[64,256]{1,0:T(8,128)(2,1)S(1)}, bf16[64,256]{1,0:T(8,128)(2,1)S(1)}, u32[]{:S(2)}, u32[]{:S(2)}) collective-permute-start(bf16[64,256]{1,0:T(8,128)(2,1)S(1)} %get-tuple-element.26), channel_id=1, source_target_pairs={{0,4},{1,6},{2,5},{3,7},{4,0},{5,2},{6,1},{7,3},{8,12},{9,14},{10,... | collective-permute-start | bytes 98312 | tf_op jit(solution)/shard_map/ppermute | solution.py:96
  8.3 2.5 %collective-permute-start = (s32[3,9]{1,0:T(4,128)S(1)}, s32[3,9]{1,0:T(4,128)S(1)}, u32[]{:S(2)}, u32[]{:S(2)}) collective-permute-start(s32[3,9]{1,0:T(4,128)S(1)} %pad_add_fusion), channel_id=1, source_target_pairs={{0,2},{2,0},{4,6},{6,4},{8,10},{10,8},{12,14},{14,12},{16,18},{18,... | collective-permute-start | bytes 332 | tf_op jit(solution)/shard_map/ppermute | solution.py:92
  10.8 0.8 collective-permute-done
  11.6 1.6 %collective-permute-start.3 = (bf16[64,256]{1,0:T(8,128)(2,1)S(1)}, bf16[64,256]{1,0:T(8,128)(2,1)S(1)}, u32[]{:S(2)}, u32[]{:S(2)}) collective-permute-start(bf16[64,256]{1,0:T(8,128)(2,1)S(1)} %get-tuple-element.26), channel_id=1, source_target_pairs={{0,8},{1,10},{2,9},{3,11},{4,12},{5,14},{6,13},{7,15},{8,0},{9,2},... | collective-permute-start | bytes 98312 | tf_op jit(solution)/shard_map/ppermute | solution.py:96
  13.5 1.2 %collective-permute-start.31 = (bf16[8,256,256]{2,1,0:T(8,128)(2,1)S(1)}, bf16[8,256,256]{2,1,0:T(8,128)(2,1)}, u32[]{:S(2)}, u32[]{:S(2)}) collective-permute-start(bf16[8,256,256]{2,1,0:T(8,128)(2,1)S(1)} %get-tuple-element.20.refs_24_), channel_id=1, source_target_pairs={{0,2},{2,0},{4,6},{6,4},{8,10},{10,8},{12,14},{14,12},{16,18},{18,... | collective-permute-start | bytes 3145736 | tf_op jit(solution)/shard_map/ppermute | solution.py:92
  14.8 0.8 collective-permute-done.3.refs_2_
  15.6 2.6 %collective-permute-start.5 = (bf16[64,256]{1,0:T(8,128)(2,1)S(1)}, bf16[64,256]{1,0:T(8,128)(2,1)S(1)}, u32[]{:S(2)}, u32[]{:S(2)}) collective-permute-start(bf16[64,256]{1,0:T(8,128)(2,1)S(1)} %get-tuple-element.26), channel_id=1, source_target_pairs={{0,16},{1,18},{2,17},{3,19},{4,20},{5,22},{6,21},{7,23},{8,24},{9,... | collective-permute-start | bytes 98312 | tf_op jit(solution)/shard_map/ppermute | solution.py:96
  18.2 2.5 %collective-permute-start.6 = (bf16[64,256]{1,0:T(8,128)(2,1)S(1)}, bf16[64,256]{1,0:T(8,128)(2,1)S(1)}, u32[]{:S(2)}, u32[]{:S(2)}) collective-permute-start(bf16[64,256]{1,0:T(8,128)(2,1)S(1)} %get-tuple-element.26), channel_id=1, source_target_pairs={{0,20},{1,22},{2,21},{3,23},{4,16},{5,18},{6,17},{7,19},{8,28},{9,... | collective-permute-start | bytes 98312 | tf_op jit(solution)/shard_map/ppermute | solution.py:96
  20.8 3.5 %collective-permute-start.7 = (bf16[64,256]{1,0:T(8,128)(2,1)S(1)}, bf16[64,256]{1,0:T(8,128)(2,1)S(1)}, u32[]{:S(2)}, u32[]{:S(2)}) collective-permute-start(bf16[64,256]{1,0:T(8,128)(2,1)S(1)} %get-tuple-element.26), channel_id=1, source_target_pairs={{0,24},{1,26},{2,25},{3,27},{4,28},{5,30},{6,29},{7,31},{8,16},{9,... | collective-permute-start | bytes 98312 | tf_op jit(solution)/shard_map/ppermute | solution.py:96
  24.2 2.2 %collective-permute-start.8 = (bf16[64,256]{1,0:T(8,128)(2,1)S(1)}, bf16[64,256]{1,0:T(8,128)(2,1)S(1)}, u32[]{:S(2)}, u32[]{:S(2)}) collective-permute-start(bf16[64,256]{1,0:T(8,128)(2,1)S(1)} %get-tuple-element.26), channel_id=1, source_target_pairs={{0,28},{1,30},{2,29},{3,31},{4,24},{5,26},{6,25},{7,27},{8,20},{9,... | collective-permute-start | bytes 98312 | tf_op jit(solution)/shard_map/ppermute | solution.py:96
  26.7 4.1 %collective-permute-done.8.refs_7_ = bf16[64,256]{1,0:T(8,128)(2,1)S(1)} collective-permute-done((bf16[64,256]{1,0:T(8,128)(2,1)S(1)}, bf16[64,256]{1,0:T(8,128)(2,1)S(1)}, u32[]{:S(2)}, u32[]{:S(2)}) %collective-permute-start.8) | collective-permute-done | bytes 32800 | tf_op jit(solution)/shard_map/ppermute | solution.py:96
  30.8 2.4 %shard_map.55 = (f32[64,256]{1,0:T(8,128)}, f32[64,256]{1,0:T(8,128)S(1)}) custom-call(s32[2]{0:T(128)S(1)} %pad_add_fusion.2.own_ref, s32[2,8]{1,0:T(2,128)S(1)} %bitcast.77, s32[2]{0:T(128)S(1)} %get-tuple-element.18.counts_ref, bf16[64,256]{1,0:T(8,128)(2,1)S(1)} %collective-permute-done.1.refs_0_, bf16[64,256]{1,0:T(8,128)(2,1)S(1)} %collective-permute-done.2.refs_1_, ...), custom_call_target="tpu_custom_call" | custom-call | flops 134217728 | bytes 2097152 | tf_op jit(solution)/shard_map/pallas_call | solution.py:57
  33.2 1.5 %collective-permute-start.10 = (f32[64,256]{1,0:T(8,128)}, f32[64,256]{1,0:T(8,128)S(1)}, u32[]{:S(2)}, u32[]{:S(2)}) collective-permute-start(f32[64,256]{1,0:T(8,128)} %get-tuple-element.11), channel_id=1, source_target_pairs={{0,0},{1,2},{2,1},{3,3},{4,4},{5,6},{6,5},{7,7},{8,8},{9,10},{10,9... | collective-permute-start | bytes 196616 | tf_op jit(solution)/shard_map/ppermute | solution.py:102
  34.7 3.5 %collective-permute-start.11 = (f32[64,256]{1,0:T(8,128)S(1)}, f32[64,256]{1,0:T(8,128)S(1)}, u32[]{:S(2)}, u32[]{:S(2)}) collective-permute-start(f32[64,256]{1,0:T(8,128)S(1)} %get-tuple-element.12), channel_id=1, source_target_pairs={{0,2},{1,0},{2,3},{3,1},{4,6},{5,4},{6,7},{7,5},{8,10},{9,8},{10,1... | collective-permute-start | bytes 196616 | tf_op jit(solution)/shard_map/ppermute | solution.py:102
  38.2 4.1 %collective-permute-done.11 = f32[64,256]{1,0:T(8,128)S(1)} collective-permute-done((f32[64,256]{1,0:T(8,128)S(1)}, f32[64,256]{1,0:T(8,128)S(1)}, u32[]{:S(2)}, u32[]{:S(2)}) %collective-permute-start.11) | collective-permute-done | bytes 65568 | tf_op jit(solution)/shard_map/ppermute | solution.py:102
  42.2 1.1 %fusion.35 = (bf16[64,256]{1,0:T(8,128)(2,1)S(1)}, f32[64,256]{1,0:T(8,128)S(1)}) fusion(bf16[4,1,256,256]{3,2,1,0:T(8,128)(2,1)} %param.7, f32[4,1,128,256]{3,2,1,0:T(8,128)} %param.5, s32[]{:T(128)S(6)} %add.28, s32[]{:T(128)S(6)} %select_n.14, f32[64,256]{1,0:T(8,128)S(1)} %collective-permute-done.10, f32[64,256]{1,0:T(8,128)S(1)} %collective-permute-done.11), kind=kOutput, calls=%fused_computation.54 | convolution fusion | flops 8454144 | bytes 425992 | tf_op jit(solution)/shard_map/dot_general | solution.py:124
  43.3 0.7 collective-permute-start.12
  44.0 0.5 collective-permute-start.13
  44.5 3.0 %collective-permute-start.15 = (bf16[64,256]{1,0:T(8,128)(2,1)S(1)}, bf16[64,256]{1,0:T(8,128)(2,1)S(1)}, u32[]{:S(2)}, u32[]{:S(2)}) collective-permute-start(bf16[64,256]{1,0:T(8,128)(2,1)S(1)} %get-tuple-element.28), channel_id=1, source_target_pairs={{0,12},{1,14},{2,13},{3,15},{4,8},{5,10},{6,9},{7,11},{8,4},{9,6},... | collective-permute-start | bytes 98312 | tf_op jit(solution)/shard_map/ppermute | solution.py:96
  47.6 1.2 %collective-permute-start.16 = (bf16[64,256]{1,0:T(8,128)(2,1)S(1)}, bf16[64,256]{1,0:T(8,128)(2,1)S(1)}, u32[]{:S(2)}, u32[]{:S(2)}) collective-permute-start(bf16[64,256]{1,0:T(8,128)(2,1)S(1)} %get-tuple-element.28), channel_id=1, source_target_pairs={{0,16},{1,18},{2,17},{3,19},{4,20},{5,22},{6,21},{7,23},{8,24},{9,... | collective-permute-start | bytes 98312 | tf_op jit(solution)/shard_map/ppermute | solution.py:96
  48.8 1.6 %collective-permute-start.17 = (bf16[64,256]{1,0:T(8,128)(2,1)S(1)}, bf16[64,256]{1,0:T(8,128)(2,1)S(1)}, u32[]{:S(2)}, u32[]{:S(2)}) collective-permute-start(bf16[64,256]{1,0:T(8,128)(2,1)S(1)} %get-tuple-element.28), channel_id=1, source_target_pairs={{0,20},{1,22},{2,21},{3,23},{4,16},{5,18},{6,17},{7,19},{8,28},{9,... | collective-permute-start | bytes 98312 | tf_op jit(solution)/shard_map/ppermute | solution.py:96
  50.4 2.0 %collective-permute-start.18 = (bf16[64,256]{1,0:T(8,128)(2,1)S(1)}, bf16[64,256]{1,0:T(8,128)(2,1)S(1)}, u32[]{:S(2)}, u32[]{:S(2)}) collective-permute-start(bf16[64,256]{1,0:T(8,128)(2,1)S(1)} %get-tuple-element.28), channel_id=1, source_target_pairs={{0,24},{1,26},{2,25},{3,27},{4,28},{5,30},{6,29},{7,31},{8,16},{9,... | collective-permute-start | bytes 98312 | tf_op jit(solution)/shard_map/ppermute | solution.py:96
  52.4 2.8 %collective-permute-start.19 = (bf16[64,256]{1,0:T(8,128)(2,1)S(1)}, bf16[64,256]{1,0:T(8,128)(2,1)S(1)}, u32[]{:S(2)}, u32[]{:S(2)}) collective-permute-start(bf16[64,256]{1,0:T(8,128)(2,1)S(1)} %get-tuple-element.28), channel_id=1, source_target_pairs={{0,28},{1,30},{2,29},{3,31},{4,24},{5,26},{6,25},{7,27},{8,20},{9,... | collective-permute-start | bytes 98312 | tf_op jit(solution)/shard_map/ppermute | solution.py:96
  55.2 1.0 %collective-permute-done.18.refs_14_ = bf16[64,256]{1,0:T(8,128)(2,1)S(1)} collective-permute-done((bf16[64,256]{1,0:T(8,128)(2,1)S(1)}, bf16[64,256]{1,0:T(8,128)(2,1)S(1)}, u32[]{:S(2)}, u32[]{:S(2)}) %collective-permute-start.18) | collective-permute-done | bytes 32800 | tf_op jit(solution)/shard_map/ppermute | solution.py:96
  56.3 2.8 %collective-permute-done.19.refs_15_ = bf16[64,256]{1,0:T(8,128)(2,1)S(1)} collective-permute-done((bf16[64,256]{1,0:T(8,128)(2,1)S(1)}, bf16[64,256]{1,0:T(8,128)(2,1)S(1)}, u32[]{:S(2)}, u32[]{:S(2)}) %collective-permute-start.19) | collective-permute-done | bytes 32800 | tf_op jit(solution)/shard_map/ppermute | solution.py:96
  59.0 1.8 %shard_map.56 = (f32[64,256]{1,0:T(8,128)S(1)}, f32[64,256]{1,0:T(8,128)S(1)}) custom-call(s32[2]{0:T(128)S(1)} %pad_add_fusion.2.own_ref, s32[2,8]{1,0:T(2,128)S(1)} %bitcast.76, s32[2]{0:T(128)S(1)} %get-tuple-element.17.counts_ref, bf16[64,256]{1,0:T(8,128)(2,1)S(1)} %collective-permute-done.1.refs_0_, ...), custom_call_target="tpu_custom_call" | custom-call | flops 134217728 | bytes 2097152 | tf_op jit(solution)/shard_map/pallas_call | solution.py:57
  60.8 0.7 collective-permute-start.21
  61.5 5.5 %collective-permute-start.22 = (f32[64,256]{1,0:T(8,128)S(1)}, f32[64,256]{1,0:T(8,128)S(1)}, u32[]{:S(2)}, u32[]{:S(2)}) collective-permute-start(f32[64,256]{1,0:T(8,128)S(1)} %get-tuple-element.14), channel_id=1, source_target_pairs={{0,2},{1,0},{2,3},{3,1},{4,6},{5,4},{6,7},{7,5},{8,10},{9,8},{10,1... | collective-permute-start | bytes 196616 | tf_op jit(solution)/shard_map/ppermute | solution.py:102
  67.0 4.1 %collective-permute-done.22 = f32[64,256]{1,0:T(8,128)S(1)} collective-permute-done((f32[64,256]{1,0:T(8,128)S(1)}, f32[64,256]{1,0:T(8,128)S(1)}, u32[]{:S(2)}, u32[]{:S(2)}) %collective-permute-start.22) | collective-permute-done | bytes 65568 | tf_op jit(solution)/shard_map/ppermute | solution.py:102
  71.1 1.1 %fusion.36 = (bf16[64,256]{1,0:T(8,128)(2,1)S(1)}, f32[64,256]{1,0:T(8,128)S(1)}) fusion(bf16[4,1,256,256]{3,2,1,0:T(8,128)(2,1)} %param.7, f32[4,1,128,256]{3,2,1,0:T(8,128)} %param.5, s32[]{:T(128)S(6)} %add.31, s32[]{:T(128)S(6)} %select_n.14, f32[64,256]{1,0:T(8,128)S(1)} %collective-permute-done.21, f32[64,256]{1,0:T(8,128)S(1)} %collective-permute-done.22), kind=kOutput, calls=%fused_computation.55 | convolution fusion | flops 8454144 | bytes 425992 | tf_op jit(solution)/shard_map/dot_general | solution.py:124
  72.2 0.7 collective-permute-start.23
  72.9 0.9 collective-permute-start.24
  73.8 2.7 %collective-permute-start.26 = (bf16[64,256]{1,0:T(8,128)(2,1)S(1)}, bf16[64,256]{1,0:T(8,128)(2,1)S(1)}, u32[]{:S(2)}, u32[]{:S(2)}) collective-permute-start(bf16[64,256]{1,0:T(8,128)(2,1)S(1)} %get-tuple-element.30), channel_id=1, source_target_pairs={{0,12},{1,14},{2,13},{3,15},{4,8},{5,10},{6,9},{7,11},{8,4},{9,6},... | collective-permute-start | bytes 98312 | tf_op jit(solution)/shard_map/ppermute | solution.py:96
  76.5 3.2 %collective-permute-start.28 = (bf16[64,256]{1,0:T(8,128)(2,1)S(1)}, bf16[64,256]{1,0:T(8,128)(2,1)S(1)}, u32[]{:S(2)}, u32[]{:S(2)}) collective-permute-start(bf16[64,256]{1,0:T(8,128)(2,1)S(1)} %get-tuple-element.30), channel_id=1, source_target_pairs={{0,20},{1,22},{2,21},{3,23},{4,16},{5,18},{6,17},{7,19},{8,28},{9,... | collective-permute-start | bytes 98312 | tf_op jit(solution)/shard_map/ppermute | solution.py:96
  79.6 1.9 %collective-permute-start.29 = (bf16[64,256]{1,0:T(8,128)(2,1)S(1)}, bf16[64,256]{1,0:T(8,128)(2,1)S(1)}, u32[]{:S(2)}, u32[]{:S(2)}) collective-permute-start(bf16[64,256]{1,0:T(8,128)(2,1)S(1)} %get-tuple-element.30), channel_id=1, source_target_pairs={{0,24},{1,26},{2,25},{3,27},{4,28},{5,30},{6,29},{7,31},{8,16},{9,... | collective-permute-start | bytes 98312 | tf_op jit(solution)/shard_map/ppermute | solution.py:96
  81.6 2.5 %collective-permute-start.30 = (bf16[64,256]{1,0:T(8,128)(2,1)S(1)}, bf16[64,256]{1,0:T(8,128)(2,1)S(1)}, u32[]{:S(2)}, u32[]{:S(2)}) collective-permute-start(bf16[64,256]{1,0:T(8,128)(2,1)S(1)} %get-tuple-element.30), channel_id=1, source_target_pairs={{0,28},{1,30},{2,29},{3,31},{4,24},{5,26},{6,25},{7,27},{8,20},{9,... | collective-permute-start | bytes 98312 | tf_op jit(solution)/shard_map/ppermute | solution.py:96
  84.1 1.5 %collective-permute-done.29.refs_22_ = bf16[64,256]{1,0:T(8,128)(2,1)S(1)} collective-permute-done((bf16[64,256]{1,0:T(8,128)(2,1)S(1)}, bf16[64,256]{1,0:T(8,128)(2,1)S(1)}, u32[]{:S(2)}, u32[]{:S(2)}) %collective-permute-start.29) | collective-permute-done | bytes 32800 | tf_op jit(solution)/shard_map/ppermute | solution.py:96
  85.6 2.8 %collective-permute-done.30.refs_23_ = bf16[64,256]{1,0:T(8,128)(2,1)S(1)} collective-permute-done((bf16[64,256]{1,0:T(8,128)(2,1)S(1)}, bf16[64,256]{1,0:T(8,128)(2,1)S(1)}, u32[]{:S(2)}, u32[]{:S(2)}) %collective-permute-start.30) | collective-permute-done | bytes 32800 | tf_op jit(solution)/shard_map/ppermute | solution.py:96
  88.5 1.7 %shard_map.57 = (f32[64,256]{1,0:T(8,128)S(1)}, f32[64,256]{1,0:T(8,128)S(1)}) custom-call(s32[2]{0:T(128)S(1)} %pad_add_fusion.2.own_ref, s32[2,8]{1,0:T(2,128)S(1)} %bitcast.75, s32[2]{0:T(128)S(1)} %get-tuple-element.19.counts_ref, bf16[64,256]{1,0:T(8,128)(2,1)S(1)} %collective-permute-done.1.refs_0_, ...), custom_call_target="tpu_custom_call" | custom-call | flops 134217728 | bytes 2097152 | tf_op jit(solution)/shard_map/pallas_call | solution.py:57
  90.2 0.7 collective-permute-start.32
  90.9 5.3 %collective-permute-start.33 = (f32[64,256]{1,0:T(8,128)S(1)}, f32[64,256]{1,0:T(8,128)S(1)}, u32[]{:S(2)}, u32[]{:S(2)}) collective-permute-start(f32[64,256]{1,0:T(8,128)S(1)} %get-tuple-element.16), channel_id=1, source_target_pairs={{0,2},{1,0},{2,3},{3,1},{4,6},{5,4},{6,7},{7,5},{8,10},{9,8},{10,1... | collective-permute-start | bytes 196616 | tf_op jit(solution)/shard_map/ppermute | solution.py:102
  96.2 3.9 %collective-permute-done.33 = f32[64,256]{1,0:T(8,128)S(1)} collective-permute-done((f32[64,256]{1,0:T(8,128)S(1)}, f32[64,256]{1,0:T(8,128)S(1)}, u32[]{:S(2)}, u32[]{:S(2)}) %collective-permute-start.33) | collective-permute-done | bytes 65568 | tf_op jit(solution)/shard_map/ppermute | solution.py:102
  100.0 1.1 %convolution_bitcast_fusion = f32[1,64,256]{2,1,0:T(8,128)S(1)} fusion(bf16[4,1,256,256]{3,2,1,0:T(8,128)(2,1)} %param.7, f32[4,1,128,256]{3,2,1,0:T(8,128)} %param.5, s32[]{:T(128)S(6)} %add.34, s32[]{:T(128)S(6)} %select_n.14, f32[64,256]{1,0:T(8,128)S(1)} %collective-permute-done.32, f32[64,256]{1,0:T(8,128)S(1)} %collective-permute-done.33), kind=kOutput, calls=%fused_computation | convolution fusion | flops 8437760 | bytes 393224 | tf_op jit(solution)/shard_map/dot_general | solution.py:124
  101.1 0.7 maximum_bitcast_fusion
  (42 shorter events, 1.0 us)
Async XLA Ops:
  0.0 8.1 %copy-start.1 = (s32[3,1,1,8]{3,2,1,0:T(1,128)S(1)}, s32[3,1,1,8]{3,2,1,0:T(1,128)}, u32[]{:S(2)}) copy-start(s32[3,1,1,8]{3,2,1,0:T(1,128)} %param.8) | copy-start | bytes 292
  0.0 8.1 %copy-start.2 = (s32[3,1,1]{0,2,1:T(1,128)S(1)}, s32[3,1,1]{0,2,1:T(1,128)}, u32[]{:S(2)}) copy-start(s32[3,1,1]{0,2,1:T(1,128)} %param.9) | copy-start | bytes 40
  2.2 28.7 %collective-permute-start.9 = (bf16[8,256,256]{2,1,0:T(8,128)(2,1)S(1)}, bf16[8,256,256]{2,1,0:T(8,128)(2,1)}, u32[]{:S(2)}, u32[]{:S(2)}) collective-permute-start(bf16[8,256,256]{2,1,0:T(8,128)(2,1)S(1)} %get-tuple-element.21.refs_8_), channel_id=1, source_target_pairs={{0,2},{2,0},{4,6},{6,4},{8,10},{10,8},{12,14},{14,12},{16,18},{18,... | collective-permute-start | bytes 3145736 | tf_op jit(solution)/shard_map/ppermute | solution.py:92
  2.7 41.8 %collective-permute-start.20 = (bf16[8,256,256]{2,1,0:T(8,128)(2,1)S(1)}, bf16[8,256,256]{2,1,0:T(8,128)(2,1)}, u32[]{:S(2)}, u32[]{:S(2)}) collective-permute-start(bf16[8,256,256]{2,1,0:T(8,128)(2,1)S(1)} %get-tuple-element.22.refs_16_), channel_id=1, source_target_pairs={{0,2},{2,0},{4,6},{6,4},{8,10},{10,8},{12,14},{14,12},{16,18},{18,... | collective-permute-start | bytes 3145736 | tf_op jit(solution)/shard_map/ppermute | solution.py:92
  4.5 8.7 %collective-permute-start.1 = (bf16[64,256]{1,0:T(8,128)(2,1)S(1)}, bf16[64,256]{1,0:T(8,128)(2,1)S(1)}, u32[]{:S(2)}, u32[]{:S(2)}) collective-permute-start(bf16[64,256]{1,0:T(8,128)(2,1)S(1)} %get-tuple-element.26), channel_id=1, source_target_pairs={{0,0},{1,2},{2,1},{3,3},{4,4},{5,6},{6,5},{7,7},{8,8},{9,10},{10,9... | collective-permute-start | bytes 98312 | tf_op jit(solution)/shard_map/ppermute | solution.py:96
  5.2 8.4 %collective-permute-start.2 = (bf16[64,256]{1,0:T(8,128)(2,1)S(1)}, bf16[64,256]{1,0:T(8,128)(2,1)S(1)}, u32[]{:S(2)}, u32[]{:S(2)}) collective-permute-start(bf16[64,256]{1,0:T(8,128)(2,1)S(1)} %get-tuple-element.26), channel_id=1, source_target_pairs={{0,4},{1,6},{2,5},{3,7},{4,0},{5,2},{6,1},{7,3},{8,12},{9,14},{10,... | collective-permute-start | bytes 98312 | tf_op jit(solution)/shard_map/ppermute | solution.py:96
  8.3 3.3 %collective-permute-start = (s32[3,9]{1,0:T(4,128)S(1)}, s32[3,9]{1,0:T(4,128)S(1)}, u32[]{:S(2)}, u32[]{:S(2)}) collective-permute-start(s32[3,9]{1,0:T(4,128)S(1)} %pad_add_fusion), channel_id=1, source_target_pairs={{0,2},{2,0},{4,6},{6,4},{8,10},{10,8},{12,14},{14,12},{16,18},{18,... | collective-permute-start | bytes 332 | tf_op jit(solution)/shard_map/ppermute | solution.py:92
  11.6 3.9 %collective-permute-start.3 = (bf16[64,256]{1,0:T(8,128)(2,1)S(1)}, bf16[64,256]{1,0:T(8,128)(2,1)S(1)}, u32[]{:S(2)}, u32[]{:S(2)}) collective-permute-start(bf16[64,256]{1,0:T(8,128)(2,1)S(1)} %get-tuple-element.26), channel_id=1, source_target_pairs={{0,8},{1,10},{2,9},{3,11},{4,12},{5,14},{6,13},{7,15},{8,0},{9,2},... | collective-permute-start | bytes 98312 | tf_op jit(solution)/shard_map/ppermute | solution.py:96
  13.2 4.9 %collective-permute-start.4 = (bf16[64,256]{1,0:T(8,128)(2,1)S(1)}, bf16[64,256]{1,0:T(8,128)(2,1)S(1)}, u32[]{:S(2)}, u32[]{:S(2)}) collective-permute-start(bf16[64,256]{1,0:T(8,128)(2,1)S(1)} %get-tuple-element.26), channel_id=1, source_target_pairs={{0,12},{1,14},{2,13},{3,15},{4,8},{5,10},{6,9},{7,11},{8,4},{9,6},... | collective-permute-start | bytes 98312 | tf_op jit(solution)/shard_map/ppermute | solution.py:96
  13.5 62.9 %collective-permute-start.31 = (bf16[8,256,256]{2,1,0:T(8,128)(2,1)S(1)}, bf16[8,256,256]{2,1,0:T(8,128)(2,1)}, u32[]{:S(2)}, u32[]{:S(2)}) collective-permute-start(bf16[8,256,256]{2,1,0:T(8,128)(2,1)S(1)} %get-tuple-element.20.refs_24_), channel_id=1, source_target_pairs={{0,2},{2,0},{4,6},{6,4},{8,10},{10,8},{12,14},{14,12},{16,18},{18,... | collective-permute-start | bytes 3145736 | tf_op jit(solution)/shard_map/ppermute | solution.py:92
  15.6 5.2 %collective-permute-start.5 = (bf16[64,256]{1,0:T(8,128)(2,1)S(1)}, bf16[64,256]{1,0:T(8,128)(2,1)S(1)}, u32[]{:S(2)}, u32[]{:S(2)}) collective-permute-start(bf16[64,256]{1,0:T(8,128)(2,1)S(1)} %get-tuple-element.26), channel_id=1, source_target_pairs={{0,16},{1,18},{2,17},{3,19},{4,20},{5,22},{6,21},{7,23},{8,24},{9,... | collective-permute-start | bytes 98312 | tf_op jit(solution)/shard_map/ppermute | solution.py:96
  18.2 6.1 %collective-permute-start.6 = (bf16[64,256]{1,0:T(8,128)(2,1)S(1)}, bf16[64,256]{1,0:T(8,128)(2,1)S(1)}, u32[]{:S(2)}, u32[]{:S(2)}) collective-permute-start(bf16[64,256]{1,0:T(8,128)(2,1)S(1)} %get-tuple-element.26), channel_id=1, source_target_pairs={{0,20},{1,22},{2,21},{3,23},{4,16},{5,18},{6,17},{7,19},{8,28},{9,... | collective-permute-start | bytes 98312 | tf_op jit(solution)/shard_map/ppermute | solution.py:96
  20.8 5.9 %collective-permute-start.7 = (bf16[64,256]{1,0:T(8,128)(2,1)S(1)}, bf16[64,256]{1,0:T(8,128)(2,1)S(1)}, u32[]{:S(2)}, u32[]{:S(2)}) collective-permute-start(bf16[64,256]{1,0:T(8,128)(2,1)S(1)} %get-tuple-element.26), channel_id=1, source_target_pairs={{0,24},{1,26},{2,25},{3,27},{4,28},{5,30},{6,29},{7,31},{8,16},{9,... | collective-permute-start | bytes 98312 | tf_op jit(solution)/shard_map/ppermute | solution.py:96
  24.2 6.6 %collective-permute-start.8 = (bf16[64,256]{1,0:T(8,128)(2,1)S(1)}, bf16[64,256]{1,0:T(8,128)(2,1)S(1)}, u32[]{:S(2)}, u32[]{:S(2)}) collective-permute-start(bf16[64,256]{1,0:T(8,128)(2,1)S(1)} %get-tuple-element.26), channel_id=1, source_target_pairs={{0,28},{1,30},{2,29},{3,31},{4,24},{5,26},{6,25},{7,27},{8,20},{9,... | collective-permute-start | bytes 98312 | tf_op jit(solution)/shard_map/ppermute | solution.py:96
  33.2 5.0 %collective-permute-start.10 = (f32[64,256]{1,0:T(8,128)}, f32[64,256]{1,0:T(8,128)S(1)}, u32[]{:S(2)}, u32[]{:S(2)}) collective-permute-start(f32[64,256]{1,0:T(8,128)} %get-tuple-element.11), channel_id=1, source_target_pairs={{0,0},{1,2},{2,1},{3,3},{4,4},{5,6},{6,5},{7,7},{8,8},{9,10},{10,9... | collective-permute-start | bytes 196616 | tf_op jit(solution)/shard_map/ppermute | solution.py:102
  34.7 7.6 %collective-permute-start.11 = (f32[64,256]{1,0:T(8,128)S(1)}, f32[64,256]{1,0:T(8,128)S(1)}, u32[]{:S(2)}, u32[]{:S(2)}) collective-permute-start(f32[64,256]{1,0:T(8,128)S(1)} %get-tuple-element.12), channel_id=1, source_target_pairs={{0,2},{1,0},{2,3},{3,1},{4,6},{5,4},{6,7},{7,5},{8,10},{9,8},{10,1... | collective-permute-start | bytes 196616 | tf_op jit(solution)/shard_map/ppermute | solution.py:102
  43.3 4.2 %collective-permute-start.12 = (bf16[64,256]{1,0:T(8,128)(2,1)S(1)}, bf16[64,256]{1,0:T(8,128)(2,1)S(1)}, u32[]{:S(2)}, u32[]{:S(2)}) collective-permute-start(bf16[64,256]{1,0:T(8,128)(2,1)S(1)} %get-tuple-element.28), channel_id=1, source_target_pairs={{0,0},{1,2},{2,1},{3,3},{4,4},{5,6},{6,5},{7,7},{8,8},{9,10},{10,9... | collective-permute-start | bytes 98312 | tf_op jit(solution)/shard_map/ppermute | solution.py:96
  44.0 4.8 %collective-permute-start.13 = (bf16[64,256]{1,0:T(8,128)(2,1)S(1)}, bf16[64,256]{1,0:T(8,128)(2,1)S(1)}, u32[]{:S(2)}, u32[]{:S(2)}) collective-permute-start(bf16[64,256]{1,0:T(8,128)(2,1)S(1)} %get-tuple-element.28), channel_id=1, source_target_pairs={{0,4},{1,6},{2,5},{3,7},{4,0},{5,2},{6,1},{7,3},{8,12},{9,14},{10,... | collective-permute-start | bytes 98312 | tf_op jit(solution)/shard_map/ppermute | solution.py:96
  44.5 5.9 %collective-permute-start.14 = (bf16[64,256]{1,0:T(8,128)(2,1)S(1)}, bf16[64,256]{1,0:T(8,128)(2,1)S(1)}, u32[]{:S(2)}, u32[]{:S(2)}) collective-permute-start(bf16[64,256]{1,0:T(8,128)(2,1)S(1)} %get-tuple-element.28), channel_id=1, source_target_pairs={{0,8},{1,10},{2,9},{3,11},{4,12},{5,14},{6,13},{7,15},{8,0},{9,2},... | collective-permute-start | bytes 98312 | tf_op jit(solution)/shard_map/ppermute | solution.py:96
  44.5 7.9 %collective-permute-start.15 = (bf16[64,256]{1,0:T(8,128)(2,1)S(1)}, bf16[64,256]{1,0:T(8,128)(2,1)S(1)}, u32[]{:S(2)}, u32[]{:S(2)}) collective-permute-start(bf16[64,256]{1,0:T(8,128)(2,1)S(1)} %get-tuple-element.28), channel_id=1, source_target_pairs={{0,12},{1,14},{2,13},{3,15},{4,8},{5,10},{6,9},{7,11},{8,4},{9,6},... | collective-permute-start | bytes 98312 | tf_op jit(solution)/shard_map/ppermute | solution.py:96
  47.6 7.7 %collective-permute-start.16 = (bf16[64,256]{1,0:T(8,128)(2,1)S(1)}, bf16[64,256]{1,0:T(8,128)(2,1)S(1)}, u32[]{:S(2)}, u32[]{:S(2)}) collective-permute-start(bf16[64,256]{1,0:T(8,128)(2,1)S(1)} %get-tuple-element.28), channel_id=1, source_target_pairs={{0,16},{1,18},{2,17},{3,19},{4,20},{5,22},{6,21},{7,23},{8,24},{9,... | collective-permute-start | bytes 98312 | tf_op jit(solution)/shard_map/ppermute | solution.py:96
  48.8 6.4 %collective-permute-start.17 = (bf16[64,256]{1,0:T(8,128)(2,1)S(1)}, bf16[64,256]{1,0:T(8,128)(2,1)S(1)}, u32[]{:S(2)}, u32[]{:S(2)}) collective-permute-start(bf16[64,256]{1,0:T(8,128)(2,1)S(1)} %get-tuple-element.28), channel_id=1, source_target_pairs={{0,20},{1,22},{2,21},{3,23},{4,16},{5,18},{6,17},{7,19},{8,28},{9,... | collective-permute-start | bytes 98312 | tf_op jit(solution)/shard_map/ppermute | solution.py:96
  50.4 5.9 %collective-permute-start.18 = (bf16[64,256]{1,0:T(8,128)(2,1)S(1)}, bf16[64,256]{1,0:T(8,128)(2,1)S(1)}, u32[]{:S(2)}, u32[]{:S(2)}) collective-permute-start(bf16[64,256]{1,0:T(8,128)(2,1)S(1)} %get-tuple-element.28), channel_id=1, source_target_pairs={{0,24},{1,26},{2,25},{3,27},{4,28},{5,30},{6,29},{7,31},{8,16},{9,... | collective-permute-start | bytes 98312 | tf_op jit(solution)/shard_map/ppermute | solution.py:96
  52.4 6.6 %collective-permute-start.19 = (bf16[64,256]{1,0:T(8,128)(2,1)S(1)}, bf16[64,256]{1,0:T(8,128)(2,1)S(1)}, u32[]{:S(2)}, u32[]{:S(2)}) collective-permute-start(bf16[64,256]{1,0:T(8,128)(2,1)S(1)} %get-tuple-element.28), channel_id=1, source_target_pairs={{0,28},{1,30},{2,29},{3,31},{4,24},{5,26},{6,25},{7,27},{8,20},{9,... | collective-permute-start | bytes 98312 | tf_op jit(solution)/shard_map/ppermute | solution.py:96
  59.0 42.1 %copy-start = (f32[64,256]{1,0:T(8,128)S(1)}, f32[64,256]{1,0:T(8,128)}, u32[]{:S(2)}) copy-start(f32[64,256]{1,0:T(8,128)} %get-tuple-element.27) | copy-start | bytes 196612
  60.8 6.2 %collective-permute-start.21 = (f32[64,256]{1,0:T(8,128)S(1)}, f32[64,256]{1,0:T(8,128)S(1)}, u32[]{:S(2)}, u32[]{:S(2)}) collective-permute-start(f32[64,256]{1,0:T(8,128)S(1)} %get-tuple-element.13), channel_id=1, source_target_pairs={{0,0},{1,2},{2,1},{3,3},{4,4},{5,6},{6,5},{7,7},{8,8},{9,10},{10,9... | collective-permute-start | bytes 196616 | tf_op jit(solution)/shard_map/ppermute | solution.py:102
  61.5 9.6 %collective-permute-start.22 = (f32[64,256]{1,0:T(8,128)S(1)}, f32[64,256]{1,0:T(8,128)S(1)}, u32[]{:S(2)}, u32[]{:S(2)}) collective-permute-start(f32[64,256]{1,0:T(8,128)S(1)} %get-tuple-element.14), channel_id=1, source_target_pairs={{0,2},{1,0},{2,3},{3,1},{4,6},{5,4},{6,7},{7,5},{8,10},{9,8},{10,1... | collective-permute-start | bytes 196616 | tf_op jit(solution)/shard_map/ppermute | solution.py:102
  72.2 4.2 %collective-permute-start.23 = (bf16[64,256]{1,0:T(8,128)(2,1)S(1)}, bf16[64,256]{1,0:T(8,128)(2,1)S(1)}, u32[]{:S(2)}, u32[]{:S(2)}) collective-permute-start(bf16[64,256]{1,0:T(8,128)(2,1)S(1)} %get-tuple-element.30), channel_id=1, source_target_pairs={{0,0},{1,2},{2,1},{3,3},{4,4},{5,6},{6,5},{7,7},{8,8},{9,10},{10,9... | collective-permute-start | bytes 98312 | tf_op jit(solution)/shard_map/ppermute | solution.py:96
  72.9 6.8 %collective-permute-start.24 = (bf16[64,256]{1,0:T(8,128)(2,1)S(1)}, bf16[64,256]{1,0:T(8,128)(2,1)S(1)}, u32[]{:S(2)}, u32[]{:S(2)}) collective-permute-start(bf16[64,256]{1,0:T(8,128)(2,1)S(1)} %get-tuple-element.30), channel_id=1, source_target_pairs={{0,4},{1,6},{2,5},{3,7},{4,0},{5,2},{6,1},{7,3},{8,12},{9,14},{10,... | collective-permute-start | bytes 98312 | tf_op jit(solution)/shard_map/ppermute | solution.py:96
  73.8 7.8 %collective-permute-start.25 = (bf16[64,256]{1,0:T(8,128)(2,1)S(1)}, bf16[64,256]{1,0:T(8,128)(2,1)S(1)}, u32[]{:S(2)}, u32[]{:S(2)}) collective-permute-start(bf16[64,256]{1,0:T(8,128)(2,1)S(1)} %get-tuple-element.30), channel_id=1, source_target_pairs={{0,8},{1,10},{2,9},{3,11},{4,12},{5,14},{6,13},{7,15},{8,0},{9,2},... | collective-permute-start | bytes 98312 | tf_op jit(solution)/shard_map/ppermute | solution.py:96
  73.8 10.3 %collective-permute-start.26 = (bf16[64,256]{1,0:T(8,128)(2,1)S(1)}, bf16[64,256]{1,0:T(8,128)(2,1)S(1)}, u32[]{:S(2)}, u32[]{:S(2)}) collective-permute-start(bf16[64,256]{1,0:T(8,128)(2,1)S(1)} %get-tuple-element.30), channel_id=1, source_target_pairs={{0,12},{1,14},{2,13},{3,15},{4,8},{5,10},{6,9},{7,11},{8,4},{9,6},... | collective-permute-start | bytes 98312 | tf_op jit(solution)/shard_map/ppermute | solution.py:96
  76.4 7.7 %collective-permute-start.27 = (bf16[64,256]{1,0:T(8,128)(2,1)S(1)}, bf16[64,256]{1,0:T(8,128)(2,1)S(1)}, u32[]{:S(2)}, u32[]{:S(2)}) collective-permute-start(bf16[64,256]{1,0:T(8,128)(2,1)S(1)} %get-tuple-element.30), channel_id=1, source_target_pairs={{0,16},{1,18},{2,17},{3,19},{4,20},{5,22},{6,21},{7,23},{8,24},{9,... | collective-permute-start | bytes 98312 | tf_op jit(solution)/shard_map/ppermute | solution.py:96
  76.5 7.7 %collective-permute-start.28 = (bf16[64,256]{1,0:T(8,128)(2,1)S(1)}, bf16[64,256]{1,0:T(8,128)(2,1)S(1)}, u32[]{:S(2)}, u32[]{:S(2)}) collective-permute-start(bf16[64,256]{1,0:T(8,128)(2,1)S(1)} %get-tuple-element.30), channel_id=1, source_target_pairs={{0,20},{1,22},{2,21},{3,23},{4,16},{5,18},{6,17},{7,19},{8,28},{9,... | collective-permute-start | bytes 98312 | tf_op jit(solution)/shard_map/ppermute | solution.py:96
  79.6 6.0 %collective-permute-start.29 = (bf16[64,256]{1,0:T(8,128)(2,1)S(1)}, bf16[64,256]{1,0:T(8,128)(2,1)S(1)}, u32[]{:S(2)}, u32[]{:S(2)}) collective-permute-start(bf16[64,256]{1,0:T(8,128)(2,1)S(1)} %get-tuple-element.30), channel_id=1, source_target_pairs={{0,24},{1,26},{2,25},{3,27},{4,28},{5,30},{6,29},{7,31},{8,16},{9,... | collective-permute-start | bytes 98312 | tf_op jit(solution)/shard_map/ppermute | solution.py:96
  81.6 6.9 %collective-permute-start.30 = (bf16[64,256]{1,0:T(8,128)(2,1)S(1)}, bf16[64,256]{1,0:T(8,128)(2,1)S(1)}, u32[]{:S(2)}, u32[]{:S(2)}) collective-permute-start(bf16[64,256]{1,0:T(8,128)(2,1)S(1)} %get-tuple-element.30), channel_id=1, source_target_pairs={{0,28},{1,30},{2,29},{3,31},{4,24},{5,26},{6,25},{7,27},{8,20},{9,... | collective-permute-start | bytes 98312 | tf_op jit(solution)/shard_map/ppermute | solution.py:96
  90.2 6.0 %collective-permute-start.32 = (f32[64,256]{1,0:T(8,128)S(1)}, f32[64,256]{1,0:T(8,128)S(1)}, u32[]{:S(2)}, u32[]{:S(2)}) collective-permute-start(f32[64,256]{1,0:T(8,128)S(1)} %get-tuple-element.15), channel_id=1, source_target_pairs={{0,0},{1,2},{2,1},{3,3},{4,4},{5,6},{6,5},{7,7},{8,8},{9,10},{10,9... | collective-permute-start | bytes 196616 | tf_op jit(solution)/shard_map/ppermute | solution.py:102
  90.9 9.1 %collective-permute-start.33 = (f32[64,256]{1,0:T(8,128)S(1)}, f32[64,256]{1,0:T(8,128)S(1)}, u32[]{:S(2)}, u32[]{:S(2)}) collective-permute-start(f32[64,256]{1,0:T(8,128)S(1)} %get-tuple-element.16), channel_id=1, source_target_pairs={{0,2},{1,0},{2,3},{3,1},{4,6},{5,4},{6,7},{7,5},{8,10},{9,8},{10,1... | collective-permute-start | bytes 196616 | tf_op jit(solution)/shard_map/ppermute | solution.py:102

commit v3 on v2

--- a/solution.py
+++ b/solution.py
@@ -26,41 +26,40 @@
     )
 
 
-def pair_kernel(levels, chips, own_ref, ids_ref, counts_ref, *refs):
-    pieces = refs[:levels * chips]
-    factor_refs = refs[levels * chips:levels * chips + 2]
-    first_ref, second_ref, store, gathered = refs[levels * chips + 2:]
-    slots, width = factor_refs[0].shape[0], factor_refs[0].shape[1]
-    chip, flipped = own_ref[0], own_ref[1]
-    for i, piece in enumerate(pieces):
-        store[i] = piece[...]
+def pair_kernel(level, chips, flipped_ref, ids_ref, counts_ref, *refs):
+    store_refs = refs[:level]
+    factor_refs = refs[level:level + 2]
+    kept_ref, other_ref, store, gathered = refs[level + 2:]
+    slots, width = factor_refs[0].shape[3], factor_refs[0].shape[4]
+    for m, piece in enumerate(store_refs):
+        store[m * chips:(m + 1) * chips] = piece[...]
 
     def place(source):
-        level, rest = source // (2 * chips), source % (2 * chips)
-        return level * chips + jnp.bitwise_xor(rest // 2, chip)
+        return source // (2 * chips) * chips + source % (2 * chips) // 2
 
     sums = []
     for g in range(2):
         gather_slots(ids_ref, counts_ref, place, g, store, gathered, slots, width)
-        sums.append(flat_dot(gathered, factor_refs[g]))
-    first_ref[...] = jnp.where(flipped == 0, sums[0], sums[1])
-    second_ref[...] = jnp.where(flipped == 0, sums[1], sums[0])
-
-
-def pair_sums(own, ids, counts, pieces, factors, chips):
-    rows, width = pieces[0].shape
-    levels = len(pieces) // chips
-    slots = factors[0].shape[0]
+        sums.append(flat_dot(gathered, factor_refs[g].at[level - 1, 0, 0]))
+    flipped = flipped_ref[0]
+    kept_ref[...] = jnp.where(flipped == 0, sums[0], sums[1])
+    other_ref[...] = jnp.where(flipped == 0, sums[1], sums[0])
+
+
+def pair_sums(flipped, ids, counts, stores, factors):
+    level = len(stores)
+    chips, rows, width = stores[0].shape
+    slots = factors[0].shape[3]
     vmem = pl.BlockSpec(memory_space=pltpu.VMEM)
     smem = pl.BlockSpec(memory_space=pltpu.SMEM)
     part = jax.ShapeDtypeStruct((rows, width), jnp.float32)
     return pl.pallas_call(
-        functools.partial(pair_kernel, levels, chips),
+        functools.partial(pair_kernel, level, chips),
         out_shape=(part, part),
-        in_specs=[smem] * 3 + [vmem] * (len(pieces) + 2),
+        in_specs=[smem] * 3 + [vmem] * (level + 2),
         out_specs=(vmem, vmem),
         scratch_shapes=[
-            pltpu.VMEM((len(pieces), rows, width), jnp.bfloat16),
+            pltpu.VMEM((level * chips, rows, width), jnp.bfloat16),
             pltpu.VMEM((rows, slots * width), jnp.bfloat16),
         ],
         compiler_params=pltpu.CompilerParams(vmem_limit_bytes=VMEM_LIMIT),
@@ -69,7 +68,7 @@
             bytes_accessed=2 * slots * width * width * 2,
             transcendentals=0,
         ),
-    )(own, ids, counts, *pieces, *factors)
+    )(flipped, ids, counts, *stores, *factors)
 
 
 def paired_shards(row_count, right_sides, factor_blocks, diag_inverses, source_ids, block_counts):
@@ -77,56 +76,73 @@
     share_rows = rhs_count // 2
     chips = row_count // 2
     row, col = lax.axis_index("rows"), lax.axis_index("cols")
-    chip, core = row // 2, row % 2
-
-    def over_both(move):
+    core = row % 2
+    flipped = jnp.bitwise_xor(core, col).astype(jnp.int32)
+    same_core = [[2 * j + k for j in range(chips)] for k in range(2)]
+
+    def over_both(x, move):
         pairs = []
         for j in range(chips):
             for k in range(2):
                 for c in range(2):
                     tj, tk, tc = move(j, k, c)
                     pairs.append(((2 * j + k) * 2 + c, (2 * tj + tk) * 2 + tc))
-        return pairs
+        return lax.ppermute(x, ("rows", "cols"), pairs)
 
     def swap_core(x):
         return lax.ppermute(x, "rows", [(i, i ^ 1) for i in range(row_count)])
 
-    def spread(x):
-        return [
-            lax.ppermute(x, ("rows", "cols"), over_both(lambda j, k, c, d=d: (j ^ d, c, k)))
-            for d in range(chips)
-        ]
-
-    def collect(first, second):
-        return [
-            lax.ppermute(x, ("rows", "cols"), over_both(lambda j, k, c, e=e: (j, c ^ e, k)))
-            for e, x in enumerate((first, second))
-        ]
+    def transpose(x):
+        return over_both(x, lambda j, k, c: (j, c, k))
+
+    def spread(x, level):
+        if level == 1:
+            return lax.all_gather(x, "rows", axis_index_groups=same_core)
+        copies = jnp.broadcast_to(x[None], (chips,) + x.shape)
+        return lax.all_to_all(copies, "rows", 0, 0, axis_index_groups=same_core)
+
+    def half(x, index):
+        return lax.dynamic_slice_in_dim(x, index * share_rows, share_rows, 1)
+
+    rhs = half(right_sides[:, 0], col)
+    solved = jnp.dot(
+        rhs[0].astype(jnp.bfloat16), diag_inverses[0, 0], preferred_element_type=jnp.float32
+    )
+    solutions = [solved]
+    stores = [spread(transpose(solved.astype(jnp.bfloat16)), 0)]
 
     described = jnp.concatenate([source_ids[:, 0, 0], block_counts[:, 0, 0][:, None]], axis=1)
     descriptions = jnp.stack([described, swap_core(described)])
-    factors = [
-        (factor_blocks[l, 0, 0], swap_core(factor_blocks[l, 0, 0])) for l in range(level_count - 1)
-    ]
-    own = jnp.stack([chip, jnp.bitwise_xor(core, col)]).astype(jnp.int32)
-
-    rhs = lax.dynamic_slice_in_dim(right_sides[:, 0], col * share_rows, share_rows, 1)
-    solutions = []
-    pieces = []
-    for l in range(level_count):
-        reduced = rhs[l]
-        if l > 0:
-            ids = descriptions[:, l - 1, :-1]
-            counts = descriptions[:, l - 1, -1]
-            first, second = pair_sums(own, ids, counts, pieces, factors[l - 1], chips)
-            arrived = collect(first, second)
-            reduced = reduced - (arrived[0] + arrived[1])
+    factors = (factor_blocks, swap_core(factor_blocks))
+    inner = slice(1, level_count - 1)
+    inner_rhs = jnp.where(
+        flipped == 0, half(right_sides[inner, 0], core), swap_core(half(right_sides[inner, 0], 1 - core))
+    )
+    inner_inverses = jnp.where(
+        flipped == 0, diag_inverses[inner, 0], swap_core(diag_inverses[inner, 0])
+    )
+
+    for l in range(1, level_count):
+        ids = descriptions[:, l - 1, :-1]
+        counts = descriptions[:, l - 1, -1]
+        kept, other = pair_sums(flipped[None], ids, counts, stores, factors)
+        if l < level_count - 1:
+            arrived = lax.ppermute(other, "cols", [(0, 1), (1, 0)])
+            reduced = inner_rhs[l - 1] - (kept + arrived)
+            inverse = inner_inverses[l - 1]
+        else:
+            first = over_both(kept, lambda j, k, c: (j, c, k))
+            second = over_both(other, lambda j, k, c: (j, 1 - c, k))
+            reduced = rhs[l] - (first + second)
+            inverse = diag_inverses[l, 0]
         solved = jnp.dot(
-            reduced.astype(jnp.bfloat16), diag_inverses[l, 0], preferred_element_type=jnp.float32
+            reduced.astype(jnp.bfloat16), inverse, preferred_element_type=jnp.float32
         )
-        solutions.append(solved)
         if l < level_count - 1:
-            pieces += spread(solved.astype(jnp.bfloat16))
+            stores.append(spread(solved.astype(jnp.bfloat16), l))
+            solutions.append(transpose(solved))
+        else:
+            solutions.append(solved)
     return jnp.stack(solutions)[:, None]
 
 
@@ -209,7 +225,7 @@
 def solution(mesh):
     row_count, col_count = mesh.shape["rows"], mesh.shape["cols"]
     chips = row_count // 2
-    if col_count == 2 and row_count == 2 * chips and chips & (chips - 1) == 0:
+    if col_count == 2 and row_count == 2 * chips:
         shards = functools.partial(paired_shards, row_count)
     else:
         shards = functools.partial(rotated_shards, col_count)

time: 102 us -> 97.2 us (0.953)
  the two profiles are of different devices: /device:TPU:0 before, /device:TPU:1 now
where the time goes in v3:
time: 97.2 us; the launch traced here: 96.6 us
  blocking collectives  36.1 us (37%)
  starting transfers between devices  30.2 us (31%)
  waiting for transfers between devices  10.6 us (11%)
  local copies, waits for them, and re-layouts  7.41 us (8%)
  other arithmetic  4.63 us (5%)
  matrix products  4.38 us (5%)
  Pallas kernels  3.14 us (3%)
    all_gather x1, blocking collectives, spread(): return lax.all_gather(x, 'rows', axis_index_groups=same_core)  24.7 us
    ppermute x5, starting transfers between devices, over_both(): return lax.ppermute(x, ('rows', 'cols'), pairs)  23.5 us
    all_to_all x1, blocking collectives, spread(): return lax.all_to_all(copies, 'rows', 0, 0, axis_index_groups=same_core)  11.5 us
    all_to_all x1, starting transfers between devices, spread(): return lax.all_to_all(copies, 'rows', 0, 0, axis_index_groups=same_core)  5.53 us
    ppermute x2, waiting for transfers between devices, paired_shards(): arrived = lax.ppermute(other, 'cols', [(0, 1), (1, 0)])  5.33 us
    all_to_all x1, waiting for transfers between devices, spread(): return lax.all_to_all(copies, 'rows', 0, 0, axis_index_groups=same_core)  4.22 us
    pallas_call x3, Pallas kernels, pair_sums(): pl.pallas_call(functools.partial(pair_kernel, level, chips), out_shape=(p...  3.14 us
    dot_general x3, matrix products, paired_shards(): jnp.dot(reduced.astype(jnp.bfloat16), inverse, preferred_element_type=jnp...  2.67 us
  transfers between devices with their start and end apart: 12, of which 4 were waited for; matrix products, arithmetic and copies ran while one was open for 12% of the time, Pallas kernels for 1%

profile of v3, /device:TPU:1, one launch (start us, length us, event | category | flops | bytes accessed | tf_op | source)
XLA Modules:
  0.0 96.6 jit_solution(18340113588416503290)
XLA Ops:
  0.0 0.1 collective-permute-start.3
  0.1 1.7 %fusion.28 = (bf16[64,256]{1,0:T(8,128)(2,1)S(1)}, f32[64,256]{1,0:T(8,128)}) fusion(bf16[4,1,256,256]{3,2,1,0:T(8,128)(2,1)} %param.7, f32[4,1,128,256]{3,2,1,0:T(8,128)} %param.5, s32[]{:T(128)S(6)} %select_n.32), kind=kOutput, calls=%fused_computation.49 | convolution fusion | flops 8404992 | bytes 262148 | tf_op jit(solution)/shard_map/dot_general | solution.py:108
  1.8 4.5 %collective-permute-start.2 = (bf16[64,256]{1,0:T(8,128)(2,1)S(1)}, bf16[64,256]{1,0:T(8,128)(2,1)S(1)}, u32[]{:S(2)}, u32[]{:S(2)}) collective-permute-start(bf16[64,256]{1,0:T(8,128)(2,1)S(1)} %get-tuple-element.23), channel_id=1, source_target_pairs={{0,0},{1,2},{2,1},{3,3},{4,4},{5,6},{6,5},{7,7},{8,8},{9,10},{10,9... | collective-permute-start | bytes 98312 | tf_op jit(solution)/shard_map/ppermute | solution.py:90
  6.3 0.7 copy.12
  6.9 0.7 copy.8
  7.7 0.1 pad_add_fusion
  7.8 0.0 collective-permute-start.1
  7.8 1.0 %slice.55 = f32[2,1,128,256]{3,2,1,0:T(8,128)S(1)} slice(f32[4,1,128,256]{3,2,1,0:T(8,128)} %param.5), slice={[1:3], [0:1], [0:128], [0:256]} | slice | bytes 524288 | tf_op jit(solution)/shard_map/slice | solution.py:119
  8.8 0.0 copy-start.3
  8.8 0.7 dynamic-slice_bitcast_fusion
  9.5 0.5 collective-permute-start
  10.0 0.0 collective-permute-done.2
  10.0 0.7 broadcast_in_dim.9
  10.7 5.5 %all-to-all-start = ((bf16[8,64,256]{2,1,0:T(8,128)(2,1)}), bf16[8,64,256]{2,1,0:T(8,128)(2,1)S(1)}, u32[]{:S(2)}, u32[]{:S(2)}) async-start(bf16[8,64,256]{2,1,0:T(8,128)(2,1)} %broadcast_in_dim.9), calls=%async_computation | async-start | bytes 524288 | tf_op jit(solution)/shard_map/all_to_all | solution.py:102
  16.2 1.7 %slice_bitcast_fusion = bf16[2,256,256]{2,1,0:T(8,128)(2,1)} fusion(bf16[4,1,256,256]{3,2,1,0:T(8,128)(2,1)} %param.7), kind=kLoop, calls=%fused_computation.2 | loop fusion | bytes 524288 | tf_op jit(solution)/shard_map/squeeze | solution.py:122
  17.9 0.3 collective-permute-start.5
  18.2 0.1 fusion.31
  18.3 0.0 collective-permute-done.1
  18.3 0.3 fusion.26
  18.5 0.0 collective-permute-done
  18.5 1.7 %bitcast_select_fusion = f32[2,64,256]{2,1,0:T(8,128)} fusion(f32[2,64,256]{2,1,0:T(8,128)} %collective-permute-done, f32[2,1,128,256]{3,2,1,0:T(8,128)} %copy-done.3, s32[]{:T(128)S(6)} %select_n.35, pred[]{:T(512)S(6)} %eq.6), kind=kLoop, calls=%fused_computation.9 | loop fusion | flops 32768 | bytes 393221 | tf_op jit(solution)/shard_map/jit(_where)/select_n | solution.py:118
  20.2 4.2 %all-to-all-done.refs_0_ = bf16[8,64,256]{2,1,0:T(8,128)(2,1)S(1)} async-done(((bf16[8,64,256]{2,1,0:T(8,128)(2,1)}), bf16[8,64,256]{2,1,0:T(8,128)(2,1)S(1)}, u32[]{:S(2)}, u32[]{:S(2)}) %all-to-all-start) | async-done | bytes 262176 | tf_op jit(solution)/shard_map/all_to_all | solution.py:102
  24.4 0.0 collective-permute-done.3.refs_2_.refs_3_.refs_4_
  24.4 1.9 %copy-done = bf16[3,1,1,8,256,256]{5,4,3,2,1,0:T(8,128)(2,1)S(1)} copy-done((bf16[3,1,1,8,256,256]{5,4,3,2,1,0:T(8,128)(2,1)S(1)}, bf16[3,1,1,8,256,256]{5,4,3,2,1,0:T(8,128)(2,1)}, u32[]{:S(2)}) %copy-start) | copy-done | bytes 3145752
  26.3 1.0 %shard_map.55 = (f32[64,256]{1,0:T(8,128)S(1)}, f32[64,256]{1,0:T(8,128)S(1)}) custom-call(s32[1]{0:T(128)} %bitcast.6.flipped_ref, s32[2,8]{1,0:T(2,128)S(1)} %bitcast.81, s32[2]{0:T(128)S(1)} %get-tuple-element.18.counts_ref, bf16[8,64,256]{2,1,0:T(8,128)(2,1)S(1)} %all-to-all-done.refs_0_, bf16[3,1,1,8,256,256]{5,4,3,2,1,0:T(8,128)(2,1)S(1)} %copy-done, ...), custom_call_target="tpu_custom_call" | custom-call | flops 134217728 | bytes 2097152 | tf_op jit(solution)/shard_map/pallas_call | solution.py:56
  27.4 0.1 collective-permute-start.4
  27.4 0.0 collective-permute-done.5
  27.5 1.0 %broadcast_select_fusion = bf16[2,256,256]{2,1,0:T(8,128)(2,1)S(1)} fusion(bf16[2,256,256]{2,1,0:T(8,128)(2,1)} %collective-permute-done.5, pred[]{:T(512)S(6)} %eq.6, bf16[4,1,256,256]{3,2,1,0:T(8,128)(2,1)S(1)} %copy-done.2), kind=kLoop, calls=%fused_computation.3 | loop fusion | flops 131072 | bytes 786433 | tf_op jit(solution)/shard_map/jit(_where)/select_n | solution.py:121
  28.4 2.1 %collective-permute-done.4 = f32[64,256]{1,0:T(8,128)S(1)} collective-permute-done((f32[64,256]{1,0:T(8,128)S(1)}, f32[64,256]{1,0:T(8,128)S(1)}, u32[]{:S(2)}, u32[]{:S(2)}) %collective-permute-start.4) | collective-permute-done | bytes 65568 | tf_op jit(solution)/shard_map/ppermute | solution.py:130
  30.5 0.8 fusion.29
  31.3 24.7 %all-gather = bf16[512,256]{1,0:T(8,128)(2,1)S(1)} all-gather(bf16[64,256]{1,0:T(8,128)(2,1)S(1)} %get-tuple-element.25), channel_id=2, replica_groups={{0,4,8,12,16,20,24,28},{2,6,10,14,18,22,26,30},{1,5,9,13,17,21,25,29},{..., dimensions={0}, use_global_device_ids=true | all-gather | bytes 294912 | tf_op jit(solution)/shard_map/all_gather | solution.py:100
  56.0 0.0 copy-done.1
  56.0 1.0 %shard_map.56 = (f32[64,256]{1,0:T(8,128)S(1)}, f32[64,256]{1,0:T(8,128)S(1)}) custom-call(s32[1]{0:T(128)} %bitcast.6.flipped_ref, s32[2,8]{1,0:T(2,128)S(1)} %bitcast.80, s32[2]{0:T(128)S(1)} %get-tuple-element.17.counts_ref, bf16[8,64,256]{2,1,0:T(8,128)(2,1)S(1)} %all-to-all-done.refs_0_, bf16[8,64,256]{2,1,0:T(8,128)(2,1)S(1)} %bitcast.77, ...), custom_call_target="tpu_custom_call" | custom-call | flops 134217728 | bytes 2097152 | tf_op jit(solution)/shard_map/pallas_call | solution.py:56
  57.1 0.2 collective-permute-start.7
  57.3 3.2 %collective-permute-done.7 = f32[64,256]{1,0:T(8,128)S(1)} collective-permute-done((f32[64,256]{1,0:T(8,128)S(1)}, f32[64,256]{1,0:T(8,128)S(1)}, u32[]{:S(2)}, u32[]{:S(2)}) %collective-permute-start.7) | collective-permute-done | bytes 65568 | tf_op jit(solution)/shard_map/ppermute | solution.py:130
  60.5 0.8 fusion.30
  61.3 11.5 %all_to_all.10.refs_2_ = bf16[8,64,256]{2,1,0:T(8,128)(2,1)S(1)} all-to-all(bf16[8,64,256]{2,1,0:T(8,128)(2,1)S(1)} %broadcast_in_dim.10), channel_id=1, replica_groups={{0,4,8,12,16,20,24,28},{2,6,10,14,18,22,26,30},{1,5,9,13,17,21,25,29},{..., dimensions={0} | all-to-all | bytes 524288 | tf_op jit(solution)/shard_map/all_to_all | solution.py:102
  72.8 1.1 %shard_map.57 = (f32[64,256]{1,0:T(8,128)S(1)}, f32[64,256]{1,0:T(8,128)S(1)}) custom-call(s32[1]{0:T(128)} %bitcast.6.flipped_ref, s32[2,8]{1,0:T(2,128)S(1)} %bitcast.79, s32[2]{0:T(128)S(1)} %get-tuple-element.19.counts_ref, bf16[8,64,256]{2,1,0:T(8,128)(2,1)S(1)} %all-to-all-done.refs_0_, bf16[8,64,256]{2,1,0:T(8,128)(2,1)S(1)} %bitcast.78, ...), custom_call_target="tpu_custom_call" | custom-call | flops 134217728 | bytes 2097152 | tf_op jit(solution)/shard_map/pallas_call | solution.py:56
  73.9 0.0 collective-permute-start.10
  73.9 13.4 %collective-permute-start.9 = (f32[64,256]{1,0:T(8,128)S(1)}, f32[64,256]{1,0:T(8,128)S(1)}, u32[]{:S(2)}, u32[]{:S(2)}) collective-permute-start(f32[64,256]{1,0:T(8,128)S(1)} %get-tuple-element.15), channel_id=1, source_target_pairs={{0,0},{1,2},{2,1},{3,3},{4,4},{5,6},{6,5},{7,7},{8,8},{9,10},{10,9... | collective-permute-start | bytes 196616 | tf_op jit(solution)/shard_map/ppermute | solution.py:90
  87.3 1.9 %collective-permute-start.6 = (f32[64,256]{1,0:T(8,128)}, f32[64,256]{1,0:T(8,128)S(1)}, u32[]{:S(2)}, u32[]{:S(2)}) collective-permute-start(f32[64,256]{1,0:T(8,128)} %get-tuple-element.26), channel_id=1, source_target_pairs={{0,0},{1,2},{2,1},{3,3},{4,4},{5,6},{6,5},{7,7},{8,8},{9,10},{10,9... | collective-permute-start | bytes 196616 | tf_op jit(solution)/shard_map/ppermute | solution.py:90
  89.3 3.6 %collective-permute-start.8 = (f32[64,256]{1,0:T(8,128)}, f32[64,256]{1,0:T(8,128)S(1)}, u32[]{:S(2)}, u32[]{:S(2)}) collective-permute-start(f32[64,256]{1,0:T(8,128)} %get-tuple-element.28), channel_id=1, source_target_pairs={{0,0},{1,2},{2,1},{3,3},{4,4},{5,6},{6,5},{7,7},{8,8},{9,10},{10,9... | collective-permute-start | bytes 196616 | tf_op jit(solution)/shard_map/ppermute | solution.py:90
  92.9 0.0 collective-permute-done.10
  92.9 0.0 collective-permute-done.9
  92.9 1.1 %convolution_bitcast_fusion = f32[1,64,256]{2,1,0:T(8,128)S(1)} fusion(bf16[4,1,256,256]{3,2,1,0:T(8,128)(2,1)} %param.7, f32[4,1,128,256]{3,2,1,0:T(8,128)} %param.5, s32[]{:T(128)S(6)} %add.38, s32[]{:T(128)S(6)} %select_n.32, f32[64,256]{1,0:T(8,128)S(1)} %collective-permute-done.9, f32[64,256]{1,0:T(8,128)S(1)} %collective-permute-done.10), kind=kOutput, calls=%fused_computation | convolution fusion | flops 8437760 | bytes 393224 | tf_op jit(solution)/shard_map/dot_general | solution.py:138
  94.0 0.0 collective-permute-done.6
  94.0 1.0 %collective-permute-done.8 = f32[64,256]{1,0:T(8,128)S(1)} collective-permute-done((f32[64,256]{1,0:T(8,128)}, f32[64,256]{1,0:T(8,128)S(1)}, u32[]{:S(2)}, u32[]{:S(2)}) %collective-permute-start.8) | collective-permute-done | bytes 65568 | tf_op jit(solution)/shard_map/ppermute | solution.py:90
  95.1 1.6 %maximum_bitcast_fusion = f32[4,1,64,256]{3,2,1,0:T(8,128)} fusion(f32[1,64,256]{2,1,0:T(8,128)S(1)} %convolution_bitcast_fusion, f32[1,64,256]{2,1,0:T(8,128)S(1)} %bitcast.84, f32[1,64,256]{2,1,0:T(8,128)S(1)} %bitcast.83, f32[1,64,256]{2,1,0:T(8,128)} %bitcast.82), kind=kLoop, calls=%fused_computation.1 | loop fusion | flops 196608 | bytes 524288 | tf_op jit(solution)/shard_map/broadcast_in_dim | solution.py:146
  (9 shorter events, 0.0 us)
Async XLA Ops:
  0.0 24.4 %collective-permute-start.3 = (bf16[3,1,1,8,256,256]{5,4,3,2,1,0:T(8,128)(2,1)}, bf16[3,1,1,8,256,256]{5,4,3,2,1,0:T(8,128)(2,1)S(1)}, u32[]{:S(2)}, u32[]{:S(2)}) collective-permute-start(bf16[3,1,1,8,256,256]{5,4,3,2,1,0:T(8,128)(2,1)} %refs_3_.1), channel_id=1, source_target_pairs={{0,2},{2,0},{4,6},{6,4},{8,10},{10,8},{12,14},{14,12},{16,18},{18,... | collective-permute-start | bytes 9437192 | tf_op jit(solution)/shard_map/ppermute | solution.py:93
  1.8 8.2 %collective-permute-start.2 = (bf16[64,256]{1,0:T(8,128)(2,1)S(1)}, bf16[64,256]{1,0:T(8,128)(2,1)S(1)}, u32[]{:S(2)}, u32[]{:S(2)}) collective-permute-start(bf16[64,256]{1,0:T(8,128)(2,1)S(1)} %get-tuple-element.23), channel_id=1, source_target_pairs={{0,0},{1,2},{2,1},{3,3},{4,4},{5,6},{6,5},{7,7},{8,8},{9,10},{10,9... | collective-permute-start | bytes 98312 | tf_op jit(solution)/shard_map/ppermute | solution.py:90
  7.8 10.5 %collective-permute-start.1 = (s32[3,9]{1,0:T(4,128)S(1)}, s32[3,9]{1,0:T(4,128)S(1)}, u32[]{:S(2)}, u32[]{:S(2)}) collective-permute-start(s32[3,9]{1,0:T(4,128)S(1)} %pad_add_fusion), channel_id=1, source_target_pairs={{0,2},{2,0},{4,6},{6,4},{8,10},{10,8},{12,14},{14,12},{16,18},{18,... | collective-permute-start | bytes 332 | tf_op jit(solution)/shard_map/ppermute | solution.py:93
  8.8 1.9 %copy-start.3 = (f32[2,1,128,256]{3,2,1,0:T(8,128)}, f32[2,1,128,256]{3,2,1,0:T(8,128)S(1)}, u32[]{:S(2)}) copy-start(f32[2,1,128,256]{3,2,1,0:T(8,128)S(1)} %slice.55) | copy-start | bytes 786436
  9.5 9.1 %collective-permute-start = (f32[2,64,256]{2,1,0:T(8,128)}, f32[2,64,256]{2,1,0:T(8,128)}, u32[]{:S(2)}, u32[]{:S(2)}) collective-permute-start(f32[2,64,256]{2,1,0:T(8,128)} %dynamic-slice_bitcast_fusion), channel_id=1, source_target_pairs={{0,2},{2,0},{4,6},{6,4},{8,10},{10,8},{12,14},{14,12},{16,18},{18,... | collective-permute-start | bytes 393224 | tf_op jit(solution)/shard_map/ppermute | solution.py:93
  10.7 13.7 %all-to-all-start = ((bf16[8,64,256]{2,1,0:T(8,128)(2,1)}), bf16[8,64,256]{2,1,0:T(8,128)(2,1)S(1)}, u32[]{:S(2)}, u32[]{:S(2)}) async-start(bf16[8,64,256]{2,1,0:T(8,128)(2,1)} %broadcast_in_dim.9), calls=%async_computation | async-start | bytes 524288 | tf_op jit(solution)/shard_map/all_to_all | solution.py:102
  17.9 9.6 %collective-permute-start.5 = (bf16[2,256,256]{2,1,0:T(8,128)(2,1)}, bf16[2,256,256]{2,1,0:T(8,128)(2,1)}, u32[]{:S(2)}, u32[]{:S(2)}) collective-permute-start(bf16[2,256,256]{2,1,0:T(8,128)(2,1)} %slice_bitcast_fusion), channel_id=1, source_target_pairs={{0,2},{2,0},{4,6},{6,4},{8,10},{10,8},{12,14},{14,12},{16,18},{18,... | collective-permute-start | bytes 786440 | tf_op jit(solution)/shard_map/ppermute | solution.py:93
  24.4 1.9 %copy-start = (bf16[3,1,1,8,256,256]{5,4,3,2,1,0:T(8,128)(2,1)S(1)}, bf16[3,1,1,8,256,256]{5,4,3,2,1,0:T(8,128)(2,1)}, u32[]{:S(2)}) copy-start(bf16[3,1,1,8,256,256]{5,4,3,2,1,0:T(8,128)(2,1)} %refs_3_.1) | copy-start | bytes 9437188
  26.3 1.1 %copy-start.2 = (bf16[4,1,256,256]{3,2,1,0:T(8,128)(2,1)S(1)}, bf16[4,1,256,256]{3,2,1,0:T(8,128)(2,1)}, u32[]{:S(2)}) copy-start(bf16[4,1,256,256]{3,2,1,0:T(8,128)(2,1)} %param.7) | copy-start | bytes 1572868
  26.3 4.2 %copy-start.4 = (f32[2,64,256]{2,1,0:T(8,128)S(1)}, f32[2,64,256]{2,1,0:T(8,128)}, u32[]{:S(2)}) copy-start(f32[2,64,256]{2,1,0:T(8,128)} %bitcast_select_fusion) | copy-start | bytes 393220
  26.3 29.7 %copy-start.1 = (bf16[3,1,1,8,256,256]{5,4,3,2,1,0:T(8,128)(2,1)S(1)}, bf16[3,1,1,8,256,256]{5,4,3,2,1,0:T(8,128)(2,1)}, u32[]{:S(2)}) copy-start(bf16[3,1,1,8,256,256]{5,4,3,2,1,0:T(8,128)(2,1)} %refs_3_.1) | copy-start | bytes 9437188
  27.4 3.2 %collective-permute-start.4 = (f32[64,256]{1,0:T(8,128)S(1)}, f32[64,256]{1,0:T(8,128)S(1)}, u32[]{:S(2)}, u32[]{:S(2)}) collective-permute-start(f32[64,256]{1,0:T(8,128)S(1)} %get-tuple-element.12), channel_id=1, source_target_pairs={{0,1},{1,0},{2,3},{3,2},{4,5},{5,4},{6,7},{7,6},{8,9},{9,8},{10,11... | collective-permute-start | bytes 196616 | tf_op jit(solution)/shard_map/ppermute | solution.py:130
  57.1 3.5 %collective-permute-start.7 = (f32[64,256]{1,0:T(8,128)S(1)}, f32[64,256]{1,0:T(8,128)S(1)}, u32[]{:S(2)}, u32[]{:S(2)}) collective-permute-start(f32[64,256]{1,0:T(8,128)S(1)} %get-tuple-element.14), channel_id=1, source_target_pairs={{0,1},{1,0},{2,3},{3,2},{4,5},{5,4},{6,7},{7,6},{8,9},{9,8},{10,11... | collective-permute-start | bytes 196616 | tf_op jit(solution)/shard_map/ppermute | solution.py:130
  73.9 19.0 %collective-permute-start.10 = (f32[64,256]{1,0:T(8,128)S(1)}, f32[64,256]{1,0:T(8,128)S(1)}, u32[]{:S(2)}, u32[]{:S(2)}) collective-permute-start(f32[64,256]{1,0:T(8,128)S(1)} %get-tuple-element.16), channel_id=1, source_target_pairs={{0,2},{1,0},{2,3},{3,1},{4,6},{5,4},{6,7},{7,5},{8,10},{9,8},{10,1... | collective-permute-start | bytes 196616 | tf_op jit(solution)/shard_map/ppermute | solution.py:90
  73.9 19.0 %collective-permute-start.9 = (f32[64,256]{1,0:T(8,128)S(1)}, f32[64,256]{1,0:T(8,128)S(1)}, u32[]{:S(2)}, u32[]{:S(2)}) collective-permute-start(f32[64,256]{1,0:T(8,128)S(1)} %get-tuple-element.15), channel_id=1, source_target_pairs={{0,0},{1,2},{2,1},{3,3},{4,4},{5,6},{6,5},{7,7},{8,8},{9,10},{10,9... | collective-permute-start | bytes 196616 | tf_op jit(solution)/shard_map/ppermute | solution.py:90
  87.3 6.7 %collective-permute-start.6 = (f32[64,256]{1,0:T(8,128)}, f32[64,256]{1,0:T(8,128)S(1)}, u32[]{:S(2)}, u32[]{:S(2)}) collective-permute-start(f32[64,256]{1,0:T(8,128)} %get-tuple-element.26), channel_id=1, source_target_pairs={{0,0},{1,2},{2,1},{3,3},{4,4},{5,6},{6,5},{7,7},{8,8},{9,10},{10,9... | collective-permute-start | bytes 196616 | tf_op jit(solution)/shard_map/ppermute | solution.py:90
  89.3 5.8 %collective-permute-start.8 = (f32[64,256]{1,0:T(8,128)}, f32[64,256]{1,0:T(8,128)S(1)}, u32[]{:S(2)}, u32[]{:S(2)}) collective-permute-start(f32[64,256]{1,0:T(8,128)} %get-tuple-element.28), channel_id=1, source_target_pairs={{0,0},{1,2},{2,1},{3,3},{4,4},{5,6},{6,5},{7,7},{8,8},{9,10},{10,9... | collective-permute-start | bytes 196616 | tf_op jit(solution)/shard_map/ppermute | solution.py:90

commit v4 on v1

--- a/solution.py
+++ b/solution.py
@@ -7,6 +7,178 @@
 from jax.experimental.pallas import tpu as pltpu
 from jax.sharding import PartitionSpec as P
 
+VMEM_LIMIT = 32 * 1024 * 1024
+
+
+VMEM = pl.BlockSpec(memory_space=pltpu.VMEM)
+SMEM = pl.BlockSpec(memory_space=pltpu.SMEM)
+
+
+def flat_dot(gathered, factor_ref):
+    slots, width = factor_ref.shape[0], factor_ref.shape[1]
+    return jnp.dot(
+        gathered[...],
+        factor_ref[...].reshape(slots * width, width),
+        preferred_element_type=jnp.float32,
+    )
+
+
+def run(kernel, outs, args, scratch=(), flops=0, transferred=0):
+    return pl.pallas_call(
+        kernel,
+        out_shape=outs,
+        in_specs=[SMEM if x.dtype == jnp.int32 else VMEM for x in args],
+        out_specs=jax.tree.map(lambda _: VMEM, outs),
+        scratch_shapes=list(scratch),
+        compiler_params=pltpu.CompilerParams(vmem_limit_bytes=VMEM_LIMIT),
+        cost_estimate=pl.CostEstimate(flops=flops, bytes_accessed=transferred, transcendentals=0),
+    )(*args)
+
+
+def half_of(ref, level, half, rows):
+    return ref[level, 0, pl.ds(pl.multiple_of(half * rows, rows), rows), :]
+
+
+def solve(reduced, inverse):
+    return jnp.dot(reduced.astype(jnp.bfloat16), inverse, preferred_element_type=jnp.float32)
+
+
+def first_kernel(place_ref, rhs_ref, inverse_ref, out_ref, rounded_ref):
+    rows = out_ref.shape[0]
+    solved = solve(half_of(rhs_ref, 0, place_ref[1], rows), inverse_ref[0, 0])
+    out_ref[...] = solved
+    rounded_ref[...] = solved.astype(jnp.bfloat16)
+
+
+def sums_kernel(level, chips, place_ref, ids_ref, other_ids_ref, *refs):
+    store_refs = refs[:level]
+    factor_refs = (refs[level], refs[level + 1].at[level - 1, 0, 0])
+    kept_ref, sent_ref, store, gathered = refs[-4:]
+    slots, width = factor_refs[0].shape[0], factor_refs[0].shape[1]
+    for m, piece in enumerate(store_refs):
+        store[m * chips:(m + 1) * chips] = piece[...]
+    sums = []
+    for ids, factor_ref in zip((ids_ref, other_ids_ref), factor_refs):
+        for k in range(slots):
+            source = ids[level - 1, 0, 0, k]
+            known = jnp.maximum(source, 0)
+            piece = store[known // (2 * chips) * chips + known % (2 * chips) // 2]
+            live = jnp.where(source >= 0, 1.0, 0.0).astype(piece.dtype)
+            gathered[:, k * width:(k + 1) * width] = piece * live
+        sums.append(flat_dot(gathered, factor_ref))
+    straight = place_ref[0] == place_ref[1]
+    kept_ref[...] = jnp.where(straight, sums[0], sums[1])
+    sent_ref[...] = jnp.where(straight, sums[1], sums[0])
+
+
+def inner_kernel(level, place_ref, kept_ref, arrived_ref, rhs_ref, other_rhs_ref, inverse_ref, other_inverse_ref, out_ref, copies_ref):
+    rows = out_ref.shape[0]
+    core = place_ref[0]
+    straight = core == place_ref[1]
+    rhs = jnp.where(straight, half_of(rhs_ref, level, core, rows), half_of(other_rhs_ref, level, core, rows))
+    inverse = jnp.where(straight, inverse_ref[level, 0], other_inverse_ref[level, 0])
+    solved = solve(rhs - (kept_ref[...] + arrived_ref[...]), inverse)
+    out_ref[...] = solved
+    rounded = solved.astype(jnp.bfloat16)
+    for i in range(copies_ref.shape[0]):
+        copies_ref[i] = rounded
+
+
+def last_kernel(place_ref, first_ref, second_ref, rhs_ref, inverse_ref, *refs):
+    done_refs, out_ref = refs[:-1], refs[-1]
+    rows, level = out_ref.shape[2], len(done_refs)
+    for m, done in enumerate(done_refs):
+        out_ref[m, 0] = done[...]
+    rhs = half_of(rhs_ref, level, place_ref[1], rows)
+    out_ref[level, 0] = solve(rhs - (first_ref[...] + second_ref[...]), inverse_ref[level, 0])
+
+
+def paired_shards(row_count, right_sides, factor_blocks, diag_inverses, source_ids, block_counts):
+    level_count, _, rhs_count, width = right_sides.shape
+    slots = factor_blocks.shape[3]
+    rows = rhs_count // 2
+    chips = row_count // 2
+    row, col = lax.axis_index("rows"), lax.axis_index("cols")
+    place = jnp.stack([row % 2, col]).astype(jnp.int32)
+    same_core = [[2 * j + k for j in range(chips)] for k in range(2)]
+    part = jax.ShapeDtypeStruct((rows, width), jnp.float32)
+    rounded_part = jax.ShapeDtypeStruct((rows, width), jnp.bfloat16)
+    copies = jax.ShapeDtypeStruct((chips, rows, width), jnp.bfloat16)
+    solve_flops = 2 * rows * width * width
+
+    def over_both(x, move):
+        pairs = []
+        for j in range(chips):
+            for k in range(2):
+                for c in range(2):
+                    tj, tk, tc = move(j, k, c)
+                    pairs.append(((2 * j + k) * 2 + c, (2 * tj + tk) * 2 + tc))
+        return lax.ppermute(x, ("rows", "cols"), pairs)
+
+    def swap_core(x):
+        return lax.ppermute(x, "rows", [(i, i ^ 1) for i in range(row_count)])
+
+    def transpose(x):
+        return over_both(x, lambda j, k, c: (j, c, k))
+
+    def spread(x):
+        return lax.all_to_all(x, "rows", 0, 0, axis_index_groups=same_core)
+
+    solved, rounded = run(
+        first_kernel, (part, rounded_part), (place, right_sides, diag_inverses), flops=solve_flops
+    )
+    finished = [solved]
+    moved = transpose(rounded)
+    stores = [spread(jnp.broadcast_to(moved[None], copies.shape))]
+
+    live_ids = jnp.where(
+        jnp.arange(slots, dtype=jnp.int32) < block_counts[..., None], source_ids, -1
+    )
+    other_factors = swap_core(factor_blocks)
+    other_ids = swap_core(live_ids)
+    other_inverses = swap_core(diag_inverses)
+    other_rhs = swap_core(right_sides)
+
+    for l in range(1, level_count):
+        kept, sent = run(
+            functools.partial(sums_kernel, l, chips),
+            (part, part),
+            (place, live_ids, other_ids, *stores, factor_blocks[l - 1, 0, 0], other_factors)
+            + tuple(finished[1:]),
+            scratch=(
+                pltpu.VMEM((l * chips, rows, width), jnp.bfloat16),
+                pltpu.VMEM((rows, slots * width), jnp.bfloat16),
+            ),
+            flops=2 * slots * solve_flops,
+            transferred=2 * slots * width * width * 2,
+        )
+        if l < level_count - 1:
+            arrived = lax.ppermute(sent, "cols", [(0, 1), (1, 0)])
+            solved, copied = run(
+                functools.partial(inner_kernel, l),
+                (part, copies),
+                (place, kept, arrived, right_sides, other_rhs, diag_inverses, other_inverses),
+                flops=solve_flops,
+            )
+            finished.append(transpose(solved))
+            stores.append(spread(copied))
+        else:
+            first = over_both(kept, lambda j, k, c: (j, c, k))
+            second = over_both(sent, lambda j, k, c: (j, 1 - c, k))
+            return run(
+                last_kernel,
+                jax.ShapeDtypeStruct((level_count, 1, rows, width), jnp.float32),
+                (place, first, second, right_sides, diag_inverses, *finished),
+                flops=solve_flops,
+            )
+
+
+def gather_slots(ids_ref, counts_ref, group, store_ref, gathered, slots, width):
+    for k in range(slots):
+        piece = store_ref[ids_ref[group, k]]
+        live = jnp.where(k < counts_ref[group], 1.0, 0.0).astype(piece.dtype)
+        gathered[:, k * width:(k + 1) * width] = piece * live
+
 
 def level_kernel(groups, ids_ref, counts_ref, store_ref, *refs):
     factor_refs = refs[:groups]
@@ -14,15 +186,8 @@
     slots, width = factor_refs[0].shape[0], factor_refs[0].shape[1]
     update = None
     for g in range(groups):
-        for k in range(slots):
-            piece = store_ref[ids_ref[g, k]]
-            live = jnp.where(k < counts_ref[g], 1.0, 0.0).astype(piece.dtype)
-            gathered[:, k * width:(k + 1) * width] = piece * live
-        term = jnp.dot(
-            gathered[...],
-            factor_refs[g][...].reshape(slots * width, width),
-            preferred_element_type=jnp.float32,
-        )
+        gather_slots(ids_ref, counts_ref, g, store_ref, gathered, slots, width)
+        term = flat_dot(gathered, factor_refs[g])
         update = term if update is None else update + term
     reduced = (rhs_ref[...] - update).astype(jnp.bfloat16)
     solved = jnp.dot(reduced, inverse_ref[...], preferred_element_type=jnp.float32)
@@ -45,7 +210,7 @@
         in_specs=[smem, smem, vmem] + [vmem] * groups + [vmem, vmem],
         out_specs=(vmem, vmem),
         scratch_shapes=[pltpu.VMEM((rows, slots * width), jnp.bfloat16)],
-        compiler_params=pltpu.CompilerParams(vmem_limit_bytes=32 * 1024 * 1024),
+        compiler_params=pltpu.CompilerParams(vmem_limit_bytes=VMEM_LIMIT),
         cost_estimate=pl.CostEstimate(
             flops=2 * rows * width * width * (groups * slots + 1),
             bytes_accessed=groups * slots * width * width * 2,
@@ -54,8 +219,7 @@
     )(ids, counts, store, *factors, rhs, inverse)
 
 
-def shards(right_sides, factor_blocks, diag_inverses, source_ids, block_counts):
-    col_count = lax.axis_size("cols")
+def rotated_shards(col_count, right_sides, factor_blocks, diag_inverses, source_ids, block_counts):
     level_count, _, rhs_count, width = right_sides.shape
     share_rows = rhs_count // col_count
     col_index = lax.axis_index("cols")
@@ -93,6 +257,12 @@
 
 
 def solution(mesh):
+    row_count, col_count = mesh.shape["rows"], mesh.shape["cols"]
+    chips = row_count // 2
+    if col_count == 2 and row_count == 2 * chips:
+        shards = functools.partial(paired_shards, row_count)
+    else:
+        shards = functools.partial(rotated_shards, col_count)
     return jax.shard_map(
         shards,
         mesh=mesh,

time: 84 us -> 79.7 us (0.949)
  the two profiles are of different devices: /device:TPU:0 before, /device:TPU:1 now
where the time goes in v4:
time: 79.7 us; the launch traced here: 78.9 us
  starting transfers between devices  35.1 us (44%)
  waiting for transfers between devices  21.2 us (27%)
  Pallas kernels  11 us (14%)
  local copies, waits for them, and re-layouts  10.6 us (13%)
  other arithmetic  0.83 us (1%)
    ppermute x5, starting transfers between devices, over_both(): return lax.ppermute(x, ('rows', 'cols'), pairs)  19.5 us
    all_to_all x3, starting transfers between devices, spread(): return lax.all_to_all(x, 'rows', 0, 0, axis_index_groups=same_core)  14.8 us
    pallas_call x7, Pallas kernels, run(): pl.pallas_call(kernel, out_shape=outs, in_specs=[SMEM if x.dtype == jnp.i...  11 us
    ppermute x5, waiting for transfers between devices, over_both(): return lax.ppermute(x, ('rows', 'cols'), pairs)  7.95 us
    ppermute x2, waiting for transfers between devices, paired_shards(): arrived = lax.ppermute(sent, 'cols', [(0, 1), (1, 0)])  7.04 us
    unnamed x16, local copies, waits for them, and re-layouts  6.32 us
    all_to_all x3, waiting for transfers between devices, spread(): return lax.all_to_all(x, 'rows', 0, 0, axis_index_groups=same_core)  6.22 us
    squeeze x1, local copies, waits for them, and re-layouts, paired_shards(): factor_blocks[l - 1, 0, 0]  3.59 us
  transfers between devices with their start and end apart: 14, of which 9 were waited for; matrix products, arithmetic and copies ran while one was open for 7% of the time, Pallas kernels for 3%

profile of v4, /device:TPU:1, one launch (start us, length us, event | category | flops | bytes accessed | tf_op | source)
XLA Modules:
  0.0 78.9 jit_solution(14637816433182983421)
XLA Ops:
  0.0 0.1 collective-permute-start.2
  0.1 0.1 pad_add_fusion.place_ref
  0.1 1.3 %shard_map.58 = (f32[64,256]{1,0:T(8,128)S(1)}, bf16[64,256]{1,0:T(8,128)(2,1)S(1)}) custom-call(s32[2]{0:T(128)S(1)} %pad_add_fusion.place_ref, f32[4,1,128,256]{3,2,1,0:T(8,128)} %rhs_ref.7, bf16[4,1,256,256]{3,2,1,0:T(8,128)(2,1)} %inverse_ref.7), custom_call_target="tpu_custom_call" | custom-call | flops 8388608 | tf_op jit(solution)/shard_map/pallas_call | solution.py:27
  1.5 0.0 copy-start.5
  1.5 0.6 copy-done.5
  2.1 4.5 %collective-permute-start.1 = (bf16[64,256]{1,0:T(8,128)(2,1)S(1)}, bf16[64,256]{1,0:T(8,128)(2,1)S(1)}, u32[]{:S(2)}, u32[]{:S(2)}) collective-permute-start(bf16[64,256]{1,0:T(8,128)(2,1)S(1)} %get-tuple-element.17), channel_id=1, source_target_pairs={{0,0},{1,2},{2,1},{3,3},{4,4},{5,6},{6,5},{7,7},{8,8},{9,10},{10,9... | collective-permute-start | bytes 98312 | tf_op jit(solution)/shard_map/ppermute | solution.py:116
  6.6 0.1 collective-permute-start.4
  6.7 0.5 collective-permute-start.5
  7.2 1.0 %collective-permute-done.1 = bf16[64,256]{1,0:T(8,128)(2,1)S(1)} collective-permute-done((bf16[64,256]{1,0:T(8,128)(2,1)S(1)}, bf16[64,256]{1,0:T(8,128)(2,1)S(1)}, u32[]{:S(2)}, u32[]{:S(2)}) %collective-permute-start.1) | collective-permute-done | bytes 32800 | tf_op jit(solution)/shard_map/ppermute | solution.py:116
  8.2 0.7 broadcast_in_dim.6
  8.9 6.1 %all-to-all-start = ((bf16[8,64,256]{2,1,0:T(8,128)(2,1)}), bf16[8,64,256]{2,1,0:T(8,128)(2,1)S(1)}, u32[]{:S(2)}, u32[]{:S(2)}) async-start(bf16[8,64,256]{2,1,0:T(8,128)(2,1)} %broadcast_in_dim.6), calls=%async_computation | async-start | bytes 524288 | tf_op jit(solution)/shard_map/all_to_all | solution.py:125
  15.0 0.8 compare_select_fusion.ids_ref
  15.8 0.0 collective-permute-start
  15.8 3.6 %slice_bitcast_fusion = (bf16[8,256,256]{2,1,0:T(8,128)(2,1)}, bf16[8,256,256]{2,1,0:T(8,128)(2,1)}, bf16[8,256,256]{2,1,0:T(8,128)(2,1)}) fusion(bf16[3,1,1,8,256,256]{5,4,3,2,1,0:T(8,128)(2,1)} %param.6), kind=kLoop, calls=%fused_computation | loop fusion | bytes 6291456 | tf_op jit(solution)/shard_map/squeeze | solution.py:146
  19.4 0.0 collective-permute-done.other_ids_ref
  19.4 4.0 %all-to-all-done.refs_0_ = bf16[8,64,256]{2,1,0:T(8,128)(2,1)S(1)} async-done(((bf16[8,64,256]{2,1,0:T(8,128)(2,1)}), bf16[8,64,256]{2,1,0:T(8,128)(2,1)S(1)}, u32[]{:S(2)}, u32[]{:S(2)}) %all-to-all-start) | async-done | bytes 262176 | tf_op jit(solution)/shard_map/all_to_all | solution.py:125
  23.4 0.0 collective-permute-done.2.refs_2_.refs_3_.refs_4_
  23.4 1.2 %copy-done.1 = bf16[8,256,256]{2,1,0:T(8,128)(2,1)S(1)} copy-done((bf16[8,256,256]{2,1,0:T(8,128)(2,1)S(1)}, bf16[8,256,256]{2,1,0:T(8,128)(2,1)}, u32[]{:S(2)}) %copy-start.1) | copy-done | bytes 1048600
  24.7 1.1 %shard_map.59 = (f32[64,256]{1,0:T(8,128)S(1)}, f32[64,256]{1,0:T(8,128)S(1)}) custom-call(s32[2]{0:T(128)S(1)} %pad_add_fusion.place_ref, s32[3,1,1,8]{3,2,1,0:T(1,128)S(1)} %compare_select_fusion.ids_ref, s32[3,1,1,8]{3,2,1,0:T(1,128)S(1)} %collective-permute-done.other_ids_ref, bf16[8,64,256]{2,1,0:T(8,128)(2,1)S(1)} %all-to-all-done.refs_0_, ...), custom_call_target="tpu_custom_call" | custom-call | flops 134217728 | bytes 2097152 | tf_op jit(solution)/shard_map/pallas_call | solution.py:27
  25.7 0.1 collective-permute-start.3
  25.8 0.0 collective-permute-done.4.other_rhs_ref
  25.8 0.0 collective-permute-done.5.other_inverse_ref
  25.8 3.9 %collective-permute-done.3.arrived_ref = f32[64,256]{1,0:T(8,128)S(1)} collective-permute-done((f32[64,256]{1,0:T(8,128)S(1)}, f32[64,256]{1,0:T(8,128)S(1)}, u32[]{:S(2)}, u32[]{:S(2)}) %collective-permute-start.3) | collective-permute-done | bytes 65568 | tf_op jit(solution)/shard_map/ppermute | solution.py:156
  29.8 1.7 %shard_map.60 = (f32[64,256]{1,0:T(8,128)S(1)}, bf16[8,64,256]{2,1,0:T(8,128)(2,1)S(1)}) custom-call(s32[2]{0:T(128)S(1)} %pad_add_fusion.place_ref, f32[64,256]{1,0:T(8,128)S(1)} %get-tuple-element.18.kept_ref, f32[64,256]{1,0:T(8,128)S(1)} %collective-permute-done.3.arrived_ref, f32[4,1,128,256]{3,2,1,0:T(8,128)} %rhs_ref.7, ...), custom_call_target="tpu_custom_call" | custom-call | flops 8388608 | tf_op jit(solution)/shard_map/pallas_call | solution.py:27
  31.5 0.0 copy-start.4
  31.5 0.7 copy-done.4
  32.2 4.0 %all-to-all-start.1 = ((bf16[8,64,256]{2,1,0:T(8,128)(2,1)}), bf16[8,64,256]{2,1,0:T(8,128)(2,1)}, u32[]{:S(2)}, u32[]{:S(2)}) async-start(bf16[8,64,256]{2,1,0:T(8,128)(2,1)} %copy-done.4), calls=%async_computation.1 | async-start | bytes 524288 | tf_op jit(solution)/shard_map/all_to_all | solution.py:125
  36.2 3.4 %collective-permute-start.6 = (f32[64,256]{1,0:T(8,128)S(1)}, f32[64,256]{1,0:T(8,128)S(1)}, u32[]{:S(2)}, u32[]{:S(2)}) collective-permute-start(f32[64,256]{1,0:T(8,128)S(1)} %get-tuple-element.21), channel_id=1, source_target_pairs={{0,0},{1,2},{2,1},{3,3},{4,4},{5,6},{6,5},{7,7},{8,8},{9,10},{10,9... | collective-permute-start | bytes 196616 | tf_op jit(solution)/shard_map/ppermute | solution.py:116
  39.7 2.5 %collective-permute-done.6.refs_4_.refs_5_.refs_1_ = f32[64,256]{1,0:T(8,128)S(1)} collective-permute-done((f32[64,256]{1,0:T(8,128)S(1)}, f32[64,256]{1,0:T(8,128)S(1)}, u32[]{:S(2)}, u32[]{:S(2)}) %collective-permute-start.6) | collective-permute-done | bytes 65568 | tf_op jit(solution)/shard_map/ppermute | solution.py:116
  42.2 1.9 %all-to-all-done.1.refs_1_ = bf16[8,64,256]{2,1,0:T(8,128)(2,1)} async-done(((bf16[8,64,256]{2,1,0:T(8,128)(2,1)}), bf16[8,64,256]{2,1,0:T(8,128)(2,1)}, u32[]{:S(2)}, u32[]{:S(2)}) %all-to-all-start.1) | async-done | bytes 262176 | tf_op jit(solution)/shard_map/all_to_all | solution.py:125
  44.1 1.2 %copy-done = bf16[8,256,256]{2,1,0:T(8,128)(2,1)S(1)} copy-done((bf16[8,256,256]{2,1,0:T(8,128)(2,1)S(1)}, bf16[8,256,256]{2,1,0:T(8,128)(2,1)}, u32[]{:S(2)}) %copy-start) | copy-done | bytes 1048600
  45.3 1.5 %shard_map.61 = (f32[64,256]{1,0:T(8,128)S(1)}, f32[64,256]{1,0:T(8,128)S(1)}) custom-call(s32[2]{0:T(128)S(1)} %pad_add_fusion.place_ref, s32[3,1,1,8]{3,2,1,0:T(1,128)S(1)} %compare_select_fusion.ids_ref, s32[3,1,1,8]{3,2,1,0:T(1,128)S(1)} %collective-permute-done.other_ids_ref, bf16[8,64,256]{2,1,0:T(8,128)(2,1)S(1)} %all-to-all-done.refs_0_, ...), custom_call_target="tpu_custom_call" | custom-call | flops 134217728 | bytes 2097152 | tf_op jit(solution)/shard_map/pallas_call | solution.py:27
  46.8 0.1 collective-permute-start.7
  46.9 3.1 %collective-permute-done.7.arrived_ref = f32[64,256]{1,0:T(8,128)S(1)} collective-permute-done((f32[64,256]{1,0:T(8,128)S(1)}, f32[64,256]{1,0:T(8,128)S(1)}, u32[]{:S(2)}, u32[]{:S(2)}) %collective-permute-start.7) | collective-permute-done | bytes 65568 | tf_op jit(solution)/shard_map/ppermute | solution.py:156
  50.0 1.7 %shard_map.62 = (f32[64,256]{1,0:T(8,128)S(1)}, bf16[8,64,256]{2,1,0:T(8,128)(2,1)S(1)}) custom-call(s32[2]{0:T(128)S(1)} %pad_add_fusion.place_ref, f32[64,256]{1,0:T(8,128)S(1)} %get-tuple-element.22.kept_ref, f32[64,256]{1,0:T(8,128)S(1)} %collective-permute-done.7.arrived_ref, f32[4,1,128,256]{3,2,1,0:T(8,128)} %rhs_ref.7, ...), custom_call_target="tpu_custom_call" | custom-call | flops 8388608 | tf_op jit(solution)/shard_map/pallas_call | solution.py:27
  51.7 0.0 copy-start.3
  51.7 0.7 copy-done.3
  52.4 0.6 copy-done.7
  53.0 4.6 %all-to-all-start.2 = ((bf16[8,64,256]{2,1,0:T(8,128)(2,1)}), bf16[8,64,256]{2,1,0:T(8,128)(2,1)}, u32[]{:S(2)}, u32[]{:S(2)}) async-start(bf16[8,64,256]{2,1,0:T(8,128)(2,1)} %copy-done.3), calls=%async_computation.2 | async-start | bytes 524288 | tf_op jit(solution)/shard_map/all_to_all | solution.py:125
  57.6 4.4 %collective-permute-start.8 = (f32[64,256]{1,0:T(8,128)}, f32[64,256]{1,0:T(8,128)S(1)}, u32[]{:S(2)}, u32[]{:S(2)}) collective-permute-start(f32[64,256]{1,0:T(8,128)} %copy-done.7), channel_id=1, source_target_pairs={{0,0},{1,2},{2,1},{3,3},{4,4},{5,6},{6,5},{7,7},{8,8},{9,10},{10,9... | collective-permute-start | bytes 196616 | tf_op jit(solution)/shard_map/ppermute | solution.py:116
  62.1 2.5 %collective-permute-done.8.refs_6_.refs_2_ = f32[64,256]{1,0:T(8,128)S(1)} collective-permute-done((f32[64,256]{1,0:T(8,128)}, f32[64,256]{1,0:T(8,128)S(1)}, u32[]{:S(2)}, u32[]{:S(2)}) %collective-permute-start.8) | collective-permute-done | bytes 65568 | tf_op jit(solution)/shard_map/ppermute | solution.py:116
  64.5 0.3 all-to-all-done.2.refs_2_
  64.8 1.2 %copy-done.2 = bf16[8,256,256]{2,1,0:T(8,128)(2,1)S(1)} copy-done((bf16[8,256,256]{2,1,0:T(8,128)(2,1)S(1)}, bf16[8,256,256]{2,1,0:T(8,128)(2,1)}, u32[]{:S(2)}) %copy-start.2) | copy-done | bytes 1048600
  66.1 1.6 %shard_map.63 = (f32[64,256]{1,0:T(8,128)S(1)}, f32[64,256]{1,0:T(8,128)S(1)}) custom-call(s32[2]{0:T(128)S(1)} %pad_add_fusion.place_ref, s32[3,1,1,8]{3,2,1,0:T(1,128)S(1)} %compare_select_fusion.ids_ref, s32[3,1,1,8]{3,2,1,0:T(1,128)S(1)} %collective-permute-done.other_ids_ref, bf16[8,64,256]{2,1,0:T(8,128)(2,1)S(1)} %all-to-all-done.refs_0_, ...), custom_call_target="tpu_custom_call" | custom-call | flops 134217728 | bytes 2097152 | tf_op jit(solution)/shard_map/pallas_call | solution.py:27
  67.7 0.0 collective-permute-start.10
  67.7 7.2 %collective-permute-start.9 = (f32[64,256]{1,0:T(8,128)S(1)}, f32[64,256]{1,0:T(8,128)S(1)}, u32[]{:S(2)}, u32[]{:S(2)}) collective-permute-start(f32[64,256]{1,0:T(8,128)S(1)} %get-tuple-element.26), channel_id=1, source_target_pairs={{0,0},{1,2},{2,1},{3,3},{4,4},{5,6},{6,5},{7,7},{8,8},{9,10},{10,9... | collective-permute-start | bytes 196616 | tf_op jit(solution)/shard_map/ppermute | solution.py:116
  74.9 1.9 %collective-permute-done.9.first_ref = f32[64,256]{1,0:T(8,128)S(1)} collective-permute-done((f32[64,256]{1,0:T(8,128)S(1)}, f32[64,256]{1,0:T(8,128)S(1)}, u32[]{:S(2)}, u32[]{:S(2)}) %collective-permute-start.9) | collective-permute-done | bytes 65568 | tf_op jit(solution)/shard_map/ppermute | solution.py:116
  76.8 2.1 %shard_map.64 = f32[4,1,64,256]{3,2,1,0:T(8,128)} custom-call(s32[2]{0:T(128)S(1)} %pad_add_fusion.place_ref, f32[64,256]{1,0:T(8,128)S(1)} %collective-permute-done.9.first_ref, f32[64,256]{1,0:T(8,128)S(1)} %collective-permute-done.10.second_ref, f32[4,1,128,256]{3,2,1,0:T(8,128)} %rhs_ref.7, bf16[4,1,256,256]{3,2,1,0:T(8,128)(2,1)} %inverse_ref.7, ...), custom_call_target="tpu_custom_call" | custom-call | flops 8388608 | tf_op jit(solution)/shard_map/pallas_call | solution.py:27
  (7 shorter events, 0.0 us)
Async XLA Ops:
  0.0 23.4 %collective-permute-start.2 = (bf16[3,1,1,8,256,256]{5,4,3,2,1,0:T(8,128)(2,1)}, bf16[3,1,1,8,256,256]{5,4,3,2,1,0:T(8,128)(2,1)S(1)}, u32[]{:S(2)}, u32[]{:S(2)}) collective-permute-start(bf16[3,1,1,8,256,256]{5,4,3,2,1,0:T(8,128)(2,1)} %param.6), channel_id=1, source_target_pairs={{0,2},{2,0},{4,6},{6,4},{8,10},{10,8},{12,14},{14,12},{16,18},{18,... | collective-permute-start | bytes 9437192 | tf_op jit(solution)/shard_map/ppermute | solution.py:119
  1.5 0.6 copy-start.5
  2.1 6.1 %collective-permute-start.1 = (bf16[64,256]{1,0:T(8,128)(2,1)S(1)}, bf16[64,256]{1,0:T(8,128)(2,1)S(1)}, u32[]{:S(2)}, u32[]{:S(2)}) collective-permute-start(bf16[64,256]{1,0:T(8,128)(2,1)S(1)} %get-tuple-element.17), channel_id=1, source_target_pairs={{0,0},{1,2},{2,1},{3,3},{4,4},{5,6},{6,5},{7,7},{8,8},{9,10},{10,9... | collective-permute-start | bytes 98312 | tf_op jit(solution)/shard_map/ppermute | solution.py:116
  6.6 19.2 %collective-permute-start.4 = (f32[4,1,128,256]{3,2,1,0:T(8,128)}, f32[4,1,128,256]{3,2,1,0:T(8,128)}, u32[]{:S(2)}, u32[]{:S(2)}) collective-permute-start(f32[4,1,128,256]{3,2,1,0:T(8,128)} %rhs_ref.7), channel_id=1, source_target_pairs={{0,2},{2,0},{4,6},{6,4},{8,10},{10,8},{12,14},{14,12},{16,18},{18,... | collective-permute-start | bytes 1572872 | tf_op jit(solution)/shard_map/ppermute | solution.py:119
  6.7 19.2 %collective-permute-start.5 = (bf16[4,1,256,256]{3,2,1,0:T(8,128)(2,1)}, bf16[4,1,256,256]{3,2,1,0:T(8,128)(2,1)}, u32[]{:S(2)}, u32[]{:S(2)}) collective-permute-start(bf16[4,1,256,256]{3,2,1,0:T(8,128)(2,1)} %inverse_ref.7), channel_id=1, source_target_pairs={{0,2},{2,0},{4,6},{6,4},{8,10},{10,8},{12,14},{14,12},{16,18},{18,... | collective-permute-start | bytes 1572872 | tf_op jit(solution)/shard_map/ppermute | solution.py:119
  8.9 14.5 %all-to-all-start = ((bf16[8,64,256]{2,1,0:T(8,128)(2,1)}), bf16[8,64,256]{2,1,0:T(8,128)(2,1)S(1)}, u32[]{:S(2)}, u32[]{:S(2)}) async-start(bf16[8,64,256]{2,1,0:T(8,128)(2,1)} %broadcast_in_dim.6), calls=%async_computation | async-start | bytes 524288 | tf_op jit(solution)/shard_map/all_to_all | solution.py:125
  15.8 3.6 %collective-permute-start = (s32[3,1,1,8]{3,2,1,0:T(1,128)S(1)}, s32[3,1,1,8]{3,2,1,0:T(1,128)S(1)}, u32[]{:S(2)}, u32[]{:S(2)}) collective-permute-start(s32[3,1,1,8]{3,2,1,0:T(1,128)S(1)} %compare_select_fusion.ids_ref), channel_id=1, source_target_pairs={{0,2},{2,0},{4,6},{6,4},{8,10},{10,8},{12,14},{14,12},{16,18},{18,... | collective-permute-start | bytes 296 | tf_op jit(solution)/shard_map/ppermute | solution.py:119
  23.4 1.2 %copy-start.1 = (bf16[8,256,256]{2,1,0:T(8,128)(2,1)S(1)}, bf16[8,256,256]{2,1,0:T(8,128)(2,1)}, u32[]{:S(2)}) copy-start(bf16[8,256,256]{2,1,0:T(8,128)(2,1)} %get-tuple-element.30.refs_1_) | copy-start | bytes 3145732
  25.7 4.0 %collective-permute-start.3 = (f32[64,256]{1,0:T(8,128)S(1)}, f32[64,256]{1,0:T(8,128)S(1)}, u32[]{:S(2)}, u32[]{:S(2)}) collective-permute-start(f32[64,256]{1,0:T(8,128)S(1)} %get-tuple-element.19), channel_id=1, source_target_pairs={{0,1},{1,0},{2,3},{3,2},{4,5},{5,4},{6,7},{7,6},{8,9},{9,8},{10,11... | collective-permute-start | bytes 196616 | tf_op jit(solution)/shard_map/ppermute | solution.py:156
  31.5 0.7 copy-start.4
  32.2 11.9 %all-to-all-start.1 = ((bf16[8,64,256]{2,1,0:T(8,128)(2,1)}), bf16[8,64,256]{2,1,0:T(8,128)(2,1)}, u32[]{:S(2)}, u32[]{:S(2)}) async-start(bf16[8,64,256]{2,1,0:T(8,128)(2,1)} %copy-done.4), calls=%async_computation.1 | async-start | bytes 524288 | tf_op jit(solution)/shard_map/all_to_all | solution.py:125
  36.2 6.0 %collective-permute-start.6 = (f32[64,256]{1,0:T(8,128)S(1)}, f32[64,256]{1,0:T(8,128)S(1)}, u32[]{:S(2)}, u32[]{:S(2)}) collective-permute-start(f32[64,256]{1,0:T(8,128)S(1)} %get-tuple-element.21), channel_id=1, source_target_pairs={{0,0},{1,2},{2,1},{3,3},{4,4},{5,6},{6,5},{7,7},{8,8},{9,10},{10,9... | collective-permute-start | bytes 196616 | tf_op jit(solution)/shard_map/ppermute | solution.py:116
  44.1 1.2 %copy-start = (bf16[8,256,256]{2,1,0:T(8,128)(2,1)S(1)}, bf16[8,256,256]{2,1,0:T(8,128)(2,1)}, u32[]{:S(2)}) copy-start(bf16[8,256,256]{2,1,0:T(8,128)(2,1)} %get-tuple-element.31.refs_2_) | copy-start | bytes 3145732
  46.8 3.2 %collective-permute-start.7 = (f32[64,256]{1,0:T(8,128)S(1)}, f32[64,256]{1,0:T(8,128)S(1)}, u32[]{:S(2)}, u32[]{:S(2)}) collective-permute-start(f32[64,256]{1,0:T(8,128)S(1)} %get-tuple-element.23), channel_id=1, source_target_pairs={{0,1},{1,0},{2,3},{3,2},{4,5},{5,4},{6,7},{7,6},{8,9},{9,8},{10,11... | collective-permute-start | bytes 196616 | tf_op jit(solution)/shard_map/ppermute | solution.py:156
  51.7 0.7 copy-start.3
  52.4 0.6 copy-start.7
  53.0 11.8 %all-to-all-start.2 = ((bf16[8,64,256]{2,1,0:T(8,128)(2,1)}), bf16[8,64,256]{2,1,0:T(8,128)(2,1)}, u32[]{:S(2)}, u32[]{:S(2)}) async-start(bf16[8,64,256]{2,1,0:T(8,128)(2,1)} %copy-done.3), calls=%async_computation.2 | async-start | bytes 524288 | tf_op jit(solution)/shard_map/all_to_all | solution.py:125
  57.6 6.9 %collective-permute-start.8 = (f32[64,256]{1,0:T(8,128)}, f32[64,256]{1,0:T(8,128)S(1)}, u32[]{:S(2)}, u32[]{:S(2)}) collective-permute-start(f32[64,256]{1,0:T(8,128)} %copy-done.7), channel_id=1, source_target_pairs={{0,0},{1,2},{2,1},{3,3},{4,4},{5,6},{6,5},{7,7},{8,8},{9,10},{10,9... | collective-permute-start | bytes 196616 | tf_op jit(solution)/shard_map/ppermute | solution.py:116
  64.8 1.2 %copy-start.2 = (bf16[8,256,256]{2,1,0:T(8,128)(2,1)S(1)}, bf16[8,256,256]{2,1,0:T(8,128)(2,1)}, u32[]{:S(2)}) copy-start(bf16[8,256,256]{2,1,0:T(8,128)(2,1)} %get-tuple-element.29.refs_3_) | copy-start | bytes 3145732
  66.1 10.8 %copy-start.6 = (f32[64,256]{1,0:T(8,128)S(1)}, f32[64,256]{1,0:T(8,128)}, u32[]{:S(2)}) copy-start(f32[64,256]{1,0:T(8,128)} %copy-done.5) | copy-start | bytes 196612
  67.7 7.2 %collective-permute-start.10 = (f32[64,256]{1,0:T(8,128)S(1)}, f32[64,256]{1,0:T(8,128)S(1)}, u32[]{:S(2)}, u32[]{:S(2)}) collective-permute-start(f32[64,256]{1,0:T(8,128)S(1)} %get-tuple-element.27), channel_id=1, source_target_pairs={{0,2},{1,0},{2,3},{3,1},{4,6},{5,4},{6,7},{7,5},{8,10},{9,8},{10,1... | collective-permute-start | bytes 196616 | tf_op jit(solution)/shard_map/ppermute | solution.py:116
  67.7 9.1 %collective-permute-start.9 = (f32[64,256]{1,0:T(8,128)S(1)}, f32[64,256]{1,0:T(8,128)S(1)}, u32[]{:S(2)}, u32[]{:S(2)}) collective-permute-start(f32[64,256]{1,0:T(8,128)S(1)} %get-tuple-element.26), channel_id=1, source_target_pairs={{0,0},{1,2},{2,1},{3,3},{4,4},{5,6},{6,5},{7,7},{8,8},{9,10},{10,9... | collective-permute-start | bytes 196616 | tf_op jit(solution)/shard_map/ppermute | solution.py:116

commit v5 on v4

--- a/solution.py
+++ b/solution.py
@@ -7,11 +7,13 @@
 from jax.experimental.pallas import tpu as pltpu
 from jax.sharding import PartitionSpec as P
 
-VMEM_LIMIT = 32 * 1024 * 1024
+VMEM_LIMIT = 16 * 1024 * 1024
 
 
 VMEM = pl.BlockSpec(memory_space=pltpu.VMEM)
 SMEM = pl.BlockSpec(memory_space=pltpu.SMEM)
+ANY = pl.BlockSpec(memory_space=pl.ANY)
+HBM = pl.BlockSpec(memory_space=pltpu.HBM)
 
 
 def flat_dot(gathered, factor_ref):
@@ -26,71 +28,115 @@
 def run(kernel, outs, args, scratch=(), flops=0, transferred=0):
     return pl.pallas_call(
         kernel,
-        out_shape=outs,
-        in_specs=[SMEM if x.dtype == jnp.int32 else VMEM for x in args],
-        out_specs=jax.tree.map(lambda _: VMEM, outs),
+        out_shape=tuple(pltpu.HBM(x.shape, x.dtype) if spec is HBM else x for x, spec in outs),
+        in_specs=[spec for _, spec in args],
+        out_specs=tuple(spec for _, spec in outs),
         scratch_shapes=list(scratch),
         compiler_params=pltpu.CompilerParams(vmem_limit_bytes=VMEM_LIMIT),
         cost_estimate=pl.CostEstimate(flops=flops, bytes_accessed=transferred, transcendentals=0),
-    )(*args)
+    )(*(pltpu.with_memory_space_constraint(x, pltpu.HBM) if spec is HBM else x for x, spec in args))
 
 
 def half_of(ref, level, half, rows):
-    return ref[level, 0, pl.ds(pl.multiple_of(half * rows, rows), rows), :]
+    return ref.at[level, 0, pl.ds(pl.multiple_of(half * rows, rows), rows), :]
 
 
 def solve(reduced, inverse):
     return jnp.dot(reduced.astype(jnp.bfloat16), inverse, preferred_element_type=jnp.float32)
 
 
-def first_kernel(place_ref, rhs_ref, inverse_ref, out_ref, rounded_ref):
+def start_copies(pairs, sems):
+    copies = [pltpu.make_async_copy(src, dst, sems.at[i]) for i, (src, dst) in enumerate(pairs)]
+    for copy in copies:
+        copy.start()
+    return copies
+
+
+def live_kernel(ids_ref, counts_ref, live_ids_ref):
+    for l in range(ids_ref.shape[0]):
+        for k in range(ids_ref.shape[3]):
+            live = k < counts_ref[l, 0, 0]
+            live_ids_ref[l, 0, 0, k] = jnp.where(live, ids_ref[l, 0, 0, k], -1)
+
+
+def first_kernel(place_ref, rhs_ref, inverse_ref, out_ref, rounded_ref, rhs, inverse, sems):
     rows = out_ref.shape[0]
-    solved = solve(half_of(rhs_ref, 0, place_ref[1], rows), inverse_ref[0, 0])
+    copies = start_copies(
+        [(half_of(rhs_ref, 0, place_ref[1], rows), rhs), (inverse_ref.at[0, 0], inverse)], sems
+    )
+    for copy in copies:
+        copy.wait()
+    solved = solve(rhs[...], inverse[...])
     out_ref[...] = solved
     rounded_ref[...] = solved.astype(jnp.bfloat16)
 
 
-def sums_kernel(level, chips, place_ref, ids_ref, other_ids_ref, *refs):
+def sums_kernel(level, chips, inner, place_ref, ids_ref, other_ids_ref, *refs):
     store_refs = refs[:level]
-    factor_refs = (refs[level], refs[level + 1].at[level - 1, 0, 0])
-    kept_ref, sent_ref, store, gathered = refs[-4:]
-    slots, width = factor_refs[0].shape[0], factor_refs[0].shape[1]
+    own_factor_ref, other_factor_ref, rhs_ref, other_rhs_ref, inverse_ref, other_inverse_ref = refs[level:level + 6]
+    kept_ref, sent_ref, own_rhs_ref, own_inverse_ref = refs[-10:-6]
+    store, gathered, own_factor, rhs, inverse, sems = refs[-6:]
+    slots, width = own_factor.shape[0], own_factor.shape[1]
+    rows = kept_ref.shape[0]
+    core, col = place_ref[0], place_ref[1]
+    straight = core == col
+    if inner:
+        pairs = [
+            (half_of(rhs_ref, level, core, rows), rhs.at[0]),
+            (half_of(other_rhs_ref, level, core, rows), rhs.at[1]),
+            (inverse_ref.at[level, 0], inverse.at[0]),
+            (other_inverse_ref.at[level, 0], inverse.at[1]),
+        ]
+    else:
+        pairs = [
+            (half_of(rhs_ref, level, col, rows), own_rhs_ref),
+            (inverse_ref.at[level, 0], own_inverse_ref),
+        ]
+    copies = start_copies([(own_factor_ref.at[level - 1, 0, 0], own_factor)] + pairs, sems)
     for m, piece in enumerate(store_refs):
         store[m * chips:(m + 1) * chips] = piece[...]
-    sums = []
-    for ids, factor_ref in zip((ids_ref, other_ids_ref), factor_refs):
+
+    def group_sum(ids, factor_ref):
         for k in range(slots):
             source = ids[level - 1, 0, 0, k]
             known = jnp.maximum(source, 0)
             piece = store[known // (2 * chips) * chips + known % (2 * chips) // 2]
             live = jnp.where(source >= 0, 1.0, 0.0).astype(piece.dtype)
             gathered[:, k * width:(k + 1) * width] = piece * live
-        sums.append(flat_dot(gathered, factor_ref))
-    straight = place_ref[0] == place_ref[1]
-    kept_ref[...] = jnp.where(straight, sums[0], sums[1])
-    sent_ref[...] = jnp.where(straight, sums[1], sums[0])
-
-
-def inner_kernel(level, place_ref, kept_ref, arrived_ref, rhs_ref, other_rhs_ref, inverse_ref, other_inverse_ref, out_ref, copies_ref):
-    rows = out_ref.shape[0]
-    core = place_ref[0]
-    straight = core == place_ref[1]
-    rhs = jnp.where(straight, half_of(rhs_ref, level, core, rows), half_of(other_rhs_ref, level, core, rows))
-    inverse = jnp.where(straight, inverse_ref[level, 0], other_inverse_ref[level, 0])
-    solved = solve(rhs - (kept_ref[...] + arrived_ref[...]), inverse)
+        return flat_dot(gathered, factor_ref)
+
+    other = group_sum(other_ids_ref, other_factor_ref.at[level - 1, 0, 0])
+    copies[0].wait()
+    own = group_sum(ids_ref, own_factor)
+    kept_ref[...] = jnp.where(straight, own, other)
+    sent_ref[...] = jnp.where(straight, other, own)
+    for copy in copies[1:]:
+        copy.wait()
+    if inner:
+        own_rhs_ref[...] = jnp.where(straight, rhs[0], rhs[1])
+        own_inverse_ref[...] = jnp.where(straight, inverse[0], inverse[1])
+
+
+def copies_kernel(rounded_ref, copies_ref, sems):
+    for copy in start_copies([(rounded_ref, copies_ref.at[i]) for i in range(copies_ref.shape[0])], sems):
+        copy.wait()
+
+
+def inner_kernel(kept_ref, arrived_ref, rhs_ref, inverse_ref, out_ref, copies_ref, rounded, sems):
+    solved = solve(rhs_ref[...] - (kept_ref[...] + arrived_ref[...]), inverse_ref[...])
+    rounded[...] = solved.astype(jnp.bfloat16)
+    copies = start_copies([(rounded, copies_ref.at[i]) for i in range(copies_ref.shape[0])], sems)
     out_ref[...] = solved
-    rounded = solved.astype(jnp.bfloat16)
-    for i in range(copies_ref.shape[0]):
-        copies_ref[i] = rounded
-
-
-def last_kernel(place_ref, first_ref, second_ref, rhs_ref, inverse_ref, *refs):
+    for copy in copies:
+        copy.wait()
+
+
+def last_kernel(first_ref, second_ref, rhs_ref, inverse_ref, *refs):
     done_refs, out_ref = refs[:-1], refs[-1]
-    rows, level = out_ref.shape[2], len(done_refs)
     for m, done in enumerate(done_refs):
         out_ref[m, 0] = done[...]
-    rhs = half_of(rhs_ref, level, place_ref[1], rows)
-    out_ref[level, 0] = solve(rhs - (first_ref[...] + second_ref[...]), inverse_ref[level, 0])
+    solved = solve(rhs_ref[...] - (first_ref[...] + second_ref[...]), inverse_ref[...])
+    out_ref[len(done_refs), 0] = solved
 
 
 def paired_shards(row_count, right_sides, factor_blocks, diag_inverses, source_ids, block_counts):
@@ -103,6 +149,7 @@
     same_core = [[2 * j + k for j in range(chips)] for k in range(2)]
     part = jax.ShapeDtypeStruct((rows, width), jnp.float32)
     rounded_part = jax.ShapeDtypeStruct((rows, width), jnp.bfloat16)
+    square = jax.ShapeDtypeStruct((width, width), jnp.bfloat16)
     copies = jax.ShapeDtypeStruct((chips, rows, width), jnp.bfloat16)
     solve_flops = 2 * rows * width * width
 
@@ -125,14 +172,30 @@
         return lax.all_to_all(x, "rows", 0, 0, axis_index_groups=same_core)
 
     solved, rounded = run(
-        first_kernel, (part, rounded_part), (place, right_sides, diag_inverses), flops=solve_flops
+        first_kernel,
+        ((part, VMEM), (rounded_part, VMEM)),
+        ((place, SMEM), (right_sides, HBM), (diag_inverses, HBM)),
+        scratch=(
+            pltpu.VMEM(part.shape, part.dtype),
+            pltpu.VMEM(square.shape, square.dtype),
+            pltpu.SemaphoreType.DMA((2,)),
+        ),
+        flops=solve_flops,
     )
     finished = [solved]
     moved = transpose(rounded)
-    stores = [spread(jnp.broadcast_to(moved[None], copies.shape))]
-
-    live_ids = jnp.where(
-        jnp.arange(slots, dtype=jnp.int32) < block_counts[..., None], source_ids, -1
+    copied, = run(
+        copies_kernel,
+        ((copies, HBM),),
+        ((moved, VMEM),),
+        scratch=(pltpu.SemaphoreType.DMA((chips,)),),
+    )
+    stores = [spread(copied)]
+
+    live_ids, = run(
+        live_kernel,
+        ((jax.ShapeDtypeStruct(source_ids.shape, source_ids.dtype), SMEM),),
+        ((source_ids, SMEM), (block_counts, SMEM)),
     )
     other_factors = swap_core(factor_blocks)
     other_ids = swap_core(live_ids)
@@ -140,24 +203,36 @@
     other_rhs = swap_core(right_sides)
 
     for l in range(1, level_count):
-        kept, sent = run(
-            functools.partial(sums_kernel, l, chips),
-            (part, part),
-            (place, live_ids, other_ids, *stores, factor_blocks[l - 1, 0, 0], other_factors)
-            + tuple(finished[1:]),
+        inner = l < level_count - 1
+        kept, sent, rhs, inverse = run(
+            functools.partial(sums_kernel, l, chips, inner),
+            ((part, VMEM), (part, VMEM), (part, VMEM), (square, VMEM)),
+            ((place, SMEM), (live_ids, SMEM), (other_ids, SMEM))
+            + tuple((store, VMEM) for store in stores)
+            + ((factor_blocks, HBM), (other_factors, VMEM))
+            + ((right_sides, HBM), (other_rhs, ANY), (diag_inverses, HBM), (other_inverses, ANY))
+            + tuple((x, ANY) for x in finished[1:]),
             scratch=(
                 pltpu.VMEM((l * chips, rows, width), jnp.bfloat16),
                 pltpu.VMEM((rows, slots * width), jnp.bfloat16),
+                pltpu.VMEM((slots, width, width), jnp.bfloat16),
+                pltpu.VMEM((2, rows, width), jnp.float32),
+                pltpu.VMEM((2, width, width), jnp.bfloat16),
+                pltpu.SemaphoreType.DMA((5,)),
             ),
             flops=2 * slots * solve_flops,
             transferred=2 * slots * width * width * 2,
         )
-        if l < level_count - 1:
+        if inner:
             arrived = lax.ppermute(sent, "cols", [(0, 1), (1, 0)])
             solved, copied = run(
-                functools.partial(inner_kernel, l),
-                (part, copies),
-                (place, kept, arrived, right_sides, other_rhs, diag_inverses, other_inverses),
+                inner_kernel,
+                ((part, VMEM), (copies, HBM)),
+                ((kept, VMEM), (arrived, VMEM), (rhs, VMEM), (inverse, VMEM)),
+                scratch=(
+                    pltpu.VMEM((rows, width), jnp.bfloat16),
+                    pltpu.SemaphoreType.DMA((chips,)),
+                ),
                 flops=solve_flops,
             )
             finished.append(transpose(solved))
@@ -165,12 +240,13 @@
         else:
             first = over_both(kept, lambda j, k, c: (j, c, k))
             second = over_both(sent, lambda j, k, c: (j, 1 - c, k))
+            out = jax.ShapeDtypeStruct((level_count, 1, rows, width), jnp.float32)
             return run(
                 last_kernel,
-                jax.ShapeDtypeStruct((level_count, 1, rows, width), jnp.float32),
-                (place, first, second, right_sides, diag_inverses, *finished),
+                ((out, VMEM),),
+                tuple((x, VMEM) for x in (first, second, rhs, inverse, *finished)),
                 flops=solve_flops,
-            )
+            )[0]
 
 
 def gather_slots(ids_ref, counts_ref, group, store_ref, gathered, slots, width):

time: 79.7 us -> 76.6 us (0.961)
  the two profiles are of different devices: /device:TPU:1 before, /device:TPU:0 now
where the time goes in v5:
time: 76.6 us; the launch traced here: 75.9 us
  starting transfers between devices  35.7 us (47%)
  waiting for transfers between devices  22.4 us (29%)
  Pallas kernels  14.8 us (19%)
  local copies, waits for them, and re-layouts  2.67 us (3%)
    all_to_all x3, starting transfers between devices, spread(): return lax.all_to_all(x, 'rows', 0, 0, axis_index_groups=same_core)  14.9 us
    pallas_call x9, Pallas kernels, run(): pl.pallas_call(kernel, out_shape=tuple((pltpu.HBM(x.shape, x.dtype) if sp...  14.8 us
    all_to_all x3, waiting for transfers between devices, spread(): return lax.all_to_all(x, 'rows', 0, 0, axis_index_groups=same_core)  14.3 us
    ppermute x2, starting transfers between devices, paired_shards(): arrived = lax.ppermute(sent, 'cols', [(0, 1), (1, 0)])  8.13 us
    ppermute x5, starting transfers between devices, over_both(): return lax.ppermute(x, ('rows', 'cols'), pairs)  6.85 us
    ppermute x4, starting transfers between devices, swap_core(): return lax.ppermute(x, 'rows', [(i, i ^ 1) for i in range(row_count)])  5.8 us
    ppermute x2, waiting for transfers between devices, paired_shards(): arrived = lax.ppermute(sent, 'cols', [(0, 1), (1, 0)])  4.49 us
    ppermute x5, waiting for transfers between devices, over_both(): return lax.ppermute(x, ('rows', 'cols'), pairs)  2.81 us
  transfers between devices with their start and end apart: 14, of which 6 were waited for; matrix products, arithmetic and copies ran while one was open for 1% of the time, Pallas kernels for 5%

profile of v5, /device:TPU:0, one launch (start us, length us, event | category | flops | bytes accessed | tf_op | source)
XLA Modules:
  0.0 75.9 jit_solution(1355593214361959875)
XLA Ops:
  0.0 0.5 collective-permute-start.2
  0.5 0.1 collective-permute-start.3
  0.5 0.5 collective-permute-start.4
  1.0 0.1 pad_add_fusion.place_ref
  1.0 1.7 %shard_map.56 = (f32[64,256]{1,0:T(8,128)S(1)}, bf16[64,256]{1,0:T(8,128)(2,1)S(1)}) custom-call(s32[2]{0:T(128)S(1)} %pad_add_fusion.place_ref, f32[4,1,128,256]{3,2,1,0:T(8,128)} %refs_5_.3, bf16[4,1,256,256]{3,2,1,0:T(8,128)(2,1)} %refs_7_.1), custom_call_target="tpu_custom_call" | custom-call | flops 8388608 | tf_op jit(solution)/shard_map/pallas_call | solution.py:29
  2.7 0.0 copy-start
  2.7 0.6 copy-done
  3.3 0.7 collective-permute-start.1
  4.0 0.0 collective-permute-done.1.rounded_ref
  4.0 0.8 %shard_map.57 = bf16[8,64,256]{2,1,0:T(8,128)(2,1)} custom-call(bf16[64,256]{1,0:T(8,128)(2,1)S(1)} %collective-permute-done.1.rounded_ref), custom_call_target="tpu_custom_call" | custom-call | tf_op jit(solution)/shard_map/pallas_call | solution.py:29
  4.8 6.8 %all-to-all-start = ((bf16[8,64,256]{2,1,0:T(8,128)(2,1)}), bf16[8,64,256]{2,1,0:T(8,128)(2,1)S(1)}, u32[]{:S(2)}, u32[]{:S(2)}) async-start(bf16[8,64,256]{2,1,0:T(8,128)(2,1)} %shard_map.57), calls=%async_computation | async-start | bytes 524288 | tf_op jit(solution)/shard_map/all_to_all | solution.py:172
  11.6 0.7 copy.6.counts_ref
  12.3 0.0 copy-start.2
  12.3 0.7 copy-done.2
  13.0 1.2 %shard_map.55.ids_ref = s32[3,1,1,8]{3,2,1,0:T(1,128)S(1)} custom-call(s32[3,1,1,8]{3,2,1,0:T(1,128)S(1)} %copy-done.2, s32[3,1,1]{2,1,0:T(1,128)S(1)} %copy.6.counts_ref), custom_call_target="tpu_custom_call" | custom-call | tf_op jit(solution)/shard_map/pallas_call | solution.py:29
  14.2 4.8 %collective-permute-start = (s32[3,1,1,8]{3,2,1,0:T(1,128)S(1)}, s32[3,1,1,8]{3,2,1,0:T(1,128)S(1)}, u32[]{:S(2)}, u32[]{:S(2)}) collective-permute-start(s32[3,1,1,8]{3,2,1,0:T(1,128)S(1)} %shard_map.55.ids_ref), channel_id=1, source_target_pairs={{0,2},{2,0},{4,6},{6,4},{8,10},{10,8},{12,14},{14,12},{16,18},{18,... | collective-permute-start | bytes 296 | tf_op jit(solution)/shard_map/ppermute | solution.py:166
  19.1 0.8 %collective-permute-done.other_ids_ref = s32[3,1,1,8]{3,2,1,0:T(1,128)S(1)} collective-permute-done((s32[3,1,1,8]{3,2,1,0:T(1,128)S(1)}, s32[3,1,1,8]{3,2,1,0:T(1,128)S(1)}, u32[]{:S(2)}, u32[]{:S(2)}) %collective-permute-start) | collective-permute-done | bytes 128 | tf_op jit(solution)/shard_map/ppermute | solution.py:166
  19.9 0.0 all-to-all-done.refs_0_
  19.9 0.0 collective-permute-done.3.refs_4_.refs_5_.refs_6_
  19.9 0.0 collective-permute-done.4.refs_6_.refs_7_.refs_8_
  19.9 0.0 collective-permute-done.2.refs_2_.refs_3_.refs_4_
  19.9 2.6 %shard_map.58 = (f32[64,256]{1,0:T(8,128)S(1)}, f32[64,256]{1,0:T(8,128)S(1)}, f32[64,256]{1,0:T(8,128)S(1)}, bf16[256,256]{1,0:T(8,128)(2,1)S(1)}) custom-call(s32[2]{0:T(128)S(1)} %pad_add_fusion.place_ref, s32[3,1,1,8]{3,2,1,0:T(1,128)S(1)} %shard_map.55.ids_ref, s32[3,1,1,8]{3,2,1,0:T(1,128)S(1)} %collective-permute-done.other_ids_ref, ...), custom_call_target="tpu_custom_call" | custom-call | flops 134217728 | bytes 2097152 | tf_op jit(solution)/shard_map/pallas_call | solution.py:29
  22.5 6.0 %collective-permute-start.5 = (f32[64,256]{1,0:T(8,128)S(1)}, f32[64,256]{1,0:T(8,128)S(1)}, u32[]{:S(2)}, u32[]{:S(2)}) collective-permute-start(f32[64,256]{1,0:T(8,128)S(1)} %get-tuple-element.25), channel_id=1, source_target_pairs={{0,1},{1,0},{2,3},{3,2},{4,5},{5,4},{6,7},{7,6},{8,9},{9,8},{10,11... | collective-permute-start | bytes 196616 | tf_op jit(solution)/shard_map/ppermute | solution.py:227
  28.5 2.2 %collective-permute-done.5.arrived_ref = f32[64,256]{1,0:T(8,128)S(1)} collective-permute-done((f32[64,256]{1,0:T(8,128)S(1)}, f32[64,256]{1,0:T(8,128)S(1)}, u32[]{:S(2)}, u32[]{:S(2)}) %collective-permute-start.5) | collective-permute-done | bytes 65568 | tf_op jit(solution)/shard_map/ppermute | solution.py:227
  30.8 0.9 %shard_map.59 = (f32[64,256]{1,0:T(8,128)S(1)}, bf16[8,64,256]{2,1,0:T(8,128)(2,1)}) custom-call(f32[64,256]{1,0:T(8,128)S(1)} %get-tuple-element.24.kept_ref, f32[64,256]{1,0:T(8,128)S(1)} %collective-permute-done.5.arrived_ref, f32[64,256]{1,0:T(8,128)S(1)} %get-tuple-element.26.rhs_ref, bf16[256,256]{1,0:T(8,128)(2,1)S(1)} %get-tuple-element.27.inverse_ref), custom_call_target="tpu_custom_call" | custom-call | flops 8388608 | tf_op jit(solution)/shard_map/pallas_call | solution.py:29
  31.7 4.1 %all-to-all-start.1 = ((bf16[8,64,256]{2,1,0:T(8,128)(2,1)}), bf16[8,64,256]{2,1,0:T(8,128)(2,1)}, u32[]{:S(2)}, u32[]{:S(2)}) async-start(bf16[8,64,256]{2,1,0:T(8,128)(2,1)} %get-tuple-element.28), calls=%async_computation.1 | async-start | bytes 524288 | tf_op jit(solution)/shard_map/all_to_all | solution.py:172
  35.8 0.7 collective-permute-start.6
  36.5 0.0 collective-permute-done.6.refs_8_.refs_9_.refs_1_
  36.5 7.6 %all-to-all-done.1.refs_1_ = bf16[8,64,256]{2,1,0:T(8,128)(2,1)} async-done(((bf16[8,64,256]{2,1,0:T(8,128)(2,1)}), bf16[8,64,256]{2,1,0:T(8,128)(2,1)}, u32[]{:S(2)}, u32[]{:S(2)}) %all-to-all-start.1) | async-done | bytes 262176 | tf_op jit(solution)/shard_map/all_to_all | solution.py:172
  44.0 2.9 %shard_map.60 = (f32[64,256]{1,0:T(8,128)S(1)}, f32[64,256]{1,0:T(8,128)S(1)}, f32[64,256]{1,0:T(8,128)S(1)}, bf16[256,256]{1,0:T(8,128)(2,1)S(1)}) custom-call(s32[2]{0:T(128)S(1)} %pad_add_fusion.place_ref, s32[3,1,1,8]{3,2,1,0:T(1,128)S(1)} %shard_map.55.ids_ref, s32[3,1,1,8]{3,2,1,0:T(1,128)S(1)} %collective-permute-done.other_ids_ref, ...), custom_call_target="tpu_custom_call" | custom-call | flops 134217728 | bytes 2097152 | tf_op jit(solution)/shard_map/pallas_call | solution.py:29
  47.0 2.1 %collective-permute-start.7 = (f32[64,256]{1,0:T(8,128)S(1)}, f32[64,256]{1,0:T(8,128)S(1)}, u32[]{:S(2)}, u32[]{:S(2)}) collective-permute-start(f32[64,256]{1,0:T(8,128)S(1)} %get-tuple-element.31), channel_id=1, source_target_pairs={{0,1},{1,0},{2,3},{3,2},{4,5},{5,4},{6,7},{7,6},{8,9},{9,8},{10,11... | collective-permute-start | bytes 196616 | tf_op jit(solution)/shard_map/ppermute | solution.py:227
  49.1 2.2 %collective-permute-done.7.arrived_ref = f32[64,256]{1,0:T(8,128)S(1)} collective-permute-done((f32[64,256]{1,0:T(8,128)S(1)}, f32[64,256]{1,0:T(8,128)S(1)}, u32[]{:S(2)}, u32[]{:S(2)}) %collective-permute-start.7) | collective-permute-done | bytes 65568 | tf_op jit(solution)/shard_map/ppermute | solution.py:227
  51.3 0.9 %shard_map.61 = (f32[64,256]{1,0:T(8,128)S(1)}, bf16[8,64,256]{2,1,0:T(8,128)(2,1)}) custom-call(f32[64,256]{1,0:T(8,128)S(1)} %get-tuple-element.30.kept_ref, f32[64,256]{1,0:T(8,128)S(1)} %collective-permute-done.7.arrived_ref, f32[64,256]{1,0:T(8,128)S(1)} %get-tuple-element.32.rhs_ref, bf16[256,256]{1,0:T(8,128)(2,1)S(1)} %get-tuple-element.33.inverse_ref), custom_call_target="tpu_custom_call" | custom-call | flops 8388608 | tf_op jit(solution)/shard_map/pallas_call | solution.py:29
  52.2 0.0 copy-start.3
  52.2 0.6 copy-done.3
  52.9 4.1 %all-to-all-start.2 = ((bf16[8,64,256]{2,1,0:T(8,128)(2,1)}), bf16[8,64,256]{2,1,0:T(8,128)(2,1)}, u32[]{:S(2)}, u32[]{:S(2)}) async-start(bf16[8,64,256]{2,1,0:T(8,128)(2,1)} %get-tuple-element.34), calls=%async_computation.2 | async-start | bytes 524288 | tf_op jit(solution)/shard_map/all_to_all | solution.py:172
  56.9 1.5 %collective-permute-start.8 = (f32[64,256]{1,0:T(8,128)}, f32[64,256]{1,0:T(8,128)S(1)}, u32[]{:S(2)}, u32[]{:S(2)}) collective-permute-start(f32[64,256]{1,0:T(8,128)} %copy-done.3), channel_id=1, source_target_pairs={{0,0},{1,2},{2,1},{3,3},{4,4},{5,6},{6,5},{7,7},{8,8},{9,10},{10,9... | collective-permute-start | bytes 196616 | tf_op jit(solution)/shard_map/ppermute | solution.py:163
  58.4 0.0 collective-permute-done.8.refs_10_.refs_2_
  58.4 6.8 %all-to-all-done.2.refs_2_ = bf16[8,64,256]{2,1,0:T(8,128)(2,1)} async-done(((bf16[8,64,256]{2,1,0:T(8,128)(2,1)}), bf16[8,64,256]{2,1,0:T(8,128)(2,1)}, u32[]{:S(2)}, u32[]{:S(2)}) %all-to-all-start.2) | async-done | bytes 262176 | tf_op jit(solution)/shard_map/all_to_all | solution.py:172
  65.2 0.0 copy-start.1
  65.2 3.0 %shard_map.62 = (f32[64,256]{1,0:T(8,128)S(1)}, f32[64,256]{1,0:T(8,128)S(1)}, f32[64,256]{1,0:T(8,128)S(1)}, bf16[256,256]{1,0:T(8,128)(2,1)S(1)}) custom-call(s32[2]{0:T(128)S(1)} %pad_add_fusion.place_ref, s32[3,1,1,8]{3,2,1,0:T(1,128)S(1)} %shard_map.55.ids_ref, s32[3,1,1,8]{3,2,1,0:T(1,128)S(1)} %collective-permute-done.other_ids_ref, ...), custom_call_target="tpu_custom_call" | custom-call | flops 134217728 | bytes 2097152 | tf_op jit(solution)/shard_map/pallas_call | solution.py:29
  68.2 0.7 collective-permute-start.9
  68.9 3.4 %collective-permute-start.10 = (f32[64,256]{1,0:T(8,128)S(1)}, f32[64,256]{1,0:T(8,128)S(1)}, u32[]{:S(2)}, u32[]{:S(2)}) collective-permute-start(f32[64,256]{1,0:T(8,128)S(1)} %get-tuple-element.37), channel_id=1, source_target_pairs={{0,2},{1,0},{2,3},{3,1},{4,6},{5,4},{6,7},{7,5},{8,10},{9,8},{10,1... | collective-permute-start | bytes 196616 | tf_op jit(solution)/shard_map/ppermute | solution.py:163
  72.2 0.0 collective-permute-done.9.first_ref
  72.2 2.8 %collective-permute-done.10.second_ref = f32[64,256]{1,0:T(8,128)S(1)} collective-permute-done((f32[64,256]{1,0:T(8,128)S(1)}, f32[64,256]{1,0:T(8,128)S(1)}, u32[]{:S(2)}, u32[]{:S(2)}) %collective-permute-start.10) | collective-permute-done | bytes 65568 | tf_op jit(solution)/shard_map/ppermute | solution.py:163
  75.0 0.0 copy-done.1
  75.0 0.9 %shard_map.63 = f32[4,1,64,256]{3,2,1,0:T(8,128)} custom-call(f32[64,256]{1,0:T(8,128)S(1)} %collective-permute-done.9.first_ref, f32[64,256]{1,0:T(8,128)S(1)} %collective-permute-done.10.second_ref, f32[64,256]{1,0:T(8,128)S(1)} %get-tuple-element.38.rhs_ref, bf16[256,256]{1,0:T(8,128)(2,1)S(1)} %get-tuple-element.39.inverse_ref, f32[64,256]{1,0:T(8,128)S(1)} %copy-done.1, ...), custom_call_target="tpu_custom_call" | custom-call | flops 8388608 | tf_op jit(solution)/shard_map/pallas_call | solution.py:29
Async XLA Ops:
  0.0 19.9 %collective-permute-start.2 = (bf16[3,1,1,8,256,256]{5,4,3,2,1,0:T(8,128)(2,1)}, bf16[3,1,1,8,256,256]{5,4,3,2,1,0:T(8,128)(2,1)S(1)}, u32[]{:S(2)}, u32[]{:S(2)}) collective-permute-start(bf16[3,1,1,8,256,256]{5,4,3,2,1,0:T(8,128)(2,1)} %refs_3_.3), channel_id=1, source_target_pairs={{0,2},{2,0},{4,6},{6,4},{8,10},{10,8},{12,14},{14,12},{16,18},{18,... | collective-permute-start | bytes 9437192 | tf_op jit(solution)/shard_map/ppermute | solution.py:166
  0.5 19.5 %collective-permute-start.3 = (f32[4,1,128,256]{3,2,1,0:T(8,128)}, f32[4,1,128,256]{3,2,1,0:T(8,128)}, u32[]{:S(2)}, u32[]{:S(2)}) collective-permute-start(f32[4,1,128,256]{3,2,1,0:T(8,128)} %refs_5_.3), channel_id=1, source_target_pairs={{0,2},{2,0},{4,6},{6,4},{8,10},{10,8},{12,14},{14,12},{16,18},{18,... | collective-permute-start | bytes 1572872 | tf_op jit(solution)/shard_map/ppermute | solution.py:166
  0.5 19.4 %collective-permute-start.4 = (bf16[4,1,256,256]{3,2,1,0:T(8,128)(2,1)}, bf16[4,1,256,256]{3,2,1,0:T(8,128)(2,1)}, u32[]{:S(2)}, u32[]{:S(2)}) collective-permute-start(bf16[4,1,256,256]{3,2,1,0:T(8,128)(2,1)} %refs_7_.1), channel_id=1, source_target_pairs={{0,2},{2,0},{4,6},{6,4},{8,10},{10,8},{12,14},{14,12},{16,18},{18,... | collective-permute-start | bytes 1572872 | tf_op jit(solution)/shard_map/ppermute | solution.py:166
  2.7 0.6 copy-start
  3.3 0.7 collective-permute-start.1
  4.8 15.1 %all-to-all-start = ((bf16[8,64,256]{2,1,0:T(8,128)(2,1)}), bf16[8,64,256]{2,1,0:T(8,128)(2,1)S(1)}, u32[]{:S(2)}, u32[]{:S(2)}) async-start(bf16[8,64,256]{2,1,0:T(8,128)(2,1)} %shard_map.57), calls=%async_computation | async-start | bytes 524288 | tf_op jit(solution)/shard_map/all_to_all | solution.py:172
  12.3 0.7 copy-start.2
  14.2 5.7 %collective-permute-start = (s32[3,1,1,8]{3,2,1,0:T(1,128)S(1)}, s32[3,1,1,8]{3,2,1,0:T(1,128)S(1)}, u32[]{:S(2)}, u32[]{:S(2)}) collective-permute-start(s32[3,1,1,8]{3,2,1,0:T(1,128)S(1)} %shard_map.55.ids_ref), channel_id=1, source_target_pairs={{0,2},{2,0},{4,6},{6,4},{8,10},{10,8},{12,14},{14,12},{16,18},{18,... | collective-permute-start | bytes 296 | tf_op jit(solution)/shard_map/ppermute | solution.py:166
  22.5 8.3 %collective-permute-start.5 = (f32[64,256]{1,0:T(8,128)S(1)}, f32[64,256]{1,0:T(8,128)S(1)}, u32[]{:S(2)}, u32[]{:S(2)}) collective-permute-start(f32[64,256]{1,0:T(8,128)S(1)} %get-tuple-element.25), channel_id=1, source_target_pairs={{0,1},{1,0},{2,3},{3,2},{4,5},{5,4},{6,7},{7,6},{8,9},{9,8},{10,11... | collective-permute-start | bytes 196616 | tf_op jit(solution)/shard_map/ppermute | solution.py:227
  31.7 12.3 %all-to-all-start.1 = ((bf16[8,64,256]{2,1,0:T(8,128)(2,1)}), bf16[8,64,256]{2,1,0:T(8,128)(2,1)}, u32[]{:S(2)}, u32[]{:S(2)}) async-start(bf16[8,64,256]{2,1,0:T(8,128)(2,1)} %get-tuple-element.28), calls=%async_computation.1 | async-start | bytes 524288 | tf_op jit(solution)/shard_map/all_to_all | solution.py:172
  35.8 0.7 collective-permute-start.6
  47.0 4.3 %collective-permute-start.7 = (f32[64,256]{1,0:T(8,128)S(1)}, f32[64,256]{1,0:T(8,128)S(1)}, u32[]{:S(2)}, u32[]{:S(2)}) collective-permute-start(f32[64,256]{1,0:T(8,128)S(1)} %get-tuple-element.31), channel_id=1, source_target_pairs={{0,1},{1,0},{2,3},{3,2},{4,5},{5,4},{6,7},{7,6},{8,9},{9,8},{10,11... | collective-permute-start | bytes 196616 | tf_op jit(solution)/shard_map/ppermute | solution.py:227
  52.2 0.6 copy-start.3
  52.9 12.3 %all-to-all-start.2 = ((bf16[8,64,256]{2,1,0:T(8,128)(2,1)}), bf16[8,64,256]{2,1,0:T(8,128)(2,1)}, u32[]{:S(2)}, u32[]{:S(2)}) async-start(bf16[8,64,256]{2,1,0:T(8,128)(2,1)} %get-tuple-element.34), calls=%async_computation.2 | async-start | bytes 524288 | tf_op jit(solution)/shard_map/all_to_all | solution.py:172
  56.9 1.5 %collective-permute-start.8 = (f32[64,256]{1,0:T(8,128)}, f32[64,256]{1,0:T(8,128)S(1)}, u32[]{:S(2)}, u32[]{:S(2)}) collective-permute-start(f32[64,256]{1,0:T(8,128)} %copy-done.3), channel_id=1, source_target_pairs={{0,0},{1,2},{2,1},{3,3},{4,4},{5,6},{6,5},{7,7},{8,8},{9,10},{10,9... | collective-permute-start | bytes 196616 | tf_op jit(solution)/shard_map/ppermute | solution.py:163
  65.2 9.8 %copy-start.1 = (f32[64,256]{1,0:T(8,128)S(1)}, f32[64,256]{1,0:T(8,128)}, u32[]{:S(2)}) copy-start(f32[64,256]{1,0:T(8,128)} %copy-done) | copy-start | bytes 196612
  68.2 4.0 %collective-permute-start.9 = (f32[64,256]{1,0:T(8,128)S(1)}, f32[64,256]{1,0:T(8,128)S(1)}, u32[]{:S(2)}, u32[]{:S(2)}) collective-permute-start(f32[64,256]{1,0:T(8,128)S(1)} %get-tuple-element.36), channel_id=1, source_target_pairs={{0,0},{1,2},{2,1},{3,3},{4,4},{5,6},{6,5},{7,7},{8,8},{9,10},{10,9... | collective-permute-start | bytes 196616 | tf_op jit(solution)/shard_map/ppermute | solution.py:163
  68.9 6.2 %collective-permute-start.10 = (f32[64,256]{1,0:T(8,128)S(1)}, f32[64,256]{1,0:T(8,128)S(1)}, u32[]{:S(2)}, u32[]{:S(2)}) collective-permute-start(f32[64,256]{1,0:T(8,128)S(1)} %get-tuple-element.37), channel_id=1, source_target_pairs={{0,2},{1,0},{2,3},{3,1},{4,6},{5,4},{6,7},{7,5},{8,10},{9,8},{10,1... | collective-permute-start | bytes 196616 | tf_op jit(solution)/shard_map/ppermute | solution.py:163

commit v6 on v4

--- a/solution.py
+++ b/solution.py
@@ -7,11 +7,13 @@
 from jax.experimental.pallas import tpu as pltpu
 from jax.sharding import PartitionSpec as P
 
-VMEM_LIMIT = 32 * 1024 * 1024
+VMEM_LIMIT = 16 * 1024 * 1024
 
 
 VMEM = pl.BlockSpec(memory_space=pltpu.VMEM)
 SMEM = pl.BlockSpec(memory_space=pltpu.SMEM)
+ANY = pl.BlockSpec(memory_space=pl.ANY)
+HBM = pl.BlockSpec(memory_space=pltpu.HBM)
 
 
 def flat_dot(gathered, factor_ref):
@@ -26,71 +28,114 @@
 def run(kernel, outs, args, scratch=(), flops=0, transferred=0):
     return pl.pallas_call(
         kernel,
-        out_shape=outs,
-        in_specs=[SMEM if x.dtype == jnp.int32 else VMEM for x in args],
-        out_specs=jax.tree.map(lambda _: VMEM, outs),
+        out_shape=tuple(pltpu.HBM(x.shape, x.dtype) if spec is HBM else x for x, spec in outs),
+        in_specs=[spec for _, spec in args],
+        out_specs=tuple(spec for _, spec in outs),
         scratch_shapes=list(scratch),
         compiler_params=pltpu.CompilerParams(vmem_limit_bytes=VMEM_LIMIT),
         cost_estimate=pl.CostEstimate(flops=flops, bytes_accessed=transferred, transcendentals=0),
-    )(*args)
+    )(*(pltpu.with_memory_space_constraint(x, pltpu.HBM) if spec is HBM else x for x, spec in args))
 
 
 def half_of(ref, level, half, rows):
-    return ref[level, 0, pl.ds(pl.multiple_of(half * rows, rows), rows), :]
+    return ref.at[level, 0, pl.ds(pl.multiple_of(half * rows, rows), rows), :]
 
 
 def solve(reduced, inverse):
     return jnp.dot(reduced.astype(jnp.bfloat16), inverse, preferred_element_type=jnp.float32)
 
 
-def first_kernel(place_ref, rhs_ref, inverse_ref, out_ref, rounded_ref):
-    rows = out_ref.shape[0]
-    solved = solve(half_of(rhs_ref, 0, place_ref[1], rows), inverse_ref[0, 0])
+def start_copies(pairs, sems):
+    copies = [pltpu.make_async_copy(src, dst, sems.at[i]) for i, (src, dst) in enumerate(pairs)]
+    for copy in copies:
+        copy.start()
+    return copies
+
+
+def own_place():
+    return lax.rem(lax.axis_index("rows"), 2), lax.axis_index("cols")
+
+
+def first_kernel(rhs_ref, inverse_ref, out_ref, rounded_ref, rhs, inverse, sems):
+    _, col = own_place()
+    copies = start_copies(
+        [(half_of(rhs_ref, 0, col, out_ref.shape[0]), rhs), (inverse_ref.at[0, 0], inverse)], sems
+    )
+    for copy in copies:
+        copy.wait()
+    solved = solve(rhs[...], inverse[...])
     out_ref[...] = solved
     rounded_ref[...] = solved.astype(jnp.bfloat16)
 
 
-def sums_kernel(level, chips, place_ref, ids_ref, other_ids_ref, *refs):
+def copies_kernel(rounded_ref, copies_ref, sems):
+    for copy in start_copies([(rounded_ref, copies_ref.at[i]) for i in range(copies_ref.shape[0])], sems):
+        copy.wait()
+
+
+def stage_kernel(
+    factor_ref, rhs_ref, other_rhs_ref, inverse_ref, other_inverse_ref,
+    own_factor_ref, own_rhs_ref, own_inverse_ref, rhs, inverse, sems,
+):
+    core, col = own_place()
+    straight = core == col
+    levels, rows = own_rhs_ref.shape[0], own_rhs_ref.shape[1]
+    pairs = [
+        (factor_ref.at[:, 0, 0], own_factor_ref),
+        (half_of(rhs_ref, levels, col, rows), own_rhs_ref.at[levels - 1]),
+        (inverse_ref.at[levels, 0], own_inverse_ref.at[levels - 1]),
+    ]
+    for l in range(1, levels):
+        pairs += [
+            (half_of(rhs_ref, l, core, rows), rhs.at[0, l - 1]),
+            (half_of(other_rhs_ref, l, core, rows), rhs.at[1, l - 1]),
+            (inverse_ref.at[l, 0], inverse.at[0, l - 1]),
+            (other_inverse_ref.at[l, 0], inverse.at[1, l - 1]),
+        ]
+    for copy in start_copies(pairs, sems):
+        copy.wait()
+    for l in range(levels - 1):
+        own_rhs_ref[l] = jnp.where(straight, rhs[0, l], rhs[1, l])
+        own_inverse_ref[l] = jnp.where(straight, inverse[0, l], inverse[1, l])
+
+
+def sums_kernel(level, chips, ids_ref, other_ids_ref, counts_ref, other_counts_ref, *refs):
     store_refs = refs[:level]
-    factor_refs = (refs[level], refs[level + 1].at[level - 1, 0, 0])
+    factor_refs = (refs[level].at[level - 1], refs[level + 1].at[level - 1, 0, 0])
     kept_ref, sent_ref, store, gathered = refs[-4:]
     slots, width = factor_refs[0].shape[0], factor_refs[0].shape[1]
+    core, col = own_place()
     for m, piece in enumerate(store_refs):
         store[m * chips:(m + 1) * chips] = piece[...]
     sums = []
-    for ids, factor_ref in zip((ids_ref, other_ids_ref), factor_refs):
+    for ids, counts, factor_ref in zip((ids_ref, other_ids_ref), (counts_ref, other_counts_ref), factor_refs):
         for k in range(slots):
             source = ids[level - 1, 0, 0, k]
-            known = jnp.maximum(source, 0)
-            piece = store[known // (2 * chips) * chips + known % (2 * chips) // 2]
-            live = jnp.where(source >= 0, 1.0, 0.0).astype(piece.dtype)
+            piece = store[source // (2 * chips) * chips + source % (2 * chips) // 2]
+            live = jnp.where(k < counts[level - 1], 1.0, 0.0).astype(piece.dtype)
             gathered[:, k * width:(k + 1) * width] = piece * live
         sums.append(flat_dot(gathered, factor_ref))
-    straight = place_ref[0] == place_ref[1]
+    straight = core == col
     kept_ref[...] = jnp.where(straight, sums[0], sums[1])
     sent_ref[...] = jnp.where(straight, sums[1], sums[0])
 
 
-def inner_kernel(level, place_ref, kept_ref, arrived_ref, rhs_ref, other_rhs_ref, inverse_ref, other_inverse_ref, out_ref, copies_ref):
-    rows = out_ref.shape[0]
-    core = place_ref[0]
-    straight = core == place_ref[1]
-    rhs = jnp.where(straight, half_of(rhs_ref, level, core, rows), half_of(other_rhs_ref, level, core, rows))
-    inverse = jnp.where(straight, inverse_ref[level, 0], other_inverse_ref[level, 0])
-    solved = solve(rhs - (kept_ref[...] + arrived_ref[...]), inverse)
+def inner_kernel(level, kept_ref, arrived_ref, rhs_ref, inverse_ref, out_ref, copies_ref, rounded, sems):
+    solved = solve(rhs_ref[level - 1] - (kept_ref[...] + arrived_ref[...]), inverse_ref[level - 1])
+    rounded[...] = solved.astype(jnp.bfloat16)
+    copies = start_copies([(rounded, copies_ref.at[i]) for i in range(copies_ref.shape[0])], sems)
     out_ref[...] = solved
-    rounded = solved.astype(jnp.bfloat16)
-    for i in range(copies_ref.shape[0]):
-        copies_ref[i] = rounded
-
-
-def last_kernel(place_ref, first_ref, second_ref, rhs_ref, inverse_ref, *refs):
+    for copy in copies:
+        copy.wait()
+
+
+def last_kernel(first_ref, second_ref, rhs_ref, inverse_ref, *refs):
     done_refs, out_ref = refs[:-1], refs[-1]
-    rows, level = out_ref.shape[2], len(done_refs)
+    level = len(done_refs)
     for m, done in enumerate(done_refs):
         out_ref[m, 0] = done[...]
-    rhs = half_of(rhs_ref, level, place_ref[1], rows)
-    out_ref[level, 0] = solve(rhs - (first_ref[...] + second_ref[...]), inverse_ref[level, 0])
+    solved = solve(rhs_ref[level - 1] - (first_ref[...] + second_ref[...]), inverse_ref[level - 1])
+    out_ref[level, 0] = solved
 
 
 def paired_shards(row_count, right_sides, factor_blocks, diag_inverses, source_ids, block_counts):
@@ -98,8 +143,7 @@
     slots = factor_blocks.shape[3]
     rows = rhs_count // 2
     chips = row_count // 2
-    row, col = lax.axis_index("rows"), lax.axis_index("cols")
-    place = jnp.stack([row % 2, col]).astype(jnp.int32)
+    later = level_count - 1
     same_core = [[2 * j + k for j in range(chips)] for k in range(2)]
     part = jax.ShapeDtypeStruct((rows, width), jnp.float32)
     rounded_part = jax.ShapeDtypeStruct((rows, width), jnp.bfloat16)
@@ -125,26 +169,58 @@
         return lax.all_to_all(x, "rows", 0, 0, axis_index_groups=same_core)
 
     solved, rounded = run(
-        first_kernel, (part, rounded_part), (place, right_sides, diag_inverses), flops=solve_flops
+        first_kernel,
+        ((part, VMEM), (rounded_part, VMEM)),
+        ((right_sides, HBM), (diag_inverses, HBM)),
+        scratch=(
+            pltpu.VMEM((rows, width), jnp.float32),
+            pltpu.VMEM((width, width), jnp.bfloat16),
+            pltpu.SemaphoreType.DMA((2,)),
+        ),
+        flops=solve_flops,
     )
     finished = [solved]
-    moved = transpose(rounded)
-    stores = [spread(jnp.broadcast_to(moved[None], copies.shape))]
-
-    live_ids = jnp.where(
-        jnp.arange(slots, dtype=jnp.int32) < block_counts[..., None], source_ids, -1
-    )
+    copied, = run(
+        copies_kernel,
+        ((copies, HBM),),
+        ((transpose(rounded), VMEM),),
+        scratch=(pltpu.SemaphoreType.DMA((chips,)),),
+    )
+    stores = [spread(copied)]
+
+    counts = block_counts.reshape(later)
+    slot_args = tuple((x, SMEM) for x in (source_ids, swap_core(source_ids), counts, swap_core(counts)))
     other_factors = swap_core(factor_blocks)
-    other_ids = swap_core(live_ids)
-    other_inverses = swap_core(diag_inverses)
-    other_rhs = swap_core(right_sides)
+    own_factors, rhs, inverses = run(
+        stage_kernel,
+        (
+            (jax.ShapeDtypeStruct((later, slots, width, width), jnp.bfloat16), VMEM),
+            (jax.ShapeDtypeStruct((later, rows, width), jnp.float32), VMEM),
+            (jax.ShapeDtypeStruct((later, width, width), jnp.bfloat16), VMEM),
+        ),
+        (
+            (factor_blocks, HBM),
+            (right_sides, HBM),
+            (swap_core(right_sides), ANY),
+            (diag_inverses, HBM),
+            (swap_core(diag_inverses), ANY),
+        ),
+        scratch=(
+            pltpu.VMEM((2, later - 1, rows, width), jnp.float32),
+            pltpu.VMEM((2, later - 1, width, width), jnp.bfloat16),
+            pltpu.SemaphoreType.DMA((3 + 4 * (later - 1),)),
+        ),
+        transferred=2 * later * slots * width * width * 2,
+    )
 
     for l in range(1, level_count):
         kept, sent = run(
             functools.partial(sums_kernel, l, chips),
-            (part, part),
-            (place, live_ids, other_ids, *stores, factor_blocks[l - 1, 0, 0], other_factors)
-            + tuple(finished[1:]),
+            ((part, VMEM), (part, VMEM)),
+            slot_args
+            + tuple((store, VMEM) for store in stores)
+            + ((own_factors, VMEM), (other_factors, VMEM))
+            + tuple((x, ANY) for x in finished[1:]),
             scratch=(
                 pltpu.VMEM((l * chips, rows, width), jnp.bfloat16),
                 pltpu.VMEM((rows, slots * width), jnp.bfloat16),
@@ -152,25 +228,29 @@
             flops=2 * slots * solve_flops,
             transferred=2 * slots * width * width * 2,
         )
-        if l < level_count - 1:
+        if l < later:
             arrived = lax.ppermute(sent, "cols", [(0, 1), (1, 0)])
             solved, copied = run(
                 functools.partial(inner_kernel, l),
-                (part, copies),
-                (place, kept, arrived, right_sides, other_rhs, diag_inverses, other_inverses),
+                ((part, VMEM), (copies, HBM)),
+                ((kept, VMEM), (arrived, VMEM), (rhs, VMEM), (inverses, VMEM)),
+                scratch=(
+                    pltpu.VMEM((rows, width), jnp.bfloat16),
+                    pltpu.SemaphoreType.DMA((chips,)),
+                ),
                 flops=solve_flops,
             )
             finished.append(transpose(solved))
             stores.append(spread(copied))
-        else:
-            first = over_both(kept, lambda j, k, c: (j, c, k))
-            second = over_both(sent, lambda j, k, c: (j, 1 - c, k))
-            return run(
-                last_kernel,
-                jax.ShapeDtypeStruct((level_count, 1, rows, width), jnp.float32),
-                (place, first, second, right_sides, diag_inverses, *finished),
-                flops=solve_flops,
-            )
+    first = over_both(kept, lambda j, k, c: (j, c, k))
+    second = over_both(sent, lambda j, k, c: (j, 1 - c, k))
+    out, = run(
+        last_kernel,
+        ((jax.ShapeDtypeStruct((level_count, 1, rows, width), jnp.float32), VMEM),),
+        tuple((x, VMEM) for x in (first, second, rhs, inverses, *finished)),
+        flops=solve_flops,
+    )
+    return out
 
 
 def gather_slots(ids_ref, counts_ref, group, store_ref, gathered, slots, width):

time: 79.7 us -> 77.5 us (0.972)
  the two profiles are of different devices: /device:TPU:1 before, /device:TPU:0 now
where the time goes in v6:
time: 77.5 us; the launch traced here: 76.8 us
  starting transfers between devices  33.3 us (43%)
  waiting for transfers between devices  22.3 us (29%)
  Pallas kernels  11 us (14%)
  local copies, waits for them, and re-layouts  9.97 us (13%)
    all_to_all x3, starting transfers between devices, spread(): return lax.all_to_all(x, 'rows', 0, 0, axis_index_groups=same_core)  14.9 us
    all_to_all x3, waiting for transfers between devices, spread(): return lax.all_to_all(x, 'rows', 0, 0, axis_index_groups=same_core)  14.7 us
    pallas_call x9, Pallas kernels, run(): pl.pallas_call(kernel, out_shape=tuple((pltpu.HBM(x.shape, x.dtype) if sp...  11 us
    unnamed x34, local copies, waits for them, and re-layouts  9.97 us
    ppermute x5, starting transfers between devices, over_both(): return lax.ppermute(x, ('rows', 'cols'), pairs)  6.64 us
    ppermute x2, starting transfers between devices, paired_shards(): arrived = lax.ppermute(sent, 'cols', [(0, 1), (1, 0)])  5.88 us
    ppermute x5, starting transfers between devices, swap_core(): return lax.ppermute(x, 'rows', [(i, i ^ 1) for i in range(row_count)])  5.81 us
    ppermute x2, waiting for transfers between devices, paired_shards(): arrived = lax.ppermute(sent, 'cols', [(0, 1), (1, 0)])  4.85 us
  transfers between devices with their start and end apart: 15, of which 5 were waited for; matrix products, arithmetic and copies ran while one was open for 0% of the time, Pallas kernels for 5%

profile of v6, /device:TPU:0, one launch (start us, length us, event | category | flops | bytes accessed | tf_op | source)
XLA Modules:
  0.0 76.8 jit_solution(8466488779954472983)
XLA Ops:
  0.0 0.5 collective-permute-start.5
  0.5 0.1 collective-permute-start.3
  0.5 0.5 collective-permute-start.4
  1.0 1.1 %shard_map.55 = (f32[64,256]{1,0:T(8,128)S(1)}, bf16[64,256]{1,0:T(8,128)(2,1)S(1)}) custom-call(f32[4,1,128,256]{3,2,1,0:T(8,128)} %rhs_ref.3, bf16[4,1,256,256]{3,2,1,0:T(8,128)(2,1)} %inverse_ref.3), custom_call_target="tpu_custom_call" | custom-call | flops 8388608 | tf_op jit(solution)/shard_map/pallas_call | solution.py:29
  2.1 0.6 copy-done.12
  2.7 0.8 %collective-permute-start.2 = (bf16[64,256]{1,0:T(8,128)(2,1)S(1)}, bf16[64,256]{1,0:T(8,128)(2,1)S(1)}, u32[]{:S(2)}, u32[]{:S(2)}) collective-permute-start(bf16[64,256]{1,0:T(8,128)(2,1)S(1)} %get-tuple-element.20), channel_id=1, source_target_pairs={{0,0},{1,2},{2,1},{3,3},{4,4},{5,6},{6,5},{7,7},{8,8},{9,10},{10,9... | collective-permute-start | bytes 98312 | tf_op jit(solution)/shard_map/ppermute | solution.py:160
  3.5 0.0 collective-permute-done.2.rounded_ref
  3.5 0.8 shard_map.56
  4.3 6.8 %all-to-all-start = ((bf16[8,64,256]{2,1,0:T(8,128)(2,1)}), bf16[8,64,256]{2,1,0:T(8,128)(2,1)S(1)}, u32[]{:S(2)}, u32[]{:S(2)}) async-start(bf16[8,64,256]{2,1,0:T(8,128)(2,1)} %shard_map.56), calls=%async_computation | async-start | bytes 524288 | tf_op jit(solution)/shard_map/all_to_all | solution.py:169
  11.1 4.8 %collective-permute-start.1 = (s32[3]{0:T(128)}, s32[3]{0:T(128)S(1)}, u32[]{:S(2)}, u32[]{:S(2)}) collective-permute-start(s32[3]{0:T(128)} %bitcast.1), channel_id=1, source_target_pairs={{0,2},{2,0},{4,6},{6,4},{8,10},{10,8},{12,14},{14,12},{16,18},{18,... | collective-permute-start | bytes 44 | tf_op jit(solution)/shard_map/ppermute | solution.py:163
  15.9 0.1 collective-permute-start
  16.0 0.0 collective-permute-done.3.other_rhs_ref
  16.0 0.0 collective-permute-done.4.other_inverse_ref
  16.0 2.2 %shard_map.57 = (bf16[3,8,256,256]{3,2,1,0:T(8,128)(2,1)S(1)}, f32[3,64,256]{2,1,0:T(8,128)S(1)}, bf16[3,256,256]{2,1,0:T(8,128)(2,1)S(1)}) custom-call(bf16[3,1,1,8,256,256]{5,4,3,2,1,0:T(8,128)(2,1)} %factor_ref.1, f32[4,1,128,256]{3,2,1,0:T(8,128)} %rhs_ref.3, f32[4,1,128,256]{3,2,1,0:T(8,128)} %collective-permute-done.3.other_rhs_ref, ...), custom_call_target="tpu_custom_call" | custom-call | bytes 6291456 | tf_op jit(solution)/shard_map/pallas_call | solution.py:29
  18.2 1.6 %copy-done = bf16[3,8,256,256]{3,2,1,0:T(8,128)(2,1)} copy-done((bf16[3,8,256,256]{3,2,1,0:T(8,128)(2,1)}, bf16[3,8,256,256]{3,2,1,0:T(8,128)(2,1)S(1)}, u32[]{:S(2)}) %copy-start) | copy-done | bytes 3145752
  19.8 0.8 copy-done.4
  20.6 0.7 copy-done.8
  21.3 0.0 collective-permute-done.1.other_counts_ref
  21.3 0.0 collective-permute-done.other_ids_ref
  21.3 0.0 all-to-all-done.refs_0_
  21.3 0.0 collective-permute-done.5.refs_2_.refs_3_.refs_4_
  21.3 1.9 %copy-done.1 = bf16[3,8,256,256]{3,2,1,0:T(8,128)(2,1)S(1)} copy-done((bf16[3,8,256,256]{3,2,1,0:T(8,128)(2,1)S(1)}, bf16[3,8,256,256]{3,2,1,0:T(8,128)(2,1)}, u32[]{:S(2)}) %copy-start.1) | copy-done | bytes 3145752
  23.2 1.1 %shard_map.58 = (f32[64,256]{1,0:T(8,128)S(1)}, f32[64,256]{1,0:T(8,128)S(1)}) custom-call(s32[3,1,1,8]{3,2,1,0:T(1,128)S(1)} %copy-done.14, s32[3,1,1,8]{3,2,1,0:T(1,128)S(1)} %collective-permute-done.other_ids_ref, s32[3]{0:T(128)S(1)} %bitcast.2, s32[3]{0:T(128)S(1)} %collective-permute-done.1.other_counts_ref, ...), custom_call_target="tpu_custom_call" | custom-call | flops 134217728 | bytes 2097152 | tf_op jit(solution)/shard_map/pallas_call | solution.py:29
  24.3 4.2 %collective-permute-start.6 = (f32[64,256]{1,0:T(8,128)S(1)}, f32[64,256]{1,0:T(8,128)S(1)}, u32[]{:S(2)}, u32[]{:S(2)}) collective-permute-start(f32[64,256]{1,0:T(8,128)S(1)} %get-tuple-element.23), channel_id=1, source_target_pairs={{0,1},{1,0},{2,3},{3,2},{4,5},{5,4},{6,7},{7,6},{8,9},{9,8},{10,11... | collective-permute-start | bytes 196616 | tf_op jit(solution)/shard_map/ppermute | solution.py:232
  28.5 2.2 %collective-permute-done.6.arrived_ref = f32[64,256]{1,0:T(8,128)S(1)} collective-permute-done((f32[64,256]{1,0:T(8,128)S(1)}, f32[64,256]{1,0:T(8,128)S(1)}, u32[]{:S(2)}, u32[]{:S(2)}) %collective-permute-start.6) | collective-permute-done | bytes 65568 | tf_op jit(solution)/shard_map/ppermute | solution.py:232
  30.7 0.9 %shard_map.59 = (f32[64,256]{1,0:T(8,128)S(1)}, bf16[8,64,256]{2,1,0:T(8,128)(2,1)}) custom-call(f32[64,256]{1,0:T(8,128)S(1)} %get-tuple-element.22.kept_ref, f32[64,256]{1,0:T(8,128)S(1)} %collective-permute-done.6.arrived_ref, f32[3,64,256]{2,1,0:T(8,128)S(1)} %copy-done.9, bf16[3,256,256]{2,1,0:T(8,128)(2,1)S(1)} %copy-done.5), custom_call_target="tpu_custom_call" | custom-call | flops 8388608 | tf_op jit(solution)/shard_map/pallas_call | solution.py:29
  31.6 4.1 %all-to-all-start.1 = ((bf16[8,64,256]{2,1,0:T(8,128)(2,1)}), bf16[8,64,256]{2,1,0:T(8,128)(2,1)}, u32[]{:S(2)}, u32[]{:S(2)}) async-start(bf16[8,64,256]{2,1,0:T(8,128)(2,1)} %get-tuple-element.26), calls=%async_computation.1 | async-start | bytes 524288 | tf_op jit(solution)/shard_map/all_to_all | solution.py:169
  35.7 0.7 collective-permute-start.7
  36.4 0.0 collective-permute-done.7.refs_4_.refs_5_.refs_1_
  36.4 7.9 %all-to-all-done.1.refs_1_ = bf16[8,64,256]{2,1,0:T(8,128)(2,1)} async-done(((bf16[8,64,256]{2,1,0:T(8,128)(2,1)}), bf16[8,64,256]{2,1,0:T(8,128)(2,1)}, u32[]{:S(2)}, u32[]{:S(2)}) %all-to-all-start.1) | async-done | bytes 262176 | tf_op jit(solution)/shard_map/all_to_all | solution.py:169
  44.3 1.9 %copy-done.2 = bf16[3,8,256,256]{3,2,1,0:T(8,128)(2,1)S(1)} copy-done((bf16[3,8,256,256]{3,2,1,0:T(8,128)(2,1)S(1)}, bf16[3,8,256,256]{3,2,1,0:T(8,128)(2,1)}, u32[]{:S(2)}) %copy-start.2) | copy-done | bytes 3145752
  46.2 1.5 %shard_map.60 = (f32[64,256]{1,0:T(8,128)S(1)}, f32[64,256]{1,0:T(8,128)S(1)}) custom-call(s32[3,1,1,8]{3,2,1,0:T(1,128)S(1)} %copy-done.14, s32[3,1,1,8]{3,2,1,0:T(1,128)S(1)} %collective-permute-done.other_ids_ref, s32[3]{0:T(128)S(1)} %bitcast.3, s32[3]{0:T(128)S(1)} %collective-permute-done.1.other_counts_ref, ...), custom_call_target="tpu_custom_call" | custom-call | flops 134217728 | bytes 2097152 | tf_op jit(solution)/shard_map/pallas_call | solution.py:29
  47.7 1.7 %collective-permute-start.8 = (f32[64,256]{1,0:T(8,128)S(1)}, f32[64,256]{1,0:T(8,128)S(1)}, u32[]{:S(2)}, u32[]{:S(2)}) collective-permute-start(f32[64,256]{1,0:T(8,128)S(1)} %get-tuple-element.29), channel_id=1, source_target_pairs={{0,1},{1,0},{2,3},{3,2},{4,5},{5,4},{6,7},{7,6},{8,9},{9,8},{10,11... | collective-permute-start | bytes 196616 | tf_op jit(solution)/shard_map/ppermute | solution.py:232
  49.5 2.6 %collective-permute-done.8.arrived_ref = f32[64,256]{1,0:T(8,128)S(1)} collective-permute-done((f32[64,256]{1,0:T(8,128)S(1)}, f32[64,256]{1,0:T(8,128)S(1)}, u32[]{:S(2)}, u32[]{:S(2)}) %collective-permute-start.8) | collective-permute-done | bytes 65568 | tf_op jit(solution)/shard_map/ppermute | solution.py:232
  52.1 0.9 %shard_map.61 = (f32[64,256]{1,0:T(8,128)S(1)}, bf16[8,64,256]{2,1,0:T(8,128)(2,1)}) custom-call(f32[64,256]{1,0:T(8,128)S(1)} %get-tuple-element.28.kept_ref, f32[64,256]{1,0:T(8,128)S(1)} %collective-permute-done.8.arrived_ref, f32[3,64,256]{2,1,0:T(8,128)S(1)} %copy-done.10, bf16[3,256,256]{2,1,0:T(8,128)(2,1)S(1)} %copy-done.6), custom_call_target="tpu_custom_call" | custom-call | flops 8388608 | tf_op jit(solution)/shard_map/pallas_call | solution.py:29
  53.0 0.0 copy-start.16
  53.0 0.6 copy-done.16
  53.6 4.0 %all-to-all-start.2 = ((bf16[8,64,256]{2,1,0:T(8,128)(2,1)}), bf16[8,64,256]{2,1,0:T(8,128)(2,1)}, u32[]{:S(2)}, u32[]{:S(2)}) async-start(bf16[8,64,256]{2,1,0:T(8,128)(2,1)} %get-tuple-element.30), calls=%async_computation.2 | async-start | bytes 524288 | tf_op jit(solution)/shard_map/all_to_all | solution.py:169
  57.7 1.5 %collective-permute-start.9 = (f32[64,256]{1,0:T(8,128)}, f32[64,256]{1,0:T(8,128)S(1)}, u32[]{:S(2)}, u32[]{:S(2)}) collective-permute-start(f32[64,256]{1,0:T(8,128)} %copy-done.16), channel_id=1, source_target_pairs={{0,0},{1,2},{2,1},{3,3},{4,4},{5,6},{6,5},{7,7},{8,8},{9,10},{10,9... | collective-permute-start | bytes 196616 | tf_op jit(solution)/shard_map/ppermute | solution.py:160
  59.2 0.0 collective-permute-done.9.refs_6_.refs_2_
  59.2 6.7 %all-to-all-done.2.refs_2_ = bf16[8,64,256]{2,1,0:T(8,128)(2,1)} async-done(((bf16[8,64,256]{2,1,0:T(8,128)(2,1)}), bf16[8,64,256]{2,1,0:T(8,128)(2,1)}, u32[]{:S(2)}, u32[]{:S(2)}) %all-to-all-start.2) | async-done | bytes 262176 | tf_op jit(solution)/shard_map/all_to_all | solution.py:169
  65.9 1.9 %copy-done.3 = bf16[3,8,256,256]{3,2,1,0:T(8,128)(2,1)S(1)} copy-done((bf16[3,8,256,256]{3,2,1,0:T(8,128)(2,1)S(1)}, bf16[3,8,256,256]{3,2,1,0:T(8,128)(2,1)}, u32[]{:S(2)}) %copy-start.3) | copy-done | bytes 3145752
  67.8 1.6 %shard_map.62 = (f32[64,256]{1,0:T(8,128)S(1)}, f32[64,256]{1,0:T(8,128)S(1)}) custom-call(s32[3,1,1,8]{3,2,1,0:T(1,128)S(1)} %copy-done.14, s32[3,1,1,8]{3,2,1,0:T(1,128)S(1)} %collective-permute-done.other_ids_ref, s32[3]{0:T(128)S(1)} %bitcast.4, s32[3]{0:T(128)S(1)} %collective-permute-done.1.other_counts_ref, ...), custom_call_target="tpu_custom_call" | custom-call | flops 134217728 | bytes 2097152 | tf_op jit(solution)/shard_map/pallas_call | solution.py:29
  69.4 0.7 collective-permute-start.10
  70.1 3.0 %collective-permute-start.11 = (f32[64,256]{1,0:T(8,128)S(1)}, f32[64,256]{1,0:T(8,128)S(1)}, u32[]{:S(2)}, u32[]{:S(2)}) collective-permute-start(f32[64,256]{1,0:T(8,128)S(1)} %get-tuple-element.33), channel_id=1, source_target_pairs={{0,2},{1,0},{2,3},{3,1},{4,6},{5,4},{6,7},{7,5},{8,10},{9,8},{10,1... | collective-permute-start | bytes 196616 | tf_op jit(solution)/shard_map/ppermute | solution.py:160
  73.1 0.0 collective-permute-done.10.first_ref
  73.1 2.8 %collective-permute-done.11.second_ref = f32[64,256]{1,0:T(8,128)S(1)} collective-permute-done((f32[64,256]{1,0:T(8,128)S(1)}, f32[64,256]{1,0:T(8,128)S(1)}, u32[]{:S(2)}, u32[]{:S(2)}) %collective-permute-start.11) | collective-permute-done | bytes 65568 | tf_op jit(solution)/shard_map/ppermute | solution.py:160
  75.9 0.9 %shard_map.63 = f32[4,1,64,256]{3,2,1,0:T(8,128)} custom-call(f32[64,256]{1,0:T(8,128)S(1)} %collective-permute-done.10.first_ref, f32[64,256]{1,0:T(8,128)S(1)} %collective-permute-done.11.second_ref, f32[3,64,256]{2,1,0:T(8,128)S(1)} %copy-done.11, bf16[3,256,256]{2,1,0:T(8,128)(2,1)S(1)} %copy-done.7, f32[64,256]{1,0:T(8,128)S(1)} %copy-done.13, ...), custom_call_target="tpu_custom_call" | custom-call | flops 8388608 | tf_op jit(solution)/shard_map/pallas_call | solution.py:29
  (25 shorter events, 0.0 us)
Async XLA Ops:
  0.0 21.3 %collective-permute-start.5 = (bf16[3,1,1,8,256,256]{5,4,3,2,1,0:T(8,128)(2,1)}, bf16[3,1,1,8,256,256]{5,4,3,2,1,0:T(8,128)(2,1)S(1)}, u32[]{:S(2)}, u32[]{:S(2)}) collective-permute-start(bf16[3,1,1,8,256,256]{5,4,3,2,1,0:T(8,128)(2,1)} %factor_ref.1), channel_id=1, source_target_pairs={{0,2},{2,0},{4,6},{6,4},{8,10},{10,8},{12,14},{14,12},{16,18},{18,... | collective-permute-start | bytes 9437192 | tf_op jit(solution)/shard_map/ppermute | solution.py:163
  0.5 15.5 %collective-permute-start.3 = (f32[4,1,128,256]{3,2,1,0:T(8,128)}, f32[4,1,128,256]{3,2,1,0:T(8,128)}, u32[]{:S(2)}, u32[]{:S(2)}) collective-permute-start(f32[4,1,128,256]{3,2,1,0:T(8,128)} %rhs_ref.3), channel_id=1, source_target_pairs={{0,2},{2,0},{4,6},{6,4},{8,10},{10,8},{12,14},{14,12},{16,18},{18,... | collective-permute-start | bytes 1572872 | tf_op jit(solution)/shard_map/ppermute | solution.py:163
  0.5 15.4 %collective-permute-start.4 = (bf16[4,1,256,256]{3,2,1,0:T(8,128)(2,1)}, bf16[4,1,256,256]{3,2,1,0:T(8,128)(2,1)}, u32[]{:S(2)}, u32[]{:S(2)}) collective-permute-start(bf16[4,1,256,256]{3,2,1,0:T(8,128)(2,1)} %inverse_ref.3), channel_id=1, source_target_pairs={{0,2},{2,0},{4,6},{6,4},{8,10},{10,8},{12,14},{14,12},{16,18},{18,... | collective-permute-start | bytes 1572872 | tf_op jit(solution)/shard_map/ppermute | solution.py:163
  2.1 0.6 copy-start.12
  2.7 18.6 %copy-start.14 = (s32[3,1,1,8]{3,2,1,0:T(1,128)S(1)}, s32[3,1,1,8]{3,2,1,0:T(1,128)}, u32[]{:S(2)}) copy-start(s32[3,1,1,8]{3,2,1,0:T(1,128)} %ids_ref.5) | copy-start | bytes 292
  2.7 18.6 %copy-start.15 = (s32[3,1,1]{0,2,1:T(1,128)S(1)}, s32[3,1,1]{0,2,1:T(1,128)}, u32[]{:S(2)}) copy-start(s32[3,1,1]{0,2,1:T(1,128)} %param.9) | copy-start | bytes 40
  2.7 0.8 %collective-permute-start.2 = (bf16[64,256]{1,0:T(8,128)(2,1)S(1)}, bf16[64,256]{1,0:T(8,128)(2,1)S(1)}, u32[]{:S(2)}, u32[]{:S(2)}) collective-permute-start(bf16[64,256]{1,0:T(8,128)(2,1)S(1)} %get-tuple-element.20), channel_id=1, source_target_pairs={{0,0},{1,2},{2,1},{3,3},{4,4},{5,6},{6,5},{7,7},{8,8},{9,10},{10,9... | collective-permute-start | bytes 98312 | tf_op jit(solution)/shard_map/ppermute | solution.py:160
  4.3 17.0 %all-to-all-start = ((bf16[8,64,256]{2,1,0:T(8,128)(2,1)}), bf16[8,64,256]{2,1,0:T(8,128)(2,1)S(1)}, u32[]{:S(2)}, u32[]{:S(2)}) async-start(bf16[8,64,256]{2,1,0:T(8,128)(2,1)} %shard_map.56), calls=%async_computation | async-start | bytes 524288 | tf_op jit(solution)/shard_map/all_to_all | solution.py:169
  11.1 10.2 %collective-permute-start.1 = (s32[3]{0:T(128)}, s32[3]{0:T(128)S(1)}, u32[]{:S(2)}, u32[]{:S(2)}) collective-permute-start(s32[3]{0:T(128)} %bitcast.1), channel_id=1, source_target_pairs={{0,2},{2,0},{4,6},{6,4},{8,10},{10,8},{12,14},{14,12},{16,18},{18,... | collective-permute-start | bytes 44 | tf_op jit(solution)/shard_map/ppermute | solution.py:163
  15.9 5.4 %collective-permute-start = (s32[3,1,1,8]{3,2,1,0:T(1,128)}, s32[3,1,1,8]{3,2,1,0:T(1,128)S(1)}, u32[]{:S(2)}, u32[]{:S(2)}) collective-permute-start(s32[3,1,1,8]{3,2,1,0:T(1,128)} %ids_ref.5), channel_id=1, source_target_pairs={{0,2},{2,0},{4,6},{6,4},{8,10},{10,8},{12,14},{14,12},{16,18},{18,... | collective-permute-start | bytes 296 | tf_op jit(solution)/shard_map/ppermute | solution.py:163
  18.2 1.6 %copy-start = (bf16[3,8,256,256]{3,2,1,0:T(8,128)(2,1)}, bf16[3,8,256,256]{3,2,1,0:T(8,128)(2,1)S(1)}, u32[]{:S(2)}) copy-start(bf16[3,8,256,256]{3,2,1,0:T(8,128)(2,1)S(1)} %get-tuple-element.21.refs_1_.refs_2_.refs_3_) | copy-start | bytes 9437188
  19.8 0.8 copy-start.4
  20.6 0.7 copy-start.8
  21.3 1.9 %copy-start.1 = (bf16[3,8,256,256]{3,2,1,0:T(8,128)(2,1)S(1)}, bf16[3,8,256,256]{3,2,1,0:T(8,128)(2,1)}, u32[]{:S(2)}) copy-start(bf16[3,8,256,256]{3,2,1,0:T(8,128)(2,1)} %copy-done) | copy-start | bytes 9437188
  23.2 7.5 %copy-start.5 = (bf16[3,256,256]{2,1,0:T(8,128)(2,1)S(1)}, bf16[3,256,256]{2,1,0:T(8,128)(2,1)}, u32[]{:S(2)}) copy-start(bf16[3,256,256]{2,1,0:T(8,128)(2,1)} %copy-done.4) | copy-start | bytes 1179652
  23.2 7.5 %copy-start.9 = (f32[3,64,256]{2,1,0:T(8,128)S(1)}, f32[3,64,256]{2,1,0:T(8,128)}, u32[]{:S(2)}) copy-start(f32[3,64,256]{2,1,0:T(8,128)} %copy-done.8) | copy-start | bytes 589828
  24.3 6.4 %collective-permute-start.6 = (f32[64,256]{1,0:T(8,128)S(1)}, f32[64,256]{1,0:T(8,128)S(1)}, u32[]{:S(2)}, u32[]{:S(2)}) collective-permute-start(f32[64,256]{1,0:T(8,128)S(1)} %get-tuple-element.23), channel_id=1, source_target_pairs={{0,1},{1,0},{2,3},{3,2},{4,5},{5,4},{6,7},{7,6},{8,9},{9,8},{10,11... | collective-permute-start | bytes 196616 | tf_op jit(solution)/shard_map/ppermute | solution.py:232
  31.6 12.7 %all-to-all-start.1 = ((bf16[8,64,256]{2,1,0:T(8,128)(2,1)}), bf16[8,64,256]{2,1,0:T(8,128)(2,1)}, u32[]{:S(2)}, u32[]{:S(2)}) async-start(bf16[8,64,256]{2,1,0:T(8,128)(2,1)} %get-tuple-element.26), calls=%async_computation.1 | async-start | bytes 524288 | tf_op jit(solution)/shard_map/all_to_all | solution.py:169
  35.7 0.7 collective-permute-start.7
  44.3 1.9 %copy-start.2 = (bf16[3,8,256,256]{3,2,1,0:T(8,128)(2,1)S(1)}, bf16[3,8,256,256]{3,2,1,0:T(8,128)(2,1)}, u32[]{:S(2)}) copy-start(bf16[3,8,256,256]{3,2,1,0:T(8,128)(2,1)} %copy-done) | copy-start | bytes 9437188
  46.2 5.9 %copy-start.6 = (bf16[3,256,256]{2,1,0:T(8,128)(2,1)S(1)}, bf16[3,256,256]{2,1,0:T(8,128)(2,1)}, u32[]{:S(2)}) copy-start(bf16[3,256,256]{2,1,0:T(8,128)(2,1)} %copy-done.4) | copy-start | bytes 1179652
  46.2 5.9 %copy-start.10 = (f32[3,64,256]{2,1,0:T(8,128)S(1)}, f32[3,64,256]{2,1,0:T(8,128)}, u32[]{:S(2)}) copy-start(f32[3,64,256]{2,1,0:T(8,128)} %copy-done.8) | copy-start | bytes 589828
  47.7 4.3 %collective-permute-start.8 = (f32[64,256]{1,0:T(8,128)S(1)}, f32[64,256]{1,0:T(8,128)S(1)}, u32[]{:S(2)}, u32[]{:S(2)}) collective-permute-start(f32[64,256]{1,0:T(8,128)S(1)} %get-tuple-element.29), channel_id=1, source_target_pairs={{0,1},{1,0},{2,3},{3,2},{4,5},{5,4},{6,7},{7,6},{8,9},{9,8},{10,11... | collective-permute-start | bytes 196616 | tf_op jit(solution)/shard_map/ppermute | solution.py:232
  53.0 0.6 copy-start.16
  53.6 12.3 %all-to-all-start.2 = ((bf16[8,64,256]{2,1,0:T(8,128)(2,1)}), bf16[8,64,256]{2,1,0:T(8,128)(2,1)}, u32[]{:S(2)}, u32[]{:S(2)}) async-start(bf16[8,64,256]{2,1,0:T(8,128)(2,1)} %get-tuple-element.30), calls=%async_computation.2 | async-start | bytes 524288 | tf_op jit(solution)/shard_map/all_to_all | solution.py:169
  57.7 1.5 %collective-permute-start.9 = (f32[64,256]{1,0:T(8,128)}, f32[64,256]{1,0:T(8,128)S(1)}, u32[]{:S(2)}, u32[]{:S(2)}) collective-permute-start(f32[64,256]{1,0:T(8,128)} %copy-done.16), channel_id=1, source_target_pairs={{0,0},{1,2},{2,1},{3,3},{4,4},{5,6},{6,5},{7,7},{8,8},{9,10},{10,9... | collective-permute-start | bytes 196616 | tf_op jit(solution)/shard_map/ppermute | solution.py:160
  65.9 1.9 %copy-start.3 = (bf16[3,8,256,256]{3,2,1,0:T(8,128)(2,1)S(1)}, bf16[3,8,256,256]{3,2,1,0:T(8,128)(2,1)}, u32[]{:S(2)}) copy-start(bf16[3,8,256,256]{3,2,1,0:T(8,128)(2,1)} %copy-done) | copy-start | bytes 9437188
  67.8 8.1 %copy-start.7 = (bf16[3,256,256]{2,1,0:T(8,128)(2,1)S(1)}, bf16[3,256,256]{2,1,0:T(8,128)(2,1)}, u32[]{:S(2)}) copy-start(bf16[3,256,256]{2,1,0:T(8,128)(2,1)} %copy-done.4) | copy-start | bytes 1179652
  67.8 8.1 %copy-start.11 = (f32[3,64,256]{2,1,0:T(8,128)S(1)}, f32[3,64,256]{2,1,0:T(8,128)}, u32[]{:S(2)}) copy-start(f32[3,64,256]{2,1,0:T(8,128)} %copy-done.8) | copy-start | bytes 589828
  67.8 8.1 %copy-start.13 = (f32[64,256]{1,0:T(8,128)S(1)}, f32[64,256]{1,0:T(8,128)}, u32[]{:S(2)}) copy-start(f32[64,256]{1,0:T(8,128)} %copy-done.12) | copy-start | bytes 196612
  69.4 3.7 %collective-permute-start.10 = (f32[64,256]{1,0:T(8,128)S(1)}, f32[64,256]{1,0:T(8,128)S(1)}, u32[]{:S(2)}, u32[]{:S(2)}) collective-permute-start(f32[64,256]{1,0:T(8,128)S(1)} %get-tuple-element.32), channel_id=1, source_target_pairs={{0,0},{1,2},{2,1},{3,3},{4,4},{5,6},{6,5},{7,7},{8,8},{9,10},{10,9... | collective-permute-start | bytes 196616 | tf_op jit(solution)/shard_map/ppermute | solution.py:160
  70.1 5.8 %collective-permute-start.11 = (f32[64,256]{1,0:T(8,128)S(1)}, f32[64,256]{1,0:T(8,128)S(1)}, u32[]{:S(2)}, u32[]{:S(2)}) collective-permute-start(f32[64,256]{1,0:T(8,128)S(1)} %get-tuple-element.33), channel_id=1, source_target_pairs={{0,2},{1,0},{2,3},{3,1},{4,6},{5,4},{6,7},{7,5},{8,10},{9,8},{10,1... | collective-permute-start | bytes 196616 | tf_op jit(solution)/shard_map/ppermute | solution.py:160

commit v7 on v6

--- a/solution.py
+++ b/solution.py
@@ -14,6 +14,8 @@
 SMEM = pl.BlockSpec(memory_space=pltpu.SMEM)
 ANY = pl.BlockSpec(memory_space=pl.ANY)
 HBM = pl.BlockSpec(memory_space=pltpu.HBM)
+FIXED = pl.BlockSpec(memory_space=pltpu.VMEM)
+PLACES = {id(HBM): pltpu.HBM, id(FIXED): pltpu.VMEM}
 
 
 def flat_dot(gathered, factor_ref):
@@ -26,15 +28,20 @@
 
 
 def run(kernel, outs, args, scratch=(), flops=0, transferred=0):
+    out_shape = tuple(PLACES[id(spec)](x.shape, x.dtype) if id(spec) in PLACES else x for x, spec in outs)
+    args = tuple(
+        (pltpu.with_memory_space_constraint(x, PLACES[id(spec)]) if id(spec) in PLACES else x, spec)
+        for x, spec in args
+    )
     return pl.pallas_call(
         kernel,
-        out_shape=tuple(pltpu.HBM(x.shape, x.dtype) if spec is HBM else x for x, spec in outs),
+        out_shape=out_shape,
         in_specs=[spec for _, spec in args],
         out_specs=tuple(spec for _, spec in outs),
         scratch_shapes=list(scratch),
         compiler_params=pltpu.CompilerParams(vmem_limit_bytes=VMEM_LIMIT),
         cost_estimate=pl.CostEstimate(flops=flops, bytes_accessed=transferred, transcendentals=0),
-    )(*(pltpu.with_memory_space_constraint(x, pltpu.HBM) if spec is HBM else x for x, spec in args))
+    )(*(x for x, _ in args))
 
 
 def half_of(ref, level, half, rows):
@@ -68,65 +75,97 @@
     rounded_ref[...] = solved.astype(jnp.bfloat16)
 
 
-def copies_kernel(rounded_ref, copies_ref, sems):
-    for copy in start_copies([(rounded_ref, copies_ref.at[i]) for i in range(copies_ref.shape[0])], sems):
-        copy.wait()
-
-
-def stage_kernel(
-    factor_ref, rhs_ref, other_rhs_ref, inverse_ref, other_inverse_ref,
-    own_factor_ref, own_rhs_ref, own_inverse_ref, rhs, inverse, sems,
-):
+def copies_kernel(rounded_ref, copies_ref):
+    for i in range(copies_ref.shape[0]):
+        copies_ref[i] = rounded_ref[...]
+
+
+def slot_sum(level, store_level, chips, ids_ref, counts_ref, store_ref, factor_ref, gathered):
+    slots, width = factor_ref.shape[0], factor_ref.shape[1]
+    for k in range(slots):
+        source = ids_ref[level - 1, 0, 0, k]
+        source_level, place = source // (2 * chips), source % (2 * chips) // 2
+        live = k < counts_ref[level - 1]
+        if store_level is None:
+            live = jnp.logical_and(live, source_level < level - 1)
+            place = jnp.minimum(source_level, level - 2) * chips + place
+        else:
+            live = jnp.logical_and(live, source_level == store_level)
+        piece = store_ref[place]
+        gathered[:, k * width:(k + 1) * width] = piece * jnp.where(live, 1.0, 0.0).astype(piece.dtype)
+    return flat_dot(gathered, factor_ref)
+
+
+def stage_kernel(level, later, chips, *refs):
+    inner = level < later
+    slot_refs = refs[:4]
+    factor_ref, other_factor_ref, rhs_ref, other_rhs_ref, inverse_ref, other_inverse_ref = refs[4:10]
+    store_refs = refs[10:9 + level]
+    outs = refs[-7 if level == 1 else -11:]
+    staged_ref, own_rhs_ref, own_inverse_ref = outs[:3]
+    rhs, inverse, sems, factor_sems = outs[-4:]
     core, col = own_place()
     straight = core == col
-    levels, rows = own_rhs_ref.shape[0], own_rhs_ref.shape[1]
-    pairs = [
-        (factor_ref.at[:, 0, 0], own_factor_ref),
-        (half_of(rhs_ref, levels, col, rows), own_rhs_ref.at[levels - 1]),
-        (inverse_ref.at[levels, 0], own_inverse_ref.at[levels - 1]),
-    ]
-    for l in range(1, levels):
-        pairs += [
-            (half_of(rhs_ref, l, core, rows), rhs.at[0, l - 1]),
-            (half_of(other_rhs_ref, l, core, rows), rhs.at[1, l - 1]),
-            (inverse_ref.at[l, 0], inverse.at[0, l - 1]),
-            (other_inverse_ref.at[l, 0], inverse.at[1, l - 1]),
+    rows = own_rhs_ref.shape[0]
+    if inner:
+        pairs = [
+            (half_of(rhs_ref, level, core, rows), rhs.at[0]),
+            (half_of(other_rhs_ref, level, core, rows), rhs.at[1]),
+            (inverse_ref.at[level, 0], inverse.at[0]),
+            (other_inverse_ref.at[level, 0], inverse.at[1]),
         ]
-    for copy in start_copies(pairs, sems):
+    else:
+        pairs = [
+            (half_of(rhs_ref, level, col, rows), own_rhs_ref),
+            (inverse_ref.at[level, 0], own_inverse_ref),
+        ]
+    factor_copies = start_copies(
+        [
+            (factor_ref.at[level - 1, 0, 0], staged_ref.at[0]),
+            (other_factor_ref.at[level - 1, 0, 0], staged_ref.at[1]),
+        ],
+        factor_sems,
+    )
+    copies = start_copies(pairs, sems)
+    if level > 1:
+        older_refs, store, gathered = outs[3:5], outs[5], outs[6]
+        for m, piece in enumerate(store_refs):
+            store[m * chips:(m + 1) * chips] = piece[...]
+    for g in range(2):
+        factor_copies[g].wait()
+        if level > 1:
+            older_refs[g][...] = slot_sum(
+                level, None, chips, slot_refs[g], slot_refs[2 + g], store, staged_ref.at[g], gathered
+            )
+    for copy in copies:
         copy.wait()
-    for l in range(levels - 1):
-        own_rhs_ref[l] = jnp.where(straight, rhs[0, l], rhs[1, l])
-        own_inverse_ref[l] = jnp.where(straight, inverse[0, l], inverse[1, l])
-
-
-def sums_kernel(level, chips, ids_ref, other_ids_ref, counts_ref, other_counts_ref, *refs):
-    store_refs = refs[:level]
-    factor_refs = (refs[level].at[level - 1], refs[level + 1].at[level - 1, 0, 0])
-    kept_ref, sent_ref, store, gathered = refs[-4:]
-    slots, width = factor_refs[0].shape[0], factor_refs[0].shape[1]
+    if inner:
+        own_rhs_ref[...] = jnp.where(straight, rhs[0], rhs[1])
+        own_inverse_ref[...] = jnp.where(straight, inverse[0], inverse[1])
+
+
+def sums_kernel(level, chips, *refs):
+    slot_refs, store_ref, staged_ref = refs[:4], refs[4], refs[5]
+    older_refs = refs[6:8]
+    kept_ref, sent_ref, gathered = refs[-3:]
     core, col = own_place()
-    for m, piece in enumerate(store_refs):
-        store[m * chips:(m + 1) * chips] = piece[...]
     sums = []
-    for ids, counts, factor_ref in zip((ids_ref, other_ids_ref), (counts_ref, other_counts_ref), factor_refs):
-        for k in range(slots):
-            source = ids[level - 1, 0, 0, k]
-            piece = store[source // (2 * chips) * chips + source % (2 * chips) // 2]
-            live = jnp.where(k < counts[level - 1], 1.0, 0.0).astype(piece.dtype)
-            gathered[:, k * width:(k + 1) * width] = piece * live
-        sums.append(flat_dot(gathered, factor_ref))
+    for g in range(2):
+        total = slot_sum(
+            level, level - 1, chips, slot_refs[g], slot_refs[2 + g], store_ref, staged_ref.at[g], gathered
+        )
+        sums.append(total + older_refs[g][...] if level > 1 else total)
     straight = core == col
     kept_ref[...] = jnp.where(straight, sums[0], sums[1])
     sent_ref[...] = jnp.where(straight, sums[1], sums[0])
 
 
-def inner_kernel(level, kept_ref, arrived_ref, rhs_ref, inverse_ref, out_ref, copies_ref, rounded, sems):
-    solved = solve(rhs_ref[level - 1] - (kept_ref[...] + arrived_ref[...]), inverse_ref[level - 1])
-    rounded[...] = solved.astype(jnp.bfloat16)
-    copies = start_copies([(rounded, copies_ref.at[i]) for i in range(copies_ref.shape[0])], sems)
+def inner_kernel(kept_ref, arrived_ref, rhs_ref, inverse_ref, out_ref, copies_ref):
+    solved = solve(rhs_ref[...] - (kept_ref[...] + arrived_ref[...]), inverse_ref[...])
     out_ref[...] = solved
-    for copy in copies:
-        copy.wait()
+    rounded = solved.astype(jnp.bfloat16)
+    for i in range(copies_ref.shape[0]):
+        copies_ref[i] = rounded
 
 
 def last_kernel(first_ref, second_ref, rhs_ref, inverse_ref, *refs):
@@ -134,7 +173,7 @@
     level = len(done_refs)
     for m, done in enumerate(done_refs):
         out_ref[m, 0] = done[...]
-    solved = solve(rhs_ref[level - 1] - (first_ref[...] + second_ref[...]), inverse_ref[level - 1])
+    solved = solve(rhs_ref[...] - (first_ref[...] + second_ref[...]), inverse_ref[...])
     out_ref[level, 0] = solved
 
 
@@ -147,6 +186,7 @@
     same_core = [[2 * j + k for j in range(chips)] for k in range(2)]
     part = jax.ShapeDtypeStruct((rows, width), jnp.float32)
     rounded_part = jax.ShapeDtypeStruct((rows, width), jnp.bfloat16)
+    square = jax.ShapeDtypeStruct((width, width), jnp.bfloat16)
     copies = jax.ShapeDtypeStruct((chips, rows, width), jnp.bfloat16)
     solve_flops = 2 * rows * width * width
 
@@ -180,64 +220,55 @@
         flops=solve_flops,
     )
     finished = [solved]
-    copied, = run(
-        copies_kernel,
-        ((copies, HBM),),
-        ((transpose(rounded), VMEM),),
-        scratch=(pltpu.SemaphoreType.DMA((chips,)),),
-    )
+    copied, = run(copies_kernel, ((copies, VMEM),), ((transpose(rounded), VMEM),))
     stores = [spread(copied)]
 
     counts = block_counts.reshape(later)
     slot_args = tuple((x, SMEM) for x in (source_ids, swap_core(source_ids), counts, swap_core(counts)))
-    other_factors = swap_core(factor_blocks)
-    own_factors, rhs, inverses = run(
-        stage_kernel,
-        (
-            (jax.ShapeDtypeStruct((later, slots, width, width), jnp.bfloat16), VMEM),
-            (jax.ShapeDtypeStruct((later, rows, width), jnp.float32), VMEM),
-            (jax.ShapeDtypeStruct((later, width, width), jnp.bfloat16), VMEM),
-        ),
-        (
-            (factor_blocks, HBM),
-            (right_sides, HBM),
-            (swap_core(right_sides), ANY),
-            (diag_inverses, HBM),
-            (swap_core(diag_inverses), ANY),
-        ),
-        scratch=(
-            pltpu.VMEM((2, later - 1, rows, width), jnp.float32),
-            pltpu.VMEM((2, later - 1, width, width), jnp.bfloat16),
-            pltpu.SemaphoreType.DMA((3 + 4 * (later - 1),)),
-        ),
-        transferred=2 * later * slots * width * width * 2,
-    )
-
+    staged_args = (
+        (factor_blocks, HBM),
+        (swap_core(factor_blocks), ANY),
+        (right_sides, HBM),
+        (swap_core(right_sides), ANY),
+        (diag_inverses, HBM),
+        (swap_core(diag_inverses), ANY),
+    )
+    staged_shape = jax.ShapeDtypeStruct((2, slots, width, width), jnp.bfloat16)
+    gathered = pltpu.VMEM((rows, slots * width), jnp.bfloat16)
+    after = ()
     for l in range(1, level_count):
+        staged, rhs, inverse, *older = run(
+            functools.partial(stage_kernel, l, later, chips),
+            ((staged_shape, FIXED), (part, VMEM), (square, VMEM)) + ((part, VMEM), (part, VMEM)) * (l > 1),
+            slot_args + staged_args + tuple((x, VMEM) for x in stores[:l - 1]) + after,
+            scratch=((pltpu.VMEM(((l - 1) * chips, rows, width), jnp.bfloat16), gathered) if l > 1 else ())
+            + (
+                pltpu.VMEM((2, rows, width), jnp.float32),
+                pltpu.VMEM((2, width, width), jnp.bfloat16),
+                pltpu.SemaphoreType.DMA((4,)),
+                pltpu.SemaphoreType.DMA((2,)),
+            ),
+            flops=2 * slots * solve_flops * (l > 1),
+            transferred=2 * slots * width * width * 2,
+        )
         kept, sent = run(
             functools.partial(sums_kernel, l, chips),
             ((part, VMEM), (part, VMEM)),
             slot_args
-            + tuple((store, VMEM) for store in stores)
-            + ((own_factors, VMEM), (other_factors, VMEM))
+            + ((stores[-1], VMEM), (staged, FIXED))
+            + tuple((x, VMEM) for x in older)
             + tuple((x, ANY) for x in finished[1:]),
-            scratch=(
-                pltpu.VMEM((l * chips, rows, width), jnp.bfloat16),
-                pltpu.VMEM((rows, slots * width), jnp.bfloat16),
-            ),
+            scratch=(gathered,),
             flops=2 * slots * solve_flops,
             transferred=2 * slots * width * width * 2,
         )
+        after = ((kept, ANY),)
         if l < later:
             arrived = lax.ppermute(sent, "cols", [(0, 1), (1, 0)])
             solved, copied = run(
-                functools.partial(inner_kernel, l),
-                ((part, VMEM), (copies, HBM)),
-                ((kept, VMEM), (arrived, VMEM), (rhs, VMEM), (inverses, VMEM)),
-                scratch=(
-                    pltpu.VMEM((rows, width), jnp.bfloat16),
-                    pltpu.SemaphoreType.DMA((chips,)),
-                ),
+                inner_kernel,
+                ((part, VMEM), (copies, VMEM)),
+                tuple((x, VMEM) for x in (kept, arrived, rhs, inverse)),
                 flops=solve_flops,
             )
             finished.append(transpose(solved))
@@ -247,7 +278,7 @@
     out, = run(
         last_kernel,
         ((jax.ShapeDtypeStruct((level_count, 1, rows, width), jnp.float32), VMEM),),
-        tuple((x, VMEM) for x in (first, second, rhs, inverses, *finished)),
+        tuple((x, VMEM) for x in (first, second, rhs, inverse, *finished)),
         flops=solve_flops,
     )
     return out

time: 77.5 us -> 88.9 us (1.15)
  local copies, waits for them, and re-layouts: 9.97 us -> 26 us
  waiting for transfers between devices: 22.3 us -> 12.2 us
  Pallas kernels: 11 us -> 14.2 us
  starting transfers between devices: 33.3 us -> 35.2 us
    unnamed x34 -> x78, local copies, waits for them, and re-layouts: 9.97 us -> 26 us
    all_to_all x3, waiting for transfers between devices: 14.7 us -> 1.7 us  [spread(): return lax.all_to_all(x, 'rows', 0, 0, axis_index_groups=same_core)]
    pallas_call x9 -> x11, Pallas kernels: 11 us -> 14.2 us  [run(): pl.pallas_call(kernel, out_shape=out_shape, in_specs=[spec for _, spec in...]
    all_to_all x3, starting transfers between devices: 14.9 us -> 18 us  [spread(): return lax.all_to_all(x, 'rows', 0, 0, axis_index_groups=same_core)]
    ppermute x2, starting transfers between devices: 5.88 us -> 4 us  [paired_shards(): arrived = lax.ppermute(sent, 'cols', [(0, 1), (1, 0)])]
    ppermute x5, waiting for transfers between devices: 2.81 us -> 4.35 us  [over_both(): return lax.ppermute(x, ('rows', 'cols'), pairs)]
    ppermute x5, waiting for transfers between devices: 0.01 us -> 1.29 us  [swap_core(): return lax.ppermute(x, 'rows', [(i, i ^ 1) for i in range(row_count)])]
  transfers between devices with their start and end apart: 15 -> 15, of which waited for: 5 -> 7; matrix products, arithmetic and copies ran while one was open for 0% -> 0% of each run, Pallas kernels for 5% -> 10%
where the time goes in v7:
time: 88.9 us; the launch traced here: 87.8 us
  starting transfers between devices  35.2 us (40%)
  local copies, waits for them, and re-layouts  26 us (29%)
  Pallas kernels  14.2 us (16%)
  waiting for transfers between devices  12.2 us (14%)
    unnamed x78, local copies, waits for them, and re-layouts  26 us
    all_to_all x3, starting transfers between devices, spread(): return lax.all_to_all(x, 'rows', 0, 0, axis_index_groups=same_core)  18 us
    pallas_call x11, Pallas kernels, run(): pl.pallas_call(kernel, out_shape=out_shape, in_specs=[spec for _, spec in...  14.2 us
    ppermute x5, starting transfers between devices, over_both(): return lax.ppermute(x, ('rows', 'cols'), pairs)  7.36 us
    ppermute x5, starting transfers between devices, swap_core(): return lax.ppermute(x, 'rows', [(i, i ^ 1) for i in range(row_count)])  5.88 us
    ppermute x2, waiting for transfers between devices, paired_shards(): arrived = lax.ppermute(sent, 'cols', [(0, 1), (1, 0)])  4.85 us
    ppermute x5, waiting for transfers between devices, over_both(): return lax.ppermute(x, ('rows', 'cols'), pairs)  4.35 us
    ppermute x2, starting transfers between devices, paired_shards(): arrived = lax.ppermute(sent, 'cols', [(0, 1), (1, 0)])  4 us
  transfers between devices with their start and end apart: 15, of which 7 were waited for; matrix products, arithmetic and copies ran while one was open for 0% of the time, Pallas kernels for 10%

profile of v7, /device:TPU:0, one launch (start us, length us, event | category | flops | bytes accessed | tf_op | source)
XLA Modules:
  0.0 87.8 jit_solution(6971660582735049299)
XLA Ops:
  1.0 1.1 %shard_map.55 = (f32[64,256]{1,0:T(8,128)S(1)}, bf16[64,256]{1,0:T(8,128)(2,1)S(1)}) custom-call(f32[4,1,128,256]{3,2,1,0:T(8,128)} %refs_6_.5, bf16[4,1,256,256]{3,2,1,0:T(8,128)(2,1)} %refs_8_.5), custom_call_target="tpu_custom_call" | custom-call | flops 8388608 | tf_op jit(solution)/shard_map/pallas_call | solution.py:36
  2.7 0.7 collective-permute-start.2
  3.4 0.7 copy-done.6
  4.1 6.9 %all-to-all-start = ((bf16[8,64,256]{2,1,0:T(8,128)(2,1)}), bf16[8,64,256]{2,1,0:T(8,128)(2,1)S(1)}, u32[]{:S(2)}, u32[]{:S(2)}) async-start(bf16[8,64,256]{2,1,0:T(8,128)(2,1)} %copy-done.6), calls=%async_computation | async-start | bytes 524288 | tf_op jit(solution)/shard_map/all_to_all | solution.py:209
  11.1 4.8 %collective-permute-start.1 = (s32[3]{0:T(128)}, s32[3]{0:T(128)S(1)}, u32[]{:S(2)}, u32[]{:S(2)}) collective-permute-start(s32[3]{0:T(128)} %bitcast.1), channel_id=1, source_target_pairs={{0,2},{2,0},{4,6},{6,4},{8,10},{10,8},{12,14},{14,12},{16,18},{18,... | collective-permute-start | bytes 44 | tf_op jit(solution)/shard_map/ppermute | solution.py:203
  16.0 0.9 collective-permute-done.1.refs_3_
  17.3 0.7 copy-done.33
  18.0 0.7 copy-done.35
  18.6 2.0 %shard_map.57 = (bf16[2,8,256,256]{3,2,1,0:T(8,128)(2,1)S(1)}, f32[64,256]{1,0:T(8,128)S(1)}, bf16[256,256]{1,0:T(8,128)(2,1)S(1)}) custom-call(s32[3,1,1,8]{3,2,1,0:T(1,128)S(1)} %copy-done.33, s32[3,1,1,8]{3,2,1,0:T(1,128)S(1)} %collective-permute-done.refs_1_, s32[3]{0:T(128)S(1)} %bitcast.2, s32[3]{0:T(128)S(1)} %collective-permute-done.1.refs_3_, ...), custom_call_target="tpu_custom_call" | custom-call | bytes 2097152 | tf_op jit(solution)/shard_map/pallas_call | solution.py:36
  20.6 1.3 %copy-done.4 = bf16[2,8,256,256]{3,2,1,0:T(8,128)(2,1)} copy-done((bf16[2,8,256,256]{3,2,1,0:T(8,128)(2,1)}, bf16[2,8,256,256]{3,2,1,0:T(8,128)(2,1)S(1)}, u32[]{:S(2)}) %copy-start.4) | copy-done | bytes 2097176
  21.9 0.6 copy-done.13
  23.2 1.6 %copy-done.5 = bf16[2,8,256,256]{3,2,1,0:T(8,128)(2,1)S(1)} copy-done((bf16[2,8,256,256]{3,2,1,0:T(8,128)(2,1)S(1)}, bf16[2,8,256,256]{3,2,1,0:T(8,128)(2,1)}, u32[]{:S(2)}) %copy-start.5) | copy-done | bytes 2097176
  24.8 1.1 %shard_map.58 = (f32[64,256]{1,0:T(8,128)S(1)}, f32[64,256]{1,0:T(8,128)S(1)}) custom-call(s32[3,1,1,8]{3,2,1,0:T(1,128)S(1)} %copy-done.34, s32[3,1,1,8]{3,2,1,0:T(1,128)S(1)} %collective-permute-done.refs_1_, s32[3]{0:T(128)S(1)} %bitcast.3, s32[3]{0:T(128)S(1)} %collective-permute-done.1.refs_3_, bf16[8,64,256]{2,1,0:T(8,128)(2,1)S(1)} %all-to-all-done.refs_4_.refs_10_, ...), custom_call_target="tpu_custom_call" | custom-call | flops 134217728 | bytes 2097152 | tf_op jit(solution)/shard_map/pallas_call | solution.py:36
  25.9 2.2 %collective-permute-start.6 = (f32[64,256]{1,0:T(8,128)S(1)}, f32[64,256]{1,0:T(8,128)S(1)}, u32[]{:S(2)}, u32[]{:S(2)}) collective-permute-start(f32[64,256]{1,0:T(8,128)S(1)} %get-tuple-element.33), channel_id=1, source_target_pairs={{0,1},{1,0},{2,3},{3,2},{4,5},{5,4},{6,7},{7,6},{8,9},{9,8},{10,11... | collective-permute-start | bytes 196616 | tf_op jit(solution)/shard_map/ppermute | solution.py:267
  28.1 2.2 %collective-permute-done.6.arrived_ref = f32[64,256]{1,0:T(8,128)S(1)} collective-permute-done((f32[64,256]{1,0:T(8,128)S(1)}, f32[64,256]{1,0:T(8,128)S(1)}, u32[]{:S(2)}, u32[]{:S(2)}) %collective-permute-start.6) | collective-permute-done | bytes 65568 | tf_op jit(solution)/shard_map/ppermute | solution.py:267
  30.5 0.7 copy-done.10
  31.2 0.6 copy-done.38
  31.8 5.6 %all-to-all-start.1 = ((bf16[8,64,256]{2,1,0:T(8,128)(2,1)}), bf16[8,64,256]{2,1,0:T(8,128)(2,1)}, u32[]{:S(2)}, u32[]{:S(2)}) async-start(bf16[8,64,256]{2,1,0:T(8,128)(2,1)} %copy-done.10), calls=%async_computation.1 | async-start | bytes 524288 | tf_op jit(solution)/shard_map/all_to_all | solution.py:209
  37.4 1.5 %collective-permute-start.7 = (f32[64,256]{1,0:T(8,128)}, f32[64,256]{1,0:T(8,128)S(1)}, u32[]{:S(2)}, u32[]{:S(2)}) collective-permute-start(f32[64,256]{1,0:T(8,128)} %copy-done.38), channel_id=1, source_target_pairs={{0,0},{1,2},{2,1},{3,3},{4,4},{5,6},{6,5},{7,7},{8,8},{9,10},{10,9... | collective-permute-start | bytes 196616 | tf_op jit(solution)/shard_map/ppermute | solution.py:200
  38.9 2.7 %shard_map.60 = (bf16[2,8,256,256]{3,2,1,0:T(8,128)(2,1)S(1)}, f32[64,256]{1,0:T(8,128)S(1)}, bf16[256,256]{1,0:T(8,128)(2,1)S(1)}, f32[64,256]{1,0:T(8,128)S(1)}, f32[64,256]{1,0:T(8,128)S(1)}) custom-call(s32[3,1,1,8]{3,2,1,0:T(1,128)S(1)} %copy-done.34, s32[3,1,1,8]{3,2,1,0:T(1,128)S(1)} %collective-permute-done.refs_1_, s32[3]{0:T(128)S(1)} %bitcast.4, ...), custom_call_target="tpu_custom_call" | custom-call | flops 134217728 | bytes 2097152 | tf_op jit(solution)/shard_map/pallas_call | solution.py:36
  41.7 1.3 %copy-done.2 = bf16[2,8,256,256]{3,2,1,0:T(8,128)(2,1)} copy-done((bf16[2,8,256,256]{3,2,1,0:T(8,128)(2,1)}, bf16[2,8,256,256]{3,2,1,0:T(8,128)(2,1)S(1)}, u32[]{:S(2)}) %copy-start.2) | copy-done | bytes 2097176
  43.0 0.6 copy-done.11
  43.7 0.6 copy-done.21
  45.5 0.6 all-to-all-done.1.refs_4_.refs_11_
  46.2 1.6 %copy-done.3 = bf16[2,8,256,256]{3,2,1,0:T(8,128)(2,1)S(1)} copy-done((bf16[2,8,256,256]{3,2,1,0:T(8,128)(2,1)S(1)}, bf16[2,8,256,256]{3,2,1,0:T(8,128)(2,1)}, u32[]{:S(2)}) %copy-start.3) | copy-done | bytes 2097176
  47.8 0.8 copy-done.30
  48.6 0.8 copy-done.32
  49.4 1.5 %shard_map.61 = (f32[64,256]{1,0:T(8,128)S(1)}, f32[64,256]{1,0:T(8,128)S(1)}) custom-call(s32[3,1,1,8]{3,2,1,0:T(1,128)S(1)} %copy-done.34, s32[3,1,1,8]{3,2,1,0:T(1,128)S(1)} %collective-permute-done.refs_1_, s32[3]{0:T(128)S(1)} %bitcast.5, s32[3]{0:T(128)S(1)} %collective-permute-done.1.refs_3_, bf16[8,64,256]{2,1,0:T(8,128)(2,1)} %all-to-all-done.1.refs_4_.refs_11_, ...), custom_call_target="tpu_custom_call" | custom-call | flops 134217728 | bytes 2097152 | tf_op jit(solution)/shard_map/pallas_call | solution.py:36
  50.9 1.8 %collective-permute-start.8 = (f32[64,256]{1,0:T(8,128)S(1)}, f32[64,256]{1,0:T(8,128)S(1)}, u32[]{:S(2)}, u32[]{:S(2)}) collective-permute-start(f32[64,256]{1,0:T(8,128)S(1)} %get-tuple-element.42), channel_id=1, source_target_pairs={{0,1},{1,0},{2,3},{3,2},{4,5},{5,4},{6,7},{7,6},{8,9},{9,8},{10,11... | collective-permute-start | bytes 196616 | tf_op jit(solution)/shard_map/ppermute | solution.py:267
  52.7 2.6 %collective-permute-done.8.arrived_ref = f32[64,256]{1,0:T(8,128)S(1)} collective-permute-done((f32[64,256]{1,0:T(8,128)S(1)}, f32[64,256]{1,0:T(8,128)S(1)}, u32[]{:S(2)}, u32[]{:S(2)}) %collective-permute-start.8) | collective-permute-done | bytes 65568 | tf_op jit(solution)/shard_map/ppermute | solution.py:267
  55.5 0.7 copy-done.9
  56.8 5.5 %all-to-all-start.2 = ((bf16[8,64,256]{2,1,0:T(8,128)(2,1)}), bf16[8,64,256]{2,1,0:T(8,128)(2,1)}, u32[]{:S(2)}, u32[]{:S(2)}) async-start(bf16[8,64,256]{2,1,0:T(8,128)(2,1)} %copy-done.9), calls=%async_computation.2 | async-start | bytes 524288 | tf_op jit(solution)/shard_map/all_to_all | solution.py:209
  62.3 1.5 %collective-permute-start.9 = (f32[64,256]{1,0:T(8,128)}, f32[64,256]{1,0:T(8,128)S(1)}, u32[]{:S(2)}, u32[]{:S(2)}) collective-permute-start(f32[64,256]{1,0:T(8,128)} %copy-done.37), channel_id=1, source_target_pairs={{0,0},{1,2},{2,1},{3,3},{4,4},{5,6},{6,5},{7,7},{8,8},{9,10},{10,9... | collective-permute-start | bytes 196616 | tf_op jit(solution)/shard_map/ppermute | solution.py:200
  63.8 3.1 %shard_map.63 = (bf16[2,8,256,256]{3,2,1,0:T(8,128)(2,1)S(1)}, f32[64,256]{1,0:T(8,128)S(1)}, bf16[256,256]{1,0:T(8,128)(2,1)S(1)}, f32[64,256]{1,0:T(8,128)S(1)}, f32[64,256]{1,0:T(8,128)S(1)}) custom-call(s32[3,1,1,8]{3,2,1,0:T(1,128)S(1)} %copy-done.34, s32[3,1,1,8]{3,2,1,0:T(1,128)S(1)} %collective-permute-done.refs_1_, s32[3]{0:T(128)S(1)} %bitcast.6, ...), custom_call_target="tpu_custom_call" | custom-call | flops 134217728 | bytes 2097152 | tf_op jit(solution)/shard_map/pallas_call | solution.py:36
  66.9 1.3 %copy-done = bf16[2,8,256,256]{3,2,1,0:T(8,128)(2,1)} copy-done((bf16[2,8,256,256]{3,2,1,0:T(8,128)(2,1)}, bf16[2,8,256,256]{3,2,1,0:T(8,128)(2,1)S(1)}, u32[]{:S(2)}) %copy-start) | copy-done | bytes 2097176
  68.2 0.6 copy-done.15
  70.1 0.6 copy-done.25
  71.3 1.1 %all-to-all-done.2.refs_4_ = bf16[8,64,256]{2,1,0:T(8,128)(2,1)} async-done(((bf16[8,64,256]{2,1,0:T(8,128)(2,1)}), bf16[8,64,256]{2,1,0:T(8,128)(2,1)}, u32[]{:S(2)}, u32[]{:S(2)}) %all-to-all-start.2) | async-done | bytes 262176 | tf_op jit(solution)/shard_map/all_to_all | solution.py:209
  72.4 1.6 %copy-done.1 = bf16[2,8,256,256]{3,2,1,0:T(8,128)(2,1)S(1)} copy-done((bf16[2,8,256,256]{3,2,1,0:T(8,128)(2,1)S(1)}, bf16[2,8,256,256]{3,2,1,0:T(8,128)(2,1)}, u32[]{:S(2)}) %copy-start.1) | copy-done | bytes 2097176
  74.0 0.8 copy-done.8
  74.8 0.8 copy-done.24
  75.7 0.8 copy-done.26
  76.5 1.5 %shard_map.64 = (f32[64,256]{1,0:T(8,128)S(1)}, f32[64,256]{1,0:T(8,128)S(1)}) custom-call(s32[3,1,1,8]{3,2,1,0:T(1,128)S(1)} %copy-done.34, s32[3,1,1,8]{3,2,1,0:T(1,128)S(1)} %collective-permute-done.refs_1_, s32[3]{0:T(128)S(1)} %bitcast.7, s32[3]{0:T(128)S(1)} %collective-permute-done.1.refs_3_, bf16[8,64,256]{2,1,0:T(8,128)(2,1)} %all-to-all-done.2.refs_4_, ...), custom_call_target="tpu_custom_call" | custom-call | flops 134217728 | bytes 2097152 | tf_op jit(solution)/shard_map/pallas_call | solution.py:36
  78.0 0.7 collective-permute-start.10
  78.7 3.1 %collective-permute-start.11 = (f32[64,256]{1,0:T(8,128)S(1)}, f32[64,256]{1,0:T(8,128)S(1)}, u32[]{:S(2)}, u32[]{:S(2)}) collective-permute-start(f32[64,256]{1,0:T(8,128)S(1)} %get-tuple-element.51), channel_id=1, source_target_pairs={{0,2},{1,0},{2,3},{3,1},{4,6},{5,4},{6,7},{7,5},{8,10},{9,8},{10,1... | collective-permute-start | bytes 196616 | tf_op jit(solution)/shard_map/ppermute | solution.py:200
  81.8 4.3 %collective-permute-done.11.second_ref = f32[64,256]{1,0:T(8,128)S(1)} collective-permute-done((f32[64,256]{1,0:T(8,128)S(1)}, f32[64,256]{1,0:T(8,128)S(1)}, u32[]{:S(2)}, u32[]{:S(2)}) %collective-permute-start.11) | collective-permute-done | bytes 65568 | tf_op jit(solution)/shard_map/ppermute | solution.py:200
  86.1 0.8 copy-done.18
  86.9 0.9 shard_map.65
  (71 shorter events, 6.8 us)
Async XLA Ops:
  0.0 17.3 %collective-permute-start.3 = (bf16[3,1,1,8,256,256]{5,4,3,2,1,0:T(8,128)(2,1)}, bf16[3,1,1,8,256,256]{5,4,3,2,1,0:T(8,128)(2,1)S(1)}, u32[]{:S(2)}, u32[]{:S(2)}) collective-permute-start(bf16[3,1,1,8,256,256]{5,4,3,2,1,0:T(8,128)(2,1)} %refs_4_.5), channel_id=1, source_target_pairs={{0,2},{2,0},{4,6},{6,4},{8,10},{10,8},{12,14},{14,12},{16,18},{18,... | collective-permute-start | bytes 9437192 | tf_op jit(solution)/shard_map/ppermute | solution.py:203
  0.5 16.8 %collective-permute-start.4 = (f32[4,1,128,256]{3,2,1,0:T(8,128)}, f32[4,1,128,256]{3,2,1,0:T(8,128)}, u32[]{:S(2)}, u32[]{:S(2)}) collective-permute-start(f32[4,1,128,256]{3,2,1,0:T(8,128)} %refs_6_.5), channel_id=1, source_target_pairs={{0,2},{2,0},{4,6},{6,4},{8,10},{10,8},{12,14},{14,12},{16,18},{18,... | collective-permute-start | bytes 1572872 | tf_op jit(solution)/shard_map/ppermute | solution.py:203
  0.5 16.7 %collective-permute-start.5 = (bf16[4,1,256,256]{3,2,1,0:T(8,128)(2,1)}, bf16[4,1,256,256]{3,2,1,0:T(8,128)(2,1)}, u32[]{:S(2)}, u32[]{:S(2)}) collective-permute-start(bf16[4,1,256,256]{3,2,1,0:T(8,128)(2,1)} %refs_8_.5), channel_id=1, source_target_pairs={{0,2},{2,0},{4,6},{6,4},{8,10},{10,8},{12,14},{14,12},{16,18},{18,... | collective-permute-start | bytes 1572872 | tf_op jit(solution)/shard_map/ppermute | solution.py:203
  2.1 0.6 copy-start.17
  2.7 0.7 collective-permute-start.2
  3.4 0.7 copy-start.6
  4.1 19.1 %copy-start.36 = (s32[3,1,1]{0,2,1:T(1,128)S(1)}, s32[3,1,1]{0,2,1:T(1,128)}, u32[]{:S(2)}) copy-start(s32[3,1,1]{0,2,1:T(1,128)} %param.9) | copy-start | bytes 40
  4.1 19.1 %all-to-all-start = ((bf16[8,64,256]{2,1,0:T(8,128)(2,1)}), bf16[8,64,256]{2,1,0:T(8,128)(2,1)S(1)}, u32[]{:S(2)}, u32[]{:S(2)}) async-start(bf16[8,64,256]{2,1,0:T(8,128)(2,1)} %copy-done.6), calls=%async_computation | async-start | bytes 524288 | tf_op jit(solution)/shard_map/all_to_all | solution.py:209
  11.0 12.1 %copy-start.34 = (s32[3,1,1,8]{3,2,1,0:T(1,128)S(1)}, s32[3,1,1,8]{3,2,1,0:T(1,128)}, u32[]{:S(2)}) copy-start(s32[3,1,1,8]{3,2,1,0:T(1,128)} %refs_0_.11) | copy-start | bytes 292
  11.1 5.8 %collective-permute-start.1 = (s32[3]{0:T(128)}, s32[3]{0:T(128)S(1)}, u32[]{:S(2)}, u32[]{:S(2)}) collective-permute-start(s32[3]{0:T(128)} %bitcast.1), channel_id=1, source_target_pairs={{0,2},{2,0},{4,6},{6,4},{8,10},{10,8},{12,14},{14,12},{16,18},{18,... | collective-permute-start | bytes 44 | tf_op jit(solution)/shard_map/ppermute | solution.py:203
  15.9 1.4 %collective-permute-start = (s32[3,1,1,8]{3,2,1,0:T(1,128)}, s32[3,1,1,8]{3,2,1,0:T(1,128)S(1)}, u32[]{:S(2)}, u32[]{:S(2)}) collective-permute-start(s32[3,1,1,8]{3,2,1,0:T(1,128)} %refs_0_.11), channel_id=1, source_target_pairs={{0,2},{2,0},{4,6},{6,4},{8,10},{10,8},{12,14},{14,12},{16,18},{18,... | collective-permute-start | bytes 296 | tf_op jit(solution)/shard_map/ppermute | solution.py:203
  17.3 0.7 copy-start.33
  17.9 0.7 copy-start.35
  20.6 1.3 %copy-start.4 = (bf16[2,8,256,256]{3,2,1,0:T(8,128)(2,1)}, bf16[2,8,256,256]{3,2,1,0:T(8,128)(2,1)S(1)}, u32[]{:S(2)}) copy-start(bf16[2,8,256,256]{3,2,1,0:T(8,128)(2,1)S(1)} %get-tuple-element.31.refs_5_) | copy-start | bytes 6291460
  21.9 0.6 copy-start.13
  23.2 1.6 %copy-start.5 = (bf16[2,8,256,256]{3,2,1,0:T(8,128)(2,1)S(1)}, bf16[2,8,256,256]{3,2,1,0:T(8,128)(2,1)}, u32[]{:S(2)}) copy-start(bf16[2,8,256,256]{3,2,1,0:T(8,128)(2,1)} %copy-done.4) | copy-start | bytes 6291460
  24.8 5.5 %copy-start.14 = (bf16[256,256]{1,0:T(8,128)(2,1)S(1)}, bf16[256,256]{1,0:T(8,128)(2,1)}, u32[]{:S(2)}) copy-start(bf16[256,256]{1,0:T(8,128)(2,1)} %copy-done.13) | copy-start | bytes 393220
  24.8 5.5 %copy-start.28 = (f32[64,256]{1,0:T(8,128)S(1)}, f32[64,256]{1,0:T(8,128)}, u32[]{:S(2)}) copy-start(f32[64,256]{1,0:T(8,128)} %copy-done.27) | copy-start | bytes 196612
  25.9 4.5 %collective-permute-start.6 = (f32[64,256]{1,0:T(8,128)S(1)}, f32[64,256]{1,0:T(8,128)S(1)}, u32[]{:S(2)}, u32[]{:S(2)}) collective-permute-start(f32[64,256]{1,0:T(8,128)S(1)} %get-tuple-element.33), channel_id=1, source_target_pairs={{0,1},{1,0},{2,3},{3,2},{4,5},{5,4},{6,7},{7,6},{8,9},{9,8},{10,11... | collective-permute-start | bytes 196616 | tf_op jit(solution)/shard_map/ppermute | solution.py:267
  30.5 0.7 copy-start.10
  31.2 0.6 copy-start.38
  31.8 14.3 %all-to-all-start.1 = ((bf16[8,64,256]{2,1,0:T(8,128)(2,1)}), bf16[8,64,256]{2,1,0:T(8,128)(2,1)}, u32[]{:S(2)}, u32[]{:S(2)}) async-start(bf16[8,64,256]{2,1,0:T(8,128)(2,1)} %copy-done.10), calls=%async_computation.1 | async-start | bytes 524288 | tf_op jit(solution)/shard_map/all_to_all | solution.py:209
  37.4 8.1 %collective-permute-start.7 = (f32[64,256]{1,0:T(8,128)}, f32[64,256]{1,0:T(8,128)S(1)}, u32[]{:S(2)}, u32[]{:S(2)}) collective-permute-start(f32[64,256]{1,0:T(8,128)} %copy-done.38), channel_id=1, source_target_pairs={{0,0},{1,2},{2,1},{3,3},{4,4},{5,6},{6,5},{7,7},{8,8},{9,10},{10,9... | collective-permute-start | bytes 196616 | tf_op jit(solution)/shard_map/ppermute | solution.py:200
  41.7 1.3 %copy-start.2 = (bf16[2,8,256,256]{3,2,1,0:T(8,128)(2,1)}, bf16[2,8,256,256]{3,2,1,0:T(8,128)(2,1)S(1)}, u32[]{:S(2)}) copy-start(bf16[2,8,256,256]{3,2,1,0:T(8,128)(2,1)S(1)} %get-tuple-element.37.refs_5_) | copy-start | bytes 6291460
  43.0 0.6 copy-start.11
  43.7 0.6 copy-start.21
  46.2 1.6 %copy-start.3 = (bf16[2,8,256,256]{3,2,1,0:T(8,128)(2,1)S(1)}, bf16[2,8,256,256]{3,2,1,0:T(8,128)(2,1)}, u32[]{:S(2)}) copy-start(bf16[2,8,256,256]{3,2,1,0:T(8,128)(2,1)} %copy-done.2) | copy-start | bytes 6291460
  47.8 0.8 copy-start.30
  48.6 0.8 copy-start.32
  49.4 5.9 %copy-start.12 = (bf16[256,256]{1,0:T(8,128)(2,1)S(1)}, bf16[256,256]{1,0:T(8,128)(2,1)}, u32[]{:S(2)}) copy-start(bf16[256,256]{1,0:T(8,128)(2,1)} %copy-done.11) | copy-start | bytes 393220
  49.4 5.9 %copy-start.22 = (f32[64,256]{1,0:T(8,128)S(1)}, f32[64,256]{1,0:T(8,128)}, u32[]{:S(2)}) copy-start(f32[64,256]{1,0:T(8,128)} %copy-done.21) | copy-start | bytes 196612
  50.9 4.4 %collective-permute-start.8 = (f32[64,256]{1,0:T(8,128)S(1)}, f32[64,256]{1,0:T(8,128)S(1)}, u32[]{:S(2)}, u32[]{:S(2)}) collective-permute-start(f32[64,256]{1,0:T(8,128)S(1)} %get-tuple-element.42), channel_id=1, source_target_pairs={{0,1},{1,0},{2,3},{3,2},{4,5},{5,4},{6,7},{7,6},{8,9},{9,8},{10,11... | collective-permute-start | bytes 196616 | tf_op jit(solution)/shard_map/ppermute | solution.py:267
  55.5 0.7 copy-start.9
  56.8 15.6 %all-to-all-start.2 = ((bf16[8,64,256]{2,1,0:T(8,128)(2,1)}), bf16[8,64,256]{2,1,0:T(8,128)(2,1)}, u32[]{:S(2)}, u32[]{:S(2)}) async-start(bf16[8,64,256]{2,1,0:T(8,128)(2,1)} %copy-done.9), calls=%async_computation.2 | async-start | bytes 524288 | tf_op jit(solution)/shard_map/all_to_all | solution.py:209
  62.3 8.4 %collective-permute-start.9 = (f32[64,256]{1,0:T(8,128)}, f32[64,256]{1,0:T(8,128)S(1)}, u32[]{:S(2)}, u32[]{:S(2)}) collective-permute-start(f32[64,256]{1,0:T(8,128)} %copy-done.37), channel_id=1, source_target_pairs={{0,0},{1,2},{2,1},{3,3},{4,4},{5,6},{6,5},{7,7},{8,8},{9,10},{10,9... | collective-permute-start | bytes 196616 | tf_op jit(solution)/shard_map/ppermute | solution.py:200
  66.9 1.3 %copy-start = (bf16[2,8,256,256]{3,2,1,0:T(8,128)(2,1)}, bf16[2,8,256,256]{3,2,1,0:T(8,128)(2,1)S(1)}, u32[]{:S(2)}) copy-start(bf16[2,8,256,256]{3,2,1,0:T(8,128)(2,1)S(1)} %get-tuple-element.46.refs_5_) | copy-start | bytes 6291460
  68.2 0.6 copy-start.15
  69.5 0.6 copy-start.23
  70.1 0.6 copy-start.25
  72.4 1.6 %copy-start.1 = (bf16[2,8,256,256]{3,2,1,0:T(8,128)(2,1)S(1)}, bf16[2,8,256,256]{3,2,1,0:T(8,128)(2,1)}, u32[]{:S(2)}) copy-start(bf16[2,8,256,256]{3,2,1,0:T(8,128)(2,1)} %copy-done) | copy-start | bytes 6291460
  74.0 0.8 copy-start.8
  74.8 0.8 copy-start.24
  75.7 0.8 copy-start.26
  76.5 9.6 %copy-start.16 = (bf16[256,256]{1,0:T(8,128)(2,1)S(1)}, bf16[256,256]{1,0:T(8,128)(2,1)}, u32[]{:S(2)}) copy-start(bf16[256,256]{1,0:T(8,128)(2,1)} %copy-done.15) | copy-start | bytes 393220
  76.5 9.6 %copy-start.20 = (f32[64,256]{1,0:T(8,128)S(1)}, f32[64,256]{1,0:T(8,128)}, u32[]{:S(2)}) copy-start(f32[64,256]{1,0:T(8,128)} %copy-done.19) | copy-start | bytes 196612
  78.0 3.8 %collective-permute-start.10 = (f32[64,256]{1,0:T(8,128)S(1)}, f32[64,256]{1,0:T(8,128)S(1)}, u32[]{:S(2)}, u32[]{:S(2)}) collective-permute-start(f32[64,256]{1,0:T(8,128)S(1)} %get-tuple-element.50), channel_id=1, source_target_pairs={{0,0},{1,2},{2,1},{3,3},{4,4},{5,6},{6,5},{7,7},{8,8},{9,10},{10,9... | collective-permute-start | bytes 196616 | tf_op jit(solution)/shard_map/ppermute | solution.py:200
  78.7 7.4 %collective-permute-start.11 = (f32[64,256]{1,0:T(8,128)S(1)}, f32[64,256]{1,0:T(8,128)S(1)}, u32[]{:S(2)}, u32[]{:S(2)}) collective-permute-start(f32[64,256]{1,0:T(8,128)S(1)} %get-tuple-element.51), channel_id=1, source_target_pairs={{0,2},{1,0},{2,3},{3,1},{4,6},{5,4},{6,7},{7,5},{8,10},{9,8},{10,1... | collective-permute-start | bytes 196616 | tf_op jit(solution)/shard_map/ppermute | solution.py:200
  86.1 0.8 copy-start.18
  (6 other events, 3.7 us)

commit v8 on v5

--- a/solution.py
+++ b/solution.py
@@ -52,34 +52,112 @@
     return copies
 
 
-def live_kernel(ids_ref, counts_ref, live_ids_ref):
-    for l in range(ids_ref.shape[0]):
-        for k in range(ids_ref.shape[3]):
-            live = k < counts_ref[l, 0, 0]
-            live_ids_ref[l, 0, 0, k] = jnp.where(live, ids_ref[l, 0, 0, k], -1)
-
-
-def first_kernel(place_ref, rhs_ref, inverse_ref, out_ref, rounded_ref, rhs, inverse, sems):
-    rows = out_ref.shape[0]
+def own_place():
+    return lax.rem(lax.axis_index("rows"), 2), lax.axis_index("cols")
+
+
+def first_kernel(rhs_ref, inverse_ref, out_ref, rounded_ref, rhs, inverse, solved, sems):
+    _, col = own_place()
+    for copy in start_copies(
+        [(half_of(rhs_ref, 0, col, rhs.shape[0]), rhs), (inverse_ref.at[0, 0], inverse)], sems
+    ):
+        copy.wait()
+    solved[...] = solve(rhs[...], inverse[...])
+    out = pltpu.make_async_copy(solved, out_ref, sems.at[2])
+    out.start()
+    rounded_ref[...] = solved[...].astype(jnp.bfloat16)
+    out.wait()
+
+
+def copies_kernel(rounded_ref, *refs):
+    copies_ref, sems = refs[-2:]
+    for copy in start_copies([(rounded_ref, copies_ref.at[i]) for i in range(copies_ref.shape[0])], sems):
+        copy.wait()
+
+
+def gather_level(level, older, chips, ids_ref, counts_ref, store, gathered, slots):
+    width = store.shape[2]
+    for i, k in enumerate(slots):
+        source = ids_ref[level - 1, 0, 0, k]
+        source_level, place = source // (2 * chips), source % (2 * chips) // 2
+        if older:
+            wanted = source_level < level - 1
+            place = jnp.minimum(source_level, level - 2) * chips + place
+        else:
+            wanted = source_level == level - 1
+        live = jnp.logical_and(k < counts_ref[level - 1], wanted)
+        gathered[:, i * width:(i + 1) * width] = store[place] * jnp.where(live, 1.0, 0.0).astype(store.dtype)
+
+
+def group_sums(level, older, chips, slot_refs, store, own_factor_ref, other_factor_ref, gathered, own_factor, sems):
+    ids_ref, other_ids_ref, counts_ref, other_counts_ref = slot_refs
+    slots = own_factor.shape[0]
+    half = slots // 2
+    parts = (range(half), range(half, slots))
     copies = start_copies(
-        [(half_of(rhs_ref, 0, place_ref[1], rows), rhs), (inverse_ref.at[0, 0], inverse)], sems
-    )
+        [
+            (own_factor_ref.at[level - 1, 0, 0, pl.ds(part[0], len(part))], own_factor.at[pl.ds(part[0], len(part))])
+            for part in parts
+        ],
+        sems,
+    )
+    yield None
+    gather_level(level, older, chips, other_ids_ref, other_counts_ref, store, gathered, range(slots))
+    other = flat_dot(gathered, other_factor_ref.at[level - 1, 0, 0])
+    own = None
+    width = store.shape[2]
+    for part, copy in zip(parts, copies):
+        piece = gathered.at[:, pl.ds(part[0] * width, len(part) * width)]
+        gather_level(level, older, chips, ids_ref, counts_ref, store, piece, part)
+        copy.wait()
+        term = flat_dot(piece, own_factor.at[pl.ds(part[0], len(part))])
+        own = term if own is None else own + term
+    yield own, other
+
+
+def older_kernel(level, chips, *refs):
+    slot_refs, (own_factor_ref, other_factor_ref) = refs[:4], refs[4:6]
+    store_refs = refs[6:5 + level]
+    out_ref, store, gathered, own_factor, sums, sems, store_sems = refs[5 + level:]
+    copies = start_copies(
+        [(piece, store.at[pl.ds(m * chips, chips)]) for m, piece in enumerate(store_refs)], store_sems
+    )
+    work = group_sums(
+        level, True, chips, slot_refs, store, own_factor_ref, other_factor_ref, gathered, own_factor, sems
+    )
+    next(work)
     for copy in copies:
         copy.wait()
-    solved = solve(rhs[...], inverse[...])
-    out_ref[...] = solved
-    rounded_ref[...] = solved.astype(jnp.bfloat16)
-
-
-def sums_kernel(level, chips, inner, place_ref, ids_ref, other_ids_ref, *refs):
-    store_refs = refs[:level]
-    own_factor_ref, other_factor_ref, rhs_ref, other_rhs_ref, inverse_ref, other_inverse_ref = refs[level:level + 6]
-    kept_ref, sent_ref, own_rhs_ref, own_inverse_ref = refs[-10:-6]
-    store, gathered, own_factor, rhs, inverse, sems = refs[-6:]
-    slots, width = own_factor.shape[0], own_factor.shape[1]
-    rows = kept_ref.shape[0]
-    core, col = place_ref[0], place_ref[1]
+    sums[0], sums[1] = next(work)
+    out = pltpu.make_async_copy(sums, out_ref, store_sems.at[0])
+    out.start()
+    out.wait()
+
+
+def sums_kernel(level, chips, *refs):
+    slot_refs, (own_factor_ref, other_factor_ref, store_ref) = refs[:4], refs[4:7]
+    kept_ref, sent_ref, store, gathered, own_factor, older, sems, store_sems = refs[-8:]
+    core, col = own_place()
+    pairs = [(store_ref, store)] + ([(refs[7], older)] if level > 1 else [])
+    copies = start_copies(pairs, store_sems)
+    work = group_sums(
+        level, False, chips, slot_refs, store, own_factor_ref, other_factor_ref, gathered, own_factor, sems
+    )
+    next(work)
+    for copy in copies:
+        copy.wait()
+    own, other = next(work)
+    if level > 1:
+        own, other = own + older[0], other + older[1]
     straight = core == col
+    kept_ref[...] = jnp.where(straight, own, other)
+    sent_ref[...] = jnp.where(straight, other, own)
+
+
+def select_kernel(level, inner, rhs_ref, other_rhs_ref, inverse_ref, other_inverse_ref, *refs):
+    own_rhs_ref, own_inverse_ref, rhs, inverse, sems = refs[-5:]
+    core, col = own_place()
+    rows = own_rhs_ref.shape[0]
     if inner:
         pairs = [
             (half_of(rhs_ref, level, core, rows), rhs.at[0]),
@@ -92,51 +170,31 @@
             (half_of(rhs_ref, level, col, rows), own_rhs_ref),
             (inverse_ref.at[level, 0], own_inverse_ref),
         ]
-    copies = start_copies([(own_factor_ref.at[level - 1, 0, 0], own_factor)] + pairs, sems)
-    for m, piece in enumerate(store_refs):
-        store[m * chips:(m + 1) * chips] = piece[...]
-
-    def group_sum(ids, factor_ref):
-        for k in range(slots):
-            source = ids[level - 1, 0, 0, k]
-            known = jnp.maximum(source, 0)
-            piece = store[known // (2 * chips) * chips + known % (2 * chips) // 2]
-            live = jnp.where(source >= 0, 1.0, 0.0).astype(piece.dtype)
-            gathered[:, k * width:(k + 1) * width] = piece * live
-        return flat_dot(gathered, factor_ref)
-
-    other = group_sum(other_ids_ref, other_factor_ref.at[level - 1, 0, 0])
-    copies[0].wait()
-    own = group_sum(ids_ref, own_factor)
-    kept_ref[...] = jnp.where(straight, own, other)
-    sent_ref[...] = jnp.where(straight, other, own)
-    for copy in copies[1:]:
+    for copy in start_copies(pairs, sems):
         copy.wait()
     if inner:
+        straight = core == col
         own_rhs_ref[...] = jnp.where(straight, rhs[0], rhs[1])
         own_inverse_ref[...] = jnp.where(straight, inverse[0], inverse[1])
 
 
-def copies_kernel(rounded_ref, copies_ref, sems):
-    for copy in start_copies([(rounded_ref, copies_ref.at[i]) for i in range(copies_ref.shape[0])], sems):
-        copy.wait()
-
-
-def inner_kernel(kept_ref, arrived_ref, rhs_ref, inverse_ref, out_ref, copies_ref, rounded, sems):
-    solved = solve(rhs_ref[...] - (kept_ref[...] + arrived_ref[...]), inverse_ref[...])
-    rounded[...] = solved.astype(jnp.bfloat16)
-    copies = start_copies([(rounded, copies_ref.at[i]) for i in range(copies_ref.shape[0])], sems)
-    out_ref[...] = solved
-    for copy in copies:
+def inner_kernel(kept_ref, arrived_ref, rhs_ref, inverse_ref, out_ref, copies_ref, solved, rounded, sems):
+    solved[...] = solve(rhs_ref[...] - (kept_ref[...] + arrived_ref[...]), inverse_ref[...])
+    rounded[...] = solved[...].astype(jnp.bfloat16)
+    chips = copies_ref.shape[0]
+    for copy in start_copies([(rounded, copies_ref.at[i]) for i in range(chips)] + [(solved, out_ref)], sems):
         copy.wait()
 
 
 def last_kernel(first_ref, second_ref, rhs_ref, inverse_ref, *refs):
-    done_refs, out_ref = refs[:-1], refs[-1]
-    for m, done in enumerate(done_refs):
-        out_ref[m, 0] = done[...]
-    solved = solve(rhs_ref[...] - (first_ref[...] + second_ref[...]), inverse_ref[...])
-    out_ref[len(done_refs), 0] = solved
+    done_refs, (out_ref, solved, sems) = refs[:-3], refs[-3:]
+    level = len(done_refs)
+    copies = start_copies([(done, out_ref.at[m, 0]) for m, done in enumerate(done_refs)], sems)
+    solved[...] = solve(rhs_ref[...] - (first_ref[...] + second_ref[...]), inverse_ref[...])
+    out = pltpu.make_async_copy(solved, out_ref.at[level, 0], sems.at[level])
+    out.start()
+    for copy in copies + [out]:
+        copy.wait()
 
 
 def paired_shards(row_count, right_sides, factor_blocks, diag_inverses, source_ids, block_counts):
@@ -144,14 +202,17 @@
     slots = factor_blocks.shape[3]
     rows = rhs_count // 2
     chips = row_count // 2
-    row, col = lax.axis_index("rows"), lax.axis_index("cols")
-    place = jnp.stack([row % 2, col]).astype(jnp.int32)
+    later = level_count - 1
     same_core = [[2 * j + k for j in range(chips)] for k in range(2)]
     part = jax.ShapeDtypeStruct((rows, width), jnp.float32)
     rounded_part = jax.ShapeDtypeStruct((rows, width), jnp.bfloat16)
     square = jax.ShapeDtypeStruct((width, width), jnp.bfloat16)
     copies = jax.ShapeDtypeStruct((chips, rows, width), jnp.bfloat16)
     solve_flops = 2 * rows * width * width
+    group_bytes = slots * width * width * 2
+
+    def buffer(x):
+        return pltpu.VMEM(x.shape, x.dtype)
 
     def over_both(x, move):
         pairs = []
@@ -173,80 +234,89 @@
 
     solved, rounded = run(
         first_kernel,
-        ((part, VMEM), (rounded_part, VMEM)),
-        ((place, SMEM), (right_sides, HBM), (diag_inverses, HBM)),
-        scratch=(
-            pltpu.VMEM(part.shape, part.dtype),
-            pltpu.VMEM(square.shape, square.dtype),
-            pltpu.SemaphoreType.DMA((2,)),
-        ),
+        ((part, HBM), (rounded_part, VMEM)),
+        ((right_sides, HBM), (diag_inverses, HBM)),
+        scratch=(buffer(part), buffer(square), buffer(part), pltpu.SemaphoreType.DMA((3,))),
         flops=solve_flops,
     )
     finished = [solved]
-    moved = transpose(rounded)
+    counts = block_counts.reshape(later)
+    other_ids, other_counts = swap_core(source_ids), swap_core(counts)
     copied, = run(
         copies_kernel,
         ((copies, HBM),),
-        ((moved, VMEM),),
+        ((transpose(rounded), VMEM), (other_ids, ANY), (other_counts, ANY)),
         scratch=(pltpu.SemaphoreType.DMA((chips,)),),
     )
     stores = [spread(copied)]
 
-    live_ids, = run(
-        live_kernel,
-        ((jax.ShapeDtypeStruct(source_ids.shape, source_ids.dtype), SMEM),),
-        ((source_ids, SMEM), (block_counts, SMEM)),
-    )
-    other_factors = swap_core(factor_blocks)
-    other_ids = swap_core(live_ids)
-    other_inverses = swap_core(diag_inverses)
-    other_rhs = swap_core(right_sides)
-
+    slot_args = tuple((x, SMEM) for x in (source_ids, other_ids, counts, other_counts))
+    factor_args = ((factor_blocks, HBM), (swap_core(factor_blocks), VMEM))
+    select_args = (
+        (right_sides, HBM),
+        (swap_core(right_sides), ANY),
+        (diag_inverses, HBM),
+        (swap_core(diag_inverses), ANY),
+    )
+    gathered = pltpu.VMEM((rows, slots * width), jnp.bfloat16)
+    own_factor = pltpu.VMEM((slots, width, width), jnp.bfloat16)
+    sums = pltpu.VMEM((2, rows, width), jnp.float32)
+    older = ()
     for l in range(1, level_count):
-        inner = l < level_count - 1
-        kept, sent, rhs, inverse = run(
-            functools.partial(sums_kernel, l, chips, inner),
-            ((part, VMEM), (part, VMEM), (part, VMEM), (square, VMEM)),
-            ((place, SMEM), (live_ids, SMEM), (other_ids, SMEM))
-            + tuple((store, VMEM) for store in stores)
-            + ((factor_blocks, HBM), (other_factors, VMEM))
-            + ((right_sides, HBM), (other_rhs, ANY), (diag_inverses, HBM), (other_inverses, ANY))
-            + tuple((x, ANY) for x in finished[1:]),
+        inner = l < later
+        kept, sent = run(
+            functools.partial(sums_kernel, l, chips),
+            ((part, VMEM), (part, VMEM)),
+            slot_args + factor_args + ((stores[-1], ANY),) + older + tuple((x, ANY) for x in finished[1:]),
             scratch=(
-                pltpu.VMEM((l * chips, rows, width), jnp.bfloat16),
-                pltpu.VMEM((rows, slots * width), jnp.bfloat16),
-                pltpu.VMEM((slots, width, width), jnp.bfloat16),
-                pltpu.VMEM((2, rows, width), jnp.float32),
-                pltpu.VMEM((2, width, width), jnp.bfloat16),
-                pltpu.SemaphoreType.DMA((5,)),
+                buffer(copies), gathered, own_factor, sums,
+                pltpu.SemaphoreType.DMA((2,)), pltpu.SemaphoreType.DMA((2,)),
             ),
             flops=2 * slots * solve_flops,
-            transferred=2 * slots * width * width * 2,
+            transferred=2 * group_bytes,
+        )
+        rhs, inverse = run(
+            functools.partial(select_kernel, l, inner),
+            ((part, VMEM), (square, VMEM)),
+            select_args + ((kept, ANY),),
+            scratch=(
+                sums, pltpu.VMEM((2, width, width), jnp.bfloat16), pltpu.SemaphoreType.DMA((4,)),
+            ),
+            transferred=4 * width * width * 2,
         )
         if inner:
             arrived = lax.ppermute(sent, "cols", [(0, 1), (1, 0)])
             solved, copied = run(
                 inner_kernel,
-                ((part, VMEM), (copies, HBM)),
-                ((kept, VMEM), (arrived, VMEM), (rhs, VMEM), (inverse, VMEM)),
-                scratch=(
-                    pltpu.VMEM((rows, width), jnp.bfloat16),
-                    pltpu.SemaphoreType.DMA((chips,)),
-                ),
+                ((part, HBM), (copies, HBM)),
+                tuple((x, VMEM) for x in (kept, arrived, rhs, inverse)),
+                scratch=(buffer(part), buffer(rounded_part), pltpu.SemaphoreType.DMA((chips + 1,))),
                 flops=solve_flops,
             )
+            older_sums, = run(
+                functools.partial(older_kernel, l + 1, chips),
+                ((jax.ShapeDtypeStruct((2, rows, width), jnp.float32), HBM),),
+                slot_args + factor_args + tuple((x, ANY) for x in stores) ,
+                scratch=(
+                    pltpu.VMEM((l * chips, rows, width), jnp.bfloat16), gathered, own_factor, sums,
+                    pltpu.SemaphoreType.DMA((2,)), pltpu.SemaphoreType.DMA((l,)),
+                ),
+                flops=2 * slots * solve_flops,
+                transferred=2 * group_bytes,
+            )
+            older = ((older_sums, HBM),)
             finished.append(transpose(solved))
             stores.append(spread(copied))
-        else:
-            first = over_both(kept, lambda j, k, c: (j, c, k))
-            second = over_both(sent, lambda j, k, c: (j, 1 - c, k))
-            out = jax.ShapeDtypeStruct((level_count, 1, rows, width), jnp.float32)
-            return run(
-                last_kernel,
-                ((out, VMEM),),
-                tuple((x, VMEM) for x in (first, second, rhs, inverse, *finished)),
-                flops=solve_flops,
-            )[0]
+    first = over_both(kept, lambda j, k, c: (j, c, k))
+    second = over_both(sent, lambda j, k, c: (j, 1 - c, k))
+    out, = run(
+        last_kernel,
+        ((jax.ShapeDtypeStruct((level_count, 1, rows, width), jnp.float32), ANY),),
+        tuple((x, VMEM) for x in (first, second, rhs, inverse)) + tuple((x, ANY) for x in finished),
+        scratch=(buffer(part), pltpu.SemaphoreType.DMA((level_count,))),
+        flops=solve_flops,
+    )
+    return out
 
 
 def gather_slots(ids_ref, counts_ref, group, store_ref, gathered, slots, width):

time: 76.6 us -> 75.2 us (0.982)
  starting transfers between devices: 35.7 us -> 26 us
  Pallas kernels: 14.8 us -> 21.8 us
  waiting for transfers between devices: 22.4 us -> 25.1 us
  local copies, waits for them, and re-layouts: 2.67 us -> 1.35 us
    ppermute x2, starting transfers between devices: 8.13 us -> 0.93 us  [paired_shards(): arrived = lax.ppermute(sent, 'cols', [(0, 1), (1, 0)])]
    pallas_call x9 -> x13, Pallas kernels: 14.8 us -> 21.8 us  [run(): pl.pallas_call(kernel, out_shape=tuple((pltpu.HBM(x.shape, x.dtype) if sp...]
    all_to_all x3, waiting for transfers between devices: 14.3 us -> 16.5 us  [spread(): return lax.all_to_all(x, 'rows', 0, 0, axis_index_groups=same_core)]
    unnamed x9 -> x10, local copies, waits for them, and re-layouts: 2.67 us -> 1.35 us
    ppermute x2, waiting for transfers between devices: 4.49 us -> 5.52 us  [paired_shards(): arrived = lax.ppermute(sent, 'cols', [(0, 1), (1, 0)])]
    all_to_all x3, starting transfers between devices: 14.9 us -> 13.9 us  [spread(): return lax.all_to_all(x, 'rows', 0, 0, axis_index_groups=same_core)]
    ppermute x5, waiting for transfers between devices: 2.81 us -> 1.81 us  [over_both(): return lax.ppermute(x, ('rows', 'cols'), pairs)]
    ppermute x4 -> x5, starting transfers between devices: 5.8 us -> 5.03 us  [swap_core(): return lax.ppermute(x, 'rows', [(i, i ^ 1) for i in range(row_count)])]
  transfers between devices with their start and end apart: 14 -> 15, of which waited for: 6 -> 8; matrix products, arithmetic and copies ran while one was open for 1% -> 0% of each run, Pallas kernels for 5% -> 19%
where the time goes in v8:
time: 75.2 us; the launch traced here: 74.4 us
  starting transfers between devices  26 us (35%)
  waiting for transfers between devices  25.1 us (33%)
  Pallas kernels  21.8 us (29%)
  local copies, waits for them, and re-layouts  1.35 us (2%)
    pallas_call x13, Pallas kernels, run(): pl.pallas_call(kernel, out_shape=tuple((pltpu.HBM(x.shape, x.dtype) if sp...  21.8 us
    all_to_all x3, waiting for transfers between devices, spread(): return lax.all_to_all(x, 'rows', 0, 0, axis_index_groups=same_core)  16.5 us
    all_to_all x3, starting transfers between devices, spread(): return lax.all_to_all(x, 'rows', 0, 0, axis_index_groups=same_core)  13.9 us
    ppermute x5, starting transfers between devices, over_both(): return lax.ppermute(x, ('rows', 'cols'), pairs)  6.1 us
    ppermute x2, waiting for transfers between devices, paired_shards(): arrived = lax.ppermute(sent, 'cols', [(0, 1), (1, 0)])  5.52 us
    ppermute x5, starting transfers between devices, swap_core(): return lax.ppermute(x, 'rows', [(i, i ^ 1) for i in range(row_count)])  5.03 us
    ppermute x5, waiting for transfers between devices, over_both(): return lax.ppermute(x, ('rows', 'cols'), pairs)  1.81 us
  transfers between devices with their start and end apart: 15, of which 8 were waited for; matrix products, arithmetic and copies ran while one was open for 0% of the time, Pallas kernels for 19%

profile of v8, /device:TPU:0, one launch (start us, length us, event | category | flops | bytes accessed | tf_op | source)
XLA Modules:
  0.0 74.4 jit_solution(15994834850379962863)
XLA Ops:
  0.0 0.5 collective-permute-start.2
  0.5 1.7 %shard_map.55 = (f32[64,256]{1,0:T(8,128)}, bf16[64,256]{1,0:T(8,128)(2,1)S(1)}) custom-call(f32[4,1,128,256]{3,2,1,0:T(8,128)} %rhs_ref.7, bf16[4,1,256,256]{3,2,1,0:T(8,128)(2,1)} %inverse_ref.7), custom_call_target="tpu_custom_call" | custom-call | flops 8388608 | tf_op jit(solution)/shard_map/pallas_call | solution.py:29
  2.2 0.7 collective-permute-start.3
  2.9 3.9 %collective-permute-start.1 = (s32[3]{0:T(128)}, s32[3]{0:T(128)S(1)}, u32[]{:S(2)}, u32[]{:S(2)}) collective-permute-start(s32[3]{0:T(128)} %bitcast.1), channel_id=1, source_target_pairs={{0,2},{2,0},{4,6},{6,4},{8,10},{10,8},{12,14},{14,12},{16,18},{18,... | collective-permute-start | bytes 44 | tf_op jit(solution)/shard_map/ppermute | solution.py:227
  6.8 0.1 collective-permute-start
  6.9 0.9 %collective-permute-done.1.refs_1_.refs_3_ = s32[3]{0:T(128)S(1)} collective-permute-done((s32[3]{0:T(128)}, s32[3]{0:T(128)S(1)}, u32[]{:S(2)}, u32[]{:S(2)}) %collective-permute-start.1) | collective-permute-done | bytes 44 | tf_op jit(solution)/shard_map/ppermute | solution.py:227
  7.8 0.4 collective-permute-done.refs_0_.refs_1_
  8.2 0.0 collective-permute-done.3.rounded_ref
  8.2 0.8 %shard_map.56 = bf16[8,64,256]{2,1,0:T(8,128)(2,1)} custom-call(bf16[64,256]{1,0:T(8,128)(2,1)S(1)} %collective-permute-done.3.rounded_ref, s32[3,1,1,8]{3,2,1,0:T(1,128)S(1)} %collective-permute-done.refs_0_.refs_1_, s32[3]{0:T(128)S(1)} %collective-permute-done.1.refs_1_.refs_3_), custom_call_target="tpu_custom_call" | custom-call | tf_op jit(solution)/shard_map/pallas_call | solution.py:29
  8.9 0.0 copy-start.2
  9.0 0.0 copy-start.4
  9.0 5.8 %all-to-all-start = ((bf16[8,64,256]{2,1,0:T(8,128)(2,1)}), bf16[8,64,256]{2,1,0:T(8,128)(2,1)S(1)}, u32[]{:S(2)}, u32[]{:S(2)}) async-start(bf16[8,64,256]{2,1,0:T(8,128)(2,1)} %shard_map.56), calls=%async_computation | async-start | bytes 524288 | tf_op jit(solution)/shard_map/all_to_all | solution.py:233
  14.8 0.5 collective-permute-start.5
  15.3 0.1 collective-permute-start.6
  15.3 9.3 %all-to-all-done.refs_6_ = bf16[8,64,256]{2,1,0:T(8,128)(2,1)S(1)} async-done(((bf16[8,64,256]{2,1,0:T(8,128)(2,1)}), bf16[8,64,256]{2,1,0:T(8,128)(2,1)S(1)}, u32[]{:S(2)}, u32[]{:S(2)}) %all-to-all-start) | async-done | bytes 262176 | tf_op jit(solution)/shard_map/all_to_all | solution.py:233
  24.6 0.0 collective-permute-done.2.refs_5_
  24.6 0.7 copy-done.1
  25.3 0.7 copy-done.3
  26.0 2.3 %shard_map.57 = (f32[64,256]{1,0:T(8,128)S(1)}, f32[64,256]{1,0:T(8,128)S(1)}) custom-call(s32[3,1,1,8]{3,2,1,0:T(1,128)S(1)} %copy-done.1, s32[3,1,1,8]{3,2,1,0:T(1,128)S(1)} %collective-permute-done.refs_0_.refs_1_, s32[3]{0:T(128)S(1)} %bitcast.2, s32[3]{0:T(128)S(1)} %collective-permute-done.1.refs_1_.refs_3_, bf16[3,1,1,8,256,256]{5,4,3,2,1,0:T(8,128)(2,1)} %refs_4_.9, ...), custom_call_target="tpu_custom_call" | custom-call | flops 134217728 | bytes 2097152 | tf_op jit(solution)/shard_map/pallas_call | solution.py:29
  28.3 0.5 collective-permute-start.4
  28.7 0.0 collective-permute-done.5.other_rhs_ref
  28.7 0.0 collective-permute-done.6.other_inverse_ref
  28.7 1.1 %shard_map.58 = (f32[64,256]{1,0:T(8,128)S(1)}, bf16[256,256]{1,0:T(8,128)(2,1)S(1)}) custom-call(f32[4,1,128,256]{3,2,1,0:T(8,128)} %rhs_ref.7, f32[4,1,128,256]{3,2,1,0:T(8,128)} %collective-permute-done.5.other_rhs_ref, bf16[4,1,256,256]{3,2,1,0:T(8,128)(2,1)} %inverse_ref.7, bf16[4,1,256,256]{3,2,1,0:T(8,128)(2,1)} %collective-permute-done.6.other_inverse_ref, ...), custom_call_target="tpu_custom_call" | custom-call | bytes 524288 | tf_op jit(solution)/shard_map/pallas_call | solution.py:29
  29.8 2.8 %collective-permute-done.4.arrived_ref = f32[64,256]{1,0:T(8,128)S(1)} collective-permute-done((f32[64,256]{1,0:T(8,128)S(1)}, f32[64,256]{1,0:T(8,128)S(1)}, u32[]{:S(2)}, u32[]{:S(2)}) %collective-permute-start.4) | collective-permute-done | bytes 65568 | tf_op jit(solution)/shard_map/ppermute | solution.py:288
  32.6 0.9 %shard_map.59 = (f32[64,256]{1,0:T(8,128)}, bf16[8,64,256]{2,1,0:T(8,128)(2,1)}) custom-call(f32[64,256]{1,0:T(8,128)S(1)} %get-tuple-element.24.refs_0_.kept_ref, f32[64,256]{1,0:T(8,128)S(1)} %collective-permute-done.4.arrived_ref, f32[64,256]{1,0:T(8,128)S(1)} %get-tuple-element.26.rhs_ref, bf16[256,256]{1,0:T(8,128)(2,1)S(1)} %get-tuple-element.27.inverse_ref), custom_call_target="tpu_custom_call" | custom-call | flops 8388608 | tf_op jit(solution)/shard_map/pallas_call | solution.py:29
  33.5 4.1 %all-to-all-start.1 = ((bf16[8,64,256]{2,1,0:T(8,128)(2,1)}), bf16[8,64,256]{2,1,0:T(8,128)(2,1)}, u32[]{:S(2)}, u32[]{:S(2)}) async-start(bf16[8,64,256]{2,1,0:T(8,128)(2,1)} %get-tuple-element.28), calls=%async_computation.1 | async-start | bytes 524288 | tf_op jit(solution)/shard_map/all_to_all | solution.py:233
  37.6 1.5 %collective-permute-start.7 = (f32[64,256]{1,0:T(8,128)}, f32[64,256]{1,0:T(8,128)S(1)}, u32[]{:S(2)}, u32[]{:S(2)}) collective-permute-start(f32[64,256]{1,0:T(8,128)} %get-tuple-element.29), channel_id=1, source_target_pairs={{0,0},{1,2},{2,1},{3,3},{4,4},{5,6},{6,5},{7,7},{8,8},{9,10},{10,9... | collective-permute-start | bytes 196616 | tf_op jit(solution)/shard_map/ppermute | solution.py:224
  39.1 0.0 copy-done.2
  39.1 2.9 %shard_map.60.refs_7_ = f32[2,64,256]{2,1,0:T(8,128)} custom-call(s32[3,1,1,8]{3,2,1,0:T(1,128)S(1)} %copy-done.2, s32[3,1,1,8]{3,2,1,0:T(1,128)S(1)} %collective-permute-done.refs_0_.refs_1_, s32[3]{0:T(128)S(1)} %bitcast.3, s32[3]{0:T(128)S(1)} %collective-permute-done.1.refs_1_.refs_3_, bf16[3,1,1,8,256,256]{5,4,3,2,1,0:T(8,128)(2,1)} %refs_4_.9, ...), custom_call_target="tpu_custom_call" | custom-call | flops 134217728 | bytes 2097152 | tf_op jit(solution)/shard_map/pallas_call | solution.py:29
  42.0 0.0 collective-permute-done.7.refs_8_.refs_1_
  42.0 3.8 %all-to-all-done.1.refs_6_.refs_7_ = bf16[8,64,256]{2,1,0:T(8,128)(2,1)} async-done(((bf16[8,64,256]{2,1,0:T(8,128)(2,1)}), bf16[8,64,256]{2,1,0:T(8,128)(2,1)}, u32[]{:S(2)}, u32[]{:S(2)}) %all-to-all-start.1) | async-done | bytes 262176 | tf_op jit(solution)/shard_map/all_to_all | solution.py:233
  45.8 2.5 %shard_map.61 = (f32[64,256]{1,0:T(8,128)S(1)}, f32[64,256]{1,0:T(8,128)S(1)}) custom-call(s32[3,1,1,8]{3,2,1,0:T(1,128)S(1)} %copy-done.2, s32[3,1,1,8]{3,2,1,0:T(1,128)S(1)} %collective-permute-done.refs_0_.refs_1_, s32[3]{0:T(128)S(1)} %bitcast.4, s32[3]{0:T(128)S(1)} %collective-permute-done.1.refs_1_.refs_3_, bf16[3,1,1,8,256,256]{5,4,3,2,1,0:T(8,128)(2,1)} %refs_4_.9, ...), custom_call_target="tpu_custom_call" | custom-call | flops 134217728 | bytes 2097152 | tf_op jit(solution)/shard_map/pallas_call | solution.py:29
  48.3 0.5 collective-permute-start.8
  48.8 1.1 %shard_map.62 = (f32[64,256]{1,0:T(8,128)S(1)}, bf16[256,256]{1,0:T(8,128)(2,1)S(1)}) custom-call(f32[4,1,128,256]{3,2,1,0:T(8,128)} %rhs_ref.7, f32[4,1,128,256]{3,2,1,0:T(8,128)} %collective-permute-done.5.other_rhs_ref, bf16[4,1,256,256]{3,2,1,0:T(8,128)(2,1)} %inverse_ref.7, bf16[4,1,256,256]{3,2,1,0:T(8,128)(2,1)} %collective-permute-done.6.other_inverse_ref, ...), custom_call_target="tpu_custom_call" | custom-call | bytes 524288 | tf_op jit(solution)/shard_map/pallas_call | solution.py:29
  49.9 2.8 %collective-permute-done.8.arrived_ref = f32[64,256]{1,0:T(8,128)S(1)} collective-permute-done((f32[64,256]{1,0:T(8,128)S(1)}, f32[64,256]{1,0:T(8,128)S(1)}, u32[]{:S(2)}, u32[]{:S(2)}) %collective-permute-start.8) | collective-permute-done | bytes 65568 | tf_op jit(solution)/shard_map/ppermute | solution.py:288
  52.6 0.9 %shard_map.63 = (f32[64,256]{1,0:T(8,128)}, bf16[8,64,256]{2,1,0:T(8,128)(2,1)}) custom-call(f32[64,256]{1,0:T(8,128)S(1)} %get-tuple-element.30.refs_0_.kept_ref, f32[64,256]{1,0:T(8,128)S(1)} %collective-permute-done.8.arrived_ref, f32[64,256]{1,0:T(8,128)S(1)} %get-tuple-element.32.rhs_ref, bf16[256,256]{1,0:T(8,128)(2,1)S(1)} %get-tuple-element.33.inverse_ref), custom_call_target="tpu_custom_call" | custom-call | flops 8388608 | tf_op jit(solution)/shard_map/pallas_call | solution.py:29
  53.6 4.1 %all-to-all-start.2 = ((bf16[8,64,256]{2,1,0:T(8,128)(2,1)}), bf16[8,64,256]{2,1,0:T(8,128)(2,1)}, u32[]{:S(2)}, u32[]{:S(2)}) async-start(bf16[8,64,256]{2,1,0:T(8,128)(2,1)} %get-tuple-element.34), calls=%async_computation.2 | async-start | bytes 524288 | tf_op jit(solution)/shard_map/all_to_all | solution.py:233
  57.7 1.5 %collective-permute-start.9 = (f32[64,256]{1,0:T(8,128)}, f32[64,256]{1,0:T(8,128)S(1)}, u32[]{:S(2)}, u32[]{:S(2)}) collective-permute-start(f32[64,256]{1,0:T(8,128)} %get-tuple-element.35), channel_id=1, source_target_pairs={{0,0},{1,2},{2,1},{3,3},{4,4},{5,6},{6,5},{7,7},{8,8},{9,10},{10,9... | collective-permute-start | bytes 196616 | tf_op jit(solution)/shard_map/ppermute | solution.py:224
  59.1 3.4 %shard_map.64.refs_7_ = f32[2,64,256]{2,1,0:T(8,128)} custom-call(s32[3,1,1,8]{3,2,1,0:T(1,128)S(1)} %copy-done.2, s32[3,1,1,8]{3,2,1,0:T(1,128)S(1)} %collective-permute-done.refs_0_.refs_1_, s32[3]{0:T(128)S(1)} %bitcast.5, s32[3]{0:T(128)S(1)} %collective-permute-done.1.refs_1_.refs_3_, bf16[3,1,1,8,256,256]{5,4,3,2,1,0:T(8,128)(2,1)} %refs_4_.9, ...), custom_call_target="tpu_custom_call" | custom-call | flops 134217728 | bytes 2097152 | tf_op jit(solution)/shard_map/pallas_call | solution.py:29
  62.5 0.0 collective-permute-done.9.refs_9_.refs_2_
  62.5 3.4 %all-to-all-done.2.refs_6_ = bf16[8,64,256]{2,1,0:T(8,128)(2,1)} async-done(((bf16[8,64,256]{2,1,0:T(8,128)(2,1)}), bf16[8,64,256]{2,1,0:T(8,128)(2,1)}, u32[]{:S(2)}, u32[]{:S(2)}) %all-to-all-start.2) | async-done | bytes 262176 | tf_op jit(solution)/shard_map/all_to_all | solution.py:233
  65.9 2.5 %shard_map.65 = (f32[64,256]{1,0:T(8,128)S(1)}, f32[64,256]{1,0:T(8,128)S(1)}) custom-call(s32[3,1,1,8]{3,2,1,0:T(1,128)S(1)} %copy-done.2, s32[3,1,1,8]{3,2,1,0:T(1,128)S(1)} %collective-permute-done.refs_0_.refs_1_, s32[3]{0:T(128)S(1)} %bitcast.6, s32[3]{0:T(128)S(1)} %collective-permute-done.1.refs_1_.refs_3_, bf16[3,1,1,8,256,256]{5,4,3,2,1,0:T(8,128)(2,1)} %refs_4_.9, ...), custom_call_target="tpu_custom_call" | custom-call | flops 134217728 | bytes 2097152 | tf_op jit(solution)/shard_map/pallas_call | solution.py:29
  68.4 0.7 collective-permute-start.10
  69.0 1.8 %collective-permute-start.11 = (f32[64,256]{1,0:T(8,128)S(1)}, f32[64,256]{1,0:T(8,128)S(1)}, u32[]{:S(2)}, u32[]{:S(2)}) collective-permute-start(f32[64,256]{1,0:T(8,128)S(1)} %get-tuple-element.37), channel_id=1, source_target_pairs={{0,2},{1,0},{2,3},{3,1},{4,6},{5,4},{6,7},{7,5},{8,10},{9,8},{10,1... | collective-permute-start | bytes 196616 | tf_op jit(solution)/shard_map/ppermute | solution.py:224
  70.8 1.0 %shard_map.66 = (f32[64,256]{1,0:T(8,128)S(1)}, bf16[256,256]{1,0:T(8,128)(2,1)S(1)}) custom-call(f32[4,1,128,256]{3,2,1,0:T(8,128)} %rhs_ref.7, f32[4,1,128,256]{3,2,1,0:T(8,128)} %collective-permute-done.5.other_rhs_ref, bf16[4,1,256,256]{3,2,1,0:T(8,128)(2,1)} %inverse_ref.7, bf16[4,1,256,256]{3,2,1,0:T(8,128)(2,1)} %collective-permute-done.6.other_inverse_ref, ...), custom_call_target="tpu_custom_call" | custom-call | bytes 524288 | tf_op jit(solution)/shard_map/pallas_call | solution.py:29
  71.8 0.0 collective-permute-done.10.first_ref
  71.8 1.8 %collective-permute-done.11.second_ref = f32[64,256]{1,0:T(8,128)S(1)} collective-permute-done((f32[64,256]{1,0:T(8,128)S(1)}, f32[64,256]{1,0:T(8,128)S(1)}, u32[]{:S(2)}, u32[]{:S(2)}) %collective-permute-start.11) | collective-permute-done | bytes 65568 | tf_op jit(solution)/shard_map/ppermute | solution.py:224
  73.6 0.8 %shard_map.67 = f32[4,1,64,256]{3,2,1,0:T(8,128)} custom-call(f32[64,256]{1,0:T(8,128)S(1)} %collective-permute-done.10.first_ref, f32[64,256]{1,0:T(8,128)S(1)} %collective-permute-done.11.second_ref, f32[64,256]{1,0:T(8,128)S(1)} %get-tuple-element.38.rhs_ref, bf16[256,256]{1,0:T(8,128)(2,1)S(1)} %get-tuple-element.39.inverse_ref, f32[64,256]{1,0:T(8,128)S(1)} %copy-done, ...), custom_call_target="tpu_custom_call" | custom-call | flops 8388608 | tf_op jit(solution)/shard_map/pallas_call | solution.py:29
  (5 shorter events, 0.0 us)
Async XLA Ops:
  0.0 24.6 %collective-permute-start.2 = (bf16[3,1,1,8,256,256]{5,4,3,2,1,0:T(8,128)(2,1)}, bf16[3,1,1,8,256,256]{5,4,3,2,1,0:T(8,128)(2,1)S(1)}, u32[]{:S(2)}, u32[]{:S(2)}) collective-permute-start(bf16[3,1,1,8,256,256]{5,4,3,2,1,0:T(8,128)(2,1)} %refs_4_.9), channel_id=1, source_target_pairs={{0,2},{2,0},{4,6},{6,4},{8,10},{10,8},{12,14},{14,12},{16,18},{18,... | collective-permute-start | bytes 9437192 | tf_op jit(solution)/shard_map/ppermute | solution.py:227
  2.2 6.0 %collective-permute-start.3 = (bf16[64,256]{1,0:T(8,128)(2,1)S(1)}, bf16[64,256]{1,0:T(8,128)(2,1)S(1)}, u32[]{:S(2)}, u32[]{:S(2)}) collective-permute-start(bf16[64,256]{1,0:T(8,128)(2,1)S(1)} %get-tuple-element.23), channel_id=1, source_target_pairs={{0,0},{1,2},{2,1},{3,3},{4,4},{5,6},{6,5},{7,7},{8,8},{9,10},{10,9... | collective-permute-start | bytes 98312 | tf_op jit(solution)/shard_map/ppermute | solution.py:224
  2.9 4.9 %collective-permute-start.1 = (s32[3]{0:T(128)}, s32[3]{0:T(128)S(1)}, u32[]{:S(2)}, u32[]{:S(2)}) collective-permute-start(s32[3]{0:T(128)} %bitcast.1), channel_id=1, source_target_pairs={{0,2},{2,0},{4,6},{6,4},{8,10},{10,8},{12,14},{14,12},{16,18},{18,... | collective-permute-start | bytes 44 | tf_op jit(solution)/shard_map/ppermute | solution.py:227
  6.8 1.4 %collective-permute-start = (s32[3,1,1,8]{3,2,1,0:T(1,128)}, s32[3,1,1,8]{3,2,1,0:T(1,128)S(1)}, u32[]{:S(2)}, u32[]{:S(2)}) collective-permute-start(s32[3,1,1,8]{3,2,1,0:T(1,128)} %refs_0_.9), channel_id=1, source_target_pairs={{0,2},{2,0},{4,6},{6,4},{8,10},{10,8},{12,14},{14,12},{16,18},{18,... | collective-permute-start | bytes 296 | tf_op jit(solution)/shard_map/ppermute | solution.py:227
  8.9 30.1 %copy-start.2 = (s32[3,1,1,8]{3,2,1,0:T(1,128)S(1)}, s32[3,1,1,8]{3,2,1,0:T(1,128)}, u32[]{:S(2)}) copy-start(s32[3,1,1,8]{3,2,1,0:T(1,128)} %refs_0_.9) | copy-start | bytes 292
  9.0 30.1 %copy-start.4 = (s32[3,1,1]{0,2,1:T(1,128)S(1)}, s32[3,1,1]{0,2,1:T(1,128)}, u32[]{:S(2)}) copy-start(s32[3,1,1]{0,2,1:T(1,128)} %param.9) | copy-start | bytes 40
  9.0 15.7 %all-to-all-start = ((bf16[8,64,256]{2,1,0:T(8,128)(2,1)}), bf16[8,64,256]{2,1,0:T(8,128)(2,1)S(1)}, u32[]{:S(2)}, u32[]{:S(2)}) async-start(bf16[8,64,256]{2,1,0:T(8,128)(2,1)} %shard_map.56), calls=%async_computation | async-start | bytes 524288 | tf_op jit(solution)/shard_map/all_to_all | solution.py:233
  14.8 13.9 %collective-permute-start.5 = (f32[4,1,128,256]{3,2,1,0:T(8,128)}, f32[4,1,128,256]{3,2,1,0:T(8,128)}, u32[]{:S(2)}, u32[]{:S(2)}) collective-permute-start(f32[4,1,128,256]{3,2,1,0:T(8,128)} %rhs_ref.7), channel_id=1, source_target_pairs={{0,2},{2,0},{4,6},{6,4},{8,10},{10,8},{12,14},{14,12},{16,18},{18,... | collective-permute-start | bytes 1572872 | tf_op jit(solution)/shard_map/ppermute | solution.py:227
  15.3 13.5 %collective-permute-start.6 = (bf16[4,1,256,256]{3,2,1,0:T(8,128)(2,1)}, bf16[4,1,256,256]{3,2,1,0:T(8,128)(2,1)}, u32[]{:S(2)}, u32[]{:S(2)}) collective-permute-start(bf16[4,1,256,256]{3,2,1,0:T(8,128)(2,1)} %inverse_ref.7), channel_id=1, source_target_pairs={{0,2},{2,0},{4,6},{6,4},{8,10},{10,8},{12,14},{14,12},{16,18},{18,... | collective-permute-start | bytes 1572872 | tf_op jit(solution)/shard_map/ppermute | solution.py:227
  24.6 0.7 copy-start.1
  25.3 0.7 copy-start.3
  28.3 4.3 %collective-permute-start.4 = (f32[64,256]{1,0:T(8,128)S(1)}, f32[64,256]{1,0:T(8,128)S(1)}, u32[]{:S(2)}, u32[]{:S(2)}) collective-permute-start(f32[64,256]{1,0:T(8,128)S(1)} %get-tuple-element.25), channel_id=1, source_target_pairs={{0,1},{1,0},{2,3},{3,2},{4,5},{5,4},{6,7},{7,6},{8,9},{9,8},{10,11... | collective-permute-start | bytes 196616 | tf_op jit(solution)/shard_map/ppermute | solution.py:288
  33.5 12.3 %all-to-all-start.1 = ((bf16[8,64,256]{2,1,0:T(8,128)(2,1)}), bf16[8,64,256]{2,1,0:T(8,128)(2,1)}, u32[]{:S(2)}, u32[]{:S(2)}) async-start(bf16[8,64,256]{2,1,0:T(8,128)(2,1)} %get-tuple-element.28), calls=%async_computation.1 | async-start | bytes 524288 | tf_op jit(solution)/shard_map/all_to_all | solution.py:233
  37.6 4.4 %collective-permute-start.7 = (f32[64,256]{1,0:T(8,128)}, f32[64,256]{1,0:T(8,128)S(1)}, u32[]{:S(2)}, u32[]{:S(2)}) collective-permute-start(f32[64,256]{1,0:T(8,128)} %get-tuple-element.29), channel_id=1, source_target_pairs={{0,0},{1,2},{2,1},{3,3},{4,4},{5,6},{6,5},{7,7},{8,8},{9,10},{10,9... | collective-permute-start | bytes 196616 | tf_op jit(solution)/shard_map/ppermute | solution.py:224
  48.3 4.3 %collective-permute-start.8 = (f32[64,256]{1,0:T(8,128)S(1)}, f32[64,256]{1,0:T(8,128)S(1)}, u32[]{:S(2)}, u32[]{:S(2)}) collective-permute-start(f32[64,256]{1,0:T(8,128)S(1)} %get-tuple-element.31), channel_id=1, source_target_pairs={{0,1},{1,0},{2,3},{3,2},{4,5},{5,4},{6,7},{7,6},{8,9},{9,8},{10,11... | collective-permute-start | bytes 196616 | tf_op jit(solution)/shard_map/ppermute | solution.py:288
  53.6 12.3 %all-to-all-start.2 = ((bf16[8,64,256]{2,1,0:T(8,128)(2,1)}), bf16[8,64,256]{2,1,0:T(8,128)(2,1)}, u32[]{:S(2)}, u32[]{:S(2)}) async-start(bf16[8,64,256]{2,1,0:T(8,128)(2,1)} %get-tuple-element.34), calls=%async_computation.2 | async-start | bytes 524288 | tf_op jit(solution)/shard_map/all_to_all | solution.py:233
  57.7 4.9 %collective-permute-start.9 = (f32[64,256]{1,0:T(8,128)}, f32[64,256]{1,0:T(8,128)S(1)}, u32[]{:S(2)}, u32[]{:S(2)}) collective-permute-start(f32[64,256]{1,0:T(8,128)} %get-tuple-element.35), channel_id=1, source_target_pairs={{0,0},{1,2},{2,1},{3,3},{4,4},{5,6},{6,5},{7,7},{8,8},{9,10},{10,9... | collective-permute-start | bytes 196616 | tf_op jit(solution)/shard_map/ppermute | solution.py:224
  62.5 11.1 %copy-start = (f32[64,256]{1,0:T(8,128)S(1)}, f32[64,256]{1,0:T(8,128)}, u32[]{:S(2)}) copy-start(f32[64,256]{1,0:T(8,128)} %get-tuple-element.40.refs_0_) | copy-start | bytes 196612
  68.4 3.4 %collective-permute-start.10 = (f32[64,256]{1,0:T(8,128)S(1)}, f32[64,256]{1,0:T(8,128)S(1)}, u32[]{:S(2)}, u32[]{:S(2)}) collective-permute-start(f32[64,256]{1,0:T(8,128)S(1)} %get-tuple-element.36.refs_0_), channel_id=1, source_target_pairs={{0,0},{1,2},{2,1},{3,3},{4,4},{5,6},{6,5},{7,7},{8,8},{9,10},{10,9... | collective-permute-start | bytes 196616 | tf_op jit(solution)/shard_map/ppermute | solution.py:224
  69.0 4.6 %collective-permute-start.11 = (f32[64,256]{1,0:T(8,128)S(1)}, f32[64,256]{1,0:T(8,128)S(1)}, u32[]{:S(2)}, u32[]{:S(2)}) collective-permute-start(f32[64,256]{1,0:T(8,128)S(1)} %get-tuple-element.37), channel_id=1, source_target_pairs={{0,2},{1,0},{2,3},{3,1},{4,6},{5,4},{6,7},{7,5},{8,10},{9,8},{10,1... | collective-permute-start | bytes 196616 | tf_op jit(solution)/shard_map/ppermute | solution.py:224

commit v9 on v1

--- a/solution.py
+++ b/solution.py
@@ -7,6 +7,258 @@
 from jax.experimental.pallas import tpu as pltpu
 from jax.sharding import PartitionSpec as P
 
+VMEM_LIMIT = 16 * 1024 * 1024
+
+
+VMEM = pl.BlockSpec(memory_space=pltpu.VMEM)
+SMEM = pl.BlockSpec(memory_space=pltpu.SMEM)
+ANY = pl.BlockSpec(memory_space=pl.ANY)
+HBM = pl.BlockSpec(memory_space=pltpu.HBM)
+
+
+def flat_dot(gathered, factor_ref):
+    slots, width = factor_ref.shape[0], factor_ref.shape[1]
+    return jnp.dot(
+        gathered[...],
+        factor_ref[...].reshape(slots * width, width),
+        preferred_element_type=jnp.float32,
+    )
+
+
+def run(kernel, outs, args, scratch=(), flops=0, transferred=0):
+    return pl.pallas_call(
+        kernel,
+        out_shape=tuple(pltpu.HBM(x.shape, x.dtype) if spec is HBM else x for x, spec in outs),
+        in_specs=[spec for _, spec in args],
+        out_specs=tuple(spec for _, spec in outs),
+        scratch_shapes=list(scratch),
+        compiler_params=pltpu.CompilerParams(vmem_limit_bytes=VMEM_LIMIT),
+        cost_estimate=pl.CostEstimate(flops=flops, bytes_accessed=transferred, transcendentals=0),
+    )(*(pltpu.with_memory_space_constraint(x, pltpu.HBM) if spec is HBM else x for x, spec in args))
+
+
+def half_of(ref, level, half, rows):
+    return ref.at[level, 0, pl.ds(pl.multiple_of(half * rows, rows), rows), :]
+
+
+def rows_of(half, rows):
+    return pl.ds(pl.multiple_of(half * rows, rows), rows)
+
+
+def solve(reduced, inverse):
+    return jnp.dot(reduced.astype(jnp.bfloat16), inverse, preferred_element_type=jnp.float32)
+
+
+def start_copies(pairs, sems):
+    copies = [pltpu.make_async_copy(src, dst, sems.at[i]) for i, (src, dst) in enumerate(pairs)]
+    for copy in copies:
+        copy.start()
+    return copies
+
+
+def gather_pieces(level, targets, half, ids_ref, counts_ref, store_refs, gathered):
+    rows, width = gathered.shape[0], store_refs[0].shape[2]
+    for k in range(ids_ref.shape[3]):
+        source = ids_ref[level - 1, 0, 0, k]
+        place = lax.rem(source, targets)
+        piece = store_refs[0][place] if half is None else store_refs[0][place, rows_of(half, rows), :]
+        for m, store in enumerate(store_refs[1:], 1):
+            piece = jnp.where(source >= m * targets, store[place], piece)
+        live = jnp.where(k < counts_ref[level - 1, 0, 0], 1.0, 0.0).astype(piece.dtype)
+        gathered[:, k * width:(k + 1) * width] = piece * live
+
+
+def first_kernel(
+    rhs_ref, inverse_ref, factor_ref, out_ref, rounded_ref, first_factor_ref, second_factor_ref,
+    rhs, inverse, solved, sems,
+):
+    col = lax.axis_index("cols")
+    copies = start_copies(
+        [
+            (rhs_ref.at[0, 0], rhs),
+            (inverse_ref.at[0, 0], inverse),
+            (factor_ref.at[1, 0, 0], second_factor_ref),
+            (factor_ref.at[0, 0, 0], first_factor_ref),
+        ],
+        sems,
+    )
+    copies[0].wait()
+    copies[1].wait()
+    solved[...] = solve(rhs[...], inverse[...])
+    out = pltpu.make_async_copy(solved.at[rows_of(col, out_ref.shape[0]), :], out_ref, sems.at[0])
+    out.start()
+    rounded_ref[...] = solved[...].astype(jnp.bfloat16)
+    for copy in copies[2:] + [out]:
+        copy.wait()
+
+
+def shared_kernel(targets, ids_ref, counts_ref, store_ref, factor_ref, *refs):
+    kept_ref, sent_ref, gathered, total = refs[-4:]
+    rows = kept_ref.shape[0]
+    col = lax.axis_index("cols")
+    gather_pieces(1, targets, None, ids_ref, counts_ref, (store_ref,), gathered)
+    total[...] = flat_dot(gathered, factor_ref)
+    kept_ref[...] = total[rows_of(col, rows), :]
+    sent_ref[...] = total[rows_of(1 - col, rows), :]
+
+
+def fetch_kernel(rhs_ref, inverse_ref, factor_ref, after_ref, own_rhs_ref, own_inverse_ref, own_factor_ref, sems):
+    del after_ref
+    rows = own_rhs_ref.shape[1]
+    col = lax.axis_index("cols")
+    pairs = [(factor_ref.at[factor_ref.shape[0] - 1, 0, 0], own_factor_ref)]
+    for l in range(own_rhs_ref.shape[0]):
+        pairs += [
+            (half_of(rhs_ref, l + 1, col, rows), own_rhs_ref.at[l]),
+            (inverse_ref.at[l + 1, 0], own_inverse_ref.at[l]),
+        ]
+    for copy in start_copies(pairs, sems):
+        copy.wait()
+
+
+def shared_solve_kernel(kept_ref, arrived_ref, rhs_ref, inverse_ref, out_ref, rounded_ref):
+    solved = solve(rhs_ref[0] - (kept_ref[...] + arrived_ref[...]), inverse_ref[0])
+    out_ref[...] = solved
+    rounded_ref[...] = solved.astype(jnp.bfloat16)
+
+
+def level_sum(level, targets, refs, gathered):
+    ids_ref, other_ids_ref, counts_ref, other_counts_ref = refs[:4]
+    factor_ref, other_factor_ref = refs[4:6]
+    store_refs = refs[6:6 + level]
+    col = lax.axis_index("cols")
+    gather_pieces(level, targets, col, ids_ref, counts_ref, store_refs, gathered)
+    own = flat_dot(gathered, factor_ref)
+    gather_pieces(level, targets, col, other_ids_ref, other_counts_ref, store_refs, gathered)
+    return own + flat_dot(gathered, other_factor_ref)
+
+
+def whole_kernel(level, targets, *refs):
+    rhs_ref, inverse_ref, out_ref, rounded_ref, gathered = refs[6 + level:]
+    update = level_sum(level, targets, refs, gathered)
+    solved = solve(rhs_ref[level - 1] - update, inverse_ref[level - 1])
+    out_ref[...] = solved
+    rounded_ref[...] = solved.astype(jnp.bfloat16)
+
+
+def last_kernel(level, targets, *refs):
+    rhs_ref, inverse_ref = refs[6 + level:8 + level]
+    done_refs = refs[8 + level:8 + 2 * level]
+    out_ref, gathered, solved, sems = refs[8 + 2 * level:]
+    copies = start_copies([(done, out_ref.at[m, 0]) for m, done in enumerate(done_refs)], sems)
+    update = level_sum(level, targets, refs, gathered)
+    solved[...] = solve(rhs_ref[level - 1] - update, inverse_ref[level - 1])
+    out = pltpu.make_async_copy(solved, out_ref.at[level, 0], sems.at[level])
+    out.start()
+    for copy in copies + [out]:
+        copy.wait()
+
+
+def paired_shards(targets, right_sides, factor_blocks, diag_inverses, source_ids, block_counts):
+    level_count, _, rhs_count, width = right_sides.shape
+    slots = factor_blocks.shape[3]
+    rows = rhs_count // 2
+    later = level_count - 1
+    part = jax.ShapeDtypeStruct((rows, width), jnp.float32)
+    rounded_part = jax.ShapeDtypeStruct((rows, width), jnp.bfloat16)
+    blocks = jax.ShapeDtypeStruct((slots, width, width), jnp.bfloat16)
+    whole = (rhs_count, width)
+    flops = 2 * rows * width * width
+    block_bytes = slots * width * width * 2
+
+    def swap(x):
+        return lax.ppermute(x, "cols", [(0, 1), (1, 0)])
+
+    solved, rounded, first_blocks, second_blocks = run(
+        first_kernel,
+        ((part, HBM), (jax.ShapeDtypeStruct(whole, jnp.bfloat16), VMEM), (blocks, VMEM), (blocks, VMEM)),
+        ((right_sides, HBM), (diag_inverses, HBM), (factor_blocks, HBM)),
+        scratch=(
+            pltpu.VMEM(whole, jnp.float32),
+            pltpu.VMEM((width, width), jnp.bfloat16),
+            pltpu.VMEM(whole, jnp.float32),
+            pltpu.SemaphoreType.DMA((4,)),
+        ),
+        flops=2 * flops,
+        transferred=2 * block_bytes,
+    )
+    finished = [solved]
+    slot_args = tuple((x, SMEM) for x in (source_ids, swap(source_ids), block_counts, swap(block_counts)))
+    other_blocks = [swap(second_blocks)]
+    own_blocks = [second_blocks]
+    stores = [lax.all_gather(rounded, "rows", axis=0)]
+
+    kept, sent = run(
+        functools.partial(shared_kernel, targets),
+        ((part, VMEM), (part, VMEM)),
+        (slot_args[0], slot_args[2], (stores[0], VMEM), (first_blocks, VMEM))
+        + ((slot_args[1][0], ANY), (slot_args[3][0], ANY)),
+        scratch=(pltpu.VMEM((rhs_count, slots * width), jnp.bfloat16), pltpu.VMEM(whole, jnp.float32)),
+        flops=2 * slots * flops,
+        transferred=block_bytes,
+    )
+    arrived = swap(sent)
+    rhs, inverses, last_blocks = run(
+        fetch_kernel,
+        (
+            (jax.ShapeDtypeStruct((later, rows, width), jnp.float32), VMEM),
+            (jax.ShapeDtypeStruct((later, width, width), jnp.bfloat16), VMEM),
+            (blocks, VMEM),
+        ),
+        ((right_sides, HBM), (diag_inverses, HBM), (factor_blocks, HBM), (kept, ANY)),
+        scratch=(pltpu.SemaphoreType.DMA((1 + 2 * later,)),),
+        transferred=block_bytes,
+    )
+    solved, rounded = run(
+        shared_solve_kernel,
+        ((part, VMEM), (rounded_part, VMEM)),
+        ((kept, VMEM), (arrived, VMEM), (rhs, VMEM), (inverses, VMEM)),
+        flops=flops,
+    )
+    finished.append(solved)
+    own_blocks.append(last_blocks)
+    other_blocks.append(swap(last_blocks))
+
+    for l in range(2, level_count):
+        stores.append(lax.all_gather(rounded, "rows", axis=0))
+        args = (
+            slot_args
+            + ((own_blocks[l - 2], VMEM), (other_blocks[l - 2], VMEM))
+            + tuple((x, VMEM) for x in stores)
+            + ((rhs, VMEM), (inverses, VMEM))
+        )
+        gathered = pltpu.VMEM((rows, slots * width), jnp.bfloat16)
+        if l < later:
+            solved, rounded = run(
+                functools.partial(whole_kernel, l, targets),
+                ((part, VMEM), (rounded_part, VMEM)),
+                args,
+                scratch=(gathered,),
+                flops=(2 * slots + 1) * flops,
+                transferred=2 * block_bytes,
+            )
+            finished.append(solved)
+    out, = run(
+        functools.partial(last_kernel, later, targets),
+        ((jax.ShapeDtypeStruct((level_count, 1, rows, width), jnp.float32), ANY),),
+        args + tuple((x, ANY) for x in finished),
+        scratch=(
+            gathered,
+            pltpu.VMEM((rows, width), jnp.float32),
+            pltpu.SemaphoreType.DMA((level_count,)),
+        ),
+        flops=(2 * slots + 1) * flops,
+        transferred=2 * block_bytes,
+    )
+    return out
+
+
+def gather_slots(ids_ref, counts_ref, group, store_ref, gathered, slots, width):
+    for k in range(slots):
+        piece = store_ref[ids_ref[group, k]]
+        live = jnp.where(k < counts_ref[group], 1.0, 0.0).astype(piece.dtype)
+        gathered[:, k * width:(k + 1) * width] = piece * live
+
 
 def level_kernel(groups, ids_ref, counts_ref, store_ref, *refs):
     factor_refs = refs[:groups]
@@ -14,15 +266,8 @@
     slots, width = factor_refs[0].shape[0], factor_refs[0].shape[1]
     update = None
     for g in range(groups):
-        for k in range(slots):
-            piece = store_ref[ids_ref[g, k]]
-            live = jnp.where(k < counts_ref[g], 1.0, 0.0).astype(piece.dtype)
-            gathered[:, k * width:(k + 1) * width] = piece * live
-        term = jnp.dot(
-            gathered[...],
-            factor_refs[g][...].reshape(slots * width, width),
-            preferred_element_type=jnp.float32,
-        )
+        gather_slots(ids_ref, counts_ref, g, store_ref, gathered, slots, width)
+        term = flat_dot(gathered, factor_refs[g])
         update = term if update is None else update + term
     reduced = (rhs_ref[...] - update).astype(jnp.bfloat16)
     solved = jnp.dot(reduced, inverse_ref[...], preferred_element_type=jnp.float32)
@@ -45,7 +290,7 @@
         in_specs=[smem, smem, vmem] + [vmem] * groups + [vmem, vmem],
         out_specs=(vmem, vmem),
         scratch_shapes=[pltpu.VMEM((rows, slots * width), jnp.bfloat16)],
-        compiler_params=pltpu.CompilerParams(vmem_limit_bytes=32 * 1024 * 1024),
+        compiler_params=pltpu.CompilerParams(vmem_limit_bytes=VMEM_LIMIT),
         cost_estimate=pl.CostEstimate(
             flops=2 * rows * width * width * (groups * slots + 1),
             bytes_accessed=groups * slots * width * width * 2,
@@ -54,8 +299,7 @@
     )(ids, counts, store, *factors, rhs, inverse)
 
 
-def shards(right_sides, factor_blocks, diag_inverses, source_ids, block_counts):
-    col_count = lax.axis_size("cols")
+def rotated_shards(col_count, right_sides, factor_blocks, diag_inverses, source_ids, block_counts):
     level_count, _, rhs_count, width = right_sides.shape
     share_rows = rhs_count // col_count
     col_index = lax.axis_index("cols")
@@ -93,6 +337,11 @@
 
 
 def solution(mesh):
+    row_count, col_count = mesh.shape["rows"], mesh.shape["cols"]
+    if col_count == 2:
+        shards = functools.partial(paired_shards, row_count)
+    else:
+        shards = functools.partial(rotated_shards, col_count)
     return jax.shard_map(
         shards,
         mesh=mesh,

time: 84 us -> 131 us (1.56)
  waiting for transfers between devices: 0.01 us -> 60.8 us
  blocking collectives: 63.6 us -> 39.6 us
  between operations: 0.08 us -> 13.5 us
  local copies, waits for them, and re-layouts: 5.46 us -> 1.33 us
  starting transfers between devices: 5.13 us -> 7.15 us
  Pallas kernels: 6.3 us -> 8.19 us
  matrix products: 1.74 us -> 0 us
  other arithmetic: 1.4 us -> 0 us
    ppermute x4 -> x5, waiting for transfers between devices: 0.01 us -> 45.8 us  [swap(): return lax.ppermute(x, 'cols', [(0, 1), (1, 0)])]
    all_gather x3 -> x2, blocking collectives: 63.6 us -> 39.6 us  [paired_shards(): stores.append(lax.all_gather(rounded, 'rows', axis=0))]
    all_gather x0 -> x1, waiting for transfers between devices: none -> 14.9 us  [paired_shards(): stores = [lax.all_gather(rounded, 'rows', axis=0)]]
    squeeze x3 -> x0, local copies, waits for them, and re-layouts: 4.03 us -> none  [the longest x1 2.06 us: shards(): factors = [[factor_blocks[l, 0, 0]] for l in range(level_count - 1)]]
    ppermute x4 -> x5, starting transfers between devices: 5.13 us -> 7.15 us  [swap(): return lax.ppermute(x, 'cols', [(0, 1), (1, 0)])]
    pallas_call x3 -> x6, Pallas kernels: 6.3 us -> 8.19 us  [run(): pl.pallas_call(kernel, out_shape=tuple((pltpu.HBM(x.shape, x.dtype) if sp...]
    dot_general x1 -> x0, matrix products: 1.74 us -> none  [shards(): jnp.dot(rhs[0].astype(jnp.bfloat16), diag_inverses[0, 0], preferred_eleme...]
  transfers between devices with their start and end apart: 4 -> 6, of which waited for: 0 -> 3; matrix products, arithmetic and copies ran while one was open for 8% -> 0% of each run, Pallas kernels for 5% -> 3%
where the time goes in v9:
time: 131 us
  waiting for transfers between devices  60.8 us (46%)
  blocking collectives  39.6 us (30%)
  between operations  13.5 us (10%)
  Pallas kernels  8.19 us (6%)
  starting transfers between devices  7.15 us (5%)
  local copies, waits for them, and re-layouts  1.33 us (1%)
    ppermute x5, waiting for transfers between devices, swap(): return lax.ppermute(x, 'cols', [(0, 1), (1, 0)])  45.8 us
    all_gather x2, blocking collectives, paired_shards(): stores.append(lax.all_gather(rounded, 'rows', axis=0))  39.6 us
    all_gather x1, waiting for transfers between devices, paired_shards(): stores = [lax.all_gather(rounded, 'rows', axis=0)]  14.9 us
    pallas_call x6, Pallas kernels, run(): pl.pallas_call(kernel, out_shape=tuple((pltpu.HBM(x.shape, x.dtype) if sp...  8.19 us
    ppermute x5, starting transfers between devices, swap(): return lax.ppermute(x, 'cols', [(0, 1), (1, 0)])  7.15 us
  transfers between devices with their start and end apart: 6, of which 3 were waited for; matrix products, arithmetic and copies ran while one was open for 0% of the time, Pallas kernels for 3%

profile of v9, /device:TPU:0, one launch (start us, length us, event | category | flops | bytes accessed | tf_op | source)
XLA Modules:
  0.0 130.5 jit_solution(7143855034714563145)
XLA Ops:
  6.5 0.0 copy-start.4
  6.5 0.0 copy-start.3
  6.5 0.0 all-gather.5.cloned.1.call-start
  6.5 2.4 %shard_map.55 = (f32[64,256]{1,0:T(8,128)}, bf16[128,256]{1,0:T(8,128)(2,1)}, bf16[8,256,256]{2,1,0:T(8,128)(2,1)S(1)}, bf16[8,256,256]{2,1,0:T(8,128)(2,1)S(1)}) custom-call(f32[4,1,128,256]{3,2,1,0:T(8,128)} %rhs_ref.3, bf16[4,1,256,256]{3,2,1,0:T(8,128)(2,1)} %inverse_ref.3, bf16[3,1,1,8,256,256]{5,4,3,2,1,0:T(8,128)(2,1)} %factor_ref.3), custom_call_target="tpu_custom_call" | custom-call | flops 16777216 | bytes 2097152 | tf_op jit(solution)/shard_map/pallas_call | solution.py:29
  9.0 0.0 all-gather.5.cloned.1.call-update
  9.0 3.0 %collective-permute-start.4 = (bf16[8,256,256]{2,1,0:T(8,128)(2,1)S(1)}, bf16[8,256,256]{2,1,0:T(8,128)(2,1)S(1)}, u32[]{:S(2)}, u32[]{:S(2)}) collective-permute-start(bf16[8,256,256]{2,1,0:T(8,128)(2,1)S(1)} %get-tuple-element.26.refs_4_), channel_id=1, source_target_pairs={{0,1},{1,0},{2,3},{3,2},{4,5},{5,4},{6,7},{7,6},{8,9},{9,8},{10,11... | collective-permute-start | bytes 3145736 | tf_op jit(solution)/shard_map/ppermute | solution.py:170
  12.0 0.0 copy-done.4
  12.0 0.1 copy.9.counts_ref.refs_2_
  12.1 0.0 collective-permute-start.1
  12.2 0.0 copy-done.3
  12.2 2.0 %collective-permute-start = (s32[3,1,1,8]{3,2,1,0:T(1,128)S(1)}, s32[3,1,1,8]{3,2,1,0:T(1,128)S(1)}, u32[]{:S(2)}, u32[]{:S(2)}) collective-permute-start(s32[3,1,1,8]{3,2,1,0:T(1,128)S(1)} %copy-done.3), channel_id=1, source_target_pairs={{0,1},{1,0},{2,3},{3,2},{4,5},{5,4},{6,7},{7,6},{8,9},{9,8},{10,11... | collective-permute-start | bytes 296 | tf_op jit(solution)/shard_map/ppermute | solution.py:170
  14.2 21.1 %collective-permute-done.1.refs_1_.refs_3_ = s32[3,1,1]{2,1,0:T(1,128)S(1)} collective-permute-done((s32[3,1,1]{2,1,0:T(1,128)S(1)}, s32[3,1,1]{2,1,0:T(1,128)S(1)}, u32[]{:S(2)}, u32[]{:S(2)}) %collective-permute-start.1) | collective-permute-done | bytes 44 | tf_op jit(solution)/shard_map/ppermute | solution.py:170
  35.3 0.0 collective-permute-done.refs_0_.refs_1_
  35.3 14.9 %all-gather.5.cloned.1.call-done = bf16[2048,256]{1,0:T(8,128)(2,1)} async-done(((bf16[128,256]{1,0:T(8,128)(2,1)}), bf16[2048,256]{1,0:T(8,128)(2,1)}) %all-gather.5.cloned.1.call-update) | async-done | bytes 1048592 | tf_op jit(solution)/shard_map/all_gather | solution.py:189
  50.2 0.0 copy-start
  50.2 1.2 copy-done
  51.4 0.9 shard_map.56
  52.3 0.0 copy-start.1
  52.3 1.5 %shard_map.57 = (f32[3,64,256]{2,1,0:T(8,128)S(1)}, bf16[3,256,256]{2,1,0:T(8,128)(2,1)S(1)}, bf16[8,256,256]{2,1,0:T(8,128)(2,1)S(1)}) custom-call(f32[4,1,128,256]{3,2,1,0:T(8,128)} %rhs_ref.3, bf16[4,1,256,256]{3,2,1,0:T(8,128)(2,1)} %inverse_ref.3, bf16[3,1,1,8,256,256]{5,4,3,2,1,0:T(8,128)(2,1)} %factor_ref.3, ...), custom_call_target="tpu_custom_call" | custom-call | bytes 1048576 | tf_op jit(solution)/shard_map/pallas_call | solution.py:29
  53.9 0.0 copy-start.2
  53.9 1.5 %collective-permute-start.2 = (bf16[8,256,256]{2,1,0:T(8,128)(2,1)S(1)}, bf16[8,256,256]{2,1,0:T(8,128)(2,1)S(1)}, u32[]{:S(2)}, u32[]{:S(2)}) collective-permute-start(bf16[8,256,256]{2,1,0:T(8,128)(2,1)S(1)} %get-tuple-element.21.refs_4_), channel_id=1, source_target_pairs={{0,1},{1,0},{2,3},{3,2},{4,5},{5,4},{6,7},{7,6},{8,9},{9,8},{10,11... | collective-permute-start | bytes 3145736 | tf_op jit(solution)/shard_map/ppermute | solution.py:170
  55.4 0.6 collective-permute-start.3
  56.0 24.7 %collective-permute-done.3.arrived_ref = f32[64,256]{1,0:T(8,128)S(1)} collective-permute-done((f32[64,256]{1,0:T(8,128)S(1)}, f32[64,256]{1,0:T(8,128)S(1)}, u32[]{:S(2)}, u32[]{:S(2)}) %collective-permute-start.3) | collective-permute-done | bytes 65568 | tf_op jit(solution)/shard_map/ppermute | solution.py:170
  80.7 0.1 shard_map.58
  80.8 20.7 %all-gather.1 = bf16[1024,256]{1,0:T(8,128)(2,1)S(1)} all-gather(bf16[64,256]{1,0:T(8,128)(2,1)S(1)} %get-tuple-element.25), channel_id=3, replica_groups=mesh['rows'=16,'cols'=2] {'rows'}, dimensions={0}, use_global_device_ids=true | all-gather | bytes 557056 | tf_op jit(solution)/shard_map/all_gather | solution.py:223
  101.6 0.0 collective-permute-done.4.refs_5_
  101.6 0.0 copy-done.1
  101.6 1.3 shard_map.59
  102.8 18.9 %all-gather.2 = bf16[1024,256]{1,0:T(8,128)(2,1)S(1)} all-gather(bf16[64,256]{1,0:T(8,128)(2,1)S(1)} %get-tuple-element.27), channel_id=4, replica_groups=mesh['rows'=16,'cols'=2] {'rows'}, dimensions={0}, use_global_device_ids=true | all-gather | bytes 557056 | tf_op jit(solution)/shard_map/all_gather | solution.py:223
  121.7 0.0 collective-permute-done.2.refs_5_
  121.7 0.0 copy-done.2
  121.7 1.9 %shard_map.60 = f32[4,1,64,256]{3,2,1,0:T(8,128)} custom-call(s32[3,1,1,8]{3,2,1,0:T(1,128)S(1)} %copy-done.3, s32[3,1,1,8]{3,2,1,0:T(1,128)S(1)} %collective-permute-done.refs_0_.refs_1_, s32[3,1,1]{2,1,0:T(1,128)S(1)} %copy.9.counts_ref.refs_2_, s32[3,1,1]{2,1,0:T(1,128)S(1)} %collective-permute-done.1.refs_1_.refs_3_, ...), custom_call_target="tpu_custom_call" | custom-call | flops 142606336 | bytes 2097152 | tf_op jit(solution)/shard_map/pallas_call | solution.py:29
Async XLA Ops:
  6.5 5.5 %copy-start.4 = (s32[3,1,1]{0,2,1:T(1,128)S(1)}, s32[3,1,1]{0,2,1:T(1,128)}, u32[]{:S(2)}) copy-start(s32[3,1,1]{0,2,1:T(1,128)} %param.9) | copy-start | bytes 40
  6.5 5.6 %copy-start.3 = (s32[3,1,1,8]{3,2,1,0:T(1,128)S(1)}, s32[3,1,1,8]{3,2,1,0:T(1,128)}, u32[]{:S(2)}) copy-start(s32[3,1,1,8]{3,2,1,0:T(1,128)} %refs_0_.3) | copy-start | bytes 292
  6.5 43.7 %all-gather.5.cloned.1.call-start = ((), (), s32[]{:S(2)}) async-start(), calls=%async_computation | async-start | bytes 1114112 | tf_op jit(solution)/shard_map/all_gather | solution.py:189
  9.0 92.6 %collective-permute-start.4 = (bf16[8,256,256]{2,1,0:T(8,128)(2,1)S(1)}, bf16[8,256,256]{2,1,0:T(8,128)(2,1)S(1)}, u32[]{:S(2)}, u32[]{:S(2)}) collective-permute-start(bf16[8,256,256]{2,1,0:T(8,128)(2,1)S(1)} %get-tuple-element.26.refs_4_), channel_id=1, source_target_pairs={{0,1},{1,0},{2,3},{3,2},{4,5},{5,4},{6,7},{7,6},{8,9},{9,8},{10,11... | collective-permute-start | bytes 3145736 | tf_op jit(solution)/shard_map/ppermute | solution.py:170
  12.1 23.1 %collective-permute-start.1 = (s32[3,1,1]{2,1,0:T(1,128)S(1)}, s32[3,1,1]{2,1,0:T(1,128)S(1)}, u32[]{:S(2)}, u32[]{:S(2)}) collective-permute-start(s32[3,1,1]{2,1,0:T(1,128)S(1)} %copy.9.counts_ref.refs_2_), channel_id=1, source_target_pairs={{0,1},{1,0},{2,3},{3,2},{4,5},{5,4},{6,7},{7,6},{8,9},{9,8},{10,11... | collective-permute-start | bytes 44 | tf_op jit(solution)/shard_map/ppermute | solution.py:170
  12.2 23.1 %collective-permute-start = (s32[3,1,1,8]{3,2,1,0:T(1,128)S(1)}, s32[3,1,1,8]{3,2,1,0:T(1,128)S(1)}, u32[]{:S(2)}, u32[]{:S(2)}) collective-permute-start(s32[3,1,1,8]{3,2,1,0:T(1,128)S(1)} %copy-done.3), channel_id=1, source_target_pairs={{0,1},{1,0},{2,3},{3,2},{4,5},{5,4},{6,7},{7,6},{8,9},{9,8},{10,11... | collective-permute-start | bytes 296 | tf_op jit(solution)/shard_map/ppermute | solution.py:170
  50.2 1.2 copy-start
  52.3 49.2 %copy-start.1 = (bf16[2048,256]{1,0:T(8,128)(2,1)S(1)}, bf16[2048,256]{1,0:T(8,128)(2,1)}, u32[]{:S(2)}) copy-start(bf16[2048,256]{1,0:T(8,128)(2,1)} %all-gather.5.cloned.1.call-done) | copy-start | bytes 3145732
  53.9 67.9 %copy-start.2 = (f32[64,256]{1,0:T(8,128)S(1)}, f32[64,256]{1,0:T(8,128)}, u32[]{:S(2)}) copy-start(f32[64,256]{1,0:T(8,128)} %get-tuple-element.28.refs_11_) | copy-start | bytes 196612
  53.9 67.8 %collective-permute-start.2 = (bf16[8,256,256]{2,1,0:T(8,128)(2,1)S(1)}, bf16[8,256,256]{2,1,0:T(8,128)(2,1)S(1)}, u32[]{:S(2)}, u32[]{:S(2)}) collective-permute-start(bf16[8,256,256]{2,1,0:T(8,128)(2,1)S(1)} %get-tuple-element.21.refs_4_), channel_id=1, source_target_pairs={{0,1},{1,0},{2,3},{3,2},{4,5},{5,4},{6,7},{7,6},{8,9},{9,8},{10,11... | collective-permute-start | bytes 3145736 | tf_op jit(solution)/shard_map/ppermute | solution.py:170
  55.4 25.3 %collective-permute-start.3 = (f32[64,256]{1,0:T(8,128)S(1)}, f32[64,256]{1,0:T(8,128)S(1)}, u32[]{:S(2)}, u32[]{:S(2)}) collective-permute-start(f32[64,256]{1,0:T(8,128)S(1)} %get-tuple-element.22), channel_id=1, source_target_pairs={{0,1},{1,0},{2,3},{3,2},{4,5},{5,4},{6,7},{7,6},{8,9},{9,8},{10,11... | collective-permute-start | bytes 196616 | tf_op jit(solution)/shard_map/ppermute | solution.py:170
Sparse Core Ops, SparseCore 0:
  9.5 40.6 all-gather.4

commit v10 on v7

--- a/solution.py
+++ b/solution.py
@@ -75,7 +75,8 @@
     rounded_ref[...] = solved.astype(jnp.bfloat16)
 
 
-def copies_kernel(rounded_ref, copies_ref):
+def copies_kernel(rounded_ref, *refs):
+    copies_ref = refs[-1]
     for i in range(copies_ref.shape[0]):
         copies_ref[i] = rounded_ref[...]
 
@@ -220,14 +221,19 @@
         flops=solve_flops,
     )
     finished = [solved]
-    copied, = run(copies_kernel, ((copies, VMEM),), ((transpose(rounded), VMEM),))
+    counts = block_counts.reshape(later)
+    other_ids, other_counts = swap_core(source_ids), swap_core(counts)
+    copied, = run(
+        copies_kernel,
+        ((copies, VMEM),),
+        ((transpose(rounded), VMEM), (other_ids, ANY), (other_counts, ANY)),
+    )
     stores = [spread(copied)]
 
-    counts = block_counts.reshape(later)
-    slot_args = tuple((x, SMEM) for x in (source_ids, swap_core(source_ids), counts, swap_core(counts)))
+    slot_args = tuple((x, SMEM) for x in (source_ids, other_ids, counts, other_counts))
     staged_args = (
         (factor_blocks, HBM),
-        (swap_core(factor_blocks), ANY),
+        (swap_core(factor_blocks), HBM),
         (right_sides, HBM),
         (swap_core(right_sides), ANY),
         (diag_inverses, HBM),

time: 88.9 us -> 75.8 us (0.85)
  local copies, waits for them, and re-layouts: 26 us -> 8.49 us
  waiting for transfers between devices: 12.2 us -> 23.9 us
  starting transfers between devices: 35.2 us -> 27.2 us
  Pallas kernels: 14.2 us -> 15.4 us
    unnamed x78 -> x24, local copies, waits for them, and re-layouts: 26 us -> 8.49 us
    all_to_all x3, waiting for transfers between devices: 1.7 us -> 13 us  [spread(): return lax.all_to_all(x, 'rows', 0, 0, axis_index_groups=same_core)]
    all_to_all x3, starting transfers between devices: 18 us -> 14 us  [spread(): return lax.all_to_all(x, 'rows', 0, 0, axis_index_groups=same_core)]
    ppermute x5, starting transfers between devices: 7.36 us -> 4.81 us  [over_both(): return lax.ppermute(x, ('rows', 'cols'), pairs)]
    pallas_call x11, Pallas kernels: 14.2 us -> 15.4 us  [run(): pl.pallas_call(kernel, out_shape=out_shape, in_specs=[spec for _, spec in...]
    ppermute x5, waiting for transfers between devices: 4.35 us -> 3.41 us  [over_both(): return lax.ppermute(x, ('rows', 'cols'), pairs)]
  transfers between devices with their start and end apart: 15 -> 15, of which waited for: 7 -> 8; matrix products, arithmetic and copies ran while one was open for 0% -> 0% of each run, Pallas kernels for 10% -> 13%
where the time goes in v10:
time: 75.8 us; the launch traced here: 75.1 us
  starting transfers between devices  27.2 us (36%)
  waiting for transfers between devices  23.9 us (32%)
  Pallas kernels  15.4 us (20%)
  local copies, waits for them, and re-layouts  8.49 us (11%)
    pallas_call x11, Pallas kernels, run(): pl.pallas_call(kernel, out_shape=out_shape, in_specs=[spec for _, spec in...  15.4 us
    all_to_all x3, starting transfers between devices, spread(): return lax.all_to_all(x, 'rows', 0, 0, axis_index_groups=same_core)  14 us
    all_to_all x3, waiting for transfers between devices, spread(): return lax.all_to_all(x, 'rows', 0, 0, axis_index_groups=same_core)  13 us
    unnamed x24, local copies, waits for them, and re-layouts  8.49 us
    ppermute x2, waiting for transfers between devices, paired_shards(): arrived = lax.ppermute(sent, 'cols', [(0, 1), (1, 0)])  5.49 us
    ppermute x5, starting transfers between devices, swap_core(): return lax.ppermute(x, 'rows', [(i, i ^ 1) for i in range(row_count)])  5.21 us
    ppermute x5, starting transfers between devices, over_both(): return lax.ppermute(x, ('rows', 'cols'), pairs)  4.81 us
    ppermute x5, waiting for transfers between devices, over_both(): return lax.ppermute(x, ('rows', 'cols'), pairs)  3.41 us
  transfers between devices with their start and end apart: 15, of which 8 were waited for; matrix products, arithmetic and copies ran while one was open for 0% of the time, Pallas kernels for 13%

profile of v10, /device:TPU:0, one launch (start us, length us, event | category | flops | bytes accessed | tf_op | source)
XLA Modules:
  0.0 75.1 jit_solution(10916614226446599003)
XLA Ops:
  0.0 0.5 collective-permute-start.3
  0.5 0.1 collective-permute-start.4
  0.5 0.5 collective-permute-start.5
  1.0 1.1 %shard_map.55 = (f32[64,256]{1,0:T(8,128)S(1)}, bf16[64,256]{1,0:T(8,128)(2,1)S(1)}) custom-call(f32[4,1,128,256]{3,2,1,0:T(8,128)} %refs_6_.5, bf16[4,1,256,256]{3,2,1,0:T(8,128)(2,1)} %refs_8_.5), custom_call_target="tpu_custom_call" | custom-call | flops 8388608 | tf_op jit(solution)/shard_map/pallas_call | solution.py:36
  2.1 0.7 collective-permute-start.2
  2.8 3.9 %collective-permute-start.1 = (s32[3]{0:T(128)}, s32[3]{0:T(128)S(1)}, u32[]{:S(2)}, u32[]{:S(2)}) collective-permute-start(s32[3]{0:T(128)} %bitcast.1), channel_id=1, source_target_pairs={{0,2},{2,0},{4,6},{6,4},{8,10},{10,8},{12,14},{14,12},{16,18},{18,... | collective-permute-start | bytes 44 | tf_op jit(solution)/shard_map/ppermute | solution.py:204
  6.7 1.0 %collective-permute-done.1.refs_1_.refs_3_ = s32[3]{0:T(128)S(1)} collective-permute-done((s32[3]{0:T(128)}, s32[3]{0:T(128)S(1)}, u32[]{:S(2)}, u32[]{:S(2)}) %collective-permute-start.1) | collective-permute-done | bytes 44 | tf_op jit(solution)/shard_map/ppermute | solution.py:204
  7.7 0.3 collective-permute-start
  8.0 1.1 %collective-permute-done.refs_0_.refs_1_ = s32[3,1,1,8]{3,2,1,0:T(1,128)S(1)} collective-permute-done((s32[3,1,1,8]{3,2,1,0:T(1,128)}, s32[3,1,1,8]{3,2,1,0:T(1,128)S(1)}, u32[]{:S(2)}, u32[]{:S(2)}) %collective-permute-start) | collective-permute-done | bytes 128 | tf_op jit(solution)/shard_map/ppermute | solution.py:204
  9.0 0.0 collective-permute-done.2.rounded_ref
  9.0 0.7 shard_map.56
  9.7 7.0 %all-to-all-start = ((bf16[8,64,256]{2,1,0:T(8,128)(2,1)}), bf16[8,64,256]{2,1,0:T(8,128)(2,1)S(1)}, u32[]{:S(2)}, u32[]{:S(2)}) async-start(bf16[8,64,256]{2,1,0:T(8,128)(2,1)} %shard_map.56), calls=%async_computation | async-start | bytes 524288 | tf_op jit(solution)/shard_map/all_to_all | solution.py:210
  16.7 0.0 collective-permute-done.4.refs_7_
  16.7 0.0 collective-permute-done.5.refs_9_
  16.7 0.0 collective-permute-done.3.refs_5_
  16.8 0.0 copy-start.8
  16.8 0.7 copy-done.8
  17.4 0.7 copy-done.10
  18.1 2.2 %shard_map.57 = (bf16[2,8,256,256]{3,2,1,0:T(8,128)(2,1)S(1)}, f32[64,256]{1,0:T(8,128)S(1)}, bf16[256,256]{1,0:T(8,128)(2,1)S(1)}) custom-call(s32[3,1,1,8]{3,2,1,0:T(1,128)S(1)} %copy-done.8, s32[3,1,1,8]{3,2,1,0:T(1,128)S(1)} %collective-permute-done.refs_0_.refs_1_, s32[3]{0:T(128)S(1)} %bitcast.2, s32[3]{0:T(128)S(1)} %collective-permute-done.1.refs_1_.refs_3_, ...), custom_call_target="tpu_custom_call" | custom-call | bytes 2097152 | tf_op jit(solution)/shard_map/pallas_call | solution.py:36
  20.4 0.6 copy-done.4
  21.0 0.6 copy-done.6
  21.6 4.4 %all-to-all-done.refs_4_.refs_10_ = bf16[8,64,256]{2,1,0:T(8,128)(2,1)S(1)} async-done(((bf16[8,64,256]{2,1,0:T(8,128)(2,1)}), bf16[8,64,256]{2,1,0:T(8,128)(2,1)S(1)}, u32[]{:S(2)}, u32[]{:S(2)}) %all-to-all-start) | async-done | bytes 262176 | tf_op jit(solution)/shard_map/all_to_all | solution.py:210
  26.0 1.1 %shard_map.58 = (f32[64,256]{1,0:T(8,128)S(1)}, f32[64,256]{1,0:T(8,128)S(1)}) custom-call(s32[3,1,1,8]{3,2,1,0:T(1,128)S(1)} %copy-done.9, s32[3,1,1,8]{3,2,1,0:T(1,128)S(1)} %collective-permute-done.refs_0_.refs_1_, s32[3]{0:T(128)S(1)} %bitcast.3, s32[3]{0:T(128)S(1)} %collective-permute-done.1.refs_1_.refs_3_, ...), custom_call_target="tpu_custom_call" | custom-call | flops 134217728 | bytes 2097152 | tf_op jit(solution)/shard_map/pallas_call | solution.py:36
  27.1 1.6 %collective-permute-start.6 = (f32[64,256]{1,0:T(8,128)S(1)}, f32[64,256]{1,0:T(8,128)S(1)}, u32[]{:S(2)}, u32[]{:S(2)}) collective-permute-start(f32[64,256]{1,0:T(8,128)S(1)} %get-tuple-element.33), channel_id=1, source_target_pairs={{0,1},{1,0},{2,3},{3,2},{4,5},{5,4},{6,7},{7,6},{8,9},{9,8},{10,11... | collective-permute-start | bytes 196616 | tf_op jit(solution)/shard_map/ppermute | solution.py:273
  28.7 2.7 %collective-permute-done.6.arrived_ref = f32[64,256]{1,0:T(8,128)S(1)} collective-permute-done((f32[64,256]{1,0:T(8,128)S(1)}, f32[64,256]{1,0:T(8,128)S(1)}, u32[]{:S(2)}, u32[]{:S(2)}) %collective-permute-start.6) | collective-permute-done | bytes 65568 | tf_op jit(solution)/shard_map/ppermute | solution.py:273
  31.4 0.9 %shard_map.59 = (f32[64,256]{1,0:T(8,128)S(1)}, bf16[8,64,256]{2,1,0:T(8,128)(2,1)}) custom-call(f32[64,256]{1,0:T(8,128)S(1)} %get-tuple-element.32.kept_ref.refs_11_, f32[64,256]{1,0:T(8,128)S(1)} %collective-permute-done.6.arrived_ref, f32[64,256]{1,0:T(8,128)S(1)} %copy-done.7, bf16[256,256]{1,0:T(8,128)(2,1)S(1)} %copy-done.5), custom_call_target="tpu_custom_call" | custom-call | flops 8388608 | tf_op jit(solution)/shard_map/pallas_call | solution.py:36
  32.3 3.6 %all-to-all-start.1 = ((bf16[8,64,256]{2,1,0:T(8,128)(2,1)}), bf16[8,64,256]{2,1,0:T(8,128)(2,1)S(1)}, u32[]{:S(2)}, u32[]{:S(2)}) async-start(bf16[8,64,256]{2,1,0:T(8,128)(2,1)} %get-tuple-element.36), calls=%async_computation.1 | async-start | bytes 524288 | tf_op jit(solution)/shard_map/all_to_all | solution.py:210
  35.9 0.7 collective-permute-start.7
  36.6 2.8 %shard_map.60 = (bf16[2,8,256,256]{3,2,1,0:T(8,128)(2,1)S(1)}, f32[64,256]{1,0:T(8,128)S(1)}, bf16[256,256]{1,0:T(8,128)(2,1)S(1)}, f32[64,256]{1,0:T(8,128)S(1)}, f32[64,256]{1,0:T(8,128)S(1)}) custom-call(s32[3,1,1,8]{3,2,1,0:T(1,128)S(1)} %copy-done.9, s32[3,1,1,8]{3,2,1,0:T(1,128)S(1)} %collective-permute-done.refs_0_.refs_1_, s32[3]{0:T(128)S(1)} %bitcast.4, ...), custom_call_target="tpu_custom_call" | custom-call | flops 134217728 | bytes 2097152 | tf_op jit(solution)/shard_map/pallas_call | solution.py:36
  39.3 1.3 %copy-done.2 = bf16[2,8,256,256]{3,2,1,0:T(8,128)(2,1)} copy-done((bf16[2,8,256,256]{3,2,1,0:T(8,128)(2,1)}, bf16[2,8,256,256]{3,2,1,0:T(8,128)(2,1)S(1)}, u32[]{:S(2)}) %copy-start.2) | copy-done | bytes 2097176
  40.7 3.5 %all-to-all-done.1.refs_4_.refs_11_ = bf16[8,64,256]{2,1,0:T(8,128)(2,1)S(1)} async-done(((bf16[8,64,256]{2,1,0:T(8,128)(2,1)}), bf16[8,64,256]{2,1,0:T(8,128)(2,1)S(1)}, u32[]{:S(2)}, u32[]{:S(2)}) %all-to-all-start.1) | async-done | bytes 262176 | tf_op jit(solution)/shard_map/all_to_all | solution.py:210
  44.1 1.6 %copy-done.3 = bf16[2,8,256,256]{3,2,1,0:T(8,128)(2,1)S(1)} copy-done((bf16[2,8,256,256]{3,2,1,0:T(8,128)(2,1)S(1)}, bf16[2,8,256,256]{3,2,1,0:T(8,128)(2,1)}, u32[]{:S(2)}) %copy-start.3) | copy-done | bytes 2097176
  45.7 1.1 %shard_map.61 = (f32[64,256]{1,0:T(8,128)S(1)}, f32[64,256]{1,0:T(8,128)S(1)}) custom-call(s32[3,1,1,8]{3,2,1,0:T(1,128)S(1)} %copy-done.9, s32[3,1,1,8]{3,2,1,0:T(1,128)S(1)} %collective-permute-done.refs_0_.refs_1_, s32[3]{0:T(128)S(1)} %bitcast.5, s32[3]{0:T(128)S(1)} %collective-permute-done.1.refs_1_.refs_3_, ...), custom_call_target="tpu_custom_call" | custom-call | flops 134217728 | bytes 2097152 | tf_op jit(solution)/shard_map/pallas_call | solution.py:36
  46.8 1.6 %collective-permute-start.8 = (f32[64,256]{1,0:T(8,128)S(1)}, f32[64,256]{1,0:T(8,128)S(1)}, u32[]{:S(2)}, u32[]{:S(2)}) collective-permute-start(f32[64,256]{1,0:T(8,128)S(1)} %get-tuple-element.42), channel_id=1, source_target_pairs={{0,1},{1,0},{2,3},{3,2},{4,5},{5,4},{6,7},{7,6},{8,9},{9,8},{10,11... | collective-permute-start | bytes 196616 | tf_op jit(solution)/shard_map/ppermute | solution.py:273
  48.4 2.7 %collective-permute-done.8.arrived_ref = f32[64,256]{1,0:T(8,128)S(1)} collective-permute-done((f32[64,256]{1,0:T(8,128)S(1)}, f32[64,256]{1,0:T(8,128)S(1)}, u32[]{:S(2)}, u32[]{:S(2)}) %collective-permute-start.8) | collective-permute-done | bytes 65568 | tf_op jit(solution)/shard_map/ppermute | solution.py:273
  51.1 0.9 %shard_map.62 = (f32[64,256]{1,0:T(8,128)S(1)}, bf16[8,64,256]{2,1,0:T(8,128)(2,1)}) custom-call(f32[64,256]{1,0:T(8,128)S(1)} %get-tuple-element.41.kept_ref.refs_12_, f32[64,256]{1,0:T(8,128)S(1)} %collective-permute-done.8.arrived_ref, f32[64,256]{1,0:T(8,128)S(1)} %get-tuple-element.43.rhs_ref, bf16[256,256]{1,0:T(8,128)(2,1)S(1)} %get-tuple-element.44.inverse_ref), custom_call_target="tpu_custom_call" | custom-call | flops 8388608 | tf_op jit(solution)/shard_map/pallas_call | solution.py:36
  52.0 3.4 %all-to-all-start.2 = ((bf16[8,64,256]{2,1,0:T(8,128)(2,1)}), bf16[8,64,256]{2,1,0:T(8,128)(2,1)S(1)}, u32[]{:S(2)}, u32[]{:S(2)}) async-start(bf16[8,64,256]{2,1,0:T(8,128)(2,1)} %get-tuple-element.45), calls=%async_computation.2 | async-start | bytes 524288 | tf_op jit(solution)/shard_map/all_to_all | solution.py:210
  55.4 0.7 collective-permute-start.9
  56.1 2.7 %shard_map.63 = (bf16[2,8,256,256]{3,2,1,0:T(8,128)(2,1)S(1)}, f32[64,256]{1,0:T(8,128)S(1)}, bf16[256,256]{1,0:T(8,128)(2,1)S(1)}, f32[64,256]{1,0:T(8,128)S(1)}, f32[64,256]{1,0:T(8,128)S(1)}) custom-call(s32[3,1,1,8]{3,2,1,0:T(1,128)S(1)} %copy-done.9, s32[3,1,1,8]{3,2,1,0:T(1,128)S(1)} %collective-permute-done.refs_0_.refs_1_, s32[3]{0:T(128)S(1)} %bitcast.6, ...), custom_call_target="tpu_custom_call" | custom-call | flops 134217728 | bytes 2097152 | tf_op jit(solution)/shard_map/pallas_call | solution.py:36
  58.8 1.4 %copy-done = bf16[2,8,256,256]{3,2,1,0:T(8,128)(2,1)} copy-done((bf16[2,8,256,256]{3,2,1,0:T(8,128)(2,1)}, bf16[2,8,256,256]{3,2,1,0:T(8,128)(2,1)S(1)}, u32[]{:S(2)}) %copy-start) | copy-done | bytes 2097176
  60.2 5.1 %all-to-all-done.2.refs_4_ = bf16[8,64,256]{2,1,0:T(8,128)(2,1)S(1)} async-done(((bf16[8,64,256]{2,1,0:T(8,128)(2,1)}), bf16[8,64,256]{2,1,0:T(8,128)(2,1)S(1)}, u32[]{:S(2)}, u32[]{:S(2)}) %all-to-all-start.2) | async-done | bytes 262176 | tf_op jit(solution)/shard_map/all_to_all | solution.py:210
  65.3 1.6 %copy-done.1 = bf16[2,8,256,256]{3,2,1,0:T(8,128)(2,1)S(1)} copy-done((bf16[2,8,256,256]{3,2,1,0:T(8,128)(2,1)S(1)}, bf16[2,8,256,256]{3,2,1,0:T(8,128)(2,1)}, u32[]{:S(2)}) %copy-start.1) | copy-done | bytes 2097176
  66.9 1.1 %shard_map.64 = (f32[64,256]{1,0:T(8,128)S(1)}, f32[64,256]{1,0:T(8,128)S(1)}) custom-call(s32[3,1,1,8]{3,2,1,0:T(1,128)S(1)} %copy-done.9, s32[3,1,1,8]{3,2,1,0:T(1,128)S(1)} %collective-permute-done.refs_0_.refs_1_, s32[3]{0:T(128)S(1)} %bitcast.7, s32[3]{0:T(128)S(1)} %collective-permute-done.1.refs_1_.refs_3_, ...), custom_call_target="tpu_custom_call" | custom-call | flops 134217728 | bytes 2097152 | tf_op jit(solution)/shard_map/pallas_call | solution.py:36
  68.0 0.7 collective-permute-start.10
  68.7 2.2 %collective-permute-start.11 = (f32[64,256]{1,0:T(8,128)S(1)}, f32[64,256]{1,0:T(8,128)S(1)}, u32[]{:S(2)}, u32[]{:S(2)}) collective-permute-start(f32[64,256]{1,0:T(8,128)S(1)} %get-tuple-element.51), channel_id=1, source_target_pairs={{0,2},{1,0},{2,3},{3,1},{4,6},{5,4},{6,7},{7,5},{8,10},{9,8},{10,1... | collective-permute-start | bytes 196616 | tf_op jit(solution)/shard_map/ppermute | solution.py:201
  70.8 0.0 collective-permute-done.10.first_ref
  70.8 3.4 %collective-permute-done.11.second_ref = f32[64,256]{1,0:T(8,128)S(1)} collective-permute-done((f32[64,256]{1,0:T(8,128)S(1)}, f32[64,256]{1,0:T(8,128)S(1)}, u32[]{:S(2)}, u32[]{:S(2)}) %collective-permute-start.11) | collective-permute-done | bytes 65568 | tf_op jit(solution)/shard_map/ppermute | solution.py:201
  74.2 0.9 %shard_map.65 = f32[4,1,64,256]{3,2,1,0:T(8,128)} custom-call(f32[64,256]{1,0:T(8,128)S(1)} %collective-permute-done.10.first_ref, f32[64,256]{1,0:T(8,128)S(1)} %collective-permute-done.11.second_ref, f32[64,256]{1,0:T(8,128)S(1)} %get-tuple-element.52.rhs_ref, bf16[256,256]{1,0:T(8,128)(2,1)S(1)} %get-tuple-element.53.inverse_ref, ...), custom_call_target="tpu_custom_call" | custom-call | flops 8388608 | tf_op jit(solution)/shard_map/pallas_call | solution.py:36
  (17 shorter events, 0.0 us)
Async XLA Ops:
  0.0 16.7 %collective-permute-start.3 = (bf16[3,1,1,8,256,256]{5,4,3,2,1,0:T(8,128)(2,1)}, bf16[3,1,1,8,256,256]{5,4,3,2,1,0:T(8,128)(2,1)}, u32[]{:S(2)}, u32[]{:S(2)}) collective-permute-start(bf16[3,1,1,8,256,256]{5,4,3,2,1,0:T(8,128)(2,1)} %refs_4_.5), channel_id=1, source_target_pairs={{0,2},{2,0},{4,6},{6,4},{8,10},{10,8},{12,14},{14,12},{16,18},{18,... | collective-permute-start | bytes 9437192 | tf_op jit(solution)/shard_map/ppermute | solution.py:204
  0.5 16.3 %collective-permute-start.4 = (f32[4,1,128,256]{3,2,1,0:T(8,128)}, f32[4,1,128,256]{3,2,1,0:T(8,128)S(1)}, u32[]{:S(2)}, u32[]{:S(2)}) collective-permute-start(f32[4,1,128,256]{3,2,1,0:T(8,128)} %refs_6_.5), channel_id=1, source_target_pairs={{0,2},{2,0},{4,6},{6,4},{8,10},{10,8},{12,14},{14,12},{16,18},{18,... | collective-permute-start | bytes 1572872 | tf_op jit(solution)/shard_map/ppermute | solution.py:204
  0.5 16.2 %collective-permute-start.5 = (bf16[4,1,256,256]{3,2,1,0:T(8,128)(2,1)}, bf16[4,1,256,256]{3,2,1,0:T(8,128)(2,1)S(1)}, u32[]{:S(2)}, u32[]{:S(2)}) collective-permute-start(bf16[4,1,256,256]{3,2,1,0:T(8,128)(2,1)} %refs_8_.5), channel_id=1, source_target_pairs={{0,2},{2,0},{4,6},{6,4},{8,10},{10,8},{12,14},{14,12},{16,18},{18,... | collective-permute-start | bytes 1572872 | tf_op jit(solution)/shard_map/ppermute | solution.py:204
  2.1 6.9 %collective-permute-start.2 = (bf16[64,256]{1,0:T(8,128)(2,1)S(1)}, bf16[64,256]{1,0:T(8,128)(2,1)S(1)}, u32[]{:S(2)}, u32[]{:S(2)}) collective-permute-start(bf16[64,256]{1,0:T(8,128)(2,1)S(1)} %get-tuple-element.30), channel_id=1, source_target_pairs={{0,0},{1,2},{2,1},{3,3},{4,4},{5,6},{6,5},{7,7},{8,8},{9,10},{10,9... | collective-permute-start | bytes 98312 | tf_op jit(solution)/shard_map/ppermute | solution.py:201
  2.8 4.9 %collective-permute-start.1 = (s32[3]{0:T(128)}, s32[3]{0:T(128)S(1)}, u32[]{:S(2)}, u32[]{:S(2)}) collective-permute-start(s32[3]{0:T(128)} %bitcast.1), channel_id=1, source_target_pairs={{0,2},{2,0},{4,6},{6,4},{8,10},{10,8},{12,14},{14,12},{16,18},{18,... | collective-permute-start | bytes 44 | tf_op jit(solution)/shard_map/ppermute | solution.py:204
  7.7 1.4 %collective-permute-start = (s32[3,1,1,8]{3,2,1,0:T(1,128)}, s32[3,1,1,8]{3,2,1,0:T(1,128)S(1)}, u32[]{:S(2)}, u32[]{:S(2)}) collective-permute-start(s32[3,1,1,8]{3,2,1,0:T(1,128)} %refs_0_.11), channel_id=1, source_target_pairs={{0,2},{2,0},{4,6},{6,4},{8,10},{10,8},{12,14},{14,12},{16,18},{18,... | collective-permute-start | bytes 296 | tf_op jit(solution)/shard_map/ppermute | solution.py:204
  9.7 16.3 %copy-start.9 = (s32[3,1,1,8]{3,2,1,0:T(1,128)S(1)}, s32[3,1,1,8]{3,2,1,0:T(1,128)}, u32[]{:S(2)}) copy-start(s32[3,1,1,8]{3,2,1,0:T(1,128)} %refs_0_.11) | copy-start | bytes 292
  9.7 16.3 %copy-start.11 = (s32[3,1,1]{0,2,1:T(1,128)S(1)}, s32[3,1,1]{0,2,1:T(1,128)}, u32[]{:S(2)}) copy-start(s32[3,1,1]{0,2,1:T(1,128)} %param.9) | copy-start | bytes 40
  9.7 16.2 %all-to-all-start = ((bf16[8,64,256]{2,1,0:T(8,128)(2,1)}), bf16[8,64,256]{2,1,0:T(8,128)(2,1)S(1)}, u32[]{:S(2)}, u32[]{:S(2)}) async-start(bf16[8,64,256]{2,1,0:T(8,128)(2,1)} %shard_map.56), calls=%async_computation | async-start | bytes 524288 | tf_op jit(solution)/shard_map/all_to_all | solution.py:210
  16.8 0.7 copy-start.8
  17.4 0.7 copy-start.10
  20.3 0.6 copy-start.4
  21.0 0.6 copy-start.6
  26.0 5.4 %copy-start.5 = (bf16[256,256]{1,0:T(8,128)(2,1)S(1)}, bf16[256,256]{1,0:T(8,128)(2,1)}, u32[]{:S(2)}) copy-start(bf16[256,256]{1,0:T(8,128)(2,1)} %copy-done.4) | copy-start | bytes 393220
  26.0 5.4 %copy-start.7 = (f32[64,256]{1,0:T(8,128)S(1)}, f32[64,256]{1,0:T(8,128)}, u32[]{:S(2)}) copy-start(f32[64,256]{1,0:T(8,128)} %copy-done.6) | copy-start | bytes 196612
  27.1 4.3 %collective-permute-start.6 = (f32[64,256]{1,0:T(8,128)S(1)}, f32[64,256]{1,0:T(8,128)S(1)}, u32[]{:S(2)}, u32[]{:S(2)}) collective-permute-start(f32[64,256]{1,0:T(8,128)S(1)} %get-tuple-element.33), channel_id=1, source_target_pairs={{0,1},{1,0},{2,3},{3,2},{4,5},{5,4},{6,7},{7,6},{8,9},{9,8},{10,11... | collective-permute-start | bytes 196616 | tf_op jit(solution)/shard_map/ppermute | solution.py:273
  32.3 11.8 %all-to-all-start.1 = ((bf16[8,64,256]{2,1,0:T(8,128)(2,1)}), bf16[8,64,256]{2,1,0:T(8,128)(2,1)S(1)}, u32[]{:S(2)}, u32[]{:S(2)}) async-start(bf16[8,64,256]{2,1,0:T(8,128)(2,1)} %get-tuple-element.36), calls=%async_computation.1 | async-start | bytes 524288 | tf_op jit(solution)/shard_map/all_to_all | solution.py:210
  35.9 4.8 %collective-permute-start.7 = (f32[64,256]{1,0:T(8,128)S(1)}, f32[64,256]{1,0:T(8,128)S(1)}, u32[]{:S(2)}, u32[]{:S(2)}) collective-permute-start(f32[64,256]{1,0:T(8,128)S(1)} %get-tuple-element.40), channel_id=1, source_target_pairs={{0,0},{1,2},{2,1},{3,3},{4,4},{5,6},{6,5},{7,7},{8,8},{9,10},{10,9... | collective-permute-start | bytes 196616 | tf_op jit(solution)/shard_map/ppermute | solution.py:201
  39.3 1.3 %copy-start.2 = (bf16[2,8,256,256]{3,2,1,0:T(8,128)(2,1)}, bf16[2,8,256,256]{3,2,1,0:T(8,128)(2,1)S(1)}, u32[]{:S(2)}) copy-start(bf16[2,8,256,256]{3,2,1,0:T(8,128)(2,1)S(1)} %get-tuple-element.37.refs_5_) | copy-start | bytes 6291460
  44.1 1.6 %copy-start.3 = (bf16[2,8,256,256]{3,2,1,0:T(8,128)(2,1)S(1)}, bf16[2,8,256,256]{3,2,1,0:T(8,128)(2,1)}, u32[]{:S(2)}) copy-start(bf16[2,8,256,256]{3,2,1,0:T(8,128)(2,1)} %copy-done.2) | copy-start | bytes 6291460
  46.8 4.3 %collective-permute-start.8 = (f32[64,256]{1,0:T(8,128)S(1)}, f32[64,256]{1,0:T(8,128)S(1)}, u32[]{:S(2)}, u32[]{:S(2)}) collective-permute-start(f32[64,256]{1,0:T(8,128)S(1)} %get-tuple-element.42), channel_id=1, source_target_pairs={{0,1},{1,0},{2,3},{3,2},{4,5},{5,4},{6,7},{7,6},{8,9},{9,8},{10,11... | collective-permute-start | bytes 196616 | tf_op jit(solution)/shard_map/ppermute | solution.py:273
  52.0 13.3 %all-to-all-start.2 = ((bf16[8,64,256]{2,1,0:T(8,128)(2,1)}), bf16[8,64,256]{2,1,0:T(8,128)(2,1)S(1)}, u32[]{:S(2)}, u32[]{:S(2)}) async-start(bf16[8,64,256]{2,1,0:T(8,128)(2,1)} %get-tuple-element.45), calls=%async_computation.2 | async-start | bytes 524288 | tf_op jit(solution)/shard_map/all_to_all | solution.py:210
  55.4 4.8 %collective-permute-start.9 = (f32[64,256]{1,0:T(8,128)S(1)}, f32[64,256]{1,0:T(8,128)S(1)}, u32[]{:S(2)}, u32[]{:S(2)}) collective-permute-start(f32[64,256]{1,0:T(8,128)S(1)} %get-tuple-element.49), channel_id=1, source_target_pairs={{0,0},{1,2},{2,1},{3,3},{4,4},{5,6},{6,5},{7,7},{8,8},{9,10},{10,9... | collective-permute-start | bytes 196616 | tf_op jit(solution)/shard_map/ppermute | solution.py:201
  58.8 1.4 %copy-start = (bf16[2,8,256,256]{3,2,1,0:T(8,128)(2,1)}, bf16[2,8,256,256]{3,2,1,0:T(8,128)(2,1)S(1)}, u32[]{:S(2)}) copy-start(bf16[2,8,256,256]{3,2,1,0:T(8,128)(2,1)S(1)} %get-tuple-element.46.refs_5_) | copy-start | bytes 6291460
  65.3 1.6 %copy-start.1 = (bf16[2,8,256,256]{3,2,1,0:T(8,128)(2,1)S(1)}, bf16[2,8,256,256]{3,2,1,0:T(8,128)(2,1)}, u32[]{:S(2)}) copy-start(bf16[2,8,256,256]{3,2,1,0:T(8,128)(2,1)} %copy-done) | copy-start | bytes 6291460
  68.0 2.8 %collective-permute-start.10 = (f32[64,256]{1,0:T(8,128)S(1)}, f32[64,256]{1,0:T(8,128)S(1)}, u32[]{:S(2)}, u32[]{:S(2)}) collective-permute-start(f32[64,256]{1,0:T(8,128)S(1)} %get-tuple-element.50), channel_id=1, source_target_pairs={{0,0},{1,2},{2,1},{3,3},{4,4},{5,6},{6,5},{7,7},{8,8},{9,10},{10,9... | collective-permute-start | bytes 196616 | tf_op jit(solution)/shard_map/ppermute | solution.py:201
  68.7 5.6 %collective-permute-start.11 = (f32[64,256]{1,0:T(8,128)S(1)}, f32[64,256]{1,0:T(8,128)S(1)}, u32[]{:S(2)}, u32[]{:S(2)}) collective-permute-start(f32[64,256]{1,0:T(8,128)S(1)} %get-tuple-element.51), channel_id=1, source_target_pairs={{0,2},{1,0},{2,3},{3,1},{4,6},{5,4},{6,7},{7,5},{8,10},{9,8},{10,1... | collective-permute-start | bytes 196616 | tf_op jit(solution)/shard_map/ppermute | solution.py:201

commit v11 on v7

--- a/solution.py
+++ b/solution.py
@@ -63,13 +63,27 @@
     return lax.rem(lax.axis_index("rows"), 2), lax.axis_index("cols")
 
 
-def first_kernel(rhs_ref, inverse_ref, out_ref, rounded_ref, rhs, inverse, sems):
+def first_kernel(
+    ids_ref, counts_ref, rhs_ref, inverse_ref, out_ref, rounded_ref, live_ids_ref,
+    ids, counts, rhs, inverse, sems,
+):
     _, col = own_place()
     copies = start_copies(
-        [(half_of(rhs_ref, 0, col, out_ref.shape[0]), rhs), (inverse_ref.at[0, 0], inverse)], sems
-    )
-    for copy in copies:
-        copy.wait()
+        [
+            (ids_ref, ids),
+            (counts_ref, counts),
+            (half_of(rhs_ref, 0, col, out_ref.shape[0]), rhs),
+            (inverse_ref.at[0, 0], inverse),
+        ],
+        sems,
+    )
+    copies[0].wait()
+    copies[1].wait()
+    for l in range(ids.shape[0]):
+        for k in range(ids.shape[3]):
+            live_ids_ref[l, 0, 0, k] = jnp.where(k < counts[l], ids[l, 0, 0, k], -1)
+    copies[2].wait()
+    copies[3].wait()
     solved = solve(rhs[...], inverse[...])
     out_ref[...] = solved
     rounded_ref[...] = solved.astype(jnp.bfloat16)
@@ -80,12 +94,13 @@
         copies_ref[i] = rounded_ref[...]
 
 
-def slot_sum(level, store_level, chips, ids_ref, counts_ref, store_ref, factor_ref, gathered):
+def slot_sum(level, store_level, chips, ids_ref, store_ref, factor_ref, gathered):
     slots, width = factor_ref.shape[0], factor_ref.shape[1]
     for k in range(slots):
-        source = ids_ref[level - 1, 0, 0, k]
+        source_id = ids_ref[level - 1, 0, 0, k]
+        source = jnp.maximum(source_id, 0)
         source_level, place = source // (2 * chips), source % (2 * chips) // 2
-        live = k < counts_ref[level - 1]
+        live = source_id >= 0
         if store_level is None:
             live = jnp.logical_and(live, source_level < level - 1)
             place = jnp.minimum(source_level, level - 2) * chips + place
@@ -98,9 +113,9 @@
 
 def stage_kernel(level, later, chips, *refs):
     inner = level < later
-    slot_refs = refs[:4]
-    factor_ref, other_factor_ref, rhs_ref, other_rhs_ref, inverse_ref, other_inverse_ref = refs[4:10]
-    store_refs = refs[10:9 + level]
+    slot_refs = refs[:2]
+    factor_ref, other_factor_ref, rhs_ref, other_rhs_ref, inverse_ref, other_inverse_ref = refs[2:8]
+    store_refs = refs[8:7 + level]
     outs = refs[-7 if level == 1 else -11:]
     staged_ref, own_rhs_ref, own_inverse_ref = outs[:3]
     rhs, inverse, sems, factor_sems = outs[-4:]
@@ -135,7 +150,7 @@
         factor_copies[g].wait()
         if level > 1:
             older_refs[g][...] = slot_sum(
-                level, None, chips, slot_refs[g], slot_refs[2 + g], store, staged_ref.at[g], gathered
+                level, None, chips, slot_refs[g], store, staged_ref.at[g], gathered
             )
     for copy in copies:
         copy.wait()
@@ -145,15 +160,13 @@
 
 
 def sums_kernel(level, chips, *refs):
-    slot_refs, store_ref, staged_ref = refs[:4], refs[4], refs[5]
-    older_refs = refs[6:8]
+    slot_refs, store_ref, staged_ref = refs[:2], refs[2], refs[3]
+    older_refs = refs[4:6]
     kept_ref, sent_ref, gathered = refs[-3:]
     core, col = own_place()
     sums = []
     for g in range(2):
-        total = slot_sum(
-            level, level - 1, chips, slot_refs[g], slot_refs[2 + g], store_ref, staged_ref.at[g], gathered
-        )
+        total = slot_sum(level, level - 1, chips, slot_refs[g], store_ref, staged_ref.at[g], gathered)
         sums.append(total + older_refs[g][...] if level > 1 else total)
     straight = core == col
     kept_ref[...] = jnp.where(straight, sums[0], sums[1])
@@ -208,14 +221,21 @@
     def spread(x):
         return lax.all_to_all(x, "rows", 0, 0, axis_index_groups=same_core)
 
-    solved, rounded = run(
+    counts = block_counts.reshape(later)
+    solved, rounded, live_ids = run(
         first_kernel,
-        ((part, VMEM), (rounded_part, VMEM)),
-        ((right_sides, HBM), (diag_inverses, HBM)),
+        (
+            (part, VMEM),
+            (rounded_part, VMEM),
+            (jax.ShapeDtypeStruct(source_ids.shape, source_ids.dtype), SMEM),
+        ),
+        ((source_ids, HBM), (counts, HBM), (right_sides, HBM), (diag_inverses, HBM)),
         scratch=(
+            pltpu.SMEM(source_ids.shape, source_ids.dtype),
+            pltpu.SMEM(counts.shape, counts.dtype),
             pltpu.VMEM((rows, width), jnp.float32),
             pltpu.VMEM((width, width), jnp.bfloat16),
-            pltpu.SemaphoreType.DMA((2,)),
+            pltpu.SemaphoreType.DMA((4,)),
         ),
         flops=solve_flops,
     )
@@ -223,15 +243,14 @@
     copied, = run(copies_kernel, ((copies, VMEM),), ((transpose(rounded), VMEM),))
     stores = [spread(copied)]
 
-    counts = block_counts.reshape(later)
-    slot_args = tuple((x, SMEM) for x in (source_ids, swap_core(source_ids), counts, swap_core(counts)))
+    slot_args = ((live_ids, SMEM), (swap_core(live_ids), SMEM))
     staged_args = (
         (factor_blocks, HBM),
-        (swap_core(factor_blocks), ANY),
+        (swap_core(factor_blocks), HBM),
         (right_sides, HBM),
-        (swap_core(right_sides), ANY),
+        (swap_core(right_sides), HBM),
         (diag_inverses, HBM),
-        (swap_core(diag_inverses), ANY),
+        (swap_core(diag_inverses), HBM),
     )
     staged_shape = jax.ShapeDtypeStruct((2, slots, width, width), jnp.bfloat16)
     gathered = pltpu.VMEM((rows, slots * width), jnp.bfloat16)

time: 88.9 us -> 68.1 us (0.77)
  local copies, waits for them, and re-layouts: 26 us -> 0.95 us
  waiting for transfers between devices: 12.2 us -> 18.7 us
  starting transfers between devices: 35.2 us -> 32 us
  Pallas kernels: 14.2 us -> 15.8 us
    unnamed x78 -> x4, local copies, waits for them, and re-layouts: 26 us -> 0.95 us
    all_to_all x3, waiting for transfers between devices: 1.7 us -> 10.6 us  [spread(): return lax.all_to_all(x, 'rows', 0, 0, axis_index_groups=same_core)]
    all_to_all x3, starting transfers between devices: 18 us -> 14 us  [spread(): return lax.all_to_all(x, 'rows', 0, 0, axis_index_groups=same_core)]
    ppermute x2, starting transfers between devices: 4 us -> 7.58 us  [paired_shards(): arrived = lax.ppermute(sent, 'cols', [(0, 1), (1, 0)])]
    ppermute x5, starting transfers between devices: 7.36 us -> 4.62 us  [over_both(): return lax.ppermute(x, ('rows', 'cols'), pairs)]
    pallas_call x11, Pallas kernels: 14.2 us -> 15.8 us  [run(): pl.pallas_call(kernel, out_shape=out_shape, in_specs=[spec for _, spec in...]
    ppermute x5, waiting for transfers between devices: 4.35 us -> 2.81 us  [over_both(): return lax.ppermute(x, ('rows', 'cols'), pairs)]
    ppermute x5 -> x4, starting transfers between devices: 5.88 us -> 5.74 us  [swap_core(): return lax.ppermute(x, 'rows', [(i, i ^ 1) for i in range(row_count)])]
  transfers between devices with their start and end apart: 15 -> 14, of which waited for: 7 -> 6; matrix products, arithmetic and copies ran while one was open for 0% -> 0% of each run, Pallas kernels for 10% -> 15%
where the time goes in v11:
time: 68.1 us; the launch traced here: 67.5 us
  starting transfers between devices  32 us (47%)
  waiting for transfers between devices  18.7 us (27%)
  Pallas kernels  15.8 us (23%)
  local copies, waits for them, and re-layouts  0.95 us (1%)
    pallas_call x11, Pallas kernels, run(): pl.pallas_call(kernel, out_shape=out_shape, in_specs=[spec for _, spec in...  15.8 us
    all_to_all x3, starting transfers between devices, spread(): return lax.all_to_all(x, 'rows', 0, 0, axis_index_groups=same_core)  14 us
    all_to_all x3, waiting for transfers between devices, spread(): return lax.all_to_all(x, 'rows', 0, 0, axis_index_groups=same_core)  10.6 us
    ppermute x2, starting transfers between devices, paired_shards(): arrived = lax.ppermute(sent, 'cols', [(0, 1), (1, 0)])  7.58 us
    ppermute x4, starting transfers between devices, swap_core(): return lax.ppermute(x, 'rows', [(i, i ^ 1) for i in range(row_count)])  5.74 us
    ppermute x5, starting transfers between devices, over_both(): return lax.ppermute(x, ('rows', 'cols'), pairs)  4.62 us
    ppermute x2, waiting for transfers between devices, paired_shards(): arrived = lax.ppermute(sent, 'cols', [(0, 1), (1, 0)])  4.49 us
    ppermute x5, waiting for transfers between devices, over_both(): return lax.ppermute(x, ('rows', 'cols'), pairs)  2.81 us
  transfers between devices with their start and end apart: 14, of which 6 were waited for; matrix products, arithmetic and copies ran while one was open for 0% of the time, Pallas kernels for 15%

profile of v11, /device:TPU:0, one launch (start us, length us, event | category | flops | bytes accessed | tf_op | source)
XLA Modules:
  0.0 67.5 jit_solution(18402638875072038867)
XLA Ops:
  0.0 0.5 collective-permute-start.2
  0.5 0.1 collective-permute-start.3
  0.5 0.5 collective-permute-start.4
  1.0 1.6 %shard_map.55 = (f32[64,256]{1,0:T(8,128)S(1)}, bf16[64,256]{1,0:T(8,128)(2,1)S(1)}, s32[3,1,1,8]{3,2,1,0:T(1,128)S(1)}) custom-call(s32[3,1,1,8]{3,2,1,0:T(1,128)} %ids_ref.1, s32[3]{0:T(128)} %bitcast.1, f32[4,1,128,256]{3,2,1,0:T(8,128)} %refs_4_.5, bf16[4,1,256,256]{3,2,1,0:T(8,128)(2,1)} %refs_6_.5), custom_call_target="tpu_custom_call" | custom-call | flops 8388608 | tf_op jit(solution)/shard_map/pallas_call | solution.py:36
  2.6 0.7 collective-permute-start.1
  3.2 0.0 collective-permute-done.1.rounded_ref
  3.2 0.7 %shard_map.56 = bf16[8,64,256]{2,1,0:T(8,128)(2,1)} custom-call(bf16[64,256]{1,0:T(8,128)(2,1)S(1)} %collective-permute-done.1.rounded_ref), custom_call_target="tpu_custom_call" | custom-call | tf_op jit(solution)/shard_map/pallas_call | solution.py:36
  4.0 6.8 %all-to-all-start = ((bf16[8,64,256]{2,1,0:T(8,128)(2,1)}), bf16[8,64,256]{2,1,0:T(8,128)(2,1)S(1)}, u32[]{:S(2)}, u32[]{:S(2)}) async-start(bf16[8,64,256]{2,1,0:T(8,128)(2,1)} %shard_map.56), calls=%async_computation | async-start | bytes 524288 | tf_op jit(solution)/shard_map/all_to_all | solution.py:222
  10.8 4.8 %collective-permute-start = (s32[3,1,1,8]{3,2,1,0:T(1,128)S(1)}, s32[3,1,1,8]{3,2,1,0:T(1,128)S(1)}, u32[]{:S(2)}, u32[]{:S(2)}) collective-permute-start(s32[3,1,1,8]{3,2,1,0:T(1,128)S(1)} %get-tuple-element.31.refs_0_), channel_id=1, source_target_pairs={{0,2},{2,0},{4,6},{6,4},{8,10},{10,8},{12,14},{14,12},{16,18},{18,... | collective-permute-start | bytes 296 | tf_op jit(solution)/shard_map/ppermute | solution.py:216
  15.6 0.8 %collective-permute-done.refs_1_ = s32[3,1,1,8]{3,2,1,0:T(1,128)S(1)} collective-permute-done((s32[3,1,1,8]{3,2,1,0:T(1,128)S(1)}, s32[3,1,1,8]{3,2,1,0:T(1,128)S(1)}, u32[]{:S(2)}, u32[]{:S(2)}) %collective-permute-start) | collective-permute-done | bytes 128 | tf_op jit(solution)/shard_map/ppermute | solution.py:216
  16.4 0.0 collective-permute-done.3.refs_5_
  16.4 0.0 copy-start
  16.4 0.0 collective-permute-done.4.refs_7_
  16.4 0.0 copy-start.1
  16.4 0.8 %copy-done.1 = bf16[4,1,256,256]{3,2,1,0:T(8,128)(2,1)} copy-done((bf16[4,1,256,256]{3,2,1,0:T(8,128)(2,1)}, bf16[4,1,256,256]{3,2,1,0:T(8,128)(2,1)S(1)}, u32[]{:S(2)}) %copy-start.1) | copy-done | bytes 524312
  17.2 0.0 collective-permute-done.2.refs_3_
  17.2 0.1 copy-done
  17.3 2.3 %shard_map.57 = (bf16[2,8,256,256]{3,2,1,0:T(8,128)(2,1)S(1)}, f32[64,256]{1,0:T(8,128)S(1)}, bf16[256,256]{1,0:T(8,128)(2,1)S(1)}) custom-call(s32[3,1,1,8]{3,2,1,0:T(1,128)S(1)} %get-tuple-element.31.refs_0_, s32[3,1,1,8]{3,2,1,0:T(1,128)S(1)} %collective-permute-done.refs_1_, bf16[3,1,1,8,256,256]{5,4,3,2,1,0:T(8,128)(2,1)} %refs_2_.5, ...), custom_call_target="tpu_custom_call" | custom-call | bytes 2097152 | tf_op jit(solution)/shard_map/pallas_call | solution.py:36
  19.6 0.0 all-to-all-done.refs_2_.refs_8_
  19.6 1.1 %shard_map.58 = (f32[64,256]{1,0:T(8,128)S(1)}, f32[64,256]{1,0:T(8,128)S(1)}) custom-call(s32[3,1,1,8]{3,2,1,0:T(1,128)S(1)} %get-tuple-element.31.refs_0_, s32[3,1,1,8]{3,2,1,0:T(1,128)S(1)} %collective-permute-done.refs_1_, bf16[8,64,256]{2,1,0:T(8,128)(2,1)S(1)} %all-to-all-done.refs_2_.refs_8_, bf16[2,8,256,256]{3,2,1,0:T(8,128)(2,1)S(1)} %get-tuple-element.33.refs_3_), custom_call_target="tpu_custom_call" | custom-call | flops 134217728 | bytes 2097152 | tf_op jit(solution)/shard_map/pallas_call | solution.py:36
  20.7 5.5 %collective-permute-start.5 = (f32[64,256]{1,0:T(8,128)S(1)}, f32[64,256]{1,0:T(8,128)S(1)}, u32[]{:S(2)}, u32[]{:S(2)}) collective-permute-start(f32[64,256]{1,0:T(8,128)S(1)} %get-tuple-element.35), channel_id=1, source_target_pairs={{0,1},{1,0},{2,3},{3,2},{4,5},{5,4},{6,7},{7,6},{8,9},{9,8},{10,11... | collective-permute-start | bytes 196616 | tf_op jit(solution)/shard_map/ppermute | solution.py:286
  26.2 2.2 %collective-permute-done.5.arrived_ref = f32[64,256]{1,0:T(8,128)S(1)} collective-permute-done((f32[64,256]{1,0:T(8,128)S(1)}, f32[64,256]{1,0:T(8,128)S(1)}, u32[]{:S(2)}, u32[]{:S(2)}) %collective-permute-start.5) | collective-permute-done | bytes 65568 | tf_op jit(solution)/shard_map/ppermute | solution.py:286
  28.4 0.9 %shard_map.59 = (f32[64,256]{1,0:T(8,128)S(1)}, bf16[8,64,256]{2,1,0:T(8,128)(2,1)}) custom-call(f32[64,256]{1,0:T(8,128)S(1)} %get-tuple-element.34.kept_ref.refs_9_, f32[64,256]{1,0:T(8,128)S(1)} %collective-permute-done.5.arrived_ref, f32[64,256]{1,0:T(8,128)S(1)} %get-tuple-element.36.rhs_ref, bf16[256,256]{1,0:T(8,128)(2,1)S(1)} %get-tuple-element.37.inverse_ref), custom_call_target="tpu_custom_call" | custom-call | flops 8388608 | tf_op jit(solution)/shard_map/pallas_call | solution.py:36
  29.3 3.4 %all-to-all-start.1 = ((bf16[8,64,256]{2,1,0:T(8,128)(2,1)}), bf16[8,64,256]{2,1,0:T(8,128)(2,1)S(1)}, u32[]{:S(2)}, u32[]{:S(2)}) async-start(bf16[8,64,256]{2,1,0:T(8,128)(2,1)} %get-tuple-element.38), calls=%async_computation.1 | async-start | bytes 524288 | tf_op jit(solution)/shard_map/all_to_all | solution.py:222
  32.7 0.7 collective-permute-start.6
  33.4 2.7 %shard_map.60 = (bf16[2,8,256,256]{3,2,1,0:T(8,128)(2,1)S(1)}, f32[64,256]{1,0:T(8,128)S(1)}, bf16[256,256]{1,0:T(8,128)(2,1)S(1)}, f32[64,256]{1,0:T(8,128)S(1)}, f32[64,256]{1,0:T(8,128)S(1)}) custom-call(s32[3,1,1,8]{3,2,1,0:T(1,128)S(1)} %get-tuple-element.31.refs_0_, s32[3,1,1,8]{3,2,1,0:T(1,128)S(1)} %collective-permute-done.refs_1_, ...), custom_call_target="tpu_custom_call" | custom-call | flops 134217728 | bytes 2097152 | tf_op jit(solution)/shard_map/pallas_call | solution.py:36
  36.2 0.0 collective-permute-done.6.refs_6_.refs_1_
  36.2 4.7 %all-to-all-done.1.refs_2_.refs_9_ = bf16[8,64,256]{2,1,0:T(8,128)(2,1)S(1)} async-done(((bf16[8,64,256]{2,1,0:T(8,128)(2,1)}), bf16[8,64,256]{2,1,0:T(8,128)(2,1)S(1)}, u32[]{:S(2)}, u32[]{:S(2)}) %all-to-all-start.1) | async-done | bytes 262176 | tf_op jit(solution)/shard_map/all_to_all | solution.py:222
  40.9 1.1 %shard_map.61 = (f32[64,256]{1,0:T(8,128)S(1)}, f32[64,256]{1,0:T(8,128)S(1)}) custom-call(s32[3,1,1,8]{3,2,1,0:T(1,128)S(1)} %get-tuple-element.31.refs_0_, s32[3,1,1,8]{3,2,1,0:T(1,128)S(1)} %collective-permute-done.refs_1_, bf16[8,64,256]{2,1,0:T(8,128)(2,1)S(1)} %all-to-all-done.1.refs_2_.refs_9_, ...), custom_call_target="tpu_custom_call" | custom-call | flops 134217728 | bytes 2097152 | tf_op jit(solution)/shard_map/pallas_call | solution.py:36
  42.0 2.1 %collective-permute-start.7 = (f32[64,256]{1,0:T(8,128)S(1)}, f32[64,256]{1,0:T(8,128)S(1)}, u32[]{:S(2)}, u32[]{:S(2)}) collective-permute-start(f32[64,256]{1,0:T(8,128)S(1)} %get-tuple-element.44), channel_id=1, source_target_pairs={{0,1},{1,0},{2,3},{3,2},{4,5},{5,4},{6,7},{7,6},{8,9},{9,8},{10,11... | collective-permute-start | bytes 196616 | tf_op jit(solution)/shard_map/ppermute | solution.py:286
  44.0 2.2 %collective-permute-done.7.arrived_ref = f32[64,256]{1,0:T(8,128)S(1)} collective-permute-done((f32[64,256]{1,0:T(8,128)S(1)}, f32[64,256]{1,0:T(8,128)S(1)}, u32[]{:S(2)}, u32[]{:S(2)}) %collective-permute-start.7) | collective-permute-done | bytes 65568 | tf_op jit(solution)/shard_map/ppermute | solution.py:286
  46.3 0.9 %shard_map.62 = (f32[64,256]{1,0:T(8,128)S(1)}, bf16[8,64,256]{2,1,0:T(8,128)(2,1)}) custom-call(f32[64,256]{1,0:T(8,128)S(1)} %get-tuple-element.43.kept_ref.refs_10_, f32[64,256]{1,0:T(8,128)S(1)} %collective-permute-done.7.arrived_ref, f32[64,256]{1,0:T(8,128)S(1)} %get-tuple-element.45.rhs_ref, bf16[256,256]{1,0:T(8,128)(2,1)S(1)} %get-tuple-element.46.inverse_ref), custom_call_target="tpu_custom_call" | custom-call | flops 8388608 | tf_op jit(solution)/shard_map/pallas_call | solution.py:36
  47.2 3.8 %all-to-all-start.2 = ((bf16[8,64,256]{2,1,0:T(8,128)(2,1)}), bf16[8,64,256]{2,1,0:T(8,128)(2,1)S(1)}, u32[]{:S(2)}, u32[]{:S(2)}) async-start(bf16[8,64,256]{2,1,0:T(8,128)(2,1)} %get-tuple-element.47), calls=%async_computation.2 | async-start | bytes 524288 | tf_op jit(solution)/shard_map/all_to_all | solution.py:222
  51.0 0.7 collective-permute-start.8
  51.6 2.7 %shard_map.63 = (bf16[2,8,256,256]{3,2,1,0:T(8,128)(2,1)S(1)}, f32[64,256]{1,0:T(8,128)S(1)}, bf16[256,256]{1,0:T(8,128)(2,1)S(1)}, f32[64,256]{1,0:T(8,128)S(1)}, f32[64,256]{1,0:T(8,128)S(1)}) custom-call(s32[3,1,1,8]{3,2,1,0:T(1,128)S(1)} %get-tuple-element.31.refs_0_, s32[3,1,1,8]{3,2,1,0:T(1,128)S(1)} %collective-permute-done.refs_1_, ...), custom_call_target="tpu_custom_call" | custom-call | flops 134217728 | bytes 2097152 | tf_op jit(solution)/shard_map/pallas_call | solution.py:36
  54.3 0.0 collective-permute-done.8.refs_7_.refs_2_
  54.4 5.8 %all-to-all-done.2.refs_2_ = bf16[8,64,256]{2,1,0:T(8,128)(2,1)S(1)} async-done(((bf16[8,64,256]{2,1,0:T(8,128)(2,1)}), bf16[8,64,256]{2,1,0:T(8,128)(2,1)S(1)}, u32[]{:S(2)}, u32[]{:S(2)}) %all-to-all-start.2) | async-done | bytes 262176 | tf_op jit(solution)/shard_map/all_to_all | solution.py:222
  60.2 1.1 %shard_map.64 = (f32[64,256]{1,0:T(8,128)S(1)}, f32[64,256]{1,0:T(8,128)S(1)}) custom-call(s32[3,1,1,8]{3,2,1,0:T(1,128)S(1)} %get-tuple-element.31.refs_0_, s32[3,1,1,8]{3,2,1,0:T(1,128)S(1)} %collective-permute-done.refs_1_, bf16[8,64,256]{2,1,0:T(8,128)(2,1)S(1)} %all-to-all-done.2.refs_2_, bf16[2,8,256,256]{3,2,1,0:T(8,128)(2,1)S(1)} %get-tuple-element.48.refs_3_, ...), custom_call_target="tpu_custom_call" | custom-call | flops 134217728 | bytes 2097152 | tf_op jit(solution)/shard_map/pallas_call | solution.py:36
  61.2 0.7 collective-permute-start.9
  61.9 2.0 %collective-permute-start.10 = (f32[64,256]{1,0:T(8,128)S(1)}, f32[64,256]{1,0:T(8,128)S(1)}, u32[]{:S(2)}, u32[]{:S(2)}) collective-permute-start(f32[64,256]{1,0:T(8,128)S(1)} %get-tuple-element.53), channel_id=1, source_target_pairs={{0,2},{1,0},{2,3},{3,1},{4,6},{5,4},{6,7},{7,5},{8,10},{9,8},{10,1... | collective-permute-start | bytes 196616 | tf_op jit(solution)/shard_map/ppermute | solution.py:213
  63.9 0.0 collective-permute-done.9.first_ref
  63.9 2.8 %collective-permute-done.10.second_ref = f32[64,256]{1,0:T(8,128)S(1)} collective-permute-done((f32[64,256]{1,0:T(8,128)S(1)}, f32[64,256]{1,0:T(8,128)S(1)}, u32[]{:S(2)}, u32[]{:S(2)}) %collective-permute-start.10) | collective-permute-done | bytes 65568 | tf_op jit(solution)/shard_map/ppermute | solution.py:213
  66.7 0.9 %shard_map.65 = f32[4,1,64,256]{3,2,1,0:T(8,128)} custom-call(f32[64,256]{1,0:T(8,128)S(1)} %collective-permute-done.9.first_ref, f32[64,256]{1,0:T(8,128)S(1)} %collective-permute-done.10.second_ref, f32[64,256]{1,0:T(8,128)S(1)} %get-tuple-element.54.rhs_ref, bf16[256,256]{1,0:T(8,128)(2,1)S(1)} %get-tuple-element.55.inverse_ref, ...), custom_call_target="tpu_custom_call" | custom-call | flops 8388608 | tf_op jit(solution)/shard_map/pallas_call | solution.py:36
Async XLA Ops:
  0.0 17.2 %collective-permute-start.2 = (bf16[3,1,1,8,256,256]{5,4,3,2,1,0:T(8,128)(2,1)}, bf16[3,1,1,8,256,256]{5,4,3,2,1,0:T(8,128)(2,1)}, u32[]{:S(2)}, u32[]{:S(2)}) collective-permute-start(bf16[3,1,1,8,256,256]{5,4,3,2,1,0:T(8,128)(2,1)} %refs_2_.5), channel_id=1, source_target_pairs={{0,2},{2,0},{4,6},{6,4},{8,10},{10,8},{12,14},{14,12},{16,18},{18,... | collective-permute-start | bytes 9437192 | tf_op jit(solution)/shard_map/ppermute | solution.py:216
  0.5 15.9 %collective-permute-start.3 = (f32[4,1,128,256]{3,2,1,0:T(8,128)}, f32[4,1,128,256]{3,2,1,0:T(8,128)S(1)}, u32[]{:S(2)}, u32[]{:S(2)}) collective-permute-start(f32[4,1,128,256]{3,2,1,0:T(8,128)} %refs_4_.5), channel_id=1, source_target_pairs={{0,2},{2,0},{4,6},{6,4},{8,10},{10,8},{12,14},{14,12},{16,18},{18,... | collective-permute-start | bytes 1572872 | tf_op jit(solution)/shard_map/ppermute | solution.py:216
  0.5 15.9 %collective-permute-start.4 = (bf16[4,1,256,256]{3,2,1,0:T(8,128)(2,1)}, bf16[4,1,256,256]{3,2,1,0:T(8,128)(2,1)S(1)}, u32[]{:S(2)}, u32[]{:S(2)}) collective-permute-start(bf16[4,1,256,256]{3,2,1,0:T(8,128)(2,1)} %refs_6_.5), channel_id=1, source_target_pairs={{0,2},{2,0},{4,6},{6,4},{8,10},{10,8},{12,14},{14,12},{16,18},{18,... | collective-permute-start | bytes 1572872 | tf_op jit(solution)/shard_map/ppermute | solution.py:216
  2.6 0.7 collective-permute-start.1
  4.0 15.6 %all-to-all-start = ((bf16[8,64,256]{2,1,0:T(8,128)(2,1)}), bf16[8,64,256]{2,1,0:T(8,128)(2,1)S(1)}, u32[]{:S(2)}, u32[]{:S(2)}) async-start(bf16[8,64,256]{2,1,0:T(8,128)(2,1)} %shard_map.56), calls=%async_computation | async-start | bytes 524288 | tf_op jit(solution)/shard_map/all_to_all | solution.py:222
  10.8 5.6 %collective-permute-start = (s32[3,1,1,8]{3,2,1,0:T(1,128)S(1)}, s32[3,1,1,8]{3,2,1,0:T(1,128)S(1)}, u32[]{:S(2)}, u32[]{:S(2)}) collective-permute-start(s32[3,1,1,8]{3,2,1,0:T(1,128)S(1)} %get-tuple-element.31.refs_0_), channel_id=1, source_target_pairs={{0,2},{2,0},{4,6},{6,4},{8,10},{10,8},{12,14},{14,12},{16,18},{18,... | collective-permute-start | bytes 296 | tf_op jit(solution)/shard_map/ppermute | solution.py:216
  16.4 1.0 %copy-start = (f32[4,1,128,256]{3,2,1,0:T(8,128)}, f32[4,1,128,256]{3,2,1,0:T(8,128)S(1)}, u32[]{:S(2)}) copy-start(f32[4,1,128,256]{3,2,1,0:T(8,128)S(1)} %collective-permute-done.3.refs_5_) | copy-start | bytes 1572868
  16.4 0.8 %copy-start.1 = (bf16[4,1,256,256]{3,2,1,0:T(8,128)(2,1)}, bf16[4,1,256,256]{3,2,1,0:T(8,128)(2,1)S(1)}, u32[]{:S(2)}) copy-start(bf16[4,1,256,256]{3,2,1,0:T(8,128)(2,1)S(1)} %collective-permute-done.4.refs_7_) | copy-start | bytes 1572868
  20.7 7.7 %collective-permute-start.5 = (f32[64,256]{1,0:T(8,128)S(1)}, f32[64,256]{1,0:T(8,128)S(1)}, u32[]{:S(2)}, u32[]{:S(2)}) collective-permute-start(f32[64,256]{1,0:T(8,128)S(1)} %get-tuple-element.35), channel_id=1, source_target_pairs={{0,1},{1,0},{2,3},{3,2},{4,5},{5,4},{6,7},{7,6},{8,9},{9,8},{10,11... | collective-permute-start | bytes 196616 | tf_op jit(solution)/shard_map/ppermute | solution.py:286
  29.3 11.6 %all-to-all-start.1 = ((bf16[8,64,256]{2,1,0:T(8,128)(2,1)}), bf16[8,64,256]{2,1,0:T(8,128)(2,1)S(1)}, u32[]{:S(2)}, u32[]{:S(2)}) async-start(bf16[8,64,256]{2,1,0:T(8,128)(2,1)} %get-tuple-element.38), calls=%async_computation.1 | async-start | bytes 524288 | tf_op jit(solution)/shard_map/all_to_all | solution.py:222
  32.7 3.4 %collective-permute-start.6 = (f32[64,256]{1,0:T(8,128)S(1)}, f32[64,256]{1,0:T(8,128)S(1)}, u32[]{:S(2)}, u32[]{:S(2)}) collective-permute-start(f32[64,256]{1,0:T(8,128)S(1)} %get-tuple-element.42), channel_id=1, source_target_pairs={{0,0},{1,2},{2,1},{3,3},{4,4},{5,6},{6,5},{7,7},{8,8},{9,10},{10,9... | collective-permute-start | bytes 196616 | tf_op jit(solution)/shard_map/ppermute | solution.py:213
  42.0 4.3 %collective-permute-start.7 = (f32[64,256]{1,0:T(8,128)S(1)}, f32[64,256]{1,0:T(8,128)S(1)}, u32[]{:S(2)}, u32[]{:S(2)}) collective-permute-start(f32[64,256]{1,0:T(8,128)S(1)} %get-tuple-element.44), channel_id=1, source_target_pairs={{0,1},{1,0},{2,3},{3,2},{4,5},{5,4},{6,7},{7,6},{8,9},{9,8},{10,11... | collective-permute-start | bytes 196616 | tf_op jit(solution)/shard_map/ppermute | solution.py:286
  47.2 13.0 %all-to-all-start.2 = ((bf16[8,64,256]{2,1,0:T(8,128)(2,1)}), bf16[8,64,256]{2,1,0:T(8,128)(2,1)S(1)}, u32[]{:S(2)}, u32[]{:S(2)}) async-start(bf16[8,64,256]{2,1,0:T(8,128)(2,1)} %get-tuple-element.47), calls=%async_computation.2 | async-start | bytes 524288 | tf_op jit(solution)/shard_map/all_to_all | solution.py:222
  51.0 3.4 %collective-permute-start.8 = (f32[64,256]{1,0:T(8,128)S(1)}, f32[64,256]{1,0:T(8,128)S(1)}, u32[]{:S(2)}, u32[]{:S(2)}) collective-permute-start(f32[64,256]{1,0:T(8,128)S(1)} %get-tuple-element.51), channel_id=1, source_target_pairs={{0,0},{1,2},{2,1},{3,3},{4,4},{5,6},{6,5},{7,7},{8,8},{9,10},{10,9... | collective-permute-start | bytes 196616 | tf_op jit(solution)/shard_map/ppermute | solution.py:213
  61.2 2.7 %collective-permute-start.9 = (f32[64,256]{1,0:T(8,128)S(1)}, f32[64,256]{1,0:T(8,128)S(1)}, u32[]{:S(2)}, u32[]{:S(2)}) collective-permute-start(f32[64,256]{1,0:T(8,128)S(1)} %get-tuple-element.52), channel_id=1, source_target_pairs={{0,0},{1,2},{2,1},{3,3},{4,4},{5,6},{6,5},{7,7},{8,8},{9,10},{10,9... | collective-permute-start | bytes 196616 | tf_op jit(solution)/shard_map/ppermute | solution.py:213
  61.9 4.8 %collective-permute-start.10 = (f32[64,256]{1,0:T(8,128)S(1)}, f32[64,256]{1,0:T(8,128)S(1)}, u32[]{:S(2)}, u32[]{:S(2)}) collective-permute-start(f32[64,256]{1,0:T(8,128)S(1)} %get-tuple-element.53), channel_id=1, source_target_pairs={{0,2},{1,0},{2,3},{3,1},{4,6},{5,4},{6,7},{7,5},{8,10},{9,8},{10,1... | collective-permute-start | bytes 196616 | tf_op jit(solution)/shard_map/ppermute | solution.py:213

commit v12 on v11

--- a/solution.py
+++ b/solution.py
@@ -89,7 +89,8 @@
     rounded_ref[...] = solved.astype(jnp.bfloat16)
 
 
-def copies_kernel(rounded_ref, copies_ref):
+def copies_kernel(rounded_ref, *refs):
+    copies_ref = refs[-1]
     for i in range(copies_ref.shape[0]):
         copies_ref[i] = rounded_ref[...]
 
@@ -240,17 +241,22 @@
         flops=solve_flops,
     )
     finished = [solved]
-    copied, = run(copies_kernel, ((copies, VMEM),), ((transpose(rounded), VMEM),))
+    moved = transpose(rounded)
+    other_ids = swap_core(live_ids)
+    sent_factors, sent_rhs, sent_inverses, _ = lax.optimization_barrier(
+        (factor_blocks, right_sides, diag_inverses, other_ids)
+    )
+    copied, = run(copies_kernel, ((copies, VMEM),), ((moved, VMEM), (other_ids, ANY)))
     stores = [spread(copied)]
 
-    slot_args = ((live_ids, SMEM), (swap_core(live_ids), SMEM))
+    slot_args = ((live_ids, SMEM), (other_ids, SMEM))
     staged_args = (
         (factor_blocks, HBM),
-        (swap_core(factor_blocks), HBM),
+        (swap_core(sent_factors), HBM),
         (right_sides, HBM),
-        (swap_core(right_sides), HBM),
+        (swap_core(sent_rhs), HBM),
         (diag_inverses, HBM),
-        (swap_core(diag_inverses), HBM),
+        (swap_core(sent_inverses), HBM),
     )
     staged_shape = jax.ShapeDtypeStruct((2, slots, width, width), jnp.bfloat16)
     gathered = pltpu.VMEM((rows, slots * width), jnp.bfloat16)

time: 68.1 us -> 69.5 us (1.021)
  waiting for transfers between devices: 18.7 us -> 23.7 us
  starting transfers between devices: 32 us -> 28.4 us
    all_to_all x3, waiting for transfers between devices: 10.6 us -> 15.5 us  [spread(): return lax.all_to_all(x, 'rows', 0, 0, axis_index_groups=same_core)]
    ppermute x4, starting transfers between devices: 5.74 us -> 1.36 us  [swap_core(): return lax.ppermute(x, 'rows', [(i, i ^ 1) for i in range(row_count)])]
  transfers between devices with their start and end apart: 14 -> 14, of which waited for: 6 -> 7; matrix products, arithmetic and copies ran while one was open for 0% -> 0% of each run, Pallas kernels for 15% -> 12%
where the time goes in v12:
time: 69.5 us; the launch traced here: 68.9 us
  starting transfers between devices  28.4 us (41%)
  waiting for transfers between devices  23.7 us (34%)
  Pallas kernels  15.8 us (23%)
  local copies, waits for them, and re-layouts  0.93 us (1%)
    pallas_call x11, Pallas kernels, run(): pl.pallas_call(kernel, out_shape=out_shape, in_specs=[spec for _, spec in...  15.8 us
    all_to_all x3, waiting for transfers between devices, spread(): return lax.all_to_all(x, 'rows', 0, 0, axis_index_groups=same_core)  15.5 us
    all_to_all x3, starting transfers between devices, spread(): return lax.all_to_all(x, 'rows', 0, 0, axis_index_groups=same_core)  14.2 us
    ppermute x2, starting transfers between devices, paired_shards(): arrived = lax.ppermute(sent, 'cols', [(0, 1), (1, 0)])  8.22 us
    ppermute x5, starting transfers between devices, over_both(): return lax.ppermute(x, ('rows', 'cols'), pairs)  4.61 us
    ppermute x2, waiting for transfers between devices, paired_shards(): arrived = lax.ppermute(sent, 'cols', [(0, 1), (1, 0)])  4.49 us
    ppermute x5, waiting for transfers between devices, over_both(): return lax.ppermute(x, ('rows', 'cols'), pairs)  2.81 us
  transfers between devices with their start and end apart: 14, of which 7 were waited for; matrix products, arithmetic and copies ran while one was open for 0% of the time, Pallas kernels for 12%

profile of v12, /device:TPU:0, one launch (start us, length us, event | category | flops | bytes accessed | tf_op | source)
XLA Modules:
  0.0 68.9 jit_solution(14663324281432087189)
XLA Ops:
  0.0 1.6 %shard_map.55 = (f32[64,256]{1,0:T(8,128)S(1)}, bf16[64,256]{1,0:T(8,128)(2,1)S(1)}, s32[3,1,1,8]{3,2,1,0:T(1,128)S(1)}) custom-call(s32[3,1,1,8]{3,2,1,0:T(1,128)} %ids_ref.1, s32[3]{0:T(128)} %bitcast.1, f32[4,1,128,256]{3,2,1,0:T(8,128)} %refs_4_.5, bf16[4,1,256,256]{3,2,1,0:T(8,128)(2,1)} %refs_6_.5), custom_call_target="tpu_custom_call" | custom-call | flops 8388608 | tf_op jit(solution)/shard_map/pallas_call | solution.py:36
  1.6 0.5 collective-permute-start
  2.1 0.8 %collective-permute-done.refs_0_.refs_1_ = s32[3,1,1,8]{3,2,1,0:T(1,128)S(1)} collective-permute-done((s32[3,1,1,8]{3,2,1,0:T(1,128)S(1)}, s32[3,1,1,8]{3,2,1,0:T(1,128)S(1)}, u32[]{:S(2)}, u32[]{:S(2)}) %collective-permute-start) | collective-permute-done | bytes 128 | tf_op jit(solution)/shard_map/ppermute | solution.py:217
  2.9 0.3 collective-permute-start.2
  3.3 0.2 collective-permute-start.3
  3.5 0.3 collective-permute-start.4
  3.8 0.7 collective-permute-start.1
  4.4 0.0 collective-permute-done.1.rounded_ref
  4.5 0.7 %shard_map.56 = bf16[8,64,256]{2,1,0:T(8,128)(2,1)} custom-call(bf16[64,256]{1,0:T(8,128)(2,1)S(1)} %collective-permute-done.1.rounded_ref, s32[3,1,1,8]{3,2,1,0:T(1,128)S(1)} %collective-permute-done.refs_0_.refs_1_), custom_call_target="tpu_custom_call" | custom-call | tf_op jit(solution)/shard_map/pallas_call | solution.py:36
  5.2 7.0 %all-to-all-start = ((bf16[8,64,256]{2,1,0:T(8,128)(2,1)}), bf16[8,64,256]{2,1,0:T(8,128)(2,1)S(1)}, u32[]{:S(2)}, u32[]{:S(2)}) async-start(bf16[8,64,256]{2,1,0:T(8,128)(2,1)} %shard_map.56), calls=%async_computation | async-start | bytes 524288 | tf_op jit(solution)/shard_map/all_to_all | solution.py:223
  12.2 0.0 collective-permute-done.3.refs_5_
  12.2 0.0 copy-start
  12.2 0.0 collective-permute-done.4.refs_7_
  12.2 0.0 copy-start.1
  12.2 0.8 %copy-done.1 = bf16[4,1,256,256]{3,2,1,0:T(8,128)(2,1)} copy-done((bf16[4,1,256,256]{3,2,1,0:T(8,128)(2,1)}, bf16[4,1,256,256]{3,2,1,0:T(8,128)(2,1)S(1)}, u32[]{:S(2)}) %copy-start.1) | copy-done | bytes 524312
  13.0 0.0 collective-permute-done.2.refs_3_
  13.0 0.1 copy-done
  13.1 2.3 %shard_map.57 = (bf16[2,8,256,256]{3,2,1,0:T(8,128)(2,1)S(1)}, f32[64,256]{1,0:T(8,128)S(1)}, bf16[256,256]{1,0:T(8,128)(2,1)S(1)}) custom-call(s32[3,1,1,8]{3,2,1,0:T(1,128)S(1)} %get-tuple-element.34.refs_0_, s32[3,1,1,8]{3,2,1,0:T(1,128)S(1)} %collective-permute-done.refs_0_.refs_1_, bf16[3,1,1,8,256,256]{5,4,3,2,1,0:T(8,128)(2,1)} %refs_2_.5, ...), custom_call_target="tpu_custom_call" | custom-call | bytes 2097152 | tf_op jit(solution)/shard_map/pallas_call | solution.py:36
  15.4 5.0 %all-to-all-done.refs_2_.refs_8_ = bf16[8,64,256]{2,1,0:T(8,128)(2,1)S(1)} async-done(((bf16[8,64,256]{2,1,0:T(8,128)(2,1)}), bf16[8,64,256]{2,1,0:T(8,128)(2,1)S(1)}, u32[]{:S(2)}, u32[]{:S(2)}) %all-to-all-start) | async-done | bytes 262176 | tf_op jit(solution)/shard_map/all_to_all | solution.py:223
  20.4 1.1 %shard_map.58 = (f32[64,256]{1,0:T(8,128)S(1)}, f32[64,256]{1,0:T(8,128)S(1)}) custom-call(s32[3,1,1,8]{3,2,1,0:T(1,128)S(1)} %get-tuple-element.34.refs_0_, s32[3,1,1,8]{3,2,1,0:T(1,128)S(1)} %collective-permute-done.refs_0_.refs_1_, bf16[8,64,256]{2,1,0:T(8,128)(2,1)S(1)} %all-to-all-done.refs_2_.refs_8_, ...), custom_call_target="tpu_custom_call" | custom-call | flops 134217728 | bytes 2097152 | tf_op jit(solution)/shard_map/pallas_call | solution.py:36
  21.4 6.1 %collective-permute-start.5 = (f32[64,256]{1,0:T(8,128)S(1)}, f32[64,256]{1,0:T(8,128)S(1)}, u32[]{:S(2)}, u32[]{:S(2)}) collective-permute-start(f32[64,256]{1,0:T(8,128)S(1)} %get-tuple-element.41), channel_id=1, source_target_pairs={{0,1},{1,0},{2,3},{3,2},{4,5},{5,4},{6,7},{7,6},{8,9},{9,8},{10,11... | collective-permute-start | bytes 196616 | tf_op jit(solution)/shard_map/ppermute | solution.py:292
  27.6 2.2 %collective-permute-done.5.arrived_ref = f32[64,256]{1,0:T(8,128)S(1)} collective-permute-done((f32[64,256]{1,0:T(8,128)S(1)}, f32[64,256]{1,0:T(8,128)S(1)}, u32[]{:S(2)}, u32[]{:S(2)}) %collective-permute-start.5) | collective-permute-done | bytes 65568 | tf_op jit(solution)/shard_map/ppermute | solution.py:292
  29.8 0.9 %shard_map.59 = (f32[64,256]{1,0:T(8,128)S(1)}, bf16[8,64,256]{2,1,0:T(8,128)(2,1)}) custom-call(f32[64,256]{1,0:T(8,128)S(1)} %get-tuple-element.40.kept_ref.refs_9_, f32[64,256]{1,0:T(8,128)S(1)} %collective-permute-done.5.arrived_ref, f32[64,256]{1,0:T(8,128)S(1)} %get-tuple-element.42.rhs_ref, bf16[256,256]{1,0:T(8,128)(2,1)S(1)} %get-tuple-element.43.inverse_ref), custom_call_target="tpu_custom_call" | custom-call | flops 8388608 | tf_op jit(solution)/shard_map/pallas_call | solution.py:36
  30.7 3.4 %all-to-all-start.1 = ((bf16[8,64,256]{2,1,0:T(8,128)(2,1)}), bf16[8,64,256]{2,1,0:T(8,128)(2,1)S(1)}, u32[]{:S(2)}, u32[]{:S(2)}) async-start(bf16[8,64,256]{2,1,0:T(8,128)(2,1)} %get-tuple-element.44), calls=%async_computation.1 | async-start | bytes 524288 | tf_op jit(solution)/shard_map/all_to_all | solution.py:223
  34.1 0.7 collective-permute-start.6
  34.8 2.7 %shard_map.60 = (bf16[2,8,256,256]{3,2,1,0:T(8,128)(2,1)S(1)}, f32[64,256]{1,0:T(8,128)S(1)}, bf16[256,256]{1,0:T(8,128)(2,1)S(1)}, f32[64,256]{1,0:T(8,128)S(1)}, f32[64,256]{1,0:T(8,128)S(1)}) custom-call(s32[3,1,1,8]{3,2,1,0:T(1,128)S(1)} %get-tuple-element.34.refs_0_, s32[3,1,1,8]{3,2,1,0:T(1,128)S(1)} %collective-permute-done.refs_0_.refs_1_, ...), custom_call_target="tpu_custom_call" | custom-call | flops 134217728 | bytes 2097152 | tf_op jit(solution)/shard_map/pallas_call | solution.py:36
  37.5 0.0 collective-permute-done.6.refs_6_.refs_1_
  37.5 4.7 %all-to-all-done.1.refs_2_.refs_9_ = bf16[8,64,256]{2,1,0:T(8,128)(2,1)S(1)} async-done(((bf16[8,64,256]{2,1,0:T(8,128)(2,1)}), bf16[8,64,256]{2,1,0:T(8,128)(2,1)S(1)}, u32[]{:S(2)}, u32[]{:S(2)}) %all-to-all-start.1) | async-done | bytes 262176 | tf_op jit(solution)/shard_map/all_to_all | solution.py:223
  42.3 1.1 %shard_map.61 = (f32[64,256]{1,0:T(8,128)S(1)}, f32[64,256]{1,0:T(8,128)S(1)}) custom-call(s32[3,1,1,8]{3,2,1,0:T(1,128)S(1)} %get-tuple-element.34.refs_0_, s32[3,1,1,8]{3,2,1,0:T(1,128)S(1)} %collective-permute-done.refs_0_.refs_1_, bf16[8,64,256]{2,1,0:T(8,128)(2,1)S(1)} %all-to-all-done.1.refs_2_.refs_9_, ...), custom_call_target="tpu_custom_call" | custom-call | flops 134217728 | bytes 2097152 | tf_op jit(solution)/shard_map/pallas_call | solution.py:36
  43.3 2.1 %collective-permute-start.7 = (f32[64,256]{1,0:T(8,128)S(1)}, f32[64,256]{1,0:T(8,128)S(1)}, u32[]{:S(2)}, u32[]{:S(2)}) collective-permute-start(f32[64,256]{1,0:T(8,128)S(1)} %get-tuple-element.50), channel_id=1, source_target_pairs={{0,1},{1,0},{2,3},{3,2},{4,5},{5,4},{6,7},{7,6},{8,9},{9,8},{10,11... | collective-permute-start | bytes 196616 | tf_op jit(solution)/shard_map/ppermute | solution.py:292
  45.4 2.2 %collective-permute-done.7.arrived_ref = f32[64,256]{1,0:T(8,128)S(1)} collective-permute-done((f32[64,256]{1,0:T(8,128)S(1)}, f32[64,256]{1,0:T(8,128)S(1)}, u32[]{:S(2)}, u32[]{:S(2)}) %collective-permute-start.7) | collective-permute-done | bytes 65568 | tf_op jit(solution)/shard_map/ppermute | solution.py:292
  47.7 0.9 %shard_map.62 = (f32[64,256]{1,0:T(8,128)S(1)}, bf16[8,64,256]{2,1,0:T(8,128)(2,1)}) custom-call(f32[64,256]{1,0:T(8,128)S(1)} %get-tuple-element.49.kept_ref.refs_10_, f32[64,256]{1,0:T(8,128)S(1)} %collective-permute-done.7.arrived_ref, f32[64,256]{1,0:T(8,128)S(1)} %get-tuple-element.51.rhs_ref, bf16[256,256]{1,0:T(8,128)(2,1)S(1)} %get-tuple-element.52.inverse_ref), custom_call_target="tpu_custom_call" | custom-call | flops 8388608 | tf_op jit(solution)/shard_map/pallas_call | solution.py:36
  48.6 3.8 %all-to-all-start.2 = ((bf16[8,64,256]{2,1,0:T(8,128)(2,1)}), bf16[8,64,256]{2,1,0:T(8,128)(2,1)S(1)}, u32[]{:S(2)}, u32[]{:S(2)}) async-start(bf16[8,64,256]{2,1,0:T(8,128)(2,1)} %get-tuple-element.53), calls=%async_computation.2 | async-start | bytes 524288 | tf_op jit(solution)/shard_map/all_to_all | solution.py:223
  52.3 0.7 collective-permute-start.8
  53.0 2.7 %shard_map.63 = (bf16[2,8,256,256]{3,2,1,0:T(8,128)(2,1)S(1)}, f32[64,256]{1,0:T(8,128)S(1)}, bf16[256,256]{1,0:T(8,128)(2,1)S(1)}, f32[64,256]{1,0:T(8,128)S(1)}, f32[64,256]{1,0:T(8,128)S(1)}) custom-call(s32[3,1,1,8]{3,2,1,0:T(1,128)S(1)} %get-tuple-element.34.refs_0_, s32[3,1,1,8]{3,2,1,0:T(1,128)S(1)} %collective-permute-done.refs_0_.refs_1_, ...), custom_call_target="tpu_custom_call" | custom-call | flops 134217728 | bytes 2097152 | tf_op jit(solution)/shard_map/pallas_call | solution.py:36
  55.7 0.0 collective-permute-done.8.refs_7_.refs_2_
  55.7 5.8 %all-to-all-done.2.refs_2_ = bf16[8,64,256]{2,1,0:T(8,128)(2,1)S(1)} async-done(((bf16[8,64,256]{2,1,0:T(8,128)(2,1)}), bf16[8,64,256]{2,1,0:T(8,128)(2,1)S(1)}, u32[]{:S(2)}, u32[]{:S(2)}) %all-to-all-start.2) | async-done | bytes 262176 | tf_op jit(solution)/shard_map/all_to_all | solution.py:223
  61.5 1.1 %shard_map.64 = (f32[64,256]{1,0:T(8,128)S(1)}, f32[64,256]{1,0:T(8,128)S(1)}) custom-call(s32[3,1,1,8]{3,2,1,0:T(1,128)S(1)} %get-tuple-element.34.refs_0_, s32[3,1,1,8]{3,2,1,0:T(1,128)S(1)} %collective-permute-done.refs_0_.refs_1_, bf16[8,64,256]{2,1,0:T(8,128)(2,1)S(1)} %all-to-all-done.2.refs_2_, ...), custom_call_target="tpu_custom_call" | custom-call | flops 134217728 | bytes 2097152 | tf_op jit(solution)/shard_map/pallas_call | solution.py:36
  62.6 0.7 collective-permute-start.9
  63.3 2.0 %collective-permute-start.10 = (f32[64,256]{1,0:T(8,128)S(1)}, f32[64,256]{1,0:T(8,128)S(1)}, u32[]{:S(2)}, u32[]{:S(2)}) collective-permute-start(f32[64,256]{1,0:T(8,128)S(1)} %get-tuple-element.59), channel_id=1, source_target_pairs={{0,2},{1,0},{2,3},{3,1},{4,6},{5,4},{6,7},{7,5},{8,10},{9,8},{10,1... | collective-permute-start | bytes 196616 | tf_op jit(solution)/shard_map/ppermute | solution.py:214
  65.3 0.0 collective-permute-done.9.first_ref
  65.3 2.8 %collective-permute-done.10.second_ref = f32[64,256]{1,0:T(8,128)S(1)} collective-permute-done((f32[64,256]{1,0:T(8,128)S(1)}, f32[64,256]{1,0:T(8,128)S(1)}, u32[]{:S(2)}, u32[]{:S(2)}) %collective-permute-start.10) | collective-permute-done | bytes 65568 | tf_op jit(solution)/shard_map/ppermute | solution.py:214
  68.1 0.9 %shard_map.65 = f32[4,1,64,256]{3,2,1,0:T(8,128)} custom-call(f32[64,256]{1,0:T(8,128)S(1)} %collective-permute-done.9.first_ref, f32[64,256]{1,0:T(8,128)S(1)} %collective-permute-done.10.second_ref, f32[64,256]{1,0:T(8,128)S(1)} %get-tuple-element.60.rhs_ref, bf16[256,256]{1,0:T(8,128)(2,1)S(1)} %get-tuple-element.61.inverse_ref, ...), custom_call_target="tpu_custom_call" | custom-call | flops 8388608 | tf_op jit(solution)/shard_map/pallas_call | solution.py:36
Async XLA Ops:
  1.6 1.3 %collective-permute-start = (s32[3,1,1,8]{3,2,1,0:T(1,128)S(1)}, s32[3,1,1,8]{3,2,1,0:T(1,128)S(1)}, u32[]{:S(2)}, u32[]{:S(2)}) collective-permute-start(s32[3,1,1,8]{3,2,1,0:T(1,128)S(1)} %get-tuple-element.34.refs_0_), channel_id=1, source_target_pairs={{0,2},{2,0},{4,6},{6,4},{8,10},{10,8},{12,14},{14,12},{16,18},{18,... | collective-permute-start | bytes 296 | tf_op jit(solution)/shard_map/ppermute | solution.py:217
  2.9 10.1 %collective-permute-start.2 = (bf16[3,1,1,8,256,256]{5,4,3,2,1,0:T(8,128)(2,1)}, bf16[3,1,1,8,256,256]{5,4,3,2,1,0:T(8,128)(2,1)}, u32[]{:S(2)}, u32[]{:S(2)}) collective-permute-start(bf16[3,1,1,8,256,256]{5,4,3,2,1,0:T(8,128)(2,1)} %refs_2_.5), channel_id=1, source_target_pairs={{0,2},{2,0},{4,6},{6,4},{8,10},{10,8},{12,14},{14,12},{16,18},{18,... | collective-permute-start | bytes 9437192 | tf_op jit(solution)/shard_map/ppermute | solution.py:217
  3.3 8.9 %collective-permute-start.3 = (f32[4,1,128,256]{3,2,1,0:T(8,128)}, f32[4,1,128,256]{3,2,1,0:T(8,128)S(1)}, u32[]{:S(2)}, u32[]{:S(2)}) collective-permute-start(f32[4,1,128,256]{3,2,1,0:T(8,128)} %refs_4_.5), channel_id=1, source_target_pairs={{0,2},{2,0},{4,6},{6,4},{8,10},{10,8},{12,14},{14,12},{16,18},{18,... | collective-permute-start | bytes 1572872 | tf_op jit(solution)/shard_map/ppermute | solution.py:217
  3.5 8.7 %collective-permute-start.4 = (bf16[4,1,256,256]{3,2,1,0:T(8,128)(2,1)}, bf16[4,1,256,256]{3,2,1,0:T(8,128)(2,1)S(1)}, u32[]{:S(2)}, u32[]{:S(2)}) collective-permute-start(bf16[4,1,256,256]{3,2,1,0:T(8,128)(2,1)} %refs_6_.5), channel_id=1, source_target_pairs={{0,2},{2,0},{4,6},{6,4},{8,10},{10,8},{12,14},{14,12},{16,18},{18,... | collective-permute-start | bytes 1572872 | tf_op jit(solution)/shard_map/ppermute | solution.py:217
  3.8 0.7 collective-permute-start.1
  5.2 15.2 %all-to-all-start = ((bf16[8,64,256]{2,1,0:T(8,128)(2,1)}), bf16[8,64,256]{2,1,0:T(8,128)(2,1)S(1)}, u32[]{:S(2)}, u32[]{:S(2)}) async-start(bf16[8,64,256]{2,1,0:T(8,128)(2,1)} %shard_map.56), calls=%async_computation | async-start | bytes 524288 | tf_op jit(solution)/shard_map/all_to_all | solution.py:223
  12.2 1.0 %copy-start = (f32[4,1,128,256]{3,2,1,0:T(8,128)}, f32[4,1,128,256]{3,2,1,0:T(8,128)S(1)}, u32[]{:S(2)}) copy-start(f32[4,1,128,256]{3,2,1,0:T(8,128)S(1)} %collective-permute-done.3.refs_5_) | copy-start | bytes 1572868
  12.2 0.8 %copy-start.1 = (bf16[4,1,256,256]{3,2,1,0:T(8,128)(2,1)}, bf16[4,1,256,256]{3,2,1,0:T(8,128)(2,1)S(1)}, u32[]{:S(2)}) copy-start(bf16[4,1,256,256]{3,2,1,0:T(8,128)(2,1)S(1)} %collective-permute-done.4.refs_7_) | copy-start | bytes 1572868
  21.4 8.4 %collective-permute-start.5 = (f32[64,256]{1,0:T(8,128)S(1)}, f32[64,256]{1,0:T(8,128)S(1)}, u32[]{:S(2)}, u32[]{:S(2)}) collective-permute-start(f32[64,256]{1,0:T(8,128)S(1)} %get-tuple-element.41), channel_id=1, source_target_pairs={{0,1},{1,0},{2,3},{3,2},{4,5},{5,4},{6,7},{7,6},{8,9},{9,8},{10,11... | collective-permute-start | bytes 196616 | tf_op jit(solution)/shard_map/ppermute | solution.py:292
  30.7 11.6 %all-to-all-start.1 = ((bf16[8,64,256]{2,1,0:T(8,128)(2,1)}), bf16[8,64,256]{2,1,0:T(8,128)(2,1)S(1)}, u32[]{:S(2)}, u32[]{:S(2)}) async-start(bf16[8,64,256]{2,1,0:T(8,128)(2,1)} %get-tuple-element.44), calls=%async_computation.1 | async-start | bytes 524288 | tf_op jit(solution)/shard_map/all_to_all | solution.py:223
  34.1 3.4 %collective-permute-start.6 = (f32[64,256]{1,0:T(8,128)S(1)}, f32[64,256]{1,0:T(8,128)S(1)}, u32[]{:S(2)}, u32[]{:S(2)}) collective-permute-start(f32[64,256]{1,0:T(8,128)S(1)} %get-tuple-element.48), channel_id=1, source_target_pairs={{0,0},{1,2},{2,1},{3,3},{4,4},{5,6},{6,5},{7,7},{8,8},{9,10},{10,9... | collective-permute-start | bytes 196616 | tf_op jit(solution)/shard_map/ppermute | solution.py:214
  43.3 4.3 %collective-permute-start.7 = (f32[64,256]{1,0:T(8,128)S(1)}, f32[64,256]{1,0:T(8,128)S(1)}, u32[]{:S(2)}, u32[]{:S(2)}) collective-permute-start(f32[64,256]{1,0:T(8,128)S(1)} %get-tuple-element.50), channel_id=1, source_target_pairs={{0,1},{1,0},{2,3},{3,2},{4,5},{5,4},{6,7},{7,6},{8,9},{9,8},{10,11... | collective-permute-start | bytes 196616 | tf_op jit(solution)/shard_map/ppermute | solution.py:292
  48.6 13.0 %all-to-all-start.2 = ((bf16[8,64,256]{2,1,0:T(8,128)(2,1)}), bf16[8,64,256]{2,1,0:T(8,128)(2,1)S(1)}, u32[]{:S(2)}, u32[]{:S(2)}) async-start(bf16[8,64,256]{2,1,0:T(8,128)(2,1)} %get-tuple-element.53), calls=%async_computation.2 | async-start | bytes 524288 | tf_op jit(solution)/shard_map/all_to_all | solution.py:223
  52.3 3.4 %collective-permute-start.8 = (f32[64,256]{1,0:T(8,128)S(1)}, f32[64,256]{1,0:T(8,128)S(1)}, u32[]{:S(2)}, u32[]{:S(2)}) collective-permute-start(f32[64,256]{1,0:T(8,128)S(1)} %get-tuple-element.57), channel_id=1, source_target_pairs={{0,0},{1,2},{2,1},{3,3},{4,4},{5,6},{6,5},{7,7},{8,8},{9,10},{10,9... | collective-permute-start | bytes 196616 | tf_op jit(solution)/shard_map/ppermute | solution.py:214
  62.6 2.7 %collective-permute-start.9 = (f32[64,256]{1,0:T(8,128)S(1)}, f32[64,256]{1,0:T(8,128)S(1)}, u32[]{:S(2)}, u32[]{:S(2)}) collective-permute-start(f32[64,256]{1,0:T(8,128)S(1)} %get-tuple-element.58), channel_id=1, source_target_pairs={{0,0},{1,2},{2,1},{3,3},{4,4},{5,6},{6,5},{7,7},{8,8},{9,10},{10,9... | collective-permute-start | bytes 196616 | tf_op jit(solution)/shard_map/ppermute | solution.py:214
  63.3 4.8 %collective-permute-start.10 = (f32[64,256]{1,0:T(8,128)S(1)}, f32[64,256]{1,0:T(8,128)S(1)}, u32[]{:S(2)}, u32[]{:S(2)}) collective-permute-start(f32[64,256]{1,0:T(8,128)S(1)} %get-tuple-element.59), channel_id=1, source_target_pairs={{0,2},{1,0},{2,3},{3,1},{4,6},{5,4},{6,7},{7,5},{8,10},{9,8},{10,1... | collective-permute-start | bytes 196616 | tf_op jit(solution)/shard_map/ppermute | solution.py:214

commit v13 on v11

--- a/solution.py
+++ b/solution.py
@@ -63,35 +63,34 @@
     return lax.rem(lax.axis_index("rows"), 2), lax.axis_index("cols")
 
 
-def first_kernel(
-    ids_ref, counts_ref, rhs_ref, inverse_ref, out_ref, rounded_ref, live_ids_ref,
-    ids, counts, rhs, inverse, sems,
-):
-    _, col = own_place()
-    copies = start_copies(
-        [
-            (ids_ref, ids),
-            (counts_ref, counts),
-            (half_of(rhs_ref, 0, col, out_ref.shape[0]), rhs),
-            (inverse_ref.at[0, 0], inverse),
-        ],
-        sems,
-    )
-    copies[0].wait()
-    copies[1].wait()
+def live_kernel(ids_ref, counts_ref, live_ids_ref, ids, counts, sems):
+    for copy in start_copies([(ids_ref, ids), (counts_ref, counts)], sems):
+        copy.wait()
     for l in range(ids.shape[0]):
         for k in range(ids.shape[3]):
             live_ids_ref[l, 0, 0, k] = jnp.where(k < counts[l], ids[l, 0, 0, k], -1)
-    copies[2].wait()
-    copies[3].wait()
-    solved = solve(rhs[...], inverse[...])
+
+
+def both_pairs(level, rows, core, rhs_refs, inverse_refs, rhs, inverse):
+    pairs = [(half_of(ref, level, core, rows), rhs.at[g]) for g, ref in enumerate(rhs_refs)]
+    return pairs + [(ref.at[level, 0], inverse.at[g]) for g, ref in enumerate(inverse_refs)]
+
+
+def first_kernel(
+    rhs_ref, other_rhs_ref, inverse_ref, other_inverse_ref, out_ref, copies_ref, rhs, inverse, sems
+):
+    core, col = own_place()
+    straight = core == col
+    pairs = both_pairs(
+        0, out_ref.shape[0], core, (rhs_ref, other_rhs_ref), (inverse_ref, other_inverse_ref), rhs, inverse
+    )
+    for copy in start_copies(pairs, sems):
+        copy.wait()
+    solved = solve(jnp.where(straight, rhs[0], rhs[1]), jnp.where(straight, inverse[0], inverse[1]))
     out_ref[...] = solved
-    rounded_ref[...] = solved.astype(jnp.bfloat16)
-
-
-def copies_kernel(rounded_ref, copies_ref):
+    rounded = solved.astype(jnp.bfloat16)
     for i in range(copies_ref.shape[0]):
-        copies_ref[i] = rounded_ref[...]
+        copies_ref[i] = rounded
 
 
 def slot_sum(level, store_level, chips, ids_ref, store_ref, factor_ref, gathered):
@@ -123,12 +122,9 @@
     straight = core == col
     rows = own_rhs_ref.shape[0]
     if inner:
-        pairs = [
-            (half_of(rhs_ref, level, core, rows), rhs.at[0]),
-            (half_of(other_rhs_ref, level, core, rows), rhs.at[1]),
-            (inverse_ref.at[level, 0], inverse.at[0]),
-            (other_inverse_ref.at[level, 0], inverse.at[1]),
-        ]
+        pairs = both_pairs(
+            level, rows, core, (rhs_ref, other_rhs_ref), (inverse_ref, other_inverse_ref), rhs, inverse
+        )
     else:
         pairs = [
             (half_of(rhs_ref, level, col, rows), own_rhs_ref),
@@ -198,7 +194,6 @@
     later = level_count - 1
     same_core = [[2 * j + k for j in range(chips)] for k in range(2)]
     part = jax.ShapeDtypeStruct((rows, width), jnp.float32)
-    rounded_part = jax.ShapeDtypeStruct((rows, width), jnp.bfloat16)
     square = jax.ShapeDtypeStruct((width, width), jnp.bfloat16)
     copies = jax.ShapeDtypeStruct((chips, rows, width), jnp.bfloat16)
     solve_flops = 2 * rows * width * width
@@ -221,36 +216,42 @@
     def spread(x):
         return lax.all_to_all(x, "rows", 0, 0, axis_index_groups=same_core)
 
-    counts = block_counts.reshape(later)
-    solved, rounded, live_ids = run(
+    other_inverses, other_rhs = swap_core(diag_inverses), swap_core(right_sides)
+    solved, copied = run(
         first_kernel,
-        (
-            (part, VMEM),
-            (rounded_part, VMEM),
-            (jax.ShapeDtypeStruct(source_ids.shape, source_ids.dtype), SMEM),
+        ((part, VMEM), (copies, VMEM)),
+        ((right_sides, HBM), (other_rhs, ANY), (diag_inverses, HBM), (other_inverses, ANY)),
+        scratch=(
+            pltpu.VMEM((2, rows, width), jnp.float32),
+            pltpu.VMEM((2, width, width), jnp.bfloat16),
+            pltpu.SemaphoreType.DMA((4,)),
         ),
-        ((source_ids, HBM), (counts, HBM), (right_sides, HBM), (diag_inverses, HBM)),
+        flops=solve_flops,
+    )
+    finished = [transpose(solved)]
+    stores = [spread(copied)]
+
+    first_ids, counts, _ = lax.optimization_barrier((source_ids, block_counts.reshape(later), solved))
+    live_ids, = run(
+        live_kernel,
+        ((jax.ShapeDtypeStruct(source_ids.shape, source_ids.dtype), SMEM),),
+        ((first_ids, HBM), (counts, HBM)),
         scratch=(
             pltpu.SMEM(source_ids.shape, source_ids.dtype),
             pltpu.SMEM(counts.shape, counts.dtype),
-            pltpu.VMEM((rows, width), jnp.float32),
-            pltpu.VMEM((width, width), jnp.bfloat16),
-            pltpu.SemaphoreType.DMA((4,)),
+            pltpu.SemaphoreType.DMA((2,)),
         ),
-        flops=solve_flops,
-    )
-    finished = [solved]
-    copied, = run(copies_kernel, ((copies, VMEM),), ((transpose(rounded), VMEM),))
-    stores = [spread(copied)]
-
-    slot_args = ((live_ids, SMEM), (swap_core(live_ids), SMEM))
+    )
+    other_ids = swap_core(live_ids)
+    sent_factors, _, _ = lax.optimization_barrier((factor_blocks, other_rhs, other_inverses))
+    slot_args = ((live_ids, SMEM), (other_ids, SMEM))
     staged_args = (
         (factor_blocks, HBM),
-        (swap_core(factor_blocks), HBM),
+        (swap_core(sent_factors), HBM),
         (right_sides, HBM),
-        (swap_core(right_sides), HBM),
+        (other_rhs, HBM),
         (diag_inverses, HBM),
-        (swap_core(diag_inverses), HBM),
+        (other_inverses, HBM),
     )
     staged_shape = jax.ShapeDtypeStruct((2, slots, width, width), jnp.bfloat16)
     gathered = pltpu.VMEM((rows, slots * width), jnp.bfloat16)
@@ -276,7 +277,7 @@
             slot_args
             + ((stores[-1], VMEM), (staged, FIXED))
             + tuple((x, VMEM) for x in older)
-            + tuple((x, ANY) for x in finished[1:]),
+            + tuple((x, ANY) for x in finished),
             scratch=(gathered,),
             flops=2 * slots * solve_flops,
             transferred=2 * slots * width * width * 2,

time: 68.1 us -> 67.8 us (level)
  starting transfers between devices: 32 us -> 26.1 us
  waiting for transfers between devices: 18.7 us -> 23.5 us
  Pallas kernels: 15.8 us -> 16.7 us
    ppermute x2, starting transfers between devices: 7.58 us -> 2 us  [paired_shards(): arrived = lax.ppermute(sent, 'cols', [(0, 1), (1, 0)])]
    ppermute x4, starting transfers between devices: 5.74 us -> 3 us  [swap_core(): return lax.ppermute(x, 'rows', [(i, i ^ 1) for i in range(row_count)])]
    ppermute x4, waiting for transfers between devices: 0.83 us -> 3.26 us  [swap_core(): return lax.ppermute(x, 'rows', [(i, i ^ 1) for i in range(row_count)])]
    ppermute x2, waiting for transfers between devices: 4.49 us -> 6.66 us  [paired_shards(): arrived = lax.ppermute(sent, 'cols', [(0, 1), (1, 0)])]
    all_to_all x3, starting transfers between devices: 14 us -> 16 us  [spread(): return lax.all_to_all(x, 'rows', 0, 0, axis_index_groups=same_core)]
    pallas_call x11, Pallas kernels: 15.8 us -> 16.7 us  [run(): pl.pallas_call(kernel, out_shape=out_shape, in_specs=[spec for _, spec in...]
  transfers between devices with their start and end apart: 14 -> 14, of which waited for: 6 -> 9; matrix products, arithmetic and copies ran while one was open for 0% -> 0% of each run, Pallas kernels for 15% -> 16%
where the time goes in v13:
time: 67.8 us; the launch traced here: 67.1 us
  starting transfers between devices  26.1 us (38%)
  waiting for transfers between devices  23.5 us (35%)
  Pallas kernels  16.7 us (25%)
    pallas_call x11, Pallas kernels, run(): pl.pallas_call(kernel, out_shape=out_shape, in_specs=[spec for _, spec in...  16.7 us
    all_to_all x3, starting transfers between devices, spread(): return lax.all_to_all(x, 'rows', 0, 0, axis_index_groups=same_core)  16 us
    all_to_all x3, waiting for transfers between devices, spread(): return lax.all_to_all(x, 'rows', 0, 0, axis_index_groups=same_core)  10.7 us
    ppermute x2, waiting for transfers between devices, paired_shards(): arrived = lax.ppermute(sent, 'cols', [(0, 1), (1, 0)])  6.66 us
    ppermute x5, starting transfers between devices, over_both(): return lax.ppermute(x, ('rows', 'cols'), pairs)  5.18 us
    ppermute x4, waiting for transfers between devices, swap_core(): return lax.ppermute(x, 'rows', [(i, i ^ 1) for i in range(row_count)])  3.26 us
    ppermute x4, starting transfers between devices, swap_core(): return lax.ppermute(x, 'rows', [(i, i ^ 1) for i in range(row_count)])  3 us
    ppermute x5, waiting for transfers between devices, over_both(): return lax.ppermute(x, ('rows', 'cols'), pairs)  2.81 us
  transfers between devices with their start and end apart: 14, of which 9 were waited for; matrix products, arithmetic and copies ran while one was open for 0% of the time, Pallas kernels for 16%

profile of v13, /device:TPU:0, one launch (start us, length us, event | category | flops | bytes accessed | tf_op | source)
XLA Modules:
  0.0 67.1 jit_solution(1933592111039818827)
XLA Ops:
  0.0 0.5 collective-permute-start
  0.5 0.1 collective-permute-start.1
  0.5 1.7 %collective-permute-done.other_rhs_ref.refs_5_ = f32[4,1,128,256]{3,2,1,0:T(8,128)S(1)} collective-permute-done((f32[4,1,128,256]{3,2,1,0:T(8,128)}, f32[4,1,128,256]{3,2,1,0:T(8,128)S(1)}, u32[]{:S(2)}, u32[]{:S(2)}) %collective-permute-start) | collective-permute-done | bytes 524320 | tf_op jit(solution)/shard_map/ppermute | solution.py:211
  2.2 0.0 copy-start
  2.2 0.7 %collective-permute-done.1.other_inverse_ref.refs_7_ = bf16[4,1,256,256]{3,2,1,0:T(8,128)(2,1)S(1)} collective-permute-done((bf16[4,1,256,256]{3,2,1,0:T(8,128)(2,1)}, bf16[4,1,256,256]{3,2,1,0:T(8,128)(2,1)S(1)}, u32[]{:S(2)}, u32[]{:S(2)}) %collective-permute-start.1) | collective-permute-done | bytes 524320 | tf_op jit(solution)/shard_map/ppermute | solution.py:211
  3.0 0.0 copy-start.1
  3.0 0.4 collective-permute-start.3
  3.3 1.9 %shard_map.55 = (f32[64,256]{1,0:T(8,128)}, bf16[8,64,256]{2,1,0:T(8,128)(2,1)}) custom-call(f32[4,1,128,256]{3,2,1,0:T(8,128)} %refs_4_.5, f32[4,1,128,256]{3,2,1,0:T(8,128)S(1)} %collective-permute-done.other_rhs_ref.refs_5_, bf16[4,1,256,256]{3,2,1,0:T(8,128)(2,1)} %refs_6_.5, bf16[4,1,256,256]{3,2,1,0:T(8,128)(2,1)S(1)} %collective-permute-done.1.other_inverse_ref.refs_7_), custom_call_target="tpu_custom_call" | custom-call | flops 8388608 | tf_op jit(solution)/shard_map/pallas_call | solution.py:36
  5.2 7.0 %all-to-all-start = ((bf16[8,64,256]{2,1,0:T(8,128)(2,1)}), bf16[8,64,256]{2,1,0:T(8,128)(2,1)S(1)}, u32[]{:S(2)}, u32[]{:S(2)}) async-start(bf16[8,64,256]{2,1,0:T(8,128)(2,1)} %get-tuple-element.36), calls=%async_computation | async-start | bytes 524288 | tf_op jit(solution)/shard_map/all_to_all | solution.py:217
  12.2 1.5 %collective-permute-start.4 = (f32[64,256]{1,0:T(8,128)}, f32[64,256]{1,0:T(8,128)S(1)}, u32[]{:S(2)}, u32[]{:S(2)}) collective-permute-start(f32[64,256]{1,0:T(8,128)} %get-tuple-element.33), channel_id=1, source_target_pairs={{0,0},{1,2},{2,1},{3,3},{4,4},{5,6},{6,5},{7,7},{8,8},{9,10},{10,9... | collective-permute-start | bytes 196616 | tf_op jit(solution)/shard_map/ppermute | solution.py:208
  13.7 1.3 %shard_map.56.refs_0_ = s32[3,1,1,8]{3,2,1,0:T(1,128)S(1)} custom-call(s32[3,1,1,8]{3,2,1,0:T(1,128)} %ids_ref, s32[3]{0:T(128)} %bitcast.1), custom_call_target="tpu_custom_call" | custom-call | tf_op jit(solution)/shard_map/pallas_call | solution.py:36
  15.1 2.1 %collective-permute-start.2 = (s32[3,1,1,8]{3,2,1,0:T(1,128)S(1)}, s32[3,1,1,8]{3,2,1,0:T(1,128)S(1)}, u32[]{:S(2)}, u32[]{:S(2)}) collective-permute-start(s32[3,1,1,8]{3,2,1,0:T(1,128)S(1)} %shard_map.56.refs_0_), channel_id=1, source_target_pairs={{0,2},{2,0},{4,6},{6,4},{8,10},{10,8},{12,14},{14,12},{16,18},{18,... | collective-permute-start | bytes 296 | tf_op jit(solution)/shard_map/ppermute | solution.py:211
  17.2 0.8 %collective-permute-done.2.refs_1_ = s32[3,1,1,8]{3,2,1,0:T(1,128)S(1)} collective-permute-done((s32[3,1,1,8]{3,2,1,0:T(1,128)S(1)}, s32[3,1,1,8]{3,2,1,0:T(1,128)S(1)}, u32[]{:S(2)}, u32[]{:S(2)}) %collective-permute-start.2) | collective-permute-done | bytes 128 | tf_op jit(solution)/shard_map/ppermute | solution.py:211
  18.0 0.0 collective-permute-done.3.refs_3_
  18.0 0.0 copy-done
  18.0 0.0 copy-done.1
  18.0 2.3 %shard_map.57 = (bf16[2,8,256,256]{3,2,1,0:T(8,128)(2,1)S(1)}, f32[64,256]{1,0:T(8,128)S(1)}, bf16[256,256]{1,0:T(8,128)(2,1)S(1)}) custom-call(s32[3,1,1,8]{3,2,1,0:T(1,128)S(1)} %shard_map.56.refs_0_, s32[3,1,1,8]{3,2,1,0:T(1,128)S(1)} %collective-permute-done.2.refs_1_, bf16[3,1,1,8,256,256]{5,4,3,2,1,0:T(8,128)(2,1)} %refs_2_.5, ...), custom_call_target="tpu_custom_call" | custom-call | bytes 2097152 | tf_op jit(solution)/shard_map/pallas_call | solution.py:36
  20.3 0.0 copy-start.2
  20.3 0.6 copy-done.2
  21.0 0.0 collective-permute-done.4.refs_4_.refs_6_.refs_0_
  21.0 0.0 copy-start.3
  21.0 0.7 %all-to-all-done.refs_2_.refs_8_ = bf16[8,64,256]{2,1,0:T(8,128)(2,1)S(1)} async-done(((bf16[8,64,256]{2,1,0:T(8,128)(2,1)}), bf16[8,64,256]{2,1,0:T(8,128)(2,1)S(1)}, u32[]{:S(2)}, u32[]{:S(2)}) %all-to-all-start) | async-done | bytes 262176 | tf_op jit(solution)/shard_map/all_to_all | solution.py:217
  21.6 1.1 %shard_map.58 = (f32[64,256]{1,0:T(8,128)S(1)}, f32[64,256]{1,0:T(8,128)S(1)}) custom-call(s32[3,1,1,8]{3,2,1,0:T(1,128)S(1)} %shard_map.56.refs_0_, s32[3,1,1,8]{3,2,1,0:T(1,128)S(1)} %collective-permute-done.2.refs_1_, bf16[8,64,256]{2,1,0:T(8,128)(2,1)S(1)} %all-to-all-done.refs_2_.refs_8_, bf16[2,8,256,256]{3,2,1,0:T(8,128)(2,1)S(1)} %get-tuple-element.38.refs_3_, ...), custom_call_target="tpu_custom_call" | custom-call | flops 134217728 | bytes 2097152 | tf_op jit(solution)/shard_map/pallas_call | solution.py:36
  22.7 1.6 %collective-permute-start.5 = (f32[64,256]{1,0:T(8,128)S(1)}, f32[64,256]{1,0:T(8,128)S(1)}, u32[]{:S(2)}, u32[]{:S(2)}) collective-permute-start(f32[64,256]{1,0:T(8,128)S(1)} %get-tuple-element.40), channel_id=1, source_target_pairs={{0,1},{1,0},{2,3},{3,2},{4,5},{5,4},{6,7},{7,6},{8,9},{9,8},{10,11... | collective-permute-start | bytes 196616 | tf_op jit(solution)/shard_map/ppermute | solution.py:287
  24.3 2.7 %collective-permute-done.5.arrived_ref = f32[64,256]{1,0:T(8,128)S(1)} collective-permute-done((f32[64,256]{1,0:T(8,128)S(1)}, f32[64,256]{1,0:T(8,128)S(1)}, u32[]{:S(2)}, u32[]{:S(2)}) %collective-permute-start.5) | collective-permute-done | bytes 65568 | tf_op jit(solution)/shard_map/ppermute | solution.py:287
  27.0 0.0 copy-done.3
  27.0 0.9 %shard_map.59 = (f32[64,256]{1,0:T(8,128)S(1)}, bf16[8,64,256]{2,1,0:T(8,128)(2,1)}) custom-call(f32[64,256]{1,0:T(8,128)S(1)} %get-tuple-element.39.kept_ref.refs_9_, f32[64,256]{1,0:T(8,128)S(1)} %collective-permute-done.5.arrived_ref, f32[64,256]{1,0:T(8,128)S(1)} %get-tuple-element.41.rhs_ref, bf16[256,256]{1,0:T(8,128)(2,1)S(1)} %copy-done.3), custom_call_target="tpu_custom_call" | custom-call | flops 8388608 | tf_op jit(solution)/shard_map/pallas_call | solution.py:36
  27.9 5.4 %all-to-all-start.1 = ((bf16[8,64,256]{2,1,0:T(8,128)(2,1)}), bf16[8,64,256]{2,1,0:T(8,128)(2,1)S(1)}, u32[]{:S(2)}, u32[]{:S(2)}) async-start(bf16[8,64,256]{2,1,0:T(8,128)(2,1)} %get-tuple-element.43), calls=%async_computation.1 | async-start | bytes 524288 | tf_op jit(solution)/shard_map/all_to_all | solution.py:217
  33.3 0.7 collective-permute-start.6
  34.0 2.7 %shard_map.60 = (bf16[2,8,256,256]{3,2,1,0:T(8,128)(2,1)S(1)}, f32[64,256]{1,0:T(8,128)S(1)}, bf16[256,256]{1,0:T(8,128)(2,1)S(1)}, f32[64,256]{1,0:T(8,128)S(1)}, f32[64,256]{1,0:T(8,128)S(1)}) custom-call(s32[3,1,1,8]{3,2,1,0:T(1,128)S(1)} %shard_map.56.refs_0_, s32[3,1,1,8]{3,2,1,0:T(1,128)S(1)} %collective-permute-done.2.refs_1_, ...), custom_call_target="tpu_custom_call" | custom-call | flops 134217728 | bytes 2097152 | tf_op jit(solution)/shard_map/pallas_call | solution.py:36
  36.7 0.0 collective-permute-done.6.refs_7_.refs_1_
  36.7 5.2 %all-to-all-done.1.refs_2_.refs_9_ = bf16[8,64,256]{2,1,0:T(8,128)(2,1)S(1)} async-done(((bf16[8,64,256]{2,1,0:T(8,128)(2,1)}), bf16[8,64,256]{2,1,0:T(8,128)(2,1)S(1)}, u32[]{:S(2)}, u32[]{:S(2)}) %all-to-all-start.1) | async-done | bytes 262176 | tf_op jit(solution)/shard_map/all_to_all | solution.py:217
  41.9 1.1 %shard_map.61 = (f32[64,256]{1,0:T(8,128)S(1)}, f32[64,256]{1,0:T(8,128)S(1)}) custom-call(s32[3,1,1,8]{3,2,1,0:T(1,128)S(1)} %shard_map.56.refs_0_, s32[3,1,1,8]{3,2,1,0:T(1,128)S(1)} %collective-permute-done.2.refs_1_, bf16[8,64,256]{2,1,0:T(8,128)(2,1)S(1)} %all-to-all-done.1.refs_2_.refs_9_, bf16[2,8,256,256]{3,2,1,0:T(8,128)(2,1)S(1)} %get-tuple-element.44.refs_3_, ...), custom_call_target="tpu_custom_call" | custom-call | flops 134217728 | bytes 2097152 | tf_op jit(solution)/shard_map/pallas_call | solution.py:36
  43.0 0.4 collective-permute-start.7
  43.4 3.9 %collective-permute-done.7.arrived_ref = f32[64,256]{1,0:T(8,128)S(1)} collective-permute-done((f32[64,256]{1,0:T(8,128)S(1)}, f32[64,256]{1,0:T(8,128)S(1)}, u32[]{:S(2)}, u32[]{:S(2)}) %collective-permute-start.7) | collective-permute-done | bytes 65568 | tf_op jit(solution)/shard_map/ppermute | solution.py:287
  47.3 0.9 %shard_map.62 = (f32[64,256]{1,0:T(8,128)S(1)}, bf16[8,64,256]{2,1,0:T(8,128)(2,1)}) custom-call(f32[64,256]{1,0:T(8,128)S(1)} %get-tuple-element.48.kept_ref.refs_10_, f32[64,256]{1,0:T(8,128)S(1)} %collective-permute-done.7.arrived_ref, f32[64,256]{1,0:T(8,128)S(1)} %get-tuple-element.50.rhs_ref, bf16[256,256]{1,0:T(8,128)(2,1)S(1)} %get-tuple-element.51.inverse_ref), custom_call_target="tpu_custom_call" | custom-call | flops 8388608 | tf_op jit(solution)/shard_map/pallas_call | solution.py:36
  48.2 3.6 %all-to-all-start.2 = ((bf16[8,64,256]{2,1,0:T(8,128)(2,1)}), bf16[8,64,256]{2,1,0:T(8,128)(2,1)S(1)}, u32[]{:S(2)}, u32[]{:S(2)}) async-start(bf16[8,64,256]{2,1,0:T(8,128)(2,1)} %get-tuple-element.52), calls=%async_computation.2 | async-start | bytes 524288 | tf_op jit(solution)/shard_map/all_to_all | solution.py:217
  51.8 0.7 collective-permute-start.8
  52.4 2.7 %shard_map.63 = (bf16[2,8,256,256]{3,2,1,0:T(8,128)(2,1)S(1)}, f32[64,256]{1,0:T(8,128)S(1)}, bf16[256,256]{1,0:T(8,128)(2,1)S(1)}, f32[64,256]{1,0:T(8,128)S(1)}, f32[64,256]{1,0:T(8,128)S(1)}) custom-call(s32[3,1,1,8]{3,2,1,0:T(1,128)S(1)} %shard_map.56.refs_0_, s32[3,1,1,8]{3,2,1,0:T(1,128)S(1)} %collective-permute-done.2.refs_1_, ...), custom_call_target="tpu_custom_call" | custom-call | flops 134217728 | bytes 2097152 | tf_op jit(solution)/shard_map/pallas_call | solution.py:36
  55.2 0.0 collective-permute-done.8.refs_8_.refs_2_
  55.2 4.8 %all-to-all-done.2.refs_2_ = bf16[8,64,256]{2,1,0:T(8,128)(2,1)S(1)} async-done(((bf16[8,64,256]{2,1,0:T(8,128)(2,1)}), bf16[8,64,256]{2,1,0:T(8,128)(2,1)S(1)}, u32[]{:S(2)}, u32[]{:S(2)}) %all-to-all-start.2) | async-done | bytes 262176 | tf_op jit(solution)/shard_map/all_to_all | solution.py:217
  60.0 1.1 %shard_map.64 = (f32[64,256]{1,0:T(8,128)S(1)}, f32[64,256]{1,0:T(8,128)S(1)}) custom-call(s32[3,1,1,8]{3,2,1,0:T(1,128)S(1)} %shard_map.56.refs_0_, s32[3,1,1,8]{3,2,1,0:T(1,128)S(1)} %collective-permute-done.2.refs_1_, bf16[8,64,256]{2,1,0:T(8,128)(2,1)S(1)} %all-to-all-done.2.refs_2_, bf16[2,8,256,256]{3,2,1,0:T(8,128)(2,1)S(1)} %get-tuple-element.53.refs_3_, ...), custom_call_target="tpu_custom_call" | custom-call | flops 134217728 | bytes 2097152 | tf_op jit(solution)/shard_map/pallas_call | solution.py:36
  61.1 0.7 collective-permute-start.9
  61.7 1.7 %collective-permute-start.10 = (f32[64,256]{1,0:T(8,128)S(1)}, f32[64,256]{1,0:T(8,128)S(1)}, u32[]{:S(2)}, u32[]{:S(2)}) collective-permute-start(f32[64,256]{1,0:T(8,128)S(1)} %get-tuple-element.58), channel_id=1, source_target_pairs={{0,2},{1,0},{2,3},{3,1},{4,6},{5,4},{6,7},{7,5},{8,10},{9,8},{10,1... | collective-permute-start | bytes 196616 | tf_op jit(solution)/shard_map/ppermute | solution.py:208
  63.5 0.0 collective-permute-done.9.first_ref
  63.5 2.8 %collective-permute-done.10.second_ref = f32[64,256]{1,0:T(8,128)S(1)} collective-permute-done((f32[64,256]{1,0:T(8,128)S(1)}, f32[64,256]{1,0:T(8,128)S(1)}, u32[]{:S(2)}, u32[]{:S(2)}) %collective-permute-start.10) | collective-permute-done | bytes 65568 | tf_op jit(solution)/shard_map/ppermute | solution.py:208
  66.3 0.9 %shard_map.65 = f32[4,1,64,256]{3,2,1,0:T(8,128)} custom-call(f32[64,256]{1,0:T(8,128)S(1)} %collective-permute-done.9.first_ref, f32[64,256]{1,0:T(8,128)S(1)} %collective-permute-done.10.second_ref, f32[64,256]{1,0:T(8,128)S(1)} %get-tuple-element.59.rhs_ref, bf16[256,256]{1,0:T(8,128)(2,1)S(1)} %get-tuple-element.60.inverse_ref, ...), custom_call_target="tpu_custom_call" | custom-call | flops 8388608 | tf_op jit(solution)/shard_map/pallas_call | solution.py:36
Async XLA Ops:
  0.0 2.2 %collective-permute-start = (f32[4,1,128,256]{3,2,1,0:T(8,128)}, f32[4,1,128,256]{3,2,1,0:T(8,128)S(1)}, u32[]{:S(2)}, u32[]{:S(2)}) collective-permute-start(f32[4,1,128,256]{3,2,1,0:T(8,128)} %refs_4_.5), channel_id=1, source_target_pairs={{0,2},{2,0},{4,6},{6,4},{8,10},{10,8},{12,14},{14,12},{16,18},{18,... | collective-permute-start | bytes 1572872 | tf_op jit(solution)/shard_map/ppermute | solution.py:211
  0.5 2.5 %collective-permute-start.1 = (bf16[4,1,256,256]{3,2,1,0:T(8,128)(2,1)}, bf16[4,1,256,256]{3,2,1,0:T(8,128)(2,1)S(1)}, u32[]{:S(2)}, u32[]{:S(2)}) collective-permute-start(bf16[4,1,256,256]{3,2,1,0:T(8,128)(2,1)} %refs_6_.5), channel_id=1, source_target_pairs={{0,2},{2,0},{4,6},{6,4},{8,10},{10,8},{12,14},{14,12},{16,18},{18,... | collective-permute-start | bytes 1572872 | tf_op jit(solution)/shard_map/ppermute | solution.py:211
  2.2 15.8 %copy-start = (f32[4,1,128,256]{3,2,1,0:T(8,128)}, f32[4,1,128,256]{3,2,1,0:T(8,128)S(1)}, u32[]{:S(2)}) copy-start(f32[4,1,128,256]{3,2,1,0:T(8,128)S(1)} %collective-permute-done.other_rhs_ref.refs_5_) | copy-start | bytes 1572868
  3.0 15.1 %copy-start.1 = (bf16[4,1,256,256]{3,2,1,0:T(8,128)(2,1)}, bf16[4,1,256,256]{3,2,1,0:T(8,128)(2,1)S(1)}, u32[]{:S(2)}) copy-start(bf16[4,1,256,256]{3,2,1,0:T(8,128)(2,1)S(1)} %collective-permute-done.1.other_inverse_ref.refs_7_) | copy-start | bytes 1572868
  3.0 15.1 %collective-permute-start.3 = (bf16[3,1,1,8,256,256]{5,4,3,2,1,0:T(8,128)(2,1)}, bf16[3,1,1,8,256,256]{5,4,3,2,1,0:T(8,128)(2,1)}, u32[]{:S(2)}, u32[]{:S(2)}) collective-permute-start(bf16[3,1,1,8,256,256]{5,4,3,2,1,0:T(8,128)(2,1)} %refs_2_.5), channel_id=1, source_target_pairs={{0,2},{2,0},{4,6},{6,4},{8,10},{10,8},{12,14},{14,12},{16,18},{18,... | collective-permute-start | bytes 9437192 | tf_op jit(solution)/shard_map/ppermute | solution.py:211
  5.2 16.4 %all-to-all-start = ((bf16[8,64,256]{2,1,0:T(8,128)(2,1)}), bf16[8,64,256]{2,1,0:T(8,128)(2,1)S(1)}, u32[]{:S(2)}, u32[]{:S(2)}) async-start(bf16[8,64,256]{2,1,0:T(8,128)(2,1)} %get-tuple-element.36), calls=%async_computation | async-start | bytes 524288 | tf_op jit(solution)/shard_map/all_to_all | solution.py:217
  12.2 8.7 %collective-permute-start.4 = (f32[64,256]{1,0:T(8,128)}, f32[64,256]{1,0:T(8,128)S(1)}, u32[]{:S(2)}, u32[]{:S(2)}) collective-permute-start(f32[64,256]{1,0:T(8,128)} %get-tuple-element.33), channel_id=1, source_target_pairs={{0,0},{1,2},{2,1},{3,3},{4,4},{5,6},{6,5},{7,7},{8,8},{9,10},{10,9... | collective-permute-start | bytes 196616 | tf_op jit(solution)/shard_map/ppermute | solution.py:208
  15.1 2.9 %collective-permute-start.2 = (s32[3,1,1,8]{3,2,1,0:T(1,128)S(1)}, s32[3,1,1,8]{3,2,1,0:T(1,128)S(1)}, u32[]{:S(2)}, u32[]{:S(2)}) collective-permute-start(s32[3,1,1,8]{3,2,1,0:T(1,128)S(1)} %shard_map.56.refs_0_), channel_id=1, source_target_pairs={{0,2},{2,0},{4,6},{6,4},{8,10},{10,8},{12,14},{14,12},{16,18},{18,... | collective-permute-start | bytes 296 | tf_op jit(solution)/shard_map/ppermute | solution.py:211
  20.3 0.7 copy-start.2
  21.0 6.1 %copy-start.3 = (bf16[256,256]{1,0:T(8,128)(2,1)S(1)}, bf16[256,256]{1,0:T(8,128)(2,1)}, u32[]{:S(2)}) copy-start(bf16[256,256]{1,0:T(8,128)(2,1)} %copy-done.2) | copy-start | bytes 393220
  22.7 4.3 %collective-permute-start.5 = (f32[64,256]{1,0:T(8,128)S(1)}, f32[64,256]{1,0:T(8,128)S(1)}, u32[]{:S(2)}, u32[]{:S(2)}) collective-permute-start(f32[64,256]{1,0:T(8,128)S(1)} %get-tuple-element.40), channel_id=1, source_target_pairs={{0,1},{1,0},{2,3},{3,2},{4,5},{5,4},{6,7},{7,6},{8,9},{9,8},{10,11... | collective-permute-start | bytes 196616 | tf_op jit(solution)/shard_map/ppermute | solution.py:287
  27.9 14.0 %all-to-all-start.1 = ((bf16[8,64,256]{2,1,0:T(8,128)(2,1)}), bf16[8,64,256]{2,1,0:T(8,128)(2,1)S(1)}, u32[]{:S(2)}, u32[]{:S(2)}) async-start(bf16[8,64,256]{2,1,0:T(8,128)(2,1)} %get-tuple-element.43), calls=%async_computation.1 | async-start | bytes 524288 | tf_op jit(solution)/shard_map/all_to_all | solution.py:217
  33.3 3.4 %collective-permute-start.6 = (f32[64,256]{1,0:T(8,128)S(1)}, f32[64,256]{1,0:T(8,128)S(1)}, u32[]{:S(2)}, u32[]{:S(2)}) collective-permute-start(f32[64,256]{1,0:T(8,128)S(1)} %get-tuple-element.47), channel_id=1, source_target_pairs={{0,0},{1,2},{2,1},{3,3},{4,4},{5,6},{6,5},{7,7},{8,8},{9,10},{10,9... | collective-permute-start | bytes 196616 | tf_op jit(solution)/shard_map/ppermute | solution.py:208
  43.0 4.3 %collective-permute-start.7 = (f32[64,256]{1,0:T(8,128)S(1)}, f32[64,256]{1,0:T(8,128)S(1)}, u32[]{:S(2)}, u32[]{:S(2)}) collective-permute-start(f32[64,256]{1,0:T(8,128)S(1)} %get-tuple-element.49), channel_id=1, source_target_pairs={{0,1},{1,0},{2,3},{3,2},{4,5},{5,4},{6,7},{7,6},{8,9},{9,8},{10,11... | collective-permute-start | bytes 196616 | tf_op jit(solution)/shard_map/ppermute | solution.py:287
  48.2 11.8 %all-to-all-start.2 = ((bf16[8,64,256]{2,1,0:T(8,128)(2,1)}), bf16[8,64,256]{2,1,0:T(8,128)(2,1)S(1)}, u32[]{:S(2)}, u32[]{:S(2)}) async-start(bf16[8,64,256]{2,1,0:T(8,128)(2,1)} %get-tuple-element.52), calls=%async_computation.2 | async-start | bytes 524288 | tf_op jit(solution)/shard_map/all_to_all | solution.py:217
  51.8 3.4 %collective-permute-start.8 = (f32[64,256]{1,0:T(8,128)S(1)}, f32[64,256]{1,0:T(8,128)S(1)}, u32[]{:S(2)}, u32[]{:S(2)}) collective-permute-start(f32[64,256]{1,0:T(8,128)S(1)} %get-tuple-element.56), channel_id=1, source_target_pairs={{0,0},{1,2},{2,1},{3,3},{4,4},{5,6},{6,5},{7,7},{8,8},{9,10},{10,9... | collective-permute-start | bytes 196616 | tf_op jit(solution)/shard_map/ppermute | solution.py:208
  61.1 2.4 %collective-permute-start.9 = (f32[64,256]{1,0:T(8,128)S(1)}, f32[64,256]{1,0:T(8,128)S(1)}, u32[]{:S(2)}, u32[]{:S(2)}) collective-permute-start(f32[64,256]{1,0:T(8,128)S(1)} %get-tuple-element.57), channel_id=1, source_target_pairs={{0,0},{1,2},{2,1},{3,3},{4,4},{5,6},{6,5},{7,7},{8,8},{9,10},{10,9... | collective-permute-start | bytes 196616 | tf_op jit(solution)/shard_map/ppermute | solution.py:208
  61.7 4.5 %collective-permute-start.10 = (f32[64,256]{1,0:T(8,128)S(1)}, f32[64,256]{1,0:T(8,128)S(1)}, u32[]{:S(2)}, u32[]{:S(2)}) collective-permute-start(f32[64,256]{1,0:T(8,128)S(1)} %get-tuple-element.58), channel_id=1, source_target_pairs={{0,2},{1,0},{2,3},{3,1},{4,6},{5,4},{6,7},{7,5},{8,10},{9,8},{10,1... | collective-permute-start | bytes 196616 | tf_op jit(solution)/shard_map/ppermute | solution.py:208

commit v14 on v11

--- a/solution.py
+++ b/solution.py
@@ -63,17 +63,17 @@
     return lax.rem(lax.axis_index("rows"), 2), lax.axis_index("cols")
 
 
-def first_kernel(
-    ids_ref, counts_ref, rhs_ref, inverse_ref, out_ref, rounded_ref, live_ids_ref,
-    ids, counts, rhs, inverse, sems,
+def prepare_kernel(
+    ids_ref, counts_ref, rhs_ref, inverse_ref, live_ids_ref, own_rhs_ref, own_inverse_ref, ids, counts, sems
 ):
-    _, col = own_place()
+    core, _ = own_place()
+    rows = own_rhs_ref.shape[0]
     copies = start_copies(
         [
             (ids_ref, ids),
             (counts_ref, counts),
-            (half_of(rhs_ref, 0, col, out_ref.shape[0]), rhs),
-            (inverse_ref.at[0, 0], inverse),
+            (half_of(rhs_ref, 0, core, rows), own_rhs_ref),
+            (inverse_ref.at[0, 0], own_inverse_ref),
         ],
         sems,
     )
@@ -84,14 +84,26 @@
             live_ids_ref[l, 0, 0, k] = jnp.where(k < counts[l], ids[l, 0, 0, k], -1)
     copies[2].wait()
     copies[3].wait()
-    solved = solve(rhs[...], inverse[...])
+
+
+def both_pairs(level, rows, core, rhs_refs, inverse_refs, rhs, inverse):
+    pairs = [(half_of(ref, level, core, rows), rhs.at[g]) for g, ref in enumerate(rhs_refs)]
+    return pairs + [(ref.at[level, 0], inverse.at[g]) for g, ref in enumerate(inverse_refs)]
+
+
+def first_kernel(rhs_ref, other_rhs_ref, inverse_ref, other_inverse_ref, *refs):
+    out_ref, copies_ref = refs[-2:]
+    core, col = own_place()
+    straight = core == col
+    other_rhs = half_of(other_rhs_ref, 0, core, out_ref.shape[0])[...]
+    solved = solve(
+        jnp.where(straight, rhs_ref[...], other_rhs),
+        jnp.where(straight, inverse_ref[...], other_inverse_ref[0, 0]),
+    )
     out_ref[...] = solved
-    rounded_ref[...] = solved.astype(jnp.bfloat16)
-
-
-def copies_kernel(rounded_ref, copies_ref):
+    rounded = solved.astype(jnp.bfloat16)
     for i in range(copies_ref.shape[0]):
-        copies_ref[i] = rounded_ref[...]
+        copies_ref[i] = rounded
 
 
 def slot_sum(level, store_level, chips, ids_ref, store_ref, factor_ref, gathered):
@@ -123,12 +135,9 @@
     straight = core == col
     rows = own_rhs_ref.shape[0]
     if inner:
-        pairs = [
-            (half_of(rhs_ref, level, core, rows), rhs.at[0]),
-            (half_of(other_rhs_ref, level, core, rows), rhs.at[1]),
-            (inverse_ref.at[level, 0], inverse.at[0]),
-            (other_inverse_ref.at[level, 0], inverse.at[1]),
-        ]
+        pairs = both_pairs(
+            level, rows, core, (rhs_ref, other_rhs_ref), (inverse_ref, other_inverse_ref), rhs, inverse
+        )
     else:
         pairs = [
             (half_of(rhs_ref, level, col, rows), own_rhs_ref),
@@ -198,7 +207,6 @@
     later = level_count - 1
     same_core = [[2 * j + k for j in range(chips)] for k in range(2)]
     part = jax.ShapeDtypeStruct((rows, width), jnp.float32)
-    rounded_part = jax.ShapeDtypeStruct((rows, width), jnp.bfloat16)
     square = jax.ShapeDtypeStruct((width, width), jnp.bfloat16)
     copies = jax.ShapeDtypeStruct((chips, rows, width), jnp.bfloat16)
     solve_flops = 2 * rows * width * width
@@ -221,36 +229,40 @@
     def spread(x):
         return lax.all_to_all(x, "rows", 0, 0, axis_index_groups=same_core)
 
+    other_inverses, other_rhs = swap_core(diag_inverses), swap_core(right_sides)
     counts = block_counts.reshape(later)
-    solved, rounded, live_ids = run(
-        first_kernel,
+    live_ids, own_rhs, own_inverse = run(
+        prepare_kernel,
         (
+            (jax.ShapeDtypeStruct(source_ids.shape, source_ids.dtype), SMEM),
             (part, VMEM),
-            (rounded_part, VMEM),
-            (jax.ShapeDtypeStruct(source_ids.shape, source_ids.dtype), SMEM),
+            (square, VMEM),
         ),
         ((source_ids, HBM), (counts, HBM), (right_sides, HBM), (diag_inverses, HBM)),
         scratch=(
             pltpu.SMEM(source_ids.shape, source_ids.dtype),
             pltpu.SMEM(counts.shape, counts.dtype),
-            pltpu.VMEM((rows, width), jnp.float32),
-            pltpu.VMEM((width, width), jnp.bfloat16),
             pltpu.SemaphoreType.DMA((4,)),
         ),
+    )
+    other_ids = swap_core(live_ids)
+    solved, copied = run(
+        first_kernel,
+        ((part, VMEM), (copies, VMEM)),
+        ((own_rhs, VMEM), (other_rhs, VMEM), (own_inverse, VMEM), (other_inverses, VMEM), (other_ids, ANY)),
         flops=solve_flops,
     )
-    finished = [solved]
-    copied, = run(copies_kernel, ((copies, VMEM),), ((transpose(rounded), VMEM),))
+    finished = []
     stores = [spread(copied)]
-
-    slot_args = ((live_ids, SMEM), (swap_core(live_ids), SMEM))
+    sent_factors, _, _, _ = lax.optimization_barrier((factor_blocks, other_rhs, other_inverses, other_ids))
+    slot_args = ((live_ids, SMEM), (other_ids, SMEM))
     staged_args = (
         (factor_blocks, HBM),
-        (swap_core(factor_blocks), HBM),
+        (swap_core(sent_factors), HBM),
         (right_sides, HBM),
-        (swap_core(right_sides), HBM),
+        (other_rhs, HBM),
         (diag_inverses, HBM),
-        (swap_core(diag_inverses), HBM),
+        (other_inverses, HBM),
     )
     staged_shape = jax.ShapeDtypeStruct((2, slots, width, width), jnp.bfloat16)
     gathered = pltpu.VMEM((rows, slots * width), jnp.bfloat16)
@@ -276,7 +288,7 @@
             slot_args
             + ((stores[-1], VMEM), (staged, FIXED))
             + tuple((x, VMEM) for x in older)
-            + tuple((x, ANY) for x in finished[1:]),
+            + tuple((x, ANY) for x in finished),
             scratch=(gathered,),
             flops=2 * slots * solve_flops,
             transferred=2 * slots * width * width * 2,
@@ -284,12 +296,16 @@
         after = ((kept, ANY),)
         if l < later:
             arrived = lax.ppermute(sent, "cols", [(0, 1), (1, 0)])
+            before = solved
             solved, copied = run(
                 inner_kernel,
                 ((part, VMEM), (copies, VMEM)),
                 tuple((x, VMEM) for x in (kept, arrived, rhs, inverse)),
                 flops=solve_flops,
             )
+            if l == 1:
+                before, solved = lax.optimization_barrier((before, solved))
+                finished.append(transpose(before))
             finished.append(transpose(solved))
             stores.append(spread(copied))
     first = over_both(kept, lambda j, k, c: (j, c, k))

time: 68.1 us -> 69.4 us (1.019)
  waiting for transfers between devices: 18.7 us -> 26.1 us
  starting transfers between devices: 32 us -> 25.3 us
    all_to_all x3, waiting for transfers between devices: 10.6 us -> 16.4 us  [spread(): return lax.all_to_all(x, 'rows', 0, 0, axis_index_groups=same_core)]
    ppermute x4, starting transfers between devices: 5.74 us -> 1.43 us  [swap_core(): return lax.ppermute(x, 'rows', [(i, i ^ 1) for i in range(row_count)])]
    ppermute x2, starting transfers between devices: 7.58 us -> 3.3 us  [paired_shards(): arrived = lax.ppermute(sent, 'cols', [(0, 1), (1, 0)])]
    all_to_all x3, starting transfers between devices: 14 us -> 15.9 us  [spread(): return lax.all_to_all(x, 'rows', 0, 0, axis_index_groups=same_core)]
    ppermute x2, waiting for transfers between devices: 4.49 us -> 6.01 us  [paired_shards(): arrived = lax.ppermute(sent, 'cols', [(0, 1), (1, 0)])]
  transfers between devices with their start and end apart: 14 -> 14, of which waited for: 6 -> 7; matrix products, arithmetic and copies ran while one was open for 0% -> 0% of each run, Pallas kernels for 15% -> 15%
where the time goes in v14:
time: 69.4 us; the launch traced here: 68.8 us
  waiting for transfers between devices  26.1 us (38%)
  starting transfers between devices  25.3 us (36%)
  Pallas kernels  16 us (23%)
  local copies, waits for them, and re-layouts  1.27 us (2%)
    all_to_all x3, waiting for transfers between devices, spread(): return lax.all_to_all(x, 'rows', 0, 0, axis_index_groups=same_core)  16.4 us
    pallas_call x11, Pallas kernels, run(): pl.pallas_call(kernel, out_shape=out_shape, in_specs=[spec for _, spec in...  16 us
    all_to_all x3, starting transfers between devices, spread(): return lax.all_to_all(x, 'rows', 0, 0, axis_index_groups=same_core)  15.9 us
    ppermute x2, waiting for transfers between devices, paired_shards(): arrived = lax.ppermute(sent, 'cols', [(0, 1), (1, 0)])  6.01 us
    ppermute x5, starting transfers between devices, over_both(): return lax.ppermute(x, ('rows', 'cols'), pairs)  4.66 us
    ppermute x2, starting transfers between devices, paired_shards(): arrived = lax.ppermute(sent, 'cols', [(0, 1), (1, 0)])  3.3 us
    ppermute x5, waiting for transfers between devices, over_both(): return lax.ppermute(x, ('rows', 'cols'), pairs)  2.81 us
    ppermute x4, starting transfers between devices, swap_core(): return lax.ppermute(x, 'rows', [(i, i ^ 1) for i in range(row_count)])  1.43 us
  transfers between devices with their start and end apart: 14, of which 7 were waited for; matrix products, arithmetic and copies ran while one was open for 0% of the time, Pallas kernels for 15%

profile of v14, /device:TPU:0, one launch (start us, length us, event | category | flops | bytes accessed | tf_op | source)
XLA Modules:
  0.0 68.8 jit_solution(17056363041777157561)
XLA Ops:
  0.0 0.5 collective-permute-start.1
  0.5 0.1 collective-permute-start.2
  0.5 1.6 %shard_map.55 = (s32[3,1,1,8]{3,2,1,0:T(1,128)S(1)}, f32[64,256]{1,0:T(8,128)S(1)}, bf16[256,256]{1,0:T(8,128)(2,1)S(1)}) custom-call(s32[3,1,1,8]{3,2,1,0:T(1,128)} %ids_ref.1, s32[3]{0:T(128)} %bitcast.1, f32[4,1,128,256]{3,2,1,0:T(8,128)} %refs_4_.5, bf16[4,1,256,256]{3,2,1,0:T(8,128)(2,1)} %refs_6_.5), custom_call_target="tpu_custom_call" | custom-call | tf_op jit(solution)/shard_map/pallas_call | solution.py:36
  2.1 0.5 collective-permute-start
  2.6 0.8 %collective-permute-done.refs_0_.refs_1_ = s32[3,1,1,8]{3,2,1,0:T(1,128)S(1)} collective-permute-done((s32[3,1,1,8]{3,2,1,0:T(1,128)S(1)}, s32[3,1,1,8]{3,2,1,0:T(1,128)S(1)}, u32[]{:S(2)}, u32[]{:S(2)}) %collective-permute-start) | collective-permute-done | bytes 128 | tf_op jit(solution)/shard_map/ppermute | solution.py:224
  3.4 0.0 collective-permute-done.1.other_rhs_ref.refs_5_
  3.4 0.0 copy-start
  3.5 0.0 collective-permute-done.2.other_inverse_ref.refs_7_
  3.5 0.0 copy-start.1
  3.5 0.4 collective-permute-start.3
  3.9 0.9 %shard_map.56 = (f32[64,256]{1,0:T(8,128)S(1)}, bf16[8,64,256]{2,1,0:T(8,128)(2,1)}) custom-call(f32[64,256]{1,0:T(8,128)S(1)} %get-tuple-element.37.rhs_ref, f32[4,1,128,256]{3,2,1,0:T(8,128)S(1)} %collective-permute-done.1.other_rhs_ref.refs_5_, bf16[256,256]{1,0:T(8,128)(2,1)S(1)} %get-tuple-element.38.inverse_ref, ...), custom_call_target="tpu_custom_call" | custom-call | flops 8388608 | tf_op jit(solution)/shard_map/pallas_call | solution.py:36
  4.8 0.6 copy-done.4
  5.4 7.0 %all-to-all-start = ((bf16[8,64,256]{2,1,0:T(8,128)(2,1)}), bf16[8,64,256]{2,1,0:T(8,128)(2,1)S(1)}, u32[]{:S(2)}, u32[]{:S(2)}) async-start(bf16[8,64,256]{2,1,0:T(8,128)(2,1)} %get-tuple-element.39), calls=%async_computation | async-start | bytes 524288 | tf_op jit(solution)/shard_map/all_to_all | solution.py:230
  12.4 0.0 collective-permute-done.3.refs_3_
  12.4 0.0 copy-done
  12.4 0.0 copy-done.1
  12.4 2.3 %shard_map.57 = (bf16[2,8,256,256]{3,2,1,0:T(8,128)(2,1)S(1)}, f32[64,256]{1,0:T(8,128)S(1)}, bf16[256,256]{1,0:T(8,128)(2,1)S(1)}) custom-call(s32[3,1,1,8]{3,2,1,0:T(1,128)S(1)} %get-tuple-element.36.refs_0_, s32[3,1,1,8]{3,2,1,0:T(1,128)S(1)} %collective-permute-done.refs_0_.refs_1_, bf16[3,1,1,8,256,256]{5,4,3,2,1,0:T(8,128)(2,1)} %refs_2_.5, ...), custom_call_target="tpu_custom_call" | custom-call | bytes 2097152 | tf_op jit(solution)/shard_map/pallas_call | solution.py:36
  14.7 0.0 copy-start.2
  14.7 0.6 copy-done.2
  15.3 6.5 %all-to-all-done.refs_2_.refs_8_ = bf16[8,64,256]{2,1,0:T(8,128)(2,1)S(1)} async-done(((bf16[8,64,256]{2,1,0:T(8,128)(2,1)}), bf16[8,64,256]{2,1,0:T(8,128)(2,1)S(1)}, u32[]{:S(2)}, u32[]{:S(2)}) %all-to-all-start) | async-done | bytes 262176 | tf_op jit(solution)/shard_map/all_to_all | solution.py:230
  21.8 1.1 %shard_map.58 = (f32[64,256]{1,0:T(8,128)S(1)}, f32[64,256]{1,0:T(8,128)S(1)}) custom-call(s32[3,1,1,8]{3,2,1,0:T(1,128)S(1)} %get-tuple-element.36.refs_0_, s32[3,1,1,8]{3,2,1,0:T(1,128)S(1)} %collective-permute-done.refs_0_.refs_1_, bf16[8,64,256]{2,1,0:T(8,128)(2,1)S(1)} %all-to-all-done.refs_2_.refs_8_, ...), custom_call_target="tpu_custom_call" | custom-call | flops 134217728 | bytes 2097152 | tf_op jit(solution)/shard_map/pallas_call | solution.py:36
  22.8 1.6 %collective-permute-start.4 = (f32[64,256]{1,0:T(8,128)S(1)}, f32[64,256]{1,0:T(8,128)S(1)}, u32[]{:S(2)}, u32[]{:S(2)}) collective-permute-start(f32[64,256]{1,0:T(8,128)S(1)} %get-tuple-element.43), channel_id=1, source_target_pairs={{0,1},{1,0},{2,3},{3,2},{4,5},{5,4},{6,7},{7,6},{8,9},{9,8},{10,11... | collective-permute-start | bytes 196616 | tf_op jit(solution)/shard_map/ppermute | solution.py:298
  24.4 2.7 %collective-permute-done.4.arrived_ref = f32[64,256]{1,0:T(8,128)S(1)} collective-permute-done((f32[64,256]{1,0:T(8,128)S(1)}, f32[64,256]{1,0:T(8,128)S(1)}, u32[]{:S(2)}, u32[]{:S(2)}) %collective-permute-start.4) | collective-permute-done | bytes 65568 | tf_op jit(solution)/shard_map/ppermute | solution.py:298
  27.2 0.0 copy-done.3
  27.2 0.9 %shard_map.59 = (f32[64,256]{1,0:T(8,128)S(1)}, bf16[8,64,256]{2,1,0:T(8,128)(2,1)}) custom-call(f32[64,256]{1,0:T(8,128)S(1)} %get-tuple-element.42.kept_ref.refs_9_, f32[64,256]{1,0:T(8,128)S(1)} %collective-permute-done.4.arrived_ref, f32[64,256]{1,0:T(8,128)S(1)} %copy-done.3, bf16[256,256]{1,0:T(8,128)(2,1)S(1)} %get-tuple-element.45.inverse_ref), custom_call_target="tpu_custom_call" | custom-call | flops 8388608 | tf_op jit(solution)/shard_map/pallas_call | solution.py:36
  28.1 3.6 %all-to-all-start.1 = ((bf16[8,64,256]{2,1,0:T(8,128)(2,1)}), bf16[8,64,256]{2,1,0:T(8,128)(2,1)S(1)}, u32[]{:S(2)}, u32[]{:S(2)}) async-start(bf16[8,64,256]{2,1,0:T(8,128)(2,1)} %get-tuple-element.46), calls=%async_computation.1 | async-start | bytes 524288 | tf_op jit(solution)/shard_map/all_to_all | solution.py:230
  31.6 0.0 copy-done.5
  31.7 0.7 collective-permute-start.5
  32.3 0.7 collective-permute-start.6
  33.0 2.7 %shard_map.60 = (bf16[2,8,256,256]{3,2,1,0:T(8,128)(2,1)S(1)}, f32[64,256]{1,0:T(8,128)S(1)}, bf16[256,256]{1,0:T(8,128)(2,1)S(1)}, f32[64,256]{1,0:T(8,128)S(1)}, f32[64,256]{1,0:T(8,128)S(1)}) custom-call(s32[3,1,1,8]{3,2,1,0:T(1,128)S(1)} %get-tuple-element.36.refs_0_, s32[3,1,1,8]{3,2,1,0:T(1,128)S(1)} %collective-permute-done.refs_0_.refs_1_, ...), custom_call_target="tpu_custom_call" | custom-call | flops 134217728 | bytes 2097152 | tf_op jit(solution)/shard_map/pallas_call | solution.py:36
  35.7 0.0 collective-permute-done.5.refs_6_.refs_0_
  35.8 0.0 collective-permute-done.6.refs_7_.refs_1_
  35.8 4.1 %all-to-all-done.1.refs_2_.refs_9_ = bf16[8,64,256]{2,1,0:T(8,128)(2,1)S(1)} async-done(((bf16[8,64,256]{2,1,0:T(8,128)(2,1)}), bf16[8,64,256]{2,1,0:T(8,128)(2,1)S(1)}, u32[]{:S(2)}, u32[]{:S(2)}) %all-to-all-start.1) | async-done | bytes 262176 | tf_op jit(solution)/shard_map/all_to_all | solution.py:230
  39.9 1.1 %shard_map.61 = (f32[64,256]{1,0:T(8,128)S(1)}, f32[64,256]{1,0:T(8,128)S(1)}) custom-call(s32[3,1,1,8]{3,2,1,0:T(1,128)S(1)} %get-tuple-element.36.refs_0_, s32[3,1,1,8]{3,2,1,0:T(1,128)S(1)} %collective-permute-done.refs_0_.refs_1_, bf16[8,64,256]{2,1,0:T(8,128)(2,1)S(1)} %all-to-all-done.1.refs_2_.refs_9_, ...), custom_call_target="tpu_custom_call" | custom-call | flops 134217728 | bytes 2097152 | tf_op jit(solution)/shard_map/pallas_call | solution.py:36
  40.9 1.7 %collective-permute-start.7 = (f32[64,256]{1,0:T(8,128)S(1)}, f32[64,256]{1,0:T(8,128)S(1)}, u32[]{:S(2)}, u32[]{:S(2)}) collective-permute-start(f32[64,256]{1,0:T(8,128)S(1)} %get-tuple-element.55), channel_id=1, source_target_pairs={{0,1},{1,0},{2,3},{3,2},{4,5},{5,4},{6,7},{7,6},{8,9},{9,8},{10,11... | collective-permute-start | bytes 196616 | tf_op jit(solution)/shard_map/ppermute | solution.py:298
  42.7 3.3 %collective-permute-done.7.arrived_ref = f32[64,256]{1,0:T(8,128)S(1)} collective-permute-done((f32[64,256]{1,0:T(8,128)S(1)}, f32[64,256]{1,0:T(8,128)S(1)}, u32[]{:S(2)}, u32[]{:S(2)}) %collective-permute-start.7) | collective-permute-done | bytes 65568 | tf_op jit(solution)/shard_map/ppermute | solution.py:298
  45.9 0.9 %shard_map.62 = (f32[64,256]{1,0:T(8,128)S(1)}, bf16[8,64,256]{2,1,0:T(8,128)(2,1)}) custom-call(f32[64,256]{1,0:T(8,128)S(1)} %get-tuple-element.54.kept_ref.refs_10_, f32[64,256]{1,0:T(8,128)S(1)} %collective-permute-done.7.arrived_ref, f32[64,256]{1,0:T(8,128)S(1)} %get-tuple-element.56.rhs_ref, bf16[256,256]{1,0:T(8,128)(2,1)S(1)} %get-tuple-element.57.inverse_ref), custom_call_target="tpu_custom_call" | custom-call | flops 8388608 | tf_op jit(solution)/shard_map/pallas_call | solution.py:36
  46.8 5.3 %all-to-all-start.2 = ((bf16[8,64,256]{2,1,0:T(8,128)(2,1)}), bf16[8,64,256]{2,1,0:T(8,128)(2,1)S(1)}, u32[]{:S(2)}, u32[]{:S(2)}) async-start(bf16[8,64,256]{2,1,0:T(8,128)(2,1)} %get-tuple-element.58), calls=%async_computation.2 | async-start | bytes 524288 | tf_op jit(solution)/shard_map/all_to_all | solution.py:230
  52.1 0.7 collective-permute-start.8
  52.8 2.7 %shard_map.63 = (bf16[2,8,256,256]{3,2,1,0:T(8,128)(2,1)S(1)}, f32[64,256]{1,0:T(8,128)S(1)}, bf16[256,256]{1,0:T(8,128)(2,1)S(1)}, f32[64,256]{1,0:T(8,128)S(1)}, f32[64,256]{1,0:T(8,128)S(1)}) custom-call(s32[3,1,1,8]{3,2,1,0:T(1,128)S(1)} %get-tuple-element.36.refs_0_, s32[3,1,1,8]{3,2,1,0:T(1,128)S(1)} %collective-permute-done.refs_0_.refs_1_, ...), custom_call_target="tpu_custom_call" | custom-call | flops 134217728 | bytes 2097152 | tf_op jit(solution)/shard_map/pallas_call | solution.py:36
  55.5 0.0 collective-permute-done.8.refs_8_.refs_2_
  55.5 5.8 %all-to-all-done.2.refs_2_ = bf16[8,64,256]{2,1,0:T(8,128)(2,1)S(1)} async-done(((bf16[8,64,256]{2,1,0:T(8,128)(2,1)}), bf16[8,64,256]{2,1,0:T(8,128)(2,1)S(1)}, u32[]{:S(2)}, u32[]{:S(2)}) %all-to-all-start.2) | async-done | bytes 262176 | tf_op jit(solution)/shard_map/all_to_all | solution.py:230
  61.4 1.1 %shard_map.64 = (f32[64,256]{1,0:T(8,128)S(1)}, f32[64,256]{1,0:T(8,128)S(1)}) custom-call(s32[3,1,1,8]{3,2,1,0:T(1,128)S(1)} %get-tuple-element.36.refs_0_, s32[3,1,1,8]{3,2,1,0:T(1,128)S(1)} %collective-permute-done.refs_0_.refs_1_, bf16[8,64,256]{2,1,0:T(8,128)(2,1)S(1)} %all-to-all-done.2.refs_2_, ...), custom_call_target="tpu_custom_call" | custom-call | flops 134217728 | bytes 2097152 | tf_op jit(solution)/shard_map/pallas_call | solution.py:36
  62.4 0.7 collective-permute-start.9
  63.1 2.0 %collective-permute-start.10 = (f32[64,256]{1,0:T(8,128)S(1)}, f32[64,256]{1,0:T(8,128)S(1)}, u32[]{:S(2)}, u32[]{:S(2)}) collective-permute-start(f32[64,256]{1,0:T(8,128)S(1)} %get-tuple-element.64), channel_id=1, source_target_pairs={{0,2},{1,0},{2,3},{3,1},{4,6},{5,4},{6,7},{7,5},{8,10},{9,8},{10,1... | collective-permute-start | bytes 196616 | tf_op jit(solution)/shard_map/ppermute | solution.py:221
  65.1 0.0 collective-permute-done.9.first_ref
  65.1 2.8 %collective-permute-done.10.second_ref = f32[64,256]{1,0:T(8,128)S(1)} collective-permute-done((f32[64,256]{1,0:T(8,128)S(1)}, f32[64,256]{1,0:T(8,128)S(1)}, u32[]{:S(2)}, u32[]{:S(2)}) %collective-permute-start.10) | collective-permute-done | bytes 65568 | tf_op jit(solution)/shard_map/ppermute | solution.py:221
  67.9 0.9 %shard_map.65 = f32[4,1,64,256]{3,2,1,0:T(8,128)} custom-call(f32[64,256]{1,0:T(8,128)S(1)} %collective-permute-done.9.first_ref, f32[64,256]{1,0:T(8,128)S(1)} %collective-permute-done.10.second_ref, f32[64,256]{1,0:T(8,128)S(1)} %get-tuple-element.65.rhs_ref, bf16[256,256]{1,0:T(8,128)(2,1)S(1)} %get-tuple-element.66.inverse_ref, ...), custom_call_target="tpu_custom_call" | custom-call | flops 8388608 | tf_op jit(solution)/shard_map/pallas_call | solution.py:36
  (3 shorter events, 0.0 us)
Async XLA Ops:
  0.0 3.4 %collective-permute-start.1 = (f32[4,1,128,256]{3,2,1,0:T(8,128)}, f32[4,1,128,256]{3,2,1,0:T(8,128)S(1)}, u32[]{:S(2)}, u32[]{:S(2)}) collective-permute-start(f32[4,1,128,256]{3,2,1,0:T(8,128)} %refs_4_.5), channel_id=1, source_target_pairs={{0,2},{2,0},{4,6},{6,4},{8,10},{10,8},{12,14},{14,12},{16,18},{18,... | collective-permute-start | bytes 1572872 | tf_op jit(solution)/shard_map/ppermute | solution.py:224
  0.5 3.0 %collective-permute-start.2 = (bf16[4,1,256,256]{3,2,1,0:T(8,128)(2,1)}, bf16[4,1,256,256]{3,2,1,0:T(8,128)(2,1)S(1)}, u32[]{:S(2)}, u32[]{:S(2)}) collective-permute-start(bf16[4,1,256,256]{3,2,1,0:T(8,128)(2,1)} %refs_6_.5), channel_id=1, source_target_pairs={{0,2},{2,0},{4,6},{6,4},{8,10},{10,8},{12,14},{14,12},{16,18},{18,... | collective-permute-start | bytes 1572872 | tf_op jit(solution)/shard_map/ppermute | solution.py:224
  2.1 1.3 %collective-permute-start = (s32[3,1,1,8]{3,2,1,0:T(1,128)S(1)}, s32[3,1,1,8]{3,2,1,0:T(1,128)S(1)}, u32[]{:S(2)}, u32[]{:S(2)}) collective-permute-start(s32[3,1,1,8]{3,2,1,0:T(1,128)S(1)} %get-tuple-element.36.refs_0_), channel_id=1, source_target_pairs={{0,2},{2,0},{4,6},{6,4},{8,10},{10,8},{12,14},{14,12},{16,18},{18,... | collective-permute-start | bytes 296 | tf_op jit(solution)/shard_map/ppermute | solution.py:224
  3.4 8.9 %copy-start = (f32[4,1,128,256]{3,2,1,0:T(8,128)}, f32[4,1,128,256]{3,2,1,0:T(8,128)S(1)}, u32[]{:S(2)}) copy-start(f32[4,1,128,256]{3,2,1,0:T(8,128)S(1)} %collective-permute-done.1.other_rhs_ref.refs_5_) | copy-start | bytes 1572868
  3.5 8.9 %copy-start.1 = (bf16[4,1,256,256]{3,2,1,0:T(8,128)(2,1)}, bf16[4,1,256,256]{3,2,1,0:T(8,128)(2,1)S(1)}, u32[]{:S(2)}) copy-start(bf16[4,1,256,256]{3,2,1,0:T(8,128)(2,1)S(1)} %collective-permute-done.2.other_inverse_ref.refs_7_) | copy-start | bytes 1572868
  3.5 8.9 %collective-permute-start.3 = (bf16[3,1,1,8,256,256]{5,4,3,2,1,0:T(8,128)(2,1)}, bf16[3,1,1,8,256,256]{5,4,3,2,1,0:T(8,128)(2,1)}, u32[]{:S(2)}, u32[]{:S(2)}) collective-permute-start(bf16[3,1,1,8,256,256]{5,4,3,2,1,0:T(8,128)(2,1)} %refs_2_.5), channel_id=1, source_target_pairs={{0,2},{2,0},{4,6},{6,4},{8,10},{10,8},{12,14},{14,12},{16,18},{18,... | collective-permute-start | bytes 9437192 | tf_op jit(solution)/shard_map/ppermute | solution.py:224
  4.8 0.6 copy-start.4
  5.4 16.4 %all-to-all-start = ((bf16[8,64,256]{2,1,0:T(8,128)(2,1)}), bf16[8,64,256]{2,1,0:T(8,128)(2,1)S(1)}, u32[]{:S(2)}, u32[]{:S(2)}) async-start(bf16[8,64,256]{2,1,0:T(8,128)(2,1)} %get-tuple-element.39), calls=%async_computation | async-start | bytes 524288 | tf_op jit(solution)/shard_map/all_to_all | solution.py:230
  14.7 0.6 copy-start.2
  15.3 16.3 %copy-start.5 = (f32[64,256]{1,0:T(8,128)S(1)}, f32[64,256]{1,0:T(8,128)}, u32[]{:S(2)}) copy-start(f32[64,256]{1,0:T(8,128)} %copy-done.4) | copy-start | bytes 196612
  21.8 5.4 %copy-start.3 = (f32[64,256]{1,0:T(8,128)S(1)}, f32[64,256]{1,0:T(8,128)}, u32[]{:S(2)}) copy-start(f32[64,256]{1,0:T(8,128)} %copy-done.2) | copy-start | bytes 196612
  22.8 4.3 %collective-permute-start.4 = (f32[64,256]{1,0:T(8,128)S(1)}, f32[64,256]{1,0:T(8,128)S(1)}, u32[]{:S(2)}, u32[]{:S(2)}) collective-permute-start(f32[64,256]{1,0:T(8,128)S(1)} %get-tuple-element.43), channel_id=1, source_target_pairs={{0,1},{1,0},{2,3},{3,2},{4,5},{5,4},{6,7},{7,6},{8,9},{9,8},{10,11... | collective-permute-start | bytes 196616 | tf_op jit(solution)/shard_map/ppermute | solution.py:298
  28.1 11.8 %all-to-all-start.1 = ((bf16[8,64,256]{2,1,0:T(8,128)(2,1)}), bf16[8,64,256]{2,1,0:T(8,128)(2,1)S(1)}, u32[]{:S(2)}, u32[]{:S(2)}) async-start(bf16[8,64,256]{2,1,0:T(8,128)(2,1)} %get-tuple-element.46), calls=%async_computation.1 | async-start | bytes 524288 | tf_op jit(solution)/shard_map/all_to_all | solution.py:230
  31.7 4.1 %collective-permute-start.5 = (f32[64,256]{1,0:T(8,128)S(1)}, f32[64,256]{1,0:T(8,128)S(1)}, u32[]{:S(2)}, u32[]{:S(2)}) collective-permute-start(f32[64,256]{1,0:T(8,128)S(1)} %copy-done.5), channel_id=1, source_target_pairs={{0,0},{1,2},{2,1},{3,3},{4,4},{5,6},{6,5},{7,7},{8,8},{9,10},{10,9... | collective-permute-start | bytes 196616 | tf_op jit(solution)/shard_map/ppermute | solution.py:221
  32.3 3.4 %collective-permute-start.6 = (f32[64,256]{1,0:T(8,128)S(1)}, f32[64,256]{1,0:T(8,128)S(1)}, u32[]{:S(2)}, u32[]{:S(2)}) collective-permute-start(f32[64,256]{1,0:T(8,128)S(1)} %get-tuple-element.53), channel_id=1, source_target_pairs={{0,0},{1,2},{2,1},{3,3},{4,4},{5,6},{6,5},{7,7},{8,8},{9,10},{10,9... | collective-permute-start | bytes 196616 | tf_op jit(solution)/shard_map/ppermute | solution.py:221
  40.9 5.0 %collective-permute-start.7 = (f32[64,256]{1,0:T(8,128)S(1)}, f32[64,256]{1,0:T(8,128)S(1)}, u32[]{:S(2)}, u32[]{:S(2)}) collective-permute-start(f32[64,256]{1,0:T(8,128)S(1)} %get-tuple-element.55), channel_id=1, source_target_pairs={{0,1},{1,0},{2,3},{3,2},{4,5},{5,4},{6,7},{7,6},{8,9},{9,8},{10,11... | collective-permute-start | bytes 196616 | tf_op jit(solution)/shard_map/ppermute | solution.py:298
  46.8 14.6 %all-to-all-start.2 = ((bf16[8,64,256]{2,1,0:T(8,128)(2,1)}), bf16[8,64,256]{2,1,0:T(8,128)(2,1)S(1)}, u32[]{:S(2)}, u32[]{:S(2)}) async-start(bf16[8,64,256]{2,1,0:T(8,128)(2,1)} %get-tuple-element.58), calls=%async_computation.2 | async-start | bytes 524288 | tf_op jit(solution)/shard_map/all_to_all | solution.py:230
  52.1 3.4 %collective-permute-start.8 = (f32[64,256]{1,0:T(8,128)S(1)}, f32[64,256]{1,0:T(8,128)S(1)}, u32[]{:S(2)}, u32[]{:S(2)}) collective-permute-start(f32[64,256]{1,0:T(8,128)S(1)} %get-tuple-element.62), channel_id=1, source_target_pairs={{0,0},{1,2},{2,1},{3,3},{4,4},{5,6},{6,5},{7,7},{8,8},{9,10},{10,9... | collective-permute-start | bytes 196616 | tf_op jit(solution)/shard_map/ppermute | solution.py:221
  62.4 2.7 %collective-permute-start.9 = (f32[64,256]{1,0:T(8,128)S(1)}, f32[64,256]{1,0:T(8,128)S(1)}, u32[]{:S(2)}, u32[]{:S(2)}) collective-permute-start(f32[64,256]{1,0:T(8,128)S(1)} %get-tuple-element.63), channel_id=1, source_target_pairs={{0,0},{1,2},{2,1},{3,3},{4,4},{5,6},{6,5},{7,7},{8,8},{9,10},{10,9... | collective-permute-start | bytes 196616 | tf_op jit(solution)/shard_map/ppermute | solution.py:221
  63.1 4.8 %collective-permute-start.10 = (f32[64,256]{1,0:T(8,128)S(1)}, f32[64,256]{1,0:T(8,128)S(1)}, u32[]{:S(2)}, u32[]{:S(2)}) collective-permute-start(f32[64,256]{1,0:T(8,128)S(1)} %get-tuple-element.64), channel_id=1, source_target_pairs={{0,2},{1,0},{2,3},{3,1},{4,6},{5,4},{6,7},{7,5},{8,10},{9,8},{10,1... | collective-permute-start | bytes 196616 | tf_op jit(solution)/shard_map/ppermute | solution.py:221

commit v15 on v14

--- a/solution.py
+++ b/solution.py
@@ -178,12 +178,13 @@
         total = slot_sum(level, level - 1, chips, slot_refs[g], store_ref, staged_ref.at[g], gathered)
         sums.append(total + older_refs[g][...] if level > 1 else total)
     straight = core == col
-    kept_ref[...] = jnp.where(straight, sums[0], sums[1])
-    sent_ref[...] = jnp.where(straight, sums[1], sums[0])
+    kept_ref[...] = jnp.where(straight, sums[0], sums[1]).astype(kept_ref.dtype)
+    sent_ref[...] = jnp.where(straight, sums[1], sums[0]).astype(sent_ref.dtype)
 
 
 def inner_kernel(kept_ref, arrived_ref, rhs_ref, inverse_ref, out_ref, copies_ref):
-    solved = solve(rhs_ref[...] - (kept_ref[...] + arrived_ref[...]), inverse_ref[...])
+    update = kept_ref[...] + arrived_ref[...].astype(jnp.float32)
+    solved = solve(rhs_ref[...] - update, inverse_ref[...])
     out_ref[...] = solved
     rounded = solved.astype(jnp.bfloat16)
     for i in range(copies_ref.shape[0]):
@@ -195,7 +196,8 @@
     level = len(done_refs)
     for m, done in enumerate(done_refs):
         out_ref[m, 0] = done[...]
-    solved = solve(rhs_ref[...] - (first_ref[...] + second_ref[...]), inverse_ref[...])
+    update = first_ref[...].astype(jnp.float32) + second_ref[...].astype(jnp.float32)
+    solved = solve(rhs_ref[...] - update, inverse_ref[...])
     out_ref[level, 0] = solved
 
 
@@ -207,6 +209,7 @@
     later = level_count - 1
     same_core = [[2 * j + k for j in range(chips)] for k in range(2)]
     part = jax.ShapeDtypeStruct((rows, width), jnp.float32)
+    rounded_part = jax.ShapeDtypeStruct((rows, width), jnp.bfloat16)
     square = jax.ShapeDtypeStruct((width, width), jnp.bfloat16)
     copies = jax.ShapeDtypeStruct((chips, rows, width), jnp.bfloat16)
     solve_flops = 2 * rows * width * width
@@ -252,7 +255,7 @@
         ((own_rhs, VMEM), (other_rhs, VMEM), (own_inverse, VMEM), (other_inverses, VMEM), (other_ids, ANY)),
         flops=solve_flops,
     )
-    finished = []
+    finished = [transpose(solved)]
     stores = [spread(copied)]
     sent_factors, _, _, _ = lax.optimization_barrier((factor_blocks, other_rhs, other_inverses, other_ids))
     slot_args = ((live_ids, SMEM), (other_ids, SMEM))
@@ -284,7 +287,7 @@
         )
         kept, sent = run(
             functools.partial(sums_kernel, l, chips),
-            ((part, VMEM), (part, VMEM)),
+            ((part if l < later else rounded_part, VMEM), (rounded_part, VMEM)),
             slot_args
             + ((stores[-1], VMEM), (staged, FIXED))
             + tuple((x, VMEM) for x in older)
@@ -296,16 +299,12 @@
         after = ((kept, ANY),)
         if l < later:
             arrived = lax.ppermute(sent, "cols", [(0, 1), (1, 0)])
-            before = solved
             solved, copied = run(
                 inner_kernel,
                 ((part, VMEM), (copies, VMEM)),
                 tuple((x, VMEM) for x in (kept, arrived, rhs, inverse)),
                 flops=solve_flops,
             )
-            if l == 1:
-                before, solved = lax.optimization_barrier((before, solved))
-                finished.append(transpose(before))
             finished.append(transpose(solved))
             stores.append(spread(copied))
     first = over_both(kept, lambda j, k, c: (j, c, k))

time: 69.4 us -> 64.6 us (0.931)
  waiting for transfers between devices: 26.1 us -> 23.2 us
  starting transfers between devices: 25.3 us -> 24 us
    all_to_all x3, starting transfers between devices: 15.9 us -> 14 us  [spread(): return lax.all_to_all(x, 'rows', 0, 0, axis_index_groups=same_core)]
    ppermute x2, waiting for transfers between devices: 6.01 us -> 4.79 us  [paired_shards(): arrived = lax.ppermute(sent, 'cols', [(0, 1), (1, 0)])]
    all_to_all x3, waiting for transfers between devices: 16.4 us -> 15.5 us  [spread(): return lax.all_to_all(x, 'rows', 0, 0, axis_index_groups=same_core)]
    ppermute x5, starting transfers between devices: 4.66 us -> 5.41 us  [over_both(): return lax.ppermute(x, ('rows', 'cols'), pairs)]
    ppermute x5, waiting for transfers between devices: 2.81 us -> 2.1 us  [over_both(): return lax.ppermute(x, ('rows', 'cols'), pairs)]
  transfers between devices with their start and end apart: 14 -> 14, of which waited for: 7 -> 7; matrix products, arithmetic and copies ran while one was open for 0% -> 0% of each run, Pallas kernels for 15% -> 16%
where the time goes in v15:
time: 64.6 us; the launch traced here: 64 us
  starting transfers between devices  24 us (37%)
  waiting for transfers between devices  23.2 us (36%)
  Pallas kernels  16 us (25%)
  local copies, waits for them, and re-layouts  0.67 us (1%)
    pallas_call x11, Pallas kernels, run(): pl.pallas_call(kernel, out_shape=out_shape, in_specs=[spec for _, spec in...  16 us
    all_to_all x3, waiting for transfers between devices, spread(): return lax.all_to_all(x, 'rows', 0, 0, axis_index_groups=same_core)  15.5 us
    all_to_all x3, starting transfers between devices, spread(): return lax.all_to_all(x, 'rows', 0, 0, axis_index_groups=same_core)  14 us
    ppermute x5, starting transfers between devices, over_both(): return lax.ppermute(x, ('rows', 'cols'), pairs)  5.41 us
    ppermute x2, waiting for transfers between devices, paired_shards(): arrived = lax.ppermute(sent, 'cols', [(0, 1), (1, 0)])  4.79 us
    ppermute x2, starting transfers between devices, paired_shards(): arrived = lax.ppermute(sent, 'cols', [(0, 1), (1, 0)])  3.17 us
    ppermute x5, waiting for transfers between devices, over_both(): return lax.ppermute(x, ('rows', 'cols'), pairs)  2.1 us
    ppermute x4, starting transfers between devices, swap_core(): return lax.ppermute(x, 'rows', [(i, i ^ 1) for i in range(row_count)])  1.43 us
  transfers between devices with their start and end apart: 14, of which 7 were waited for; matrix products, arithmetic and copies ran while one was open for 0% of the time, Pallas kernels for 16%

profile of v15, /device:TPU:0, one launch (start us, length us, event | category | flops | bytes accessed | tf_op | source)
XLA Modules:
  0.0 64.0 jit_solution(9202873888834368135)
XLA Ops:
  0.0 0.5 collective-permute-start.1
  0.5 0.1 collective-permute-start.2
  0.5 1.6 %shard_map.55 = (s32[3,1,1,8]{3,2,1,0:T(1,128)S(1)}, f32[64,256]{1,0:T(8,128)S(1)}, bf16[256,256]{1,0:T(8,128)(2,1)S(1)}) custom-call(s32[3,1,1,8]{3,2,1,0:T(1,128)} %ids_ref.1, s32[3]{0:T(128)} %bitcast.1, f32[4,1,128,256]{3,2,1,0:T(8,128)} %refs_4_.5, bf16[4,1,256,256]{3,2,1,0:T(8,128)(2,1)} %refs_6_.5), custom_call_target="tpu_custom_call" | custom-call | tf_op jit(solution)/shard_map/pallas_call | solution.py:36
  2.1 0.5 collective-permute-start
  2.6 0.8 %collective-permute-done.refs_0_.refs_1_ = s32[3,1,1,8]{3,2,1,0:T(1,128)S(1)} collective-permute-done((s32[3,1,1,8]{3,2,1,0:T(1,128)S(1)}, s32[3,1,1,8]{3,2,1,0:T(1,128)S(1)}, u32[]{:S(2)}, u32[]{:S(2)}) %collective-permute-start) | collective-permute-done | bytes 128 | tf_op jit(solution)/shard_map/ppermute | solution.py:227
  3.4 0.0 collective-permute-done.1.other_rhs_ref.refs_5_
  3.4 0.0 copy-start
  3.5 0.0 collective-permute-done.2.other_inverse_ref.refs_7_
  3.5 0.0 copy-start.1
  3.5 0.4 collective-permute-start.3
  3.9 0.9 %shard_map.56 = (f32[64,256]{1,0:T(8,128)}, bf16[8,64,256]{2,1,0:T(8,128)(2,1)}) custom-call(f32[64,256]{1,0:T(8,128)S(1)} %get-tuple-element.35.rhs_ref, f32[4,1,128,256]{3,2,1,0:T(8,128)S(1)} %collective-permute-done.1.other_rhs_ref.refs_5_, bf16[256,256]{1,0:T(8,128)(2,1)S(1)} %get-tuple-element.36.inverse_ref, ...), custom_call_target="tpu_custom_call" | custom-call | flops 8388608 | tf_op jit(solution)/shard_map/pallas_call | solution.py:36
  4.8 7.0 %all-to-all-start = ((bf16[8,64,256]{2,1,0:T(8,128)(2,1)}), bf16[8,64,256]{2,1,0:T(8,128)(2,1)S(1)}, u32[]{:S(2)}, u32[]{:S(2)}) async-start(bf16[8,64,256]{2,1,0:T(8,128)(2,1)} %get-tuple-element.37), calls=%async_computation | async-start | bytes 524288 | tf_op jit(solution)/shard_map/all_to_all | solution.py:233
  11.8 1.5 %collective-permute-start.4 = (f32[64,256]{1,0:T(8,128)}, f32[64,256]{1,0:T(8,128)S(1)}, u32[]{:S(2)}, u32[]{:S(2)}) collective-permute-start(f32[64,256]{1,0:T(8,128)} %get-tuple-element.40), channel_id=1, source_target_pairs={{0,0},{1,2},{2,1},{3,3},{4,4},{5,6},{6,5},{7,7},{8,8},{9,10},{10,9... | collective-permute-start | bytes 196616 | tf_op jit(solution)/shard_map/ppermute | solution.py:224
  13.2 0.0 collective-permute-done.3.refs_3_
  13.2 0.0 copy-done
  13.2 0.0 copy-done.1
  13.2 2.3 %shard_map.57 = (bf16[2,8,256,256]{3,2,1,0:T(8,128)(2,1)S(1)}, f32[64,256]{1,0:T(8,128)S(1)}, bf16[256,256]{1,0:T(8,128)(2,1)S(1)}) custom-call(s32[3,1,1,8]{3,2,1,0:T(1,128)S(1)} %get-tuple-element.34.refs_0_, s32[3,1,1,8]{3,2,1,0:T(1,128)S(1)} %collective-permute-done.refs_0_.refs_1_, bf16[3,1,1,8,256,256]{5,4,3,2,1,0:T(8,128)(2,1)} %refs_2_.5, ...), custom_call_target="tpu_custom_call" | custom-call | bytes 2097152 | tf_op jit(solution)/shard_map/pallas_call | solution.py:36
  15.5 0.0 copy-start.2
  15.5 0.7 %copy-done.2 = bf16[256,256]{1,0:T(8,128)(2,1)} copy-done((bf16[256,256]{1,0:T(8,128)(2,1)}, bf16[256,256]{1,0:T(8,128)(2,1)S(1)}, u32[]{:S(2)}) %copy-start.2) | copy-done | bytes 131096
  16.2 0.0 collective-permute-done.4.refs_4_.refs_6_.refs_0_
  16.2 0.0 copy-start.3
  16.2 5.0 %all-to-all-done.refs_2_.refs_8_ = bf16[8,64,256]{2,1,0:T(8,128)(2,1)S(1)} async-done(((bf16[8,64,256]{2,1,0:T(8,128)(2,1)}), bf16[8,64,256]{2,1,0:T(8,128)(2,1)S(1)}, u32[]{:S(2)}, u32[]{:S(2)}) %all-to-all-start) | async-done | bytes 262176 | tf_op jit(solution)/shard_map/all_to_all | solution.py:233
  21.2 1.1 %shard_map.58 = (f32[64,256]{1,0:T(8,128)S(1)}, bf16[64,256]{1,0:T(8,128)(2,1)S(1)}) custom-call(s32[3,1,1,8]{3,2,1,0:T(1,128)S(1)} %get-tuple-element.34.refs_0_, s32[3,1,1,8]{3,2,1,0:T(1,128)S(1)} %collective-permute-done.refs_0_.refs_1_, bf16[8,64,256]{2,1,0:T(8,128)(2,1)S(1)} %all-to-all-done.refs_2_.refs_8_, ...), custom_call_target="tpu_custom_call" | custom-call | flops 134217728 | bytes 2097152 | tf_op jit(solution)/shard_map/pallas_call | solution.py:36
  22.2 1.6 %collective-permute-start.5 = (bf16[64,256]{1,0:T(8,128)(2,1)S(1)}, bf16[64,256]{1,0:T(8,128)(2,1)S(1)}, u32[]{:S(2)}, u32[]{:S(2)}) collective-permute-start(bf16[64,256]{1,0:T(8,128)(2,1)S(1)} %get-tuple-element.42), channel_id=1, source_target_pairs={{0,1},{1,0},{2,3},{3,2},{4,5},{5,4},{6,7},{7,6},{8,9},{9,8},{10,11... | collective-permute-start | bytes 98312 | tf_op jit(solution)/shard_map/ppermute | solution.py:301
  23.8 2.4 %collective-permute-done.5.arrived_ref = bf16[64,256]{1,0:T(8,128)(2,1)S(1)} collective-permute-done((bf16[64,256]{1,0:T(8,128)(2,1)S(1)}, bf16[64,256]{1,0:T(8,128)(2,1)S(1)}, u32[]{:S(2)}, u32[]{:S(2)}) %collective-permute-start.5) | collective-permute-done | bytes 32800 | tf_op jit(solution)/shard_map/ppermute | solution.py:301
  26.2 0.0 copy-done.3
  26.2 0.9 %shard_map.59 = (f32[64,256]{1,0:T(8,128)S(1)}, bf16[8,64,256]{2,1,0:T(8,128)(2,1)}) custom-call(f32[64,256]{1,0:T(8,128)S(1)} %get-tuple-element.41.kept_ref.refs_9_, bf16[64,256]{1,0:T(8,128)(2,1)S(1)} %collective-permute-done.5.arrived_ref, f32[64,256]{1,0:T(8,128)S(1)} %get-tuple-element.43.rhs_ref, bf16[256,256]{1,0:T(8,128)(2,1)S(1)} %copy-done.3), custom_call_target="tpu_custom_call" | custom-call | flops 8388608 | tf_op jit(solution)/shard_map/pallas_call | solution.py:36
  27.1 3.6 %all-to-all-start.1 = ((bf16[8,64,256]{2,1,0:T(8,128)(2,1)}), bf16[8,64,256]{2,1,0:T(8,128)(2,1)S(1)}, u32[]{:S(2)}, u32[]{:S(2)}) async-start(bf16[8,64,256]{2,1,0:T(8,128)(2,1)} %get-tuple-element.45), calls=%async_computation.1 | async-start | bytes 524288 | tf_op jit(solution)/shard_map/all_to_all | solution.py:233
  30.7 0.7 %collective-permute-start.6 = (f32[64,256]{1,0:T(8,128)S(1)}, f32[64,256]{1,0:T(8,128)S(1)}, u32[]{:S(2)}, u32[]{:S(2)}) collective-permute-start(f32[64,256]{1,0:T(8,128)S(1)} %get-tuple-element.49), channel_id=1, source_target_pairs={{0,0},{1,2},{2,1},{3,3},{4,4},{5,6},{6,5},{7,7},{8,8},{9,10},{10,9... | collective-permute-start | bytes 196616 | tf_op jit(solution)/shard_map/ppermute | solution.py:224
  31.3 2.7 %shard_map.60 = (bf16[2,8,256,256]{3,2,1,0:T(8,128)(2,1)S(1)}, f32[64,256]{1,0:T(8,128)S(1)}, bf16[256,256]{1,0:T(8,128)(2,1)S(1)}, f32[64,256]{1,0:T(8,128)S(1)}, f32[64,256]{1,0:T(8,128)S(1)}) custom-call(s32[3,1,1,8]{3,2,1,0:T(1,128)S(1)} %get-tuple-element.34.refs_0_, s32[3,1,1,8]{3,2,1,0:T(1,128)S(1)} %collective-permute-done.refs_0_.refs_1_, ...), custom_call_target="tpu_custom_call" | custom-call | flops 134217728 | bytes 2097152 | tf_op jit(solution)/shard_map/pallas_call | solution.py:36
  34.1 0.0 collective-permute-done.6.refs_7_.refs_1_
  34.1 4.8 %all-to-all-done.1.refs_2_.refs_9_ = bf16[8,64,256]{2,1,0:T(8,128)(2,1)S(1)} async-done(((bf16[8,64,256]{2,1,0:T(8,128)(2,1)}), bf16[8,64,256]{2,1,0:T(8,128)(2,1)S(1)}, u32[]{:S(2)}, u32[]{:S(2)}) %all-to-all-start.1) | async-done | bytes 262176 | tf_op jit(solution)/shard_map/all_to_all | solution.py:233
  38.9 1.1 %shard_map.61 = (f32[64,256]{1,0:T(8,128)S(1)}, bf16[64,256]{1,0:T(8,128)(2,1)S(1)}) custom-call(s32[3,1,1,8]{3,2,1,0:T(1,128)S(1)} %get-tuple-element.34.refs_0_, s32[3,1,1,8]{3,2,1,0:T(1,128)S(1)} %collective-permute-done.refs_0_.refs_1_, bf16[8,64,256]{2,1,0:T(8,128)(2,1)S(1)} %all-to-all-done.1.refs_2_.refs_9_, ...), custom_call_target="tpu_custom_call" | custom-call | flops 134217728 | bytes 2097152 | tf_op jit(solution)/shard_map/pallas_call | solution.py:36
  40.0 1.6 %collective-permute-start.7 = (bf16[64,256]{1,0:T(8,128)(2,1)S(1)}, bf16[64,256]{1,0:T(8,128)(2,1)S(1)}, u32[]{:S(2)}, u32[]{:S(2)}) collective-permute-start(bf16[64,256]{1,0:T(8,128)(2,1)S(1)} %get-tuple-element.51), channel_id=1, source_target_pairs={{0,1},{1,0},{2,3},{3,2},{4,5},{5,4},{6,7},{7,6},{8,9},{9,8},{10,11... | collective-permute-start | bytes 98312 | tf_op jit(solution)/shard_map/ppermute | solution.py:301
  41.6 2.4 %collective-permute-done.7.arrived_ref = bf16[64,256]{1,0:T(8,128)(2,1)S(1)} collective-permute-done((bf16[64,256]{1,0:T(8,128)(2,1)S(1)}, bf16[64,256]{1,0:T(8,128)(2,1)S(1)}, u32[]{:S(2)}, u32[]{:S(2)}) %collective-permute-start.7) | collective-permute-done | bytes 32800 | tf_op jit(solution)/shard_map/ppermute | solution.py:301
  44.0 0.9 %shard_map.62 = (f32[64,256]{1,0:T(8,128)S(1)}, bf16[8,64,256]{2,1,0:T(8,128)(2,1)}) custom-call(f32[64,256]{1,0:T(8,128)S(1)} %get-tuple-element.50.kept_ref.refs_10_, bf16[64,256]{1,0:T(8,128)(2,1)S(1)} %collective-permute-done.7.arrived_ref, f32[64,256]{1,0:T(8,128)S(1)} %get-tuple-element.52.rhs_ref, bf16[256,256]{1,0:T(8,128)(2,1)S(1)} %get-tuple-element.53.inverse_ref), custom_call_target="tpu_custom_call" | custom-call | flops 8388608 | tf_op jit(solution)/shard_map/pallas_call | solution.py:36
  44.8 3.5 %all-to-all-start.2 = ((bf16[8,64,256]{2,1,0:T(8,128)(2,1)}), bf16[8,64,256]{2,1,0:T(8,128)(2,1)S(1)}, u32[]{:S(2)}, u32[]{:S(2)}) async-start(bf16[8,64,256]{2,1,0:T(8,128)(2,1)} %get-tuple-element.54), calls=%async_computation.2 | async-start | bytes 524288 | tf_op jit(solution)/shard_map/all_to_all | solution.py:233
  48.3 0.7 %collective-permute-start.8 = (f32[64,256]{1,0:T(8,128)S(1)}, f32[64,256]{1,0:T(8,128)S(1)}, u32[]{:S(2)}, u32[]{:S(2)}) collective-permute-start(f32[64,256]{1,0:T(8,128)S(1)} %get-tuple-element.58), channel_id=1, source_target_pairs={{0,0},{1,2},{2,1},{3,3},{4,4},{5,6},{6,5},{7,7},{8,8},{9,10},{10,9... | collective-permute-start | bytes 196616 | tf_op jit(solution)/shard_map/ppermute | solution.py:224
  49.0 2.7 %shard_map.63 = (bf16[2,8,256,256]{3,2,1,0:T(8,128)(2,1)S(1)}, f32[64,256]{1,0:T(8,128)S(1)}, bf16[256,256]{1,0:T(8,128)(2,1)S(1)}, f32[64,256]{1,0:T(8,128)S(1)}, f32[64,256]{1,0:T(8,128)S(1)}) custom-call(s32[3,1,1,8]{3,2,1,0:T(1,128)S(1)} %get-tuple-element.34.refs_0_, s32[3,1,1,8]{3,2,1,0:T(1,128)S(1)} %collective-permute-done.refs_0_.refs_1_, ...), custom_call_target="tpu_custom_call" | custom-call | flops 134217728 | bytes 2097152 | tf_op jit(solution)/shard_map/pallas_call | solution.py:36
  51.7 0.0 collective-permute-done.8.refs_8_.refs_2_
  51.7 5.7 %all-to-all-done.2.refs_2_ = bf16[8,64,256]{2,1,0:T(8,128)(2,1)S(1)} async-done(((bf16[8,64,256]{2,1,0:T(8,128)(2,1)}), bf16[8,64,256]{2,1,0:T(8,128)(2,1)S(1)}, u32[]{:S(2)}, u32[]{:S(2)}) %all-to-all-start.2) | async-done | bytes 262176 | tf_op jit(solution)/shard_map/all_to_all | solution.py:233
  57.4 1.1 %shard_map.64 = (bf16[64,256]{1,0:T(8,128)(2,1)S(1)}, bf16[64,256]{1,0:T(8,128)(2,1)S(1)}) custom-call(s32[3,1,1,8]{3,2,1,0:T(1,128)S(1)} %get-tuple-element.34.refs_0_, s32[3,1,1,8]{3,2,1,0:T(1,128)S(1)} %collective-permute-done.refs_0_.refs_1_, bf16[8,64,256]{2,1,0:T(8,128)(2,1)S(1)} %all-to-all-done.2.refs_2_, ...), custom_call_target="tpu_custom_call" | custom-call | flops 134217728 | bytes 2097152 | tf_op jit(solution)/shard_map/pallas_call | solution.py:36
  58.4 0.7 %collective-permute-start.9 = (bf16[64,256]{1,0:T(8,128)(2,1)S(1)}, bf16[64,256]{1,0:T(8,128)(2,1)S(1)}, u32[]{:S(2)}, u32[]{:S(2)}) collective-permute-start(bf16[64,256]{1,0:T(8,128)(2,1)S(1)} %get-tuple-element.59), channel_id=1, source_target_pairs={{0,0},{1,2},{2,1},{3,3},{4,4},{5,6},{6,5},{7,7},{8,8},{9,10},{10,9... | collective-permute-start | bytes 98312 | tf_op jit(solution)/shard_map/ppermute | solution.py:224
  59.1 2.0 %collective-permute-start.10 = (bf16[64,256]{1,0:T(8,128)(2,1)S(1)}, bf16[64,256]{1,0:T(8,128)(2,1)S(1)}, u32[]{:S(2)}, u32[]{:S(2)}) collective-permute-start(bf16[64,256]{1,0:T(8,128)(2,1)S(1)} %get-tuple-element.60), channel_id=1, source_target_pairs={{0,2},{1,0},{2,3},{3,1},{4,6},{5,4},{6,7},{7,5},{8,10},{9,8},{10,1... | collective-permute-start | bytes 98312 | tf_op jit(solution)/shard_map/ppermute | solution.py:224
  61.0 0.0 collective-permute-done.9.first_ref
  61.0 2.1 %collective-permute-done.10.second_ref = bf16[64,256]{1,0:T(8,128)(2,1)S(1)} collective-permute-done((bf16[64,256]{1,0:T(8,128)(2,1)S(1)}, bf16[64,256]{1,0:T(8,128)(2,1)S(1)}, u32[]{:S(2)}, u32[]{:S(2)}) %collective-permute-start.10) | collective-permute-done | bytes 32800 | tf_op jit(solution)/shard_map/ppermute | solution.py:224
  63.1 0.9 %shard_map.65 = f32[4,1,64,256]{3,2,1,0:T(8,128)} custom-call(bf16[64,256]{1,0:T(8,128)(2,1)S(1)} %collective-permute-done.9.first_ref, bf16[64,256]{1,0:T(8,128)(2,1)S(1)} %collective-permute-done.10.second_ref, f32[64,256]{1,0:T(8,128)S(1)} %get-tuple-element.61.rhs_ref, bf16[256,256]{1,0:T(8,128)(2,1)S(1)} %get-tuple-element.62.inverse_ref, ...), custom_call_target="tpu_custom_call" | custom-call | flops 8388608 | tf_op jit(solution)/shard_map/pallas_call | solution.py:36
Async XLA Ops:
  0.0 3.4 %collective-permute-start.1 = (f32[4,1,128,256]{3,2,1,0:T(8,128)}, f32[4,1,128,256]{3,2,1,0:T(8,128)S(1)}, u32[]{:S(2)}, u32[]{:S(2)}) collective-permute-start(f32[4,1,128,256]{3,2,1,0:T(8,128)} %refs_4_.5), channel_id=1, source_target_pairs={{0,2},{2,0},{4,6},{6,4},{8,10},{10,8},{12,14},{14,12},{16,18},{18,... | collective-permute-start | bytes 1572872 | tf_op jit(solution)/shard_map/ppermute | solution.py:227
  0.5 3.0 %collective-permute-start.2 = (bf16[4,1,256,256]{3,2,1,0:T(8,128)(2,1)}, bf16[4,1,256,256]{3,2,1,0:T(8,128)(2,1)S(1)}, u32[]{:S(2)}, u32[]{:S(2)}) collective-permute-start(bf16[4,1,256,256]{3,2,1,0:T(8,128)(2,1)} %refs_6_.5), channel_id=1, source_target_pairs={{0,2},{2,0},{4,6},{6,4},{8,10},{10,8},{12,14},{14,12},{16,18},{18,... | collective-permute-start | bytes 1572872 | tf_op jit(solution)/shard_map/ppermute | solution.py:227
  2.1 1.3 %collective-permute-start = (s32[3,1,1,8]{3,2,1,0:T(1,128)S(1)}, s32[3,1,1,8]{3,2,1,0:T(1,128)S(1)}, u32[]{:S(2)}, u32[]{:S(2)}) collective-permute-start(s32[3,1,1,8]{3,2,1,0:T(1,128)S(1)} %get-tuple-element.34.refs_0_), channel_id=1, source_target_pairs={{0,2},{2,0},{4,6},{6,4},{8,10},{10,8},{12,14},{14,12},{16,18},{18,... | collective-permute-start | bytes 296 | tf_op jit(solution)/shard_map/ppermute | solution.py:227
  3.4 9.8 %copy-start = (f32[4,1,128,256]{3,2,1,0:T(8,128)}, f32[4,1,128,256]{3,2,1,0:T(8,128)S(1)}, u32[]{:S(2)}) copy-start(f32[4,1,128,256]{3,2,1,0:T(8,128)S(1)} %collective-permute-done.1.other_rhs_ref.refs_5_) | copy-start | bytes 1572868
  3.5 9.8 %copy-start.1 = (bf16[4,1,256,256]{3,2,1,0:T(8,128)(2,1)}, bf16[4,1,256,256]{3,2,1,0:T(8,128)(2,1)S(1)}, u32[]{:S(2)}) copy-start(bf16[4,1,256,256]{3,2,1,0:T(8,128)(2,1)S(1)} %collective-permute-done.2.other_inverse_ref.refs_7_) | copy-start | bytes 1572868
  3.5 9.8 %collective-permute-start.3 = (bf16[3,1,1,8,256,256]{5,4,3,2,1,0:T(8,128)(2,1)}, bf16[3,1,1,8,256,256]{5,4,3,2,1,0:T(8,128)(2,1)}, u32[]{:S(2)}, u32[]{:S(2)}) collective-permute-start(bf16[3,1,1,8,256,256]{5,4,3,2,1,0:T(8,128)(2,1)} %refs_2_.5), channel_id=1, source_target_pairs={{0,2},{2,0},{4,6},{6,4},{8,10},{10,8},{12,14},{14,12},{16,18},{18,... | collective-permute-start | bytes 9437192 | tf_op jit(solution)/shard_map/ppermute | solution.py:227
  4.8 16.4 %all-to-all-start = ((bf16[8,64,256]{2,1,0:T(8,128)(2,1)}), bf16[8,64,256]{2,1,0:T(8,128)(2,1)S(1)}, u32[]{:S(2)}, u32[]{:S(2)}) async-start(bf16[8,64,256]{2,1,0:T(8,128)(2,1)} %get-tuple-element.37), calls=%async_computation | async-start | bytes 524288 | tf_op jit(solution)/shard_map/all_to_all | solution.py:233
  11.8 4.4 %collective-permute-start.4 = (f32[64,256]{1,0:T(8,128)}, f32[64,256]{1,0:T(8,128)S(1)}, u32[]{:S(2)}, u32[]{:S(2)}) collective-permute-start(f32[64,256]{1,0:T(8,128)} %get-tuple-element.40), channel_id=1, source_target_pairs={{0,0},{1,2},{2,1},{3,3},{4,4},{5,6},{6,5},{7,7},{8,8},{9,10},{10,9... | collective-permute-start | bytes 196616 | tf_op jit(solution)/shard_map/ppermute | solution.py:224
  15.5 0.7 %copy-start.2 = (bf16[256,256]{1,0:T(8,128)(2,1)}, bf16[256,256]{1,0:T(8,128)(2,1)S(1)}, u32[]{:S(2)}) copy-start(bf16[256,256]{1,0:T(8,128)(2,1)S(1)} %get-tuple-element.44.inverse_ref) | copy-start | bytes 393220
  16.2 10.0 %copy-start.3 = (bf16[256,256]{1,0:T(8,128)(2,1)S(1)}, bf16[256,256]{1,0:T(8,128)(2,1)}, u32[]{:S(2)}) copy-start(bf16[256,256]{1,0:T(8,128)(2,1)} %copy-done.2) | copy-start | bytes 393220
  22.2 4.0 %collective-permute-start.5 = (bf16[64,256]{1,0:T(8,128)(2,1)S(1)}, bf16[64,256]{1,0:T(8,128)(2,1)S(1)}, u32[]{:S(2)}, u32[]{:S(2)}) collective-permute-start(bf16[64,256]{1,0:T(8,128)(2,1)S(1)} %get-tuple-element.42), channel_id=1, source_target_pairs={{0,1},{1,0},{2,3},{3,2},{4,5},{5,4},{6,7},{7,6},{8,9},{9,8},{10,11... | collective-permute-start | bytes 98312 | tf_op jit(solution)/shard_map/ppermute | solution.py:301
  27.1 11.8 %all-to-all-start.1 = ((bf16[8,64,256]{2,1,0:T(8,128)(2,1)}), bf16[8,64,256]{2,1,0:T(8,128)(2,1)S(1)}, u32[]{:S(2)}, u32[]{:S(2)}) async-start(bf16[8,64,256]{2,1,0:T(8,128)(2,1)} %get-tuple-element.45), calls=%async_computation.1 | async-start | bytes 524288 | tf_op jit(solution)/shard_map/all_to_all | solution.py:233
  30.7 3.4 %collective-permute-start.6 = (f32[64,256]{1,0:T(8,128)S(1)}, f32[64,256]{1,0:T(8,128)S(1)}, u32[]{:S(2)}, u32[]{:S(2)}) collective-permute-start(f32[64,256]{1,0:T(8,128)S(1)} %get-tuple-element.49), channel_id=1, source_target_pairs={{0,0},{1,2},{2,1},{3,3},{4,4},{5,6},{6,5},{7,7},{8,8},{9,10},{10,9... | collective-permute-start | bytes 196616 | tf_op jit(solution)/shard_map/ppermute | solution.py:224
  40.0 4.0 %collective-permute-start.7 = (bf16[64,256]{1,0:T(8,128)(2,1)S(1)}, bf16[64,256]{1,0:T(8,128)(2,1)S(1)}, u32[]{:S(2)}, u32[]{:S(2)}) collective-permute-start(bf16[64,256]{1,0:T(8,128)(2,1)S(1)} %get-tuple-element.51), channel_id=1, source_target_pairs={{0,1},{1,0},{2,3},{3,2},{4,5},{5,4},{6,7},{7,6},{8,9},{9,8},{10,11... | collective-permute-start | bytes 98312 | tf_op jit(solution)/shard_map/ppermute | solution.py:301
  44.8 12.5 %all-to-all-start.2 = ((bf16[8,64,256]{2,1,0:T(8,128)(2,1)}), bf16[8,64,256]{2,1,0:T(8,128)(2,1)S(1)}, u32[]{:S(2)}, u32[]{:S(2)}) async-start(bf16[8,64,256]{2,1,0:T(8,128)(2,1)} %get-tuple-element.54), calls=%async_computation.2 | async-start | bytes 524288 | tf_op jit(solution)/shard_map/all_to_all | solution.py:233
  48.3 3.4 %collective-permute-start.8 = (f32[64,256]{1,0:T(8,128)S(1)}, f32[64,256]{1,0:T(8,128)S(1)}, u32[]{:S(2)}, u32[]{:S(2)}) collective-permute-start(f32[64,256]{1,0:T(8,128)S(1)} %get-tuple-element.58), channel_id=1, source_target_pairs={{0,0},{1,2},{2,1},{3,3},{4,4},{5,6},{6,5},{7,7},{8,8},{9,10},{10,9... | collective-permute-start | bytes 196616 | tf_op jit(solution)/shard_map/ppermute | solution.py:224
  58.4 2.6 %collective-permute-start.9 = (bf16[64,256]{1,0:T(8,128)(2,1)S(1)}, bf16[64,256]{1,0:T(8,128)(2,1)S(1)}, u32[]{:S(2)}, u32[]{:S(2)}) collective-permute-start(bf16[64,256]{1,0:T(8,128)(2,1)S(1)} %get-tuple-element.59), channel_id=1, source_target_pairs={{0,0},{1,2},{2,1},{3,3},{4,4},{5,6},{6,5},{7,7},{8,8},{9,10},{10,9... | collective-permute-start | bytes 98312 | tf_op jit(solution)/shard_map/ppermute | solution.py:224
  59.1 4.1 %collective-permute-start.10 = (bf16[64,256]{1,0:T(8,128)(2,1)S(1)}, bf16[64,256]{1,0:T(8,128)(2,1)S(1)}, u32[]{:S(2)}, u32[]{:S(2)}) collective-permute-start(bf16[64,256]{1,0:T(8,128)(2,1)S(1)} %get-tuple-element.60), channel_id=1, source_target_pairs={{0,2},{1,0},{2,3},{3,1},{4,6},{5,4},{6,7},{7,5},{8,10},{9,8},{10,1... | collective-permute-start | bytes 98312 | tf_op jit(solution)/shard_map/ppermute | solution.py:224

commit v16 on v15

--- a/solution.py
+++ b/solution.py
@@ -248,16 +248,17 @@
             pltpu.SemaphoreType.DMA((4,)),
         ),
     )
-    other_ids = swap_core(live_ids)
     solved, copied = run(
         first_kernel,
         ((part, VMEM), (copies, VMEM)),
-        ((own_rhs, VMEM), (other_rhs, VMEM), (own_inverse, VMEM), (other_inverses, VMEM), (other_ids, ANY)),
+        ((own_rhs, VMEM), (other_rhs, VMEM), (own_inverse, VMEM), (other_inverses, VMEM)),
         flops=solve_flops,
     )
     finished = [transpose(solved)]
     stores = [spread(copied)]
-    sent_factors, _, _, _ = lax.optimization_barrier((factor_blocks, other_rhs, other_inverses, other_ids))
+    sent_factors, _, _ = lax.optimization_barrier((factor_blocks, other_rhs, other_inverses))
+    sent_ids, solved = lax.optimization_barrier((live_ids, solved))
+    other_ids = swap_core(sent_ids)
     slot_args = ((live_ids, SMEM), (other_ids, SMEM))
     staged_args = (
         (factor_blocks, HBM),

time: 64.6 us -> 65.7 us (1.017)
  starting transfers between devices: 24 us -> 25.7 us
    all_to_all x3, waiting for transfers between devices: 15.5 us -> 11.9 us  [spread(): return lax.all_to_all(x, 'rows', 0, 0, axis_index_groups=same_core)]
    ppermute x4, waiting for transfers between devices: 0.83 us -> 3.26 us  [swap_core(): return lax.ppermute(x, 'rows', [(i, i ^ 1) for i in range(row_count)])]
    ppermute x4, starting transfers between devices: 1.43 us -> 3 us  [swap_core(): return lax.ppermute(x, 'rows', [(i, i ^ 1) for i in range(row_count)])]
  transfers between devices with their start and end apart: 14 -> 14, of which waited for: 7 -> 9; matrix products, arithmetic and copies ran while one was open for 0% -> 0% of each run, Pallas kernels for 16% -> 16%
where the time goes in v16:
time: 65.7 us; the launch traced here: 65.1 us
  starting transfers between devices  25.7 us (39%)
  waiting for transfers between devices  22.6 us (34%)
  Pallas kernels  16 us (24%)
  local copies, waits for them, and re-layouts  0.67 us (1%)
    pallas_call x11, Pallas kernels, run(): pl.pallas_call(kernel, out_shape=out_shape, in_specs=[spec for _, spec in...  16 us
    all_to_all x3, starting transfers between devices, spread(): return lax.all_to_all(x, 'rows', 0, 0, axis_index_groups=same_core)  14.4 us
    all_to_all x3, waiting for transfers between devices, spread(): return lax.all_to_all(x, 'rows', 0, 0, axis_index_groups=same_core)  11.9 us
    ppermute x5, starting transfers between devices, over_both(): return lax.ppermute(x, ('rows', 'cols'), pairs)  5.68 us
    ppermute x2, waiting for transfers between devices, paired_shards(): arrived = lax.ppermute(sent, 'cols', [(0, 1), (1, 0)])  5.38 us
    ppermute x4, waiting for transfers between devices, swap_core(): return lax.ppermute(x, 'rows', [(i, i ^ 1) for i in range(row_count)])  3.26 us
    ppermute x4, starting transfers between devices, swap_core(): return lax.ppermute(x, 'rows', [(i, i ^ 1) for i in range(row_count)])  3 us
    ppermute x2, starting transfers between devices, paired_shards(): arrived = lax.ppermute(sent, 'cols', [(0, 1), (1, 0)])  2.58 us
  transfers between devices with their start and end apart: 14, of which 9 were waited for; matrix products, arithmetic and copies ran while one was open for 0% of the time, Pallas kernels for 16%

profile of v16, /device:TPU:0, one launch (start us, length us, event | category | flops | bytes accessed | tf_op | source)
XLA Modules:
  0.0 65.1 jit_solution(10740008128433994022)
XLA Ops:
  0.0 0.5 collective-permute-start
  0.5 0.1 collective-permute-start.1
  0.5 1.7 %collective-permute-done.other_rhs_ref.refs_5_ = f32[4,1,128,256]{3,2,1,0:T(8,128)S(1)} collective-permute-done((f32[4,1,128,256]{3,2,1,0:T(8,128)}, f32[4,1,128,256]{3,2,1,0:T(8,128)S(1)}, u32[]{:S(2)}, u32[]{:S(2)}) %collective-permute-start) | collective-permute-done | bytes 524320 | tf_op jit(solution)/shard_map/ppermute | solution.py:227
  2.2 0.0 copy-start
  2.2 0.7 %collective-permute-done.1.other_inverse_ref.refs_7_ = bf16[4,1,256,256]{3,2,1,0:T(8,128)(2,1)S(1)} collective-permute-done((bf16[4,1,256,256]{3,2,1,0:T(8,128)(2,1)}, bf16[4,1,256,256]{3,2,1,0:T(8,128)(2,1)S(1)}, u32[]{:S(2)}, u32[]{:S(2)}) %collective-permute-start.1) | collective-permute-done | bytes 524320 | tf_op jit(solution)/shard_map/ppermute | solution.py:227
  3.0 0.0 copy-start.1
  3.0 0.4 collective-permute-start.3
  3.3 1.6 %shard_map.55 = (s32[3,1,1,8]{3,2,1,0:T(1,128)S(1)}, f32[64,256]{1,0:T(8,128)S(1)}, bf16[256,256]{1,0:T(8,128)(2,1)S(1)}) custom-call(s32[3,1,1,8]{3,2,1,0:T(1,128)} %ids_ref.1, s32[3]{0:T(128)} %bitcast.1, f32[4,1,128,256]{3,2,1,0:T(8,128)} %refs_4_.5, bf16[4,1,256,256]{3,2,1,0:T(8,128)(2,1)} %refs_6_.5), custom_call_target="tpu_custom_call" | custom-call | tf_op jit(solution)/shard_map/pallas_call | solution.py:36
  4.9 0.9 %shard_map.56 = (f32[64,256]{1,0:T(8,128)}, bf16[8,64,256]{2,1,0:T(8,128)(2,1)}) custom-call(f32[64,256]{1,0:T(8,128)S(1)} %get-tuple-element.36.rhs_ref, f32[4,1,128,256]{3,2,1,0:T(8,128)S(1)} %collective-permute-done.other_rhs_ref.refs_5_, bf16[256,256]{1,0:T(8,128)(2,1)S(1)} %get-tuple-element.37.inverse_ref, ...), custom_call_target="tpu_custom_call" | custom-call | flops 8388608 | tf_op jit(solution)/shard_map/pallas_call | solution.py:36
  5.8 7.0 %all-to-all-start = ((bf16[8,64,256]{2,1,0:T(8,128)(2,1)}), bf16[8,64,256]{2,1,0:T(8,128)(2,1)S(1)}, u32[]{:S(2)}, u32[]{:S(2)}) async-start(bf16[8,64,256]{2,1,0:T(8,128)(2,1)} %get-tuple-element.40), calls=%async_computation | async-start | bytes 524288 | tf_op jit(solution)/shard_map/all_to_all | solution.py:233
  12.8 1.5 %collective-permute-start.4 = (f32[64,256]{1,0:T(8,128)}, f32[64,256]{1,0:T(8,128)S(1)}, u32[]{:S(2)}, u32[]{:S(2)}) collective-permute-start(f32[64,256]{1,0:T(8,128)} %get-tuple-element.38), channel_id=1, source_target_pairs={{0,0},{1,2},{2,1},{3,3},{4,4},{5,6},{6,5},{7,7},{8,8},{9,10},{10,9... | collective-permute-start | bytes 196616 | tf_op jit(solution)/shard_map/ppermute | solution.py:224
  14.3 2.1 %collective-permute-start.2 = (s32[3,1,1,8]{3,2,1,0:T(1,128)S(1)}, s32[3,1,1,8]{3,2,1,0:T(1,128)S(1)}, u32[]{:S(2)}, u32[]{:S(2)}) collective-permute-start(s32[3,1,1,8]{3,2,1,0:T(1,128)S(1)} %get-tuple-element.39.refs_0_), channel_id=1, source_target_pairs={{0,2},{2,0},{4,6},{6,4},{8,10},{10,8},{12,14},{14,12},{16,18},{18,... | collective-permute-start | bytes 296 | tf_op jit(solution)/shard_map/ppermute | solution.py:227
  16.4 0.8 %collective-permute-done.2.refs_1_ = s32[3,1,1,8]{3,2,1,0:T(1,128)S(1)} collective-permute-done((s32[3,1,1,8]{3,2,1,0:T(1,128)S(1)}, s32[3,1,1,8]{3,2,1,0:T(1,128)S(1)}, u32[]{:S(2)}, u32[]{:S(2)}) %collective-permute-start.2) | collective-permute-done | bytes 128 | tf_op jit(solution)/shard_map/ppermute | solution.py:227
  17.3 0.0 collective-permute-done.3.refs_3_
  17.3 0.0 copy-done
  17.3 0.0 copy-done.1
  17.3 2.3 %shard_map.57 = (bf16[2,8,256,256]{3,2,1,0:T(8,128)(2,1)S(1)}, f32[64,256]{1,0:T(8,128)S(1)}, bf16[256,256]{1,0:T(8,128)(2,1)S(1)}) custom-call(s32[3,1,1,8]{3,2,1,0:T(1,128)S(1)} %get-tuple-element.39.refs_0_, s32[3,1,1,8]{3,2,1,0:T(1,128)S(1)} %collective-permute-done.2.refs_1_, bf16[3,1,1,8,256,256]{5,4,3,2,1,0:T(8,128)(2,1)} %refs_2_.5, ...), custom_call_target="tpu_custom_call" | custom-call | bytes 2097152 | tf_op jit(solution)/shard_map/pallas_call | solution.py:36
  19.5 0.0 copy-start.2
  19.6 0.7 %copy-done.2 = bf16[256,256]{1,0:T(8,128)(2,1)} copy-done((bf16[256,256]{1,0:T(8,128)(2,1)}, bf16[256,256]{1,0:T(8,128)(2,1)S(1)}, u32[]{:S(2)}) %copy-start.2) | copy-done | bytes 131096
  20.2 0.0 collective-permute-done.4.refs_4_.refs_6_.refs_0_
  20.2 0.0 copy-start.3
  20.2 2.0 %all-to-all-done.refs_2_.refs_8_ = bf16[8,64,256]{2,1,0:T(8,128)(2,1)S(1)} async-done(((bf16[8,64,256]{2,1,0:T(8,128)(2,1)}), bf16[8,64,256]{2,1,0:T(8,128)(2,1)S(1)}, u32[]{:S(2)}, u32[]{:S(2)}) %all-to-all-start) | async-done | bytes 262176 | tf_op jit(solution)/shard_map/all_to_all | solution.py:233
  22.2 1.1 %shard_map.58 = (f32[64,256]{1,0:T(8,128)S(1)}, bf16[64,256]{1,0:T(8,128)(2,1)S(1)}) custom-call(s32[3,1,1,8]{3,2,1,0:T(1,128)S(1)} %get-tuple-element.39.refs_0_, s32[3,1,1,8]{3,2,1,0:T(1,128)S(1)} %collective-permute-done.2.refs_1_, bf16[8,64,256]{2,1,0:T(8,128)(2,1)S(1)} %all-to-all-done.refs_2_.refs_8_, ...), custom_call_target="tpu_custom_call" | custom-call | flops 134217728 | bytes 2097152 | tf_op jit(solution)/shard_map/pallas_call | solution.py:36
  23.3 1.6 %collective-permute-start.5 = (bf16[64,256]{1,0:T(8,128)(2,1)S(1)}, bf16[64,256]{1,0:T(8,128)(2,1)S(1)}, u32[]{:S(2)}, u32[]{:S(2)}) collective-permute-start(bf16[64,256]{1,0:T(8,128)(2,1)S(1)} %get-tuple-element.44), channel_id=1, source_target_pairs={{0,1},{1,0},{2,3},{3,2},{4,5},{5,4},{6,7},{7,6},{8,9},{9,8},{10,11... | collective-permute-start | bytes 98312 | tf_op jit(solution)/shard_map/ppermute | solution.py:302
  24.9 2.4 %collective-permute-done.5.arrived_ref = bf16[64,256]{1,0:T(8,128)(2,1)S(1)} collective-permute-done((bf16[64,256]{1,0:T(8,128)(2,1)S(1)}, bf16[64,256]{1,0:T(8,128)(2,1)S(1)}, u32[]{:S(2)}, u32[]{:S(2)}) %collective-permute-start.5) | collective-permute-done | bytes 32800 | tf_op jit(solution)/shard_map/ppermute | solution.py:302
  27.3 0.0 copy-done.3
  27.3 0.9 %shard_map.59 = (f32[64,256]{1,0:T(8,128)S(1)}, bf16[8,64,256]{2,1,0:T(8,128)(2,1)}) custom-call(f32[64,256]{1,0:T(8,128)S(1)} %get-tuple-element.43.kept_ref.refs_9_, bf16[64,256]{1,0:T(8,128)(2,1)S(1)} %collective-permute-done.5.arrived_ref, f32[64,256]{1,0:T(8,128)S(1)} %get-tuple-element.45.rhs_ref, bf16[256,256]{1,0:T(8,128)(2,1)S(1)} %copy-done.3), custom_call_target="tpu_custom_call" | custom-call | flops 8388608 | tf_op jit(solution)/shard_map/pallas_call | solution.py:36
  28.2 4.0 %all-to-all-start.1 = ((bf16[8,64,256]{2,1,0:T(8,128)(2,1)}), bf16[8,64,256]{2,1,0:T(8,128)(2,1)S(1)}, u32[]{:S(2)}, u32[]{:S(2)}) async-start(bf16[8,64,256]{2,1,0:T(8,128)(2,1)} %get-tuple-element.47), calls=%async_computation.1 | async-start | bytes 524288 | tf_op jit(solution)/shard_map/all_to_all | solution.py:233
  32.1 0.7 %collective-permute-start.6 = (f32[64,256]{1,0:T(8,128)S(1)}, f32[64,256]{1,0:T(8,128)S(1)}, u32[]{:S(2)}, u32[]{:S(2)}) collective-permute-start(f32[64,256]{1,0:T(8,128)S(1)} %get-tuple-element.51), channel_id=1, source_target_pairs={{0,0},{1,2},{2,1},{3,3},{4,4},{5,6},{6,5},{7,7},{8,8},{9,10},{10,9... | collective-permute-start | bytes 196616 | tf_op jit(solution)/shard_map/ppermute | solution.py:224
  32.8 2.7 %shard_map.60 = (bf16[2,8,256,256]{3,2,1,0:T(8,128)(2,1)S(1)}, f32[64,256]{1,0:T(8,128)S(1)}, bf16[256,256]{1,0:T(8,128)(2,1)S(1)}, f32[64,256]{1,0:T(8,128)S(1)}, f32[64,256]{1,0:T(8,128)S(1)}) custom-call(s32[3,1,1,8]{3,2,1,0:T(1,128)S(1)} %get-tuple-element.39.refs_0_, s32[3,1,1,8]{3,2,1,0:T(1,128)S(1)} %collective-permute-done.2.refs_1_, ...), custom_call_target="tpu_custom_call" | custom-call | flops 134217728 | bytes 2097152 | tf_op jit(solution)/shard_map/pallas_call | solution.py:36
  35.5 0.0 collective-permute-done.6.refs_7_.refs_1_
  35.6 5.0 %all-to-all-done.1.refs_2_.refs_9_ = bf16[8,64,256]{2,1,0:T(8,128)(2,1)S(1)} async-done(((bf16[8,64,256]{2,1,0:T(8,128)(2,1)}), bf16[8,64,256]{2,1,0:T(8,128)(2,1)S(1)}, u32[]{:S(2)}, u32[]{:S(2)}) %all-to-all-start.1) | async-done | bytes 262176 | tf_op jit(solution)/shard_map/all_to_all | solution.py:233
  40.6 1.1 %shard_map.61 = (f32[64,256]{1,0:T(8,128)S(1)}, bf16[64,256]{1,0:T(8,128)(2,1)S(1)}) custom-call(s32[3,1,1,8]{3,2,1,0:T(1,128)S(1)} %get-tuple-element.39.refs_0_, s32[3,1,1,8]{3,2,1,0:T(1,128)S(1)} %collective-permute-done.2.refs_1_, bf16[8,64,256]{2,1,0:T(8,128)(2,1)S(1)} %all-to-all-done.1.refs_2_.refs_9_, ...), custom_call_target="tpu_custom_call" | custom-call | flops 134217728 | bytes 2097152 | tf_op jit(solution)/shard_map/pallas_call | solution.py:36
  41.6 1.0 %collective-permute-start.7 = (bf16[64,256]{1,0:T(8,128)(2,1)S(1)}, bf16[64,256]{1,0:T(8,128)(2,1)S(1)}, u32[]{:S(2)}, u32[]{:S(2)}) collective-permute-start(bf16[64,256]{1,0:T(8,128)(2,1)S(1)} %get-tuple-element.53), channel_id=1, source_target_pairs={{0,1},{1,0},{2,3},{3,2},{4,5},{5,4},{6,7},{7,6},{8,9},{9,8},{10,11... | collective-permute-start | bytes 98312 | tf_op jit(solution)/shard_map/ppermute | solution.py:302
  42.6 3.0 %collective-permute-done.7.arrived_ref = bf16[64,256]{1,0:T(8,128)(2,1)S(1)} collective-permute-done((bf16[64,256]{1,0:T(8,128)(2,1)S(1)}, bf16[64,256]{1,0:T(8,128)(2,1)S(1)}, u32[]{:S(2)}, u32[]{:S(2)}) %collective-permute-start.7) | collective-permute-done | bytes 32800 | tf_op jit(solution)/shard_map/ppermute | solution.py:302
  45.6 0.9 %shard_map.62 = (f32[64,256]{1,0:T(8,128)S(1)}, bf16[8,64,256]{2,1,0:T(8,128)(2,1)}) custom-call(f32[64,256]{1,0:T(8,128)S(1)} %get-tuple-element.52.kept_ref.refs_10_, bf16[64,256]{1,0:T(8,128)(2,1)S(1)} %collective-permute-done.7.arrived_ref, f32[64,256]{1,0:T(8,128)S(1)} %get-tuple-element.54.rhs_ref, bf16[256,256]{1,0:T(8,128)(2,1)S(1)} %get-tuple-element.55.inverse_ref), custom_call_target="tpu_custom_call" | custom-call | flops 8388608 | tf_op jit(solution)/shard_map/pallas_call | solution.py:36
  46.5 3.4 %all-to-all-start.2 = ((bf16[8,64,256]{2,1,0:T(8,128)(2,1)}), bf16[8,64,256]{2,1,0:T(8,128)(2,1)S(1)}, u32[]{:S(2)}, u32[]{:S(2)}) async-start(bf16[8,64,256]{2,1,0:T(8,128)(2,1)} %get-tuple-element.56), calls=%async_computation.2 | async-start | bytes 524288 | tf_op jit(solution)/shard_map/all_to_all | solution.py:233
  49.9 0.7 %collective-permute-start.8 = (f32[64,256]{1,0:T(8,128)S(1)}, f32[64,256]{1,0:T(8,128)S(1)}, u32[]{:S(2)}, u32[]{:S(2)}) collective-permute-start(f32[64,256]{1,0:T(8,128)S(1)} %get-tuple-element.60), channel_id=1, source_target_pairs={{0,0},{1,2},{2,1},{3,3},{4,4},{5,6},{6,5},{7,7},{8,8},{9,10},{10,9... | collective-permute-start | bytes 196616 | tf_op jit(solution)/shard_map/ppermute | solution.py:224
  50.6 2.7 %shard_map.63 = (bf16[2,8,256,256]{3,2,1,0:T(8,128)(2,1)S(1)}, f32[64,256]{1,0:T(8,128)S(1)}, bf16[256,256]{1,0:T(8,128)(2,1)S(1)}, f32[64,256]{1,0:T(8,128)S(1)}, f32[64,256]{1,0:T(8,128)S(1)}) custom-call(s32[3,1,1,8]{3,2,1,0:T(1,128)S(1)} %get-tuple-element.39.refs_0_, s32[3,1,1,8]{3,2,1,0:T(1,128)S(1)} %collective-permute-done.2.refs_1_, ...), custom_call_target="tpu_custom_call" | custom-call | flops 134217728 | bytes 2097152 | tf_op jit(solution)/shard_map/pallas_call | solution.py:36
  53.3 0.0 collective-permute-done.8.refs_8_.refs_2_
  53.3 4.8 %all-to-all-done.2.refs_2_ = bf16[8,64,256]{2,1,0:T(8,128)(2,1)S(1)} async-done(((bf16[8,64,256]{2,1,0:T(8,128)(2,1)}), bf16[8,64,256]{2,1,0:T(8,128)(2,1)S(1)}, u32[]{:S(2)}, u32[]{:S(2)}) %all-to-all-start.2) | async-done | bytes 262176 | tf_op jit(solution)/shard_map/all_to_all | solution.py:233
  58.1 1.1 %shard_map.64 = (bf16[64,256]{1,0:T(8,128)(2,1)S(1)}, bf16[64,256]{1,0:T(8,128)(2,1)S(1)}) custom-call(s32[3,1,1,8]{3,2,1,0:T(1,128)S(1)} %get-tuple-element.39.refs_0_, s32[3,1,1,8]{3,2,1,0:T(1,128)S(1)} %collective-permute-done.2.refs_1_, bf16[8,64,256]{2,1,0:T(8,128)(2,1)S(1)} %all-to-all-done.2.refs_2_, ...), custom_call_target="tpu_custom_call" | custom-call | flops 134217728 | bytes 2097152 | tf_op jit(solution)/shard_map/pallas_call | solution.py:36
  59.2 0.7 %collective-permute-start.9 = (bf16[64,256]{1,0:T(8,128)(2,1)S(1)}, bf16[64,256]{1,0:T(8,128)(2,1)S(1)}, u32[]{:S(2)}, u32[]{:S(2)}) collective-permute-start(bf16[64,256]{1,0:T(8,128)(2,1)S(1)} %get-tuple-element.61), channel_id=1, source_target_pairs={{0,0},{1,2},{2,1},{3,3},{4,4},{5,6},{6,5},{7,7},{8,8},{9,10},{10,9... | collective-permute-start | bytes 98312 | tf_op jit(solution)/shard_map/ppermute | solution.py:224
  59.9 2.2 %collective-permute-start.10 = (bf16[64,256]{1,0:T(8,128)(2,1)S(1)}, bf16[64,256]{1,0:T(8,128)(2,1)S(1)}, u32[]{:S(2)}, u32[]{:S(2)}) collective-permute-start(bf16[64,256]{1,0:T(8,128)(2,1)S(1)} %get-tuple-element.62), channel_id=1, source_target_pairs={{0,2},{1,0},{2,3},{3,1},{4,6},{5,4},{6,7},{7,5},{8,10},{9,8},{10,1... | collective-permute-start | bytes 98312 | tf_op jit(solution)/shard_map/ppermute | solution.py:224
  62.1 0.0 collective-permute-done.9.first_ref
  62.1 2.1 %collective-permute-done.10.second_ref = bf16[64,256]{1,0:T(8,128)(2,1)S(1)} collective-permute-done((bf16[64,256]{1,0:T(8,128)(2,1)S(1)}, bf16[64,256]{1,0:T(8,128)(2,1)S(1)}, u32[]{:S(2)}, u32[]{:S(2)}) %collective-permute-start.10) | collective-permute-done | bytes 32800 | tf_op jit(solution)/shard_map/ppermute | solution.py:224
  64.2 0.9 %shard_map.65 = f32[4,1,64,256]{3,2,1,0:T(8,128)} custom-call(bf16[64,256]{1,0:T(8,128)(2,1)S(1)} %collective-permute-done.9.first_ref, bf16[64,256]{1,0:T(8,128)(2,1)S(1)} %collective-permute-done.10.second_ref, f32[64,256]{1,0:T(8,128)S(1)} %get-tuple-element.63.rhs_ref, bf16[256,256]{1,0:T(8,128)(2,1)S(1)} %get-tuple-element.64.inverse_ref, ...), custom_call_target="tpu_custom_call" | custom-call | flops 8388608 | tf_op jit(solution)/shard_map/pallas_call | solution.py:36
Async XLA Ops:
  0.0 2.2 %collective-permute-start = (f32[4,1,128,256]{3,2,1,0:T(8,128)}, f32[4,1,128,256]{3,2,1,0:T(8,128)S(1)}, u32[]{:S(2)}, u32[]{:S(2)}) collective-permute-start(f32[4,1,128,256]{3,2,1,0:T(8,128)} %refs_4_.5), channel_id=1, source_target_pairs={{0,2},{2,0},{4,6},{6,4},{8,10},{10,8},{12,14},{14,12},{16,18},{18,... | collective-permute-start | bytes 1572872 | tf_op jit(solution)/shard_map/ppermute | solution.py:227
  0.5 2.5 %collective-permute-start.1 = (bf16[4,1,256,256]{3,2,1,0:T(8,128)(2,1)}, bf16[4,1,256,256]{3,2,1,0:T(8,128)(2,1)S(1)}, u32[]{:S(2)}, u32[]{:S(2)}) collective-permute-start(bf16[4,1,256,256]{3,2,1,0:T(8,128)(2,1)} %refs_6_.5), channel_id=1, source_target_pairs={{0,2},{2,0},{4,6},{6,4},{8,10},{10,8},{12,14},{14,12},{16,18},{18,... | collective-permute-start | bytes 1572872 | tf_op jit(solution)/shard_map/ppermute | solution.py:227
  2.2 15.1 %copy-start = (f32[4,1,128,256]{3,2,1,0:T(8,128)}, f32[4,1,128,256]{3,2,1,0:T(8,128)S(1)}, u32[]{:S(2)}) copy-start(f32[4,1,128,256]{3,2,1,0:T(8,128)S(1)} %collective-permute-done.other_rhs_ref.refs_5_) | copy-start | bytes 1572868
  3.0 14.3 %copy-start.1 = (bf16[4,1,256,256]{3,2,1,0:T(8,128)(2,1)}, bf16[4,1,256,256]{3,2,1,0:T(8,128)(2,1)S(1)}, u32[]{:S(2)}) copy-start(bf16[4,1,256,256]{3,2,1,0:T(8,128)(2,1)S(1)} %collective-permute-done.1.other_inverse_ref.refs_7_) | copy-start | bytes 1572868
  3.0 14.3 %collective-permute-start.3 = (bf16[3,1,1,8,256,256]{5,4,3,2,1,0:T(8,128)(2,1)}, bf16[3,1,1,8,256,256]{5,4,3,2,1,0:T(8,128)(2,1)}, u32[]{:S(2)}, u32[]{:S(2)}) collective-permute-start(bf16[3,1,1,8,256,256]{5,4,3,2,1,0:T(8,128)(2,1)} %refs_2_.5), channel_id=1, source_target_pairs={{0,2},{2,0},{4,6},{6,4},{8,10},{10,8},{12,14},{14,12},{16,18},{18,... | collective-permute-start | bytes 9437192 | tf_op jit(solution)/shard_map/ppermute | solution.py:227
  5.8 16.4 %all-to-all-start = ((bf16[8,64,256]{2,1,0:T(8,128)(2,1)}), bf16[8,64,256]{2,1,0:T(8,128)(2,1)S(1)}, u32[]{:S(2)}, u32[]{:S(2)}) async-start(bf16[8,64,256]{2,1,0:T(8,128)(2,1)} %get-tuple-element.40), calls=%async_computation | async-start | bytes 524288 | tf_op jit(solution)/shard_map/all_to_all | solution.py:233
  12.8 7.4 %collective-permute-start.4 = (f32[64,256]{1,0:T(8,128)}, f32[64,256]{1,0:T(8,128)S(1)}, u32[]{:S(2)}, u32[]{:S(2)}) collective-permute-start(f32[64,256]{1,0:T(8,128)} %get-tuple-element.38), channel_id=1, source_target_pairs={{0,0},{1,2},{2,1},{3,3},{4,4},{5,6},{6,5},{7,7},{8,8},{9,10},{10,9... | collective-permute-start | bytes 196616 | tf_op jit(solution)/shard_map/ppermute | solution.py:224
  14.3 2.9 %collective-permute-start.2 = (s32[3,1,1,8]{3,2,1,0:T(1,128)S(1)}, s32[3,1,1,8]{3,2,1,0:T(1,128)S(1)}, u32[]{:S(2)}, u32[]{:S(2)}) collective-permute-start(s32[3,1,1,8]{3,2,1,0:T(1,128)S(1)} %get-tuple-element.39.refs_0_), channel_id=1, source_target_pairs={{0,2},{2,0},{4,6},{6,4},{8,10},{10,8},{12,14},{14,12},{16,18},{18,... | collective-permute-start | bytes 296 | tf_op jit(solution)/shard_map/ppermute | solution.py:227
  19.5 0.7 %copy-start.2 = (bf16[256,256]{1,0:T(8,128)(2,1)}, bf16[256,256]{1,0:T(8,128)(2,1)S(1)}, u32[]{:S(2)}) copy-start(bf16[256,256]{1,0:T(8,128)(2,1)S(1)} %get-tuple-element.46.inverse_ref) | copy-start | bytes 393220
  20.2 7.1 %copy-start.3 = (bf16[256,256]{1,0:T(8,128)(2,1)S(1)}, bf16[256,256]{1,0:T(8,128)(2,1)}, u32[]{:S(2)}) copy-start(bf16[256,256]{1,0:T(8,128)(2,1)} %copy-done.2) | copy-start | bytes 393220
  23.3 4.0 %collective-permute-start.5 = (bf16[64,256]{1,0:T(8,128)(2,1)S(1)}, bf16[64,256]{1,0:T(8,128)(2,1)S(1)}, u32[]{:S(2)}, u32[]{:S(2)}) collective-permute-start(bf16[64,256]{1,0:T(8,128)(2,1)S(1)} %get-tuple-element.44), channel_id=1, source_target_pairs={{0,1},{1,0},{2,3},{3,2},{4,5},{5,4},{6,7},{7,6},{8,9},{9,8},{10,11... | collective-permute-start | bytes 98312 | tf_op jit(solution)/shard_map/ppermute | solution.py:302
  28.2 12.4 %all-to-all-start.1 = ((bf16[8,64,256]{2,1,0:T(8,128)(2,1)}), bf16[8,64,256]{2,1,0:T(8,128)(2,1)S(1)}, u32[]{:S(2)}, u32[]{:S(2)}) async-start(bf16[8,64,256]{2,1,0:T(8,128)(2,1)} %get-tuple-element.47), calls=%async_computation.1 | async-start | bytes 524288 | tf_op jit(solution)/shard_map/all_to_all | solution.py:233
  32.1 3.4 %collective-permute-start.6 = (f32[64,256]{1,0:T(8,128)S(1)}, f32[64,256]{1,0:T(8,128)S(1)}, u32[]{:S(2)}, u32[]{:S(2)}) collective-permute-start(f32[64,256]{1,0:T(8,128)S(1)} %get-tuple-element.51), channel_id=1, source_target_pairs={{0,0},{1,2},{2,1},{3,3},{4,4},{5,6},{6,5},{7,7},{8,8},{9,10},{10,9... | collective-permute-start | bytes 196616 | tf_op jit(solution)/shard_map/ppermute | solution.py:224
  41.6 4.0 %collective-permute-start.7 = (bf16[64,256]{1,0:T(8,128)(2,1)S(1)}, bf16[64,256]{1,0:T(8,128)(2,1)S(1)}, u32[]{:S(2)}, u32[]{:S(2)}) collective-permute-start(bf16[64,256]{1,0:T(8,128)(2,1)S(1)} %get-tuple-element.53), channel_id=1, source_target_pairs={{0,1},{1,0},{2,3},{3,2},{4,5},{5,4},{6,7},{7,6},{8,9},{9,8},{10,11... | collective-permute-start | bytes 98312 | tf_op jit(solution)/shard_map/ppermute | solution.py:302
  46.5 11.7 %all-to-all-start.2 = ((bf16[8,64,256]{2,1,0:T(8,128)(2,1)}), bf16[8,64,256]{2,1,0:T(8,128)(2,1)S(1)}, u32[]{:S(2)}, u32[]{:S(2)}) async-start(bf16[8,64,256]{2,1,0:T(8,128)(2,1)} %get-tuple-element.56), calls=%async_computation.2 | async-start | bytes 524288 | tf_op jit(solution)/shard_map/all_to_all | solution.py:233
  49.9 3.4 %collective-permute-start.8 = (f32[64,256]{1,0:T(8,128)S(1)}, f32[64,256]{1,0:T(8,128)S(1)}, u32[]{:S(2)}, u32[]{:S(2)}) collective-permute-start(f32[64,256]{1,0:T(8,128)S(1)} %get-tuple-element.60), channel_id=1, source_target_pairs={{0,0},{1,2},{2,1},{3,3},{4,4},{5,6},{6,5},{7,7},{8,8},{9,10},{10,9... | collective-permute-start | bytes 196616 | tf_op jit(solution)/shard_map/ppermute | solution.py:224
  59.2 2.9 %collective-permute-start.9 = (bf16[64,256]{1,0:T(8,128)(2,1)S(1)}, bf16[64,256]{1,0:T(8,128)(2,1)S(1)}, u32[]{:S(2)}, u32[]{:S(2)}) collective-permute-start(bf16[64,256]{1,0:T(8,128)(2,1)S(1)} %get-tuple-element.61), channel_id=1, source_target_pairs={{0,0},{1,2},{2,1},{3,3},{4,4},{5,6},{6,5},{7,7},{8,8},{9,10},{10,9... | collective-permute-start | bytes 98312 | tf_op jit(solution)/shard_map/ppermute | solution.py:224
  59.9 4.3 %collective-permute-start.10 = (bf16[64,256]{1,0:T(8,128)(2,1)S(1)}, bf16[64,256]{1,0:T(8,128)(2,1)S(1)}, u32[]{:S(2)}, u32[]{:S(2)}) collective-permute-start(bf16[64,256]{1,0:T(8,128)(2,1)S(1)} %get-tuple-element.62), channel_id=1, source_target_pairs={{0,2},{1,0},{2,3},{3,1},{4,6},{5,4},{6,7},{7,5},{8,10},{9,8},{10,1... | collective-permute-start | bytes 98312 | tf_op jit(solution)/shard_map/ppermute | solution.py:224

commit v17 on v16

--- a/solution.py
+++ b/solution.py
@@ -256,7 +256,7 @@
     )
     finished = [transpose(solved)]
     stores = [spread(copied)]
-    sent_factors, _, _ = lax.optimization_barrier((factor_blocks, other_rhs, other_inverses))
+    sent_factors, _, _, _ = lax.optimization_barrier((factor_blocks, other_rhs, other_inverses, live_ids))
     sent_ids, solved = lax.optimization_barrier((live_ids, solved))
     other_ids = swap_core(sent_ids)
     slot_args = ((live_ids, SMEM), (other_ids, SMEM))

time: 65.7 us -> 64.1 us (0.976)
  waiting for transfers between devices: 22.6 us -> 21 us
    ppermute x4, waiting for transfers between devices: 3.26 us -> 1.66 us  [swap_core(): return lax.ppermute(x, 'rows', [(i, i ^ 1) for i in range(row_count)])]
where the time goes in v17:
time: 64.1 us; the launch traced here: 63.5 us
  starting transfers between devices  25.7 us (40%)
  waiting for transfers between devices  21 us (33%)
  Pallas kernels  16 us (25%)
  local copies, waits for them, and re-layouts  0.67 us (1%)
    pallas_call x11, Pallas kernels, run(): pl.pallas_call(kernel, out_shape=out_shape, in_specs=[spec for _, spec in...  16 us
    all_to_all x3, starting transfers between devices, spread(): return lax.all_to_all(x, 'rows', 0, 0, axis_index_groups=same_core)  14.3 us
    all_to_all x3, waiting for transfers between devices, spread(): return lax.all_to_all(x, 'rows', 0, 0, axis_index_groups=same_core)  11.9 us
    ppermute x5, starting transfers between devices, over_both(): return lax.ppermute(x, ('rows', 'cols'), pairs)  5.71 us
    ppermute x2, waiting for transfers between devices, paired_shards(): arrived = lax.ppermute(sent, 'cols', [(0, 1), (1, 0)])  5.34 us
    ppermute x4, starting transfers between devices, swap_core(): return lax.ppermute(x, 'rows', [(i, i ^ 1) for i in range(row_count)])  3 us
    ppermute x2, starting transfers between devices, paired_shards(): arrived = lax.ppermute(sent, 'cols', [(0, 1), (1, 0)])  2.62 us
    ppermute x5, waiting for transfers between devices, over_both(): return lax.ppermute(x, ('rows', 'cols'), pairs)  2.1 us
  transfers between devices with their start and end apart: 14, of which 9 were waited for; matrix products, arithmetic and copies ran while one was open for 0% of the time, Pallas kernels for 16%

profile of v17, /device:TPU:0, one launch (start us, length us, event | category | flops | bytes accessed | tf_op | source)
XLA Modules:
  0.0 63.5 jit_solution(8100329678367568520)
XLA Ops:
  0.0 0.5 collective-permute-start
  0.5 0.1 collective-permute-start.1
  0.5 1.6 %shard_map.55 = (s32[3,1,1,8]{3,2,1,0:T(1,128)S(1)}, f32[64,256]{1,0:T(8,128)S(1)}, bf16[256,256]{1,0:T(8,128)(2,1)S(1)}) custom-call(s32[3,1,1,8]{3,2,1,0:T(1,128)} %ids_ref.1, s32[3]{0:T(128)} %bitcast.1, f32[4,1,128,256]{3,2,1,0:T(8,128)} %refs_4_.5, bf16[4,1,256,256]{3,2,1,0:T(8,128)(2,1)} %refs_6_.5), custom_call_target="tpu_custom_call" | custom-call | tf_op jit(solution)/shard_map/pallas_call | solution.py:36
  2.1 0.1 collective-permute-done.other_rhs_ref.refs_5_
  2.2 0.0 copy-start
  2.2 0.7 %collective-permute-done.1.other_inverse_ref.refs_7_ = bf16[4,1,256,256]{3,2,1,0:T(8,128)(2,1)S(1)} collective-permute-done((bf16[4,1,256,256]{3,2,1,0:T(8,128)(2,1)}, bf16[4,1,256,256]{3,2,1,0:T(8,128)(2,1)S(1)}, u32[]{:S(2)}, u32[]{:S(2)}) %collective-permute-start.1) | collective-permute-done | bytes 524320 | tf_op jit(solution)/shard_map/ppermute | solution.py:227
  3.0 0.0 copy-start.1
  3.0 0.4 collective-permute-start.3
  3.3 0.9 %shard_map.56 = (f32[64,256]{1,0:T(8,128)}, bf16[8,64,256]{2,1,0:T(8,128)(2,1)}) custom-call(f32[64,256]{1,0:T(8,128)S(1)} %get-tuple-element.36.rhs_ref, f32[4,1,128,256]{3,2,1,0:T(8,128)S(1)} %collective-permute-done.other_rhs_ref.refs_5_, bf16[256,256]{1,0:T(8,128)(2,1)S(1)} %get-tuple-element.37.inverse_ref, ...), custom_call_target="tpu_custom_call" | custom-call | flops 8388608 | tf_op jit(solution)/shard_map/pallas_call | solution.py:36
  4.2 7.0 %all-to-all-start = ((bf16[8,64,256]{2,1,0:T(8,128)(2,1)}), bf16[8,64,256]{2,1,0:T(8,128)(2,1)S(1)}, u32[]{:S(2)}, u32[]{:S(2)}) async-start(bf16[8,64,256]{2,1,0:T(8,128)(2,1)} %get-tuple-element.40), calls=%async_computation | async-start | bytes 524288 | tf_op jit(solution)/shard_map/all_to_all | solution.py:233
  11.2 1.5 %collective-permute-start.4 = (f32[64,256]{1,0:T(8,128)}, f32[64,256]{1,0:T(8,128)S(1)}, u32[]{:S(2)}, u32[]{:S(2)}) collective-permute-start(f32[64,256]{1,0:T(8,128)} %get-tuple-element.38), channel_id=1, source_target_pairs={{0,0},{1,2},{2,1},{3,3},{4,4},{5,6},{6,5},{7,7},{8,8},{9,10},{10,9... | collective-permute-start | bytes 196616 | tf_op jit(solution)/shard_map/ppermute | solution.py:224
  12.7 2.1 %collective-permute-start.2 = (s32[3,1,1,8]{3,2,1,0:T(1,128)S(1)}, s32[3,1,1,8]{3,2,1,0:T(1,128)S(1)}, u32[]{:S(2)}, u32[]{:S(2)}) collective-permute-start(s32[3,1,1,8]{3,2,1,0:T(1,128)S(1)} %get-tuple-element.39.refs_0_), channel_id=1, source_target_pairs={{0,2},{2,0},{4,6},{6,4},{8,10},{10,8},{12,14},{14,12},{16,18},{18,... | collective-permute-start | bytes 296 | tf_op jit(solution)/shard_map/ppermute | solution.py:227
  14.8 0.8 %collective-permute-done.2.refs_1_ = s32[3,1,1,8]{3,2,1,0:T(1,128)S(1)} collective-permute-done((s32[3,1,1,8]{3,2,1,0:T(1,128)S(1)}, s32[3,1,1,8]{3,2,1,0:T(1,128)S(1)}, u32[]{:S(2)}, u32[]{:S(2)}) %collective-permute-start.2) | collective-permute-done | bytes 128 | tf_op jit(solution)/shard_map/ppermute | solution.py:227
  15.6 0.0 collective-permute-done.3.refs_3_
  15.6 0.0 copy-done
  15.6 0.0 copy-done.1
  15.6 2.3 %shard_map.57 = (bf16[2,8,256,256]{3,2,1,0:T(8,128)(2,1)S(1)}, f32[64,256]{1,0:T(8,128)S(1)}, bf16[256,256]{1,0:T(8,128)(2,1)S(1)}) custom-call(s32[3,1,1,8]{3,2,1,0:T(1,128)S(1)} %get-tuple-element.39.refs_0_, s32[3,1,1,8]{3,2,1,0:T(1,128)S(1)} %collective-permute-done.2.refs_1_, bf16[3,1,1,8,256,256]{5,4,3,2,1,0:T(8,128)(2,1)} %refs_2_.5, ...), custom_call_target="tpu_custom_call" | custom-call | bytes 2097152 | tf_op jit(solution)/shard_map/pallas_call | solution.py:36
  17.9 0.0 copy-start.2
  17.9 0.7 %copy-done.2 = bf16[256,256]{1,0:T(8,128)(2,1)} copy-done((bf16[256,256]{1,0:T(8,128)(2,1)}, bf16[256,256]{1,0:T(8,128)(2,1)S(1)}, u32[]{:S(2)}) %copy-start.2) | copy-done | bytes 131096
  18.6 0.0 collective-permute-done.4.refs_4_.refs_6_.refs_0_
  18.6 0.0 copy-start.3
  18.6 2.1 %all-to-all-done.refs_2_.refs_8_ = bf16[8,64,256]{2,1,0:T(8,128)(2,1)S(1)} async-done(((bf16[8,64,256]{2,1,0:T(8,128)(2,1)}), bf16[8,64,256]{2,1,0:T(8,128)(2,1)S(1)}, u32[]{:S(2)}, u32[]{:S(2)}) %all-to-all-start) | async-done | bytes 262176 | tf_op jit(solution)/shard_map/all_to_all | solution.py:233
  20.6 1.1 %shard_map.58 = (f32[64,256]{1,0:T(8,128)S(1)}, bf16[64,256]{1,0:T(8,128)(2,1)S(1)}) custom-call(s32[3,1,1,8]{3,2,1,0:T(1,128)S(1)} %get-tuple-element.39.refs_0_, s32[3,1,1,8]{3,2,1,0:T(1,128)S(1)} %collective-permute-done.2.refs_1_, bf16[8,64,256]{2,1,0:T(8,128)(2,1)S(1)} %all-to-all-done.refs_2_.refs_8_, ...), custom_call_target="tpu_custom_call" | custom-call | flops 134217728 | bytes 2097152 | tf_op jit(solution)/shard_map/pallas_call | solution.py:36
  21.7 1.6 %collective-permute-start.5 = (bf16[64,256]{1,0:T(8,128)(2,1)S(1)}, bf16[64,256]{1,0:T(8,128)(2,1)S(1)}, u32[]{:S(2)}, u32[]{:S(2)}) collective-permute-start(bf16[64,256]{1,0:T(8,128)(2,1)S(1)} %get-tuple-element.44), channel_id=1, source_target_pairs={{0,1},{1,0},{2,3},{3,2},{4,5},{5,4},{6,7},{7,6},{8,9},{9,8},{10,11... | collective-permute-start | bytes 98312 | tf_op jit(solution)/shard_map/ppermute | solution.py:302
  23.3 2.4 %collective-permute-done.5.arrived_ref = bf16[64,256]{1,0:T(8,128)(2,1)S(1)} collective-permute-done((bf16[64,256]{1,0:T(8,128)(2,1)S(1)}, bf16[64,256]{1,0:T(8,128)(2,1)S(1)}, u32[]{:S(2)}, u32[]{:S(2)}) %collective-permute-start.5) | collective-permute-done | bytes 32800 | tf_op jit(solution)/shard_map/ppermute | solution.py:302
  25.7 0.0 copy-done.3
  25.7 0.9 %shard_map.59 = (f32[64,256]{1,0:T(8,128)S(1)}, bf16[8,64,256]{2,1,0:T(8,128)(2,1)}) custom-call(f32[64,256]{1,0:T(8,128)S(1)} %get-tuple-element.43.kept_ref.refs_9_, bf16[64,256]{1,0:T(8,128)(2,1)S(1)} %collective-permute-done.5.arrived_ref, f32[64,256]{1,0:T(8,128)S(1)} %get-tuple-element.45.rhs_ref, bf16[256,256]{1,0:T(8,128)(2,1)S(1)} %copy-done.3), custom_call_target="tpu_custom_call" | custom-call | flops 8388608 | tf_op jit(solution)/shard_map/pallas_call | solution.py:36
  26.6 3.9 %all-to-all-start.1 = ((bf16[8,64,256]{2,1,0:T(8,128)(2,1)}), bf16[8,64,256]{2,1,0:T(8,128)(2,1)S(1)}, u32[]{:S(2)}, u32[]{:S(2)}) async-start(bf16[8,64,256]{2,1,0:T(8,128)(2,1)} %get-tuple-element.47), calls=%async_computation.1 | async-start | bytes 524288 | tf_op jit(solution)/shard_map/all_to_all | solution.py:233
  30.5 0.7 %collective-permute-start.6 = (f32[64,256]{1,0:T(8,128)S(1)}, f32[64,256]{1,0:T(8,128)S(1)}, u32[]{:S(2)}, u32[]{:S(2)}) collective-permute-start(f32[64,256]{1,0:T(8,128)S(1)} %get-tuple-element.51), channel_id=1, source_target_pairs={{0,0},{1,2},{2,1},{3,3},{4,4},{5,6},{6,5},{7,7},{8,8},{9,10},{10,9... | collective-permute-start | bytes 196616 | tf_op jit(solution)/shard_map/ppermute | solution.py:224
  31.2 2.7 %shard_map.60 = (bf16[2,8,256,256]{3,2,1,0:T(8,128)(2,1)S(1)}, f32[64,256]{1,0:T(8,128)S(1)}, bf16[256,256]{1,0:T(8,128)(2,1)S(1)}, f32[64,256]{1,0:T(8,128)S(1)}, f32[64,256]{1,0:T(8,128)S(1)}) custom-call(s32[3,1,1,8]{3,2,1,0:T(1,128)S(1)} %get-tuple-element.39.refs_0_, s32[3,1,1,8]{3,2,1,0:T(1,128)S(1)} %collective-permute-done.2.refs_1_, ...), custom_call_target="tpu_custom_call" | custom-call | flops 134217728 | bytes 2097152 | tf_op jit(solution)/shard_map/pallas_call | solution.py:36
  33.9 0.0 collective-permute-done.6.refs_7_.refs_1_
  33.9 5.0 %all-to-all-done.1.refs_2_.refs_9_ = bf16[8,64,256]{2,1,0:T(8,128)(2,1)S(1)} async-done(((bf16[8,64,256]{2,1,0:T(8,128)(2,1)}), bf16[8,64,256]{2,1,0:T(8,128)(2,1)S(1)}, u32[]{:S(2)}, u32[]{:S(2)}) %all-to-all-start.1) | async-done | bytes 262176 | tf_op jit(solution)/shard_map/all_to_all | solution.py:233
  38.9 1.1 %shard_map.61 = (f32[64,256]{1,0:T(8,128)S(1)}, bf16[64,256]{1,0:T(8,128)(2,1)S(1)}) custom-call(s32[3,1,1,8]{3,2,1,0:T(1,128)S(1)} %get-tuple-element.39.refs_0_, s32[3,1,1,8]{3,2,1,0:T(1,128)S(1)} %collective-permute-done.2.refs_1_, bf16[8,64,256]{2,1,0:T(8,128)(2,1)S(1)} %all-to-all-done.1.refs_2_.refs_9_, ...), custom_call_target="tpu_custom_call" | custom-call | flops 134217728 | bytes 2097152 | tf_op jit(solution)/shard_map/pallas_call | solution.py:36
  40.0 1.0 %collective-permute-start.7 = (bf16[64,256]{1,0:T(8,128)(2,1)S(1)}, bf16[64,256]{1,0:T(8,128)(2,1)S(1)}, u32[]{:S(2)}, u32[]{:S(2)}) collective-permute-start(bf16[64,256]{1,0:T(8,128)(2,1)S(1)} %get-tuple-element.53), channel_id=1, source_target_pairs={{0,1},{1,0},{2,3},{3,2},{4,5},{5,4},{6,7},{7,6},{8,9},{9,8},{10,11... | collective-permute-start | bytes 98312 | tf_op jit(solution)/shard_map/ppermute | solution.py:302
  41.0 2.9 %collective-permute-done.7.arrived_ref = bf16[64,256]{1,0:T(8,128)(2,1)S(1)} collective-permute-done((bf16[64,256]{1,0:T(8,128)(2,1)S(1)}, bf16[64,256]{1,0:T(8,128)(2,1)S(1)}, u32[]{:S(2)}, u32[]{:S(2)}) %collective-permute-start.7) | collective-permute-done | bytes 32800 | tf_op jit(solution)/shard_map/ppermute | solution.py:302
  44.0 0.9 %shard_map.62 = (f32[64,256]{1,0:T(8,128)S(1)}, bf16[8,64,256]{2,1,0:T(8,128)(2,1)}) custom-call(f32[64,256]{1,0:T(8,128)S(1)} %get-tuple-element.52.kept_ref.refs_10_, bf16[64,256]{1,0:T(8,128)(2,1)S(1)} %collective-permute-done.7.arrived_ref, f32[64,256]{1,0:T(8,128)S(1)} %get-tuple-element.54.rhs_ref, bf16[256,256]{1,0:T(8,128)(2,1)S(1)} %get-tuple-element.55.inverse_ref), custom_call_target="tpu_custom_call" | custom-call | flops 8388608 | tf_op jit(solution)/shard_map/pallas_call | solution.py:36
  44.9 3.4 %all-to-all-start.2 = ((bf16[8,64,256]{2,1,0:T(8,128)(2,1)}), bf16[8,64,256]{2,1,0:T(8,128)(2,1)S(1)}, u32[]{:S(2)}, u32[]{:S(2)}) async-start(bf16[8,64,256]{2,1,0:T(8,128)(2,1)} %get-tuple-element.56), calls=%async_computation.2 | async-start | bytes 524288 | tf_op jit(solution)/shard_map/all_to_all | solution.py:233
  48.3 0.7 %collective-permute-start.8 = (f32[64,256]{1,0:T(8,128)S(1)}, f32[64,256]{1,0:T(8,128)S(1)}, u32[]{:S(2)}, u32[]{:S(2)}) collective-permute-start(f32[64,256]{1,0:T(8,128)S(1)} %get-tuple-element.60), channel_id=1, source_target_pairs={{0,0},{1,2},{2,1},{3,3},{4,4},{5,6},{6,5},{7,7},{8,8},{9,10},{10,9... | collective-permute-start | bytes 196616 | tf_op jit(solution)/shard_map/ppermute | solution.py:224
  49.0 2.7 %shard_map.63 = (bf16[2,8,256,256]{3,2,1,0:T(8,128)(2,1)S(1)}, f32[64,256]{1,0:T(8,128)S(1)}, bf16[256,256]{1,0:T(8,128)(2,1)S(1)}, f32[64,256]{1,0:T(8,128)S(1)}, f32[64,256]{1,0:T(8,128)S(1)}) custom-call(s32[3,1,1,8]{3,2,1,0:T(1,128)S(1)} %get-tuple-element.39.refs_0_, s32[3,1,1,8]{3,2,1,0:T(1,128)S(1)} %collective-permute-done.2.refs_1_, ...), custom_call_target="tpu_custom_call" | custom-call | flops 134217728 | bytes 2097152 | tf_op jit(solution)/shard_map/pallas_call | solution.py:36
  51.7 0.0 collective-permute-done.8.refs_8_.refs_2_
  51.7 4.8 %all-to-all-done.2.refs_2_ = bf16[8,64,256]{2,1,0:T(8,128)(2,1)S(1)} async-done(((bf16[8,64,256]{2,1,0:T(8,128)(2,1)}), bf16[8,64,256]{2,1,0:T(8,128)(2,1)S(1)}, u32[]{:S(2)}, u32[]{:S(2)}) %all-to-all-start.2) | async-done | bytes 262176 | tf_op jit(solution)/shard_map/all_to_all | solution.py:233
  56.5 1.1 %shard_map.64 = (bf16[64,256]{1,0:T(8,128)(2,1)S(1)}, bf16[64,256]{1,0:T(8,128)(2,1)S(1)}) custom-call(s32[3,1,1,8]{3,2,1,0:T(1,128)S(1)} %get-tuple-element.39.refs_0_, s32[3,1,1,8]{3,2,1,0:T(1,128)S(1)} %collective-permute-done.2.refs_1_, bf16[8,64,256]{2,1,0:T(8,128)(2,1)S(1)} %all-to-all-done.2.refs_2_, ...), custom_call_target="tpu_custom_call" | custom-call | flops 134217728 | bytes 2097152 | tf_op jit(solution)/shard_map/pallas_call | solution.py:36
  57.6 0.7 %collective-permute-start.9 = (bf16[64,256]{1,0:T(8,128)(2,1)S(1)}, bf16[64,256]{1,0:T(8,128)(2,1)S(1)}, u32[]{:S(2)}, u32[]{:S(2)}) collective-permute-start(bf16[64,256]{1,0:T(8,128)(2,1)S(1)} %get-tuple-element.61), channel_id=1, source_target_pairs={{0,0},{1,2},{2,1},{3,3},{4,4},{5,6},{6,5},{7,7},{8,8},{9,10},{10,9... | collective-permute-start | bytes 98312 | tf_op jit(solution)/shard_map/ppermute | solution.py:224
  58.2 2.3 %collective-permute-start.10 = (bf16[64,256]{1,0:T(8,128)(2,1)S(1)}, bf16[64,256]{1,0:T(8,128)(2,1)S(1)}, u32[]{:S(2)}, u32[]{:S(2)}) collective-permute-start(bf16[64,256]{1,0:T(8,128)(2,1)S(1)} %get-tuple-element.62), channel_id=1, source_target_pairs={{0,2},{1,0},{2,3},{3,1},{4,6},{5,4},{6,7},{7,5},{8,10},{9,8},{10,1... | collective-permute-start | bytes 98312 | tf_op jit(solution)/shard_map/ppermute | solution.py:224
  60.5 0.0 collective-permute-done.9.first_ref
  60.5 2.1 %collective-permute-done.10.second_ref = bf16[64,256]{1,0:T(8,128)(2,1)S(1)} collective-permute-done((bf16[64,256]{1,0:T(8,128)(2,1)S(1)}, bf16[64,256]{1,0:T(8,128)(2,1)S(1)}, u32[]{:S(2)}, u32[]{:S(2)}) %collective-permute-start.10) | collective-permute-done | bytes 32800 | tf_op jit(solution)/shard_map/ppermute | solution.py:224
  62.6 0.9 %shard_map.65 = f32[4,1,64,256]{3,2,1,0:T(8,128)} custom-call(bf16[64,256]{1,0:T(8,128)(2,1)S(1)} %collective-permute-done.9.first_ref, bf16[64,256]{1,0:T(8,128)(2,1)S(1)} %collective-permute-done.10.second_ref, f32[64,256]{1,0:T(8,128)S(1)} %get-tuple-element.63.rhs_ref, bf16[256,256]{1,0:T(8,128)(2,1)S(1)} %get-tuple-element.64.inverse_ref, ...), custom_call_target="tpu_custom_call" | custom-call | flops 8388608 | tf_op jit(solution)/shard_map/pallas_call | solution.py:36
Async XLA Ops:
  0.0 2.2 %collective-permute-start = (f32[4,1,128,256]{3,2,1,0:T(8,128)}, f32[4,1,128,256]{3,2,1,0:T(8,128)S(1)}, u32[]{:S(2)}, u32[]{:S(2)}) collective-permute-start(f32[4,1,128,256]{3,2,1,0:T(8,128)} %refs_4_.5), channel_id=1, source_target_pairs={{0,2},{2,0},{4,6},{6,4},{8,10},{10,8},{12,14},{14,12},{16,18},{18,... | collective-permute-start | bytes 1572872 | tf_op jit(solution)/shard_map/ppermute | solution.py:227
  0.5 2.5 %collective-permute-start.1 = (bf16[4,1,256,256]{3,2,1,0:T(8,128)(2,1)}, bf16[4,1,256,256]{3,2,1,0:T(8,128)(2,1)S(1)}, u32[]{:S(2)}, u32[]{:S(2)}) collective-permute-start(bf16[4,1,256,256]{3,2,1,0:T(8,128)(2,1)} %refs_6_.5), channel_id=1, source_target_pairs={{0,2},{2,0},{4,6},{6,4},{8,10},{10,8},{12,14},{14,12},{16,18},{18,... | collective-permute-start | bytes 1572872 | tf_op jit(solution)/shard_map/ppermute | solution.py:227
  2.2 13.4 %copy-start = (f32[4,1,128,256]{3,2,1,0:T(8,128)}, f32[4,1,128,256]{3,2,1,0:T(8,128)S(1)}, u32[]{:S(2)}) copy-start(f32[4,1,128,256]{3,2,1,0:T(8,128)S(1)} %collective-permute-done.other_rhs_ref.refs_5_) | copy-start | bytes 1572868
  3.0 12.7 %copy-start.1 = (bf16[4,1,256,256]{3,2,1,0:T(8,128)(2,1)}, bf16[4,1,256,256]{3,2,1,0:T(8,128)(2,1)S(1)}, u32[]{:S(2)}) copy-start(bf16[4,1,256,256]{3,2,1,0:T(8,128)(2,1)S(1)} %collective-permute-done.1.other_inverse_ref.refs_7_) | copy-start | bytes 1572868
  3.0 12.7 %collective-permute-start.3 = (bf16[3,1,1,8,256,256]{5,4,3,2,1,0:T(8,128)(2,1)}, bf16[3,1,1,8,256,256]{5,4,3,2,1,0:T(8,128)(2,1)}, u32[]{:S(2)}, u32[]{:S(2)}) collective-permute-start(bf16[3,1,1,8,256,256]{5,4,3,2,1,0:T(8,128)(2,1)} %refs_2_.5), channel_id=1, source_target_pairs={{0,2},{2,0},{4,6},{6,4},{8,10},{10,8},{12,14},{14,12},{16,18},{18,... | collective-permute-start | bytes 9437192 | tf_op jit(solution)/shard_map/ppermute | solution.py:227
  4.2 16.4 %all-to-all-start = ((bf16[8,64,256]{2,1,0:T(8,128)(2,1)}), bf16[8,64,256]{2,1,0:T(8,128)(2,1)S(1)}, u32[]{:S(2)}, u32[]{:S(2)}) async-start(bf16[8,64,256]{2,1,0:T(8,128)(2,1)} %get-tuple-element.40), calls=%async_computation | async-start | bytes 524288 | tf_op jit(solution)/shard_map/all_to_all | solution.py:233
  11.2 7.4 %collective-permute-start.4 = (f32[64,256]{1,0:T(8,128)}, f32[64,256]{1,0:T(8,128)S(1)}, u32[]{:S(2)}, u32[]{:S(2)}) collective-permute-start(f32[64,256]{1,0:T(8,128)} %get-tuple-element.38), channel_id=1, source_target_pairs={{0,0},{1,2},{2,1},{3,3},{4,4},{5,6},{6,5},{7,7},{8,8},{9,10},{10,9... | collective-permute-start | bytes 196616 | tf_op jit(solution)/shard_map/ppermute | solution.py:224
  12.7 2.9 %collective-permute-start.2 = (s32[3,1,1,8]{3,2,1,0:T(1,128)S(1)}, s32[3,1,1,8]{3,2,1,0:T(1,128)S(1)}, u32[]{:S(2)}, u32[]{:S(2)}) collective-permute-start(s32[3,1,1,8]{3,2,1,0:T(1,128)S(1)} %get-tuple-element.39.refs_0_), channel_id=1, source_target_pairs={{0,2},{2,0},{4,6},{6,4},{8,10},{10,8},{12,14},{14,12},{16,18},{18,... | collective-permute-start | bytes 296 | tf_op jit(solution)/shard_map/ppermute | solution.py:227
  17.9 0.7 %copy-start.2 = (bf16[256,256]{1,0:T(8,128)(2,1)}, bf16[256,256]{1,0:T(8,128)(2,1)S(1)}, u32[]{:S(2)}) copy-start(bf16[256,256]{1,0:T(8,128)(2,1)S(1)} %get-tuple-element.46.inverse_ref) | copy-start | bytes 393220
  18.6 7.1 %copy-start.3 = (bf16[256,256]{1,0:T(8,128)(2,1)S(1)}, bf16[256,256]{1,0:T(8,128)(2,1)}, u32[]{:S(2)}) copy-start(bf16[256,256]{1,0:T(8,128)(2,1)} %copy-done.2) | copy-start | bytes 393220
  21.7 4.0 %collective-permute-start.5 = (bf16[64,256]{1,0:T(8,128)(2,1)S(1)}, bf16[64,256]{1,0:T(8,128)(2,1)S(1)}, u32[]{:S(2)}, u32[]{:S(2)}) collective-permute-start(bf16[64,256]{1,0:T(8,128)(2,1)S(1)} %get-tuple-element.44), channel_id=1, source_target_pairs={{0,1},{1,0},{2,3},{3,2},{4,5},{5,4},{6,7},{7,6},{8,9},{9,8},{10,11... | collective-permute-start | bytes 98312 | tf_op jit(solution)/shard_map/ppermute | solution.py:302
  26.6 12.4 %all-to-all-start.1 = ((bf16[8,64,256]{2,1,0:T(8,128)(2,1)}), bf16[8,64,256]{2,1,0:T(8,128)(2,1)S(1)}, u32[]{:S(2)}, u32[]{:S(2)}) async-start(bf16[8,64,256]{2,1,0:T(8,128)(2,1)} %get-tuple-element.47), calls=%async_computation.1 | async-start | bytes 524288 | tf_op jit(solution)/shard_map/all_to_all | solution.py:233
  30.5 3.4 %collective-permute-start.6 = (f32[64,256]{1,0:T(8,128)S(1)}, f32[64,256]{1,0:T(8,128)S(1)}, u32[]{:S(2)}, u32[]{:S(2)}) collective-permute-start(f32[64,256]{1,0:T(8,128)S(1)} %get-tuple-element.51), channel_id=1, source_target_pairs={{0,0},{1,2},{2,1},{3,3},{4,4},{5,6},{6,5},{7,7},{8,8},{9,10},{10,9... | collective-permute-start | bytes 196616 | tf_op jit(solution)/shard_map/ppermute | solution.py:224
  40.0 4.0 %collective-permute-start.7 = (bf16[64,256]{1,0:T(8,128)(2,1)S(1)}, bf16[64,256]{1,0:T(8,128)(2,1)S(1)}, u32[]{:S(2)}, u32[]{:S(2)}) collective-permute-start(bf16[64,256]{1,0:T(8,128)(2,1)S(1)} %get-tuple-element.53), channel_id=1, source_target_pairs={{0,1},{1,0},{2,3},{3,2},{4,5},{5,4},{6,7},{7,6},{8,9},{9,8},{10,11... | collective-permute-start | bytes 98312 | tf_op jit(solution)/shard_map/ppermute | solution.py:302
  44.9 11.7 %all-to-all-start.2 = ((bf16[8,64,256]{2,1,0:T(8,128)(2,1)}), bf16[8,64,256]{2,1,0:T(8,128)(2,1)S(1)}, u32[]{:S(2)}, u32[]{:S(2)}) async-start(bf16[8,64,256]{2,1,0:T(8,128)(2,1)} %get-tuple-element.56), calls=%async_computation.2 | async-start | bytes 524288 | tf_op jit(solution)/shard_map/all_to_all | solution.py:233
  48.3 3.4 %collective-permute-start.8 = (f32[64,256]{1,0:T(8,128)S(1)}, f32[64,256]{1,0:T(8,128)S(1)}, u32[]{:S(2)}, u32[]{:S(2)}) collective-permute-start(f32[64,256]{1,0:T(8,128)S(1)} %get-tuple-element.60), channel_id=1, source_target_pairs={{0,0},{1,2},{2,1},{3,3},{4,4},{5,6},{6,5},{7,7},{8,8},{9,10},{10,9... | collective-permute-start | bytes 196616 | tf_op jit(solution)/shard_map/ppermute | solution.py:224
  57.6 2.9 %collective-permute-start.9 = (bf16[64,256]{1,0:T(8,128)(2,1)S(1)}, bf16[64,256]{1,0:T(8,128)(2,1)S(1)}, u32[]{:S(2)}, u32[]{:S(2)}) collective-permute-start(bf16[64,256]{1,0:T(8,128)(2,1)S(1)} %get-tuple-element.61), channel_id=1, source_target_pairs={{0,0},{1,2},{2,1},{3,3},{4,4},{5,6},{6,5},{7,7},{8,8},{9,10},{10,9... | collective-permute-start | bytes 98312 | tf_op jit(solution)/shard_map/ppermute | solution.py:224
  58.2 4.4 %collective-permute-start.10 = (bf16[64,256]{1,0:T(8,128)(2,1)S(1)}, bf16[64,256]{1,0:T(8,128)(2,1)S(1)}, u32[]{:S(2)}, u32[]{:S(2)}) collective-permute-start(bf16[64,256]{1,0:T(8,128)(2,1)S(1)} %get-tuple-element.62), channel_id=1, source_target_pairs={{0,2},{1,0},{2,3},{3,1},{4,6},{5,4},{6,7},{7,5},{8,10},{9,8},{10,1... | collective-permute-start | bytes 98312 | tf_op jit(solution)/shard_map/ppermute | solution.py:224

commit v18 on v17

--- a/solution.py
+++ b/solution.py
@@ -183,8 +183,7 @@
 
 
 def inner_kernel(kept_ref, arrived_ref, rhs_ref, inverse_ref, out_ref, copies_ref):
-    update = kept_ref[...] + arrived_ref[...].astype(jnp.float32)
-    solved = solve(rhs_ref[...] - update, inverse_ref[...])
+    solved = solve(rhs_ref[...] - (kept_ref[...] + arrived_ref[...]), inverse_ref[...])
     out_ref[...] = solved
     rounded = solved.astype(jnp.bfloat16)
     for i in range(copies_ref.shape[0]):
@@ -288,7 +287,7 @@
         )
         kept, sent = run(
             functools.partial(sums_kernel, l, chips),
-            ((part if l < later else rounded_part, VMEM), (rounded_part, VMEM)),
+            ((part if l < later else rounded_part, VMEM),) * 2,
             slot_args
             + ((stores[-1], VMEM), (staged, FIXED))
             + tuple((x, VMEM) for x in older)

time: 64.1 us -> 64.8 us (1.011)
  waiting for transfers between devices: 21 us -> 22.2 us
    ppermute x2, waiting for transfers between devices: 5.34 us -> 6.31 us  [paired_shards(): arrived = lax.ppermute(sent, 'cols', [(0, 1), (1, 0)])]
where the time goes in v18:
time: 64.8 us; the launch traced here: 64.2 us
  starting transfers between devices  25.2 us (39%)
  waiting for transfers between devices  22.2 us (34%)
  Pallas kernels  16 us (25%)
  local copies, waits for them, and re-layouts  0.67 us (1%)
    pallas_call x11, Pallas kernels, run(): pl.pallas_call(kernel, out_shape=out_shape, in_specs=[spec for _, spec in...  16 us
    all_to_all x3, starting transfers between devices, spread(): return lax.all_to_all(x, 'rows', 0, 0, axis_index_groups=same_core)  14.6 us
    all_to_all x3, waiting for transfers between devices, spread(): return lax.all_to_all(x, 'rows', 0, 0, axis_index_groups=same_core)  12.1 us
    ppermute x2, waiting for transfers between devices, paired_shards(): arrived = lax.ppermute(sent, 'cols', [(0, 1), (1, 0)])  6.31 us
    ppermute x5, starting transfers between devices, over_both(): return lax.ppermute(x, ('rows', 'cols'), pairs)  5.3 us
    ppermute x4, starting transfers between devices, swap_core(): return lax.ppermute(x, 'rows', [(i, i ^ 1) for i in range(row_count)])  3 us
    ppermute x2, starting transfers between devices, paired_shards(): arrived = lax.ppermute(sent, 'cols', [(0, 1), (1, 0)])  2.35 us
    ppermute x5, waiting for transfers between devices, over_both(): return lax.ppermute(x, ('rows', 'cols'), pairs)  2.1 us
  transfers between devices with their start and end apart: 14, of which 9 were waited for; matrix products, arithmetic and copies ran while one was open for 0% of the time, Pallas kernels for 16%

profile of v18, /device:TPU:0, one launch (start us, length us, event | category | flops | bytes accessed | tf_op | source)
XLA Modules:
  0.0 64.2 jit_solution(13719349392634420763)
XLA Ops:
  0.0 0.5 collective-permute-start
  0.5 0.1 collective-permute-start.1
  0.5 1.6 %shard_map.55 = (s32[3,1,1,8]{3,2,1,0:T(1,128)S(1)}, f32[64,256]{1,0:T(8,128)S(1)}, bf16[256,256]{1,0:T(8,128)(2,1)S(1)}) custom-call(s32[3,1,1,8]{3,2,1,0:T(1,128)} %ids_ref.1, s32[3]{0:T(128)} %bitcast.1, f32[4,1,128,256]{3,2,1,0:T(8,128)} %refs_4_.5, bf16[4,1,256,256]{3,2,1,0:T(8,128)(2,1)} %refs_6_.5), custom_call_target="tpu_custom_call" | custom-call | tf_op jit(solution)/shard_map/pallas_call | solution.py:36
  2.1 0.1 collective-permute-done.other_rhs_ref.refs_5_
  2.2 0.0 copy-start
  2.2 0.7 %collective-permute-done.1.other_inverse_ref.refs_7_ = bf16[4,1,256,256]{3,2,1,0:T(8,128)(2,1)S(1)} collective-permute-done((bf16[4,1,256,256]{3,2,1,0:T(8,128)(2,1)}, bf16[4,1,256,256]{3,2,1,0:T(8,128)(2,1)S(1)}, u32[]{:S(2)}, u32[]{:S(2)}) %collective-permute-start.1) | collective-permute-done | bytes 524320 | tf_op jit(solution)/shard_map/ppermute | solution.py:226
  3.0 0.0 copy-start.1
  3.0 0.4 collective-permute-start.3
  3.3 0.9 %shard_map.56 = (f32[64,256]{1,0:T(8,128)}, bf16[8,64,256]{2,1,0:T(8,128)(2,1)}) custom-call(f32[64,256]{1,0:T(8,128)S(1)} %get-tuple-element.36.rhs_ref, f32[4,1,128,256]{3,2,1,0:T(8,128)S(1)} %collective-permute-done.other_rhs_ref.refs_5_, bf16[256,256]{1,0:T(8,128)(2,1)S(1)} %get-tuple-element.37.inverse_ref, ...), custom_call_target="tpu_custom_call" | custom-call | flops 8388608 | tf_op jit(solution)/shard_map/pallas_call | solution.py:36
  4.2 7.0 %all-to-all-start = ((bf16[8,64,256]{2,1,0:T(8,128)(2,1)}), bf16[8,64,256]{2,1,0:T(8,128)(2,1)S(1)}, u32[]{:S(2)}, u32[]{:S(2)}) async-start(bf16[8,64,256]{2,1,0:T(8,128)(2,1)} %get-tuple-element.40), calls=%async_computation | async-start | bytes 524288 | tf_op jit(solution)/shard_map/all_to_all | solution.py:232
  11.2 1.5 %collective-permute-start.4 = (f32[64,256]{1,0:T(8,128)}, f32[64,256]{1,0:T(8,128)S(1)}, u32[]{:S(2)}, u32[]{:S(2)}) collective-permute-start(f32[64,256]{1,0:T(8,128)} %get-tuple-element.38), channel_id=1, source_target_pairs={{0,0},{1,2},{2,1},{3,3},{4,4},{5,6},{6,5},{7,7},{8,8},{9,10},{10,9... | collective-permute-start | bytes 196616 | tf_op jit(solution)/shard_map/ppermute | solution.py:223
  12.7 2.1 %collective-permute-start.2 = (s32[3,1,1,8]{3,2,1,0:T(1,128)S(1)}, s32[3,1,1,8]{3,2,1,0:T(1,128)S(1)}, u32[]{:S(2)}, u32[]{:S(2)}) collective-permute-start(s32[3,1,1,8]{3,2,1,0:T(1,128)S(1)} %get-tuple-element.39.refs_0_), channel_id=1, source_target_pairs={{0,2},{2,0},{4,6},{6,4},{8,10},{10,8},{12,14},{14,12},{16,18},{18,... | collective-permute-start | bytes 296 | tf_op jit(solution)/shard_map/ppermute | solution.py:226
  14.8 0.8 %collective-permute-done.2.refs_1_ = s32[3,1,1,8]{3,2,1,0:T(1,128)S(1)} collective-permute-done((s32[3,1,1,8]{3,2,1,0:T(1,128)S(1)}, s32[3,1,1,8]{3,2,1,0:T(1,128)S(1)}, u32[]{:S(2)}, u32[]{:S(2)}) %collective-permute-start.2) | collective-permute-done | bytes 128 | tf_op jit(solution)/shard_map/ppermute | solution.py:226
  15.6 0.0 collective-permute-done.3.refs_3_
  15.6 0.0 copy-done
  15.6 0.0 copy-done.1
  15.6 2.3 %shard_map.57 = (bf16[2,8,256,256]{3,2,1,0:T(8,128)(2,1)S(1)}, f32[64,256]{1,0:T(8,128)S(1)}, bf16[256,256]{1,0:T(8,128)(2,1)S(1)}) custom-call(s32[3,1,1,8]{3,2,1,0:T(1,128)S(1)} %get-tuple-element.39.refs_0_, s32[3,1,1,8]{3,2,1,0:T(1,128)S(1)} %collective-permute-done.2.refs_1_, bf16[3,1,1,8,256,256]{5,4,3,2,1,0:T(8,128)(2,1)} %refs_2_.5, ...), custom_call_target="tpu_custom_call" | custom-call | bytes 2097152 | tf_op jit(solution)/shard_map/pallas_call | solution.py:36
  17.9 0.0 copy-start.2
  17.9 0.7 %copy-done.2 = bf16[256,256]{1,0:T(8,128)(2,1)} copy-done((bf16[256,256]{1,0:T(8,128)(2,1)}, bf16[256,256]{1,0:T(8,128)(2,1)S(1)}, u32[]{:S(2)}) %copy-start.2) | copy-done | bytes 131096
  18.6 0.0 collective-permute-done.4.refs_4_.refs_6_.refs_0_
  18.6 0.0 copy-start.3
  18.6 2.1 %all-to-all-done.refs_2_.refs_8_ = bf16[8,64,256]{2,1,0:T(8,128)(2,1)S(1)} async-done(((bf16[8,64,256]{2,1,0:T(8,128)(2,1)}), bf16[8,64,256]{2,1,0:T(8,128)(2,1)S(1)}, u32[]{:S(2)}, u32[]{:S(2)}) %all-to-all-start) | async-done | bytes 262176 | tf_op jit(solution)/shard_map/all_to_all | solution.py:232
  20.6 1.1 %shard_map.58 = (f32[64,256]{1,0:T(8,128)S(1)}, f32[64,256]{1,0:T(8,128)S(1)}) custom-call(s32[3,1,1,8]{3,2,1,0:T(1,128)S(1)} %get-tuple-element.39.refs_0_, s32[3,1,1,8]{3,2,1,0:T(1,128)S(1)} %collective-permute-done.2.refs_1_, bf16[8,64,256]{2,1,0:T(8,128)(2,1)S(1)} %all-to-all-done.refs_2_.refs_8_, ...), custom_call_target="tpu_custom_call" | custom-call | flops 134217728 | bytes 2097152 | tf_op jit(solution)/shard_map/pallas_call | solution.py:36
  21.7 1.6 %collective-permute-start.5 = (f32[64,256]{1,0:T(8,128)S(1)}, f32[64,256]{1,0:T(8,128)S(1)}, u32[]{:S(2)}, u32[]{:S(2)}) collective-permute-start(f32[64,256]{1,0:T(8,128)S(1)} %get-tuple-element.44), channel_id=1, source_target_pairs={{0,1},{1,0},{2,3},{3,2},{4,5},{5,4},{6,7},{7,6},{8,9},{9,8},{10,11... | collective-permute-start | bytes 196616 | tf_op jit(solution)/shard_map/ppermute | solution.py:301
  23.3 2.7 %collective-permute-done.5.arrived_ref = f32[64,256]{1,0:T(8,128)S(1)} collective-permute-done((f32[64,256]{1,0:T(8,128)S(1)}, f32[64,256]{1,0:T(8,128)S(1)}, u32[]{:S(2)}, u32[]{:S(2)}) %collective-permute-start.5) | collective-permute-done | bytes 65568 | tf_op jit(solution)/shard_map/ppermute | solution.py:301
  26.0 0.0 copy-done.3
  26.0 0.9 %shard_map.59 = (f32[64,256]{1,0:T(8,128)S(1)}, bf16[8,64,256]{2,1,0:T(8,128)(2,1)}) custom-call(f32[64,256]{1,0:T(8,128)S(1)} %get-tuple-element.43.kept_ref.refs_9_, f32[64,256]{1,0:T(8,128)S(1)} %collective-permute-done.5.arrived_ref, f32[64,256]{1,0:T(8,128)S(1)} %get-tuple-element.45.rhs_ref, bf16[256,256]{1,0:T(8,128)(2,1)S(1)} %copy-done.3), custom_call_target="tpu_custom_call" | custom-call | flops 8388608 | tf_op jit(solution)/shard_map/pallas_call | solution.py:36
  26.9 4.0 %all-to-all-start.1 = ((bf16[8,64,256]{2,1,0:T(8,128)(2,1)}), bf16[8,64,256]{2,1,0:T(8,128)(2,1)S(1)}, u32[]{:S(2)}, u32[]{:S(2)}) async-start(bf16[8,64,256]{2,1,0:T(8,128)(2,1)} %get-tuple-element.47), calls=%async_computation.1 | async-start | bytes 524288 | tf_op jit(solution)/shard_map/all_to_all | solution.py:232
  30.9 0.7 %collective-permute-start.6 = (f32[64,256]{1,0:T(8,128)S(1)}, f32[64,256]{1,0:T(8,128)S(1)}, u32[]{:S(2)}, u32[]{:S(2)}) collective-permute-start(f32[64,256]{1,0:T(8,128)S(1)} %get-tuple-element.51), channel_id=1, source_target_pairs={{0,0},{1,2},{2,1},{3,3},{4,4},{5,6},{6,5},{7,7},{8,8},{9,10},{10,9... | collective-permute-start | bytes 196616 | tf_op jit(solution)/shard_map/ppermute | solution.py:223
  31.6 2.7 %shard_map.60 = (bf16[2,8,256,256]{3,2,1,0:T(8,128)(2,1)S(1)}, f32[64,256]{1,0:T(8,128)S(1)}, bf16[256,256]{1,0:T(8,128)(2,1)S(1)}, f32[64,256]{1,0:T(8,128)S(1)}, f32[64,256]{1,0:T(8,128)S(1)}) custom-call(s32[3,1,1,8]{3,2,1,0:T(1,128)S(1)} %get-tuple-element.39.refs_0_, s32[3,1,1,8]{3,2,1,0:T(1,128)S(1)} %collective-permute-done.2.refs_1_, ...), custom_call_target="tpu_custom_call" | custom-call | flops 134217728 | bytes 2097152 | tf_op jit(solution)/shard_map/pallas_call | solution.py:36
  34.3 0.0 collective-permute-done.6.refs_7_.refs_1_
  34.3 5.2 %all-to-all-done.1.refs_2_.refs_9_ = bf16[8,64,256]{2,1,0:T(8,128)(2,1)S(1)} async-done(((bf16[8,64,256]{2,1,0:T(8,128)(2,1)}), bf16[8,64,256]{2,1,0:T(8,128)(2,1)S(1)}, u32[]{:S(2)}, u32[]{:S(2)}) %all-to-all-start.1) | async-done | bytes 262176 | tf_op jit(solution)/shard_map/all_to_all | solution.py:232
  39.5 1.1 %shard_map.61 = (f32[64,256]{1,0:T(8,128)S(1)}, f32[64,256]{1,0:T(8,128)S(1)}) custom-call(s32[3,1,1,8]{3,2,1,0:T(1,128)S(1)} %get-tuple-element.39.refs_0_, s32[3,1,1,8]{3,2,1,0:T(1,128)S(1)} %collective-permute-done.2.refs_1_, bf16[8,64,256]{2,1,0:T(8,128)(2,1)S(1)} %all-to-all-done.1.refs_2_.refs_9_, ...), custom_call_target="tpu_custom_call" | custom-call | flops 134217728 | bytes 2097152 | tf_op jit(solution)/shard_map/pallas_call | solution.py:36
  40.6 0.8 %collective-permute-start.7 = (f32[64,256]{1,0:T(8,128)S(1)}, f32[64,256]{1,0:T(8,128)S(1)}, u32[]{:S(2)}, u32[]{:S(2)}) collective-permute-start(f32[64,256]{1,0:T(8,128)S(1)} %get-tuple-element.53), channel_id=1, source_target_pairs={{0,1},{1,0},{2,3},{3,2},{4,5},{5,4},{6,7},{7,6},{8,9},{9,8},{10,11... | collective-permute-start | bytes 196616 | tf_op jit(solution)/shard_map/ppermute | solution.py:301
  41.4 3.6 %collective-permute-done.7.arrived_ref = f32[64,256]{1,0:T(8,128)S(1)} collective-permute-done((f32[64,256]{1,0:T(8,128)S(1)}, f32[64,256]{1,0:T(8,128)S(1)}, u32[]{:S(2)}, u32[]{:S(2)}) %collective-permute-start.7) | collective-permute-done | bytes 65568 | tf_op jit(solution)/shard_map/ppermute | solution.py:301
  44.9 0.9 %shard_map.62 = (f32[64,256]{1,0:T(8,128)S(1)}, bf16[8,64,256]{2,1,0:T(8,128)(2,1)}) custom-call(f32[64,256]{1,0:T(8,128)S(1)} %get-tuple-element.52.kept_ref.refs_10_, f32[64,256]{1,0:T(8,128)S(1)} %collective-permute-done.7.arrived_ref, f32[64,256]{1,0:T(8,128)S(1)} %get-tuple-element.54.rhs_ref, bf16[256,256]{1,0:T(8,128)(2,1)S(1)} %get-tuple-element.55.inverse_ref), custom_call_target="tpu_custom_call" | custom-call | flops 8388608 | tf_op jit(solution)/shard_map/pallas_call | solution.py:36
  45.8 3.6 %all-to-all-start.2 = ((bf16[8,64,256]{2,1,0:T(8,128)(2,1)}), bf16[8,64,256]{2,1,0:T(8,128)(2,1)S(1)}, u32[]{:S(2)}, u32[]{:S(2)}) async-start(bf16[8,64,256]{2,1,0:T(8,128)(2,1)} %get-tuple-element.56), calls=%async_computation.2 | async-start | bytes 524288 | tf_op jit(solution)/shard_map/all_to_all | solution.py:232
  49.4 0.7 %collective-permute-start.8 = (f32[64,256]{1,0:T(8,128)S(1)}, f32[64,256]{1,0:T(8,128)S(1)}, u32[]{:S(2)}, u32[]{:S(2)}) collective-permute-start(f32[64,256]{1,0:T(8,128)S(1)} %get-tuple-element.60), channel_id=1, source_target_pairs={{0,0},{1,2},{2,1},{3,3},{4,4},{5,6},{6,5},{7,7},{8,8},{9,10},{10,9... | collective-permute-start | bytes 196616 | tf_op jit(solution)/shard_map/ppermute | solution.py:223
  50.1 2.7 %shard_map.63 = (bf16[2,8,256,256]{3,2,1,0:T(8,128)(2,1)S(1)}, f32[64,256]{1,0:T(8,128)S(1)}, bf16[256,256]{1,0:T(8,128)(2,1)S(1)}, f32[64,256]{1,0:T(8,128)S(1)}, f32[64,256]{1,0:T(8,128)S(1)}) custom-call(s32[3,1,1,8]{3,2,1,0:T(1,128)S(1)} %get-tuple-element.39.refs_0_, s32[3,1,1,8]{3,2,1,0:T(1,128)S(1)} %collective-permute-done.2.refs_1_, ...), custom_call_target="tpu_custom_call" | custom-call | flops 134217728 | bytes 2097152 | tf_op jit(solution)/shard_map/pallas_call | solution.py:36
  52.8 0.0 collective-permute-done.8.refs_8_.refs_2_
  52.8 4.8 %all-to-all-done.2.refs_2_ = bf16[8,64,256]{2,1,0:T(8,128)(2,1)S(1)} async-done(((bf16[8,64,256]{2,1,0:T(8,128)(2,1)}), bf16[8,64,256]{2,1,0:T(8,128)(2,1)S(1)}, u32[]{:S(2)}, u32[]{:S(2)}) %all-to-all-start.2) | async-done | bytes 262176 | tf_op jit(solution)/shard_map/all_to_all | solution.py:232
  57.6 1.1 %shard_map.64 = (bf16[64,256]{1,0:T(8,128)(2,1)S(1)}, bf16[64,256]{1,0:T(8,128)(2,1)S(1)}) custom-call(s32[3,1,1,8]{3,2,1,0:T(1,128)S(1)} %get-tuple-element.39.refs_0_, s32[3,1,1,8]{3,2,1,0:T(1,128)S(1)} %collective-permute-done.2.refs_1_, bf16[8,64,256]{2,1,0:T(8,128)(2,1)S(1)} %all-to-all-done.2.refs_2_, ...), custom_call_target="tpu_custom_call" | custom-call | flops 134217728 | bytes 2097152 | tf_op jit(solution)/shard_map/pallas_call | solution.py:36
  58.7 0.7 %collective-permute-start.9 = (bf16[64,256]{1,0:T(8,128)(2,1)S(1)}, bf16[64,256]{1,0:T(8,128)(2,1)S(1)}, u32[]{:S(2)}, u32[]{:S(2)}) collective-permute-start(bf16[64,256]{1,0:T(8,128)(2,1)S(1)} %get-tuple-element.61), channel_id=1, source_target_pairs={{0,0},{1,2},{2,1},{3,3},{4,4},{5,6},{6,5},{7,7},{8,8},{9,10},{10,9... | collective-permute-start | bytes 98312 | tf_op jit(solution)/shard_map/ppermute | solution.py:223
  59.4 1.8 %collective-permute-start.10 = (bf16[64,256]{1,0:T(8,128)(2,1)S(1)}, bf16[64,256]{1,0:T(8,128)(2,1)S(1)}, u32[]{:S(2)}, u32[]{:S(2)}) collective-permute-start(bf16[64,256]{1,0:T(8,128)(2,1)S(1)} %get-tuple-element.62), channel_id=1, source_target_pairs={{0,2},{1,0},{2,3},{3,1},{4,6},{5,4},{6,7},{7,5},{8,10},{9,8},{10,1... | collective-permute-start | bytes 98312 | tf_op jit(solution)/shard_map/ppermute | solution.py:223
  61.2 0.0 collective-permute-done.9.first_ref
  61.2 2.1 %collective-permute-done.10.second_ref = bf16[64,256]{1,0:T(8,128)(2,1)S(1)} collective-permute-done((bf16[64,256]{1,0:T(8,128)(2,1)S(1)}, bf16[64,256]{1,0:T(8,128)(2,1)S(1)}, u32[]{:S(2)}, u32[]{:S(2)}) %collective-permute-start.10) | collective-permute-done | bytes 32800 | tf_op jit(solution)/shard_map/ppermute | solution.py:223
  63.3 0.9 %shard_map.65 = f32[4,1,64,256]{3,2,1,0:T(8,128)} custom-call(bf16[64,256]{1,0:T(8,128)(2,1)S(1)} %collective-permute-done.9.first_ref, bf16[64,256]{1,0:T(8,128)(2,1)S(1)} %collective-permute-done.10.second_ref, f32[64,256]{1,0:T(8,128)S(1)} %get-tuple-element.63.rhs_ref, bf16[256,256]{1,0:T(8,128)(2,1)S(1)} %get-tuple-element.64.inverse_ref, ...), custom_call_target="tpu_custom_call" | custom-call | flops 8388608 | tf_op jit(solution)/shard_map/pallas_call | solution.py:36
Async XLA Ops:
  0.0 2.2 %collective-permute-start = (f32[4,1,128,256]{3,2,1,0:T(8,128)}, f32[4,1,128,256]{3,2,1,0:T(8,128)S(1)}, u32[]{:S(2)}, u32[]{:S(2)}) collective-permute-start(f32[4,1,128,256]{3,2,1,0:T(8,128)} %refs_4_.5), channel_id=1, source_target_pairs={{0,2},{2,0},{4,6},{6,4},{8,10},{10,8},{12,14},{14,12},{16,18},{18,... | collective-permute-start | bytes 1572872 | tf_op jit(solution)/shard_map/ppermute | solution.py:226
  0.5 2.5 %collective-permute-start.1 = (bf16[4,1,256,256]{3,2,1,0:T(8,128)(2,1)}, bf16[4,1,256,256]{3,2,1,0:T(8,128)(2,1)S(1)}, u32[]{:S(2)}, u32[]{:S(2)}) collective-permute-start(bf16[4,1,256,256]{3,2,1,0:T(8,128)(2,1)} %refs_6_.5), channel_id=1, source_target_pairs={{0,2},{2,0},{4,6},{6,4},{8,10},{10,8},{12,14},{14,12},{16,18},{18,... | collective-permute-start | bytes 1572872 | tf_op jit(solution)/shard_map/ppermute | solution.py:226
  2.2 13.4 %copy-start = (f32[4,1,128,256]{3,2,1,0:T(8,128)}, f32[4,1,128,256]{3,2,1,0:T(8,128)S(1)}, u32[]{:S(2)}) copy-start(f32[4,1,128,256]{3,2,1,0:T(8,128)S(1)} %collective-permute-done.other_rhs_ref.refs_5_) | copy-start | bytes 1572868
  3.0 12.7 %copy-start.1 = (bf16[4,1,256,256]{3,2,1,0:T(8,128)(2,1)}, bf16[4,1,256,256]{3,2,1,0:T(8,128)(2,1)S(1)}, u32[]{:S(2)}) copy-start(bf16[4,1,256,256]{3,2,1,0:T(8,128)(2,1)S(1)} %collective-permute-done.1.other_inverse_ref.refs_7_) | copy-start | bytes 1572868
  3.0 12.7 %collective-permute-start.3 = (bf16[3,1,1,8,256,256]{5,4,3,2,1,0:T(8,128)(2,1)}, bf16[3,1,1,8,256,256]{5,4,3,2,1,0:T(8,128)(2,1)}, u32[]{:S(2)}, u32[]{:S(2)}) collective-permute-start(bf16[3,1,1,8,256,256]{5,4,3,2,1,0:T(8,128)(2,1)} %refs_2_.5), channel_id=1, source_target_pairs={{0,2},{2,0},{4,6},{6,4},{8,10},{10,8},{12,14},{14,12},{16,18},{18,... | collective-permute-start | bytes 9437192 | tf_op jit(solution)/shard_map/ppermute | solution.py:226
  4.2 16.4 %all-to-all-start = ((bf16[8,64,256]{2,1,0:T(8,128)(2,1)}), bf16[8,64,256]{2,1,0:T(8,128)(2,1)S(1)}, u32[]{:S(2)}, u32[]{:S(2)}) async-start(bf16[8,64,256]{2,1,0:T(8,128)(2,1)} %get-tuple-element.40), calls=%async_computation | async-start | bytes 524288 | tf_op jit(solution)/shard_map/all_to_all | solution.py:232
  11.2 7.4 %collective-permute-start.4 = (f32[64,256]{1,0:T(8,128)}, f32[64,256]{1,0:T(8,128)S(1)}, u32[]{:S(2)}, u32[]{:S(2)}) collective-permute-start(f32[64,256]{1,0:T(8,128)} %get-tuple-element.38), channel_id=1, source_target_pairs={{0,0},{1,2},{2,1},{3,3},{4,4},{5,6},{6,5},{7,7},{8,8},{9,10},{10,9... | collective-permute-start | bytes 196616 | tf_op jit(solution)/shard_map/ppermute | solution.py:223
  12.7 2.9 %collective-permute-start.2 = (s32[3,1,1,8]{3,2,1,0:T(1,128)S(1)}, s32[3,1,1,8]{3,2,1,0:T(1,128)S(1)}, u32[]{:S(2)}, u32[]{:S(2)}) collective-permute-start(s32[3,1,1,8]{3,2,1,0:T(1,128)S(1)} %get-tuple-element.39.refs_0_), channel_id=1, source_target_pairs={{0,2},{2,0},{4,6},{6,4},{8,10},{10,8},{12,14},{14,12},{16,18},{18,... | collective-permute-start | bytes 296 | tf_op jit(solution)/shard_map/ppermute | solution.py:226
  17.9 0.7 %copy-start.2 = (bf16[256,256]{1,0:T(8,128)(2,1)}, bf16[256,256]{1,0:T(8,128)(2,1)S(1)}, u32[]{:S(2)}) copy-start(bf16[256,256]{1,0:T(8,128)(2,1)S(1)} %get-tuple-element.46.inverse_ref) | copy-start | bytes 393220
  18.6 7.5 %copy-start.3 = (bf16[256,256]{1,0:T(8,128)(2,1)S(1)}, bf16[256,256]{1,0:T(8,128)(2,1)}, u32[]{:S(2)}) copy-start(bf16[256,256]{1,0:T(8,128)(2,1)} %copy-done.2) | copy-start | bytes 393220
  21.7 4.3 %collective-permute-start.5 = (f32[64,256]{1,0:T(8,128)S(1)}, f32[64,256]{1,0:T(8,128)S(1)}, u32[]{:S(2)}, u32[]{:S(2)}) collective-permute-start(f32[64,256]{1,0:T(8,128)S(1)} %get-tuple-element.44), channel_id=1, source_target_pairs={{0,1},{1,0},{2,3},{3,2},{4,5},{5,4},{6,7},{7,6},{8,9},{9,8},{10,11... | collective-permute-start | bytes 196616 | tf_op jit(solution)/shard_map/ppermute | solution.py:301
  26.9 12.6 %all-to-all-start.1 = ((bf16[8,64,256]{2,1,0:T(8,128)(2,1)}), bf16[8,64,256]{2,1,0:T(8,128)(2,1)S(1)}, u32[]{:S(2)}, u32[]{:S(2)}) async-start(bf16[8,64,256]{2,1,0:T(8,128)(2,1)} %get-tuple-element.47), calls=%async_computation.1 | async-start | bytes 524288 | tf_op jit(solution)/shard_map/all_to_all | solution.py:232
  30.9 3.4 %collective-permute-start.6 = (f32[64,256]{1,0:T(8,128)S(1)}, f32[64,256]{1,0:T(8,128)S(1)}, u32[]{:S(2)}, u32[]{:S(2)}) collective-permute-start(f32[64,256]{1,0:T(8,128)S(1)} %get-tuple-element.51), channel_id=1, source_target_pairs={{0,0},{1,2},{2,1},{3,3},{4,4},{5,6},{6,5},{7,7},{8,8},{9,10},{10,9... | collective-permute-start | bytes 196616 | tf_op jit(solution)/shard_map/ppermute | solution.py:223
  40.6 4.3 %collective-permute-start.7 = (f32[64,256]{1,0:T(8,128)S(1)}, f32[64,256]{1,0:T(8,128)S(1)}, u32[]{:S(2)}, u32[]{:S(2)}) collective-permute-start(f32[64,256]{1,0:T(8,128)S(1)} %get-tuple-element.53), channel_id=1, source_target_pairs={{0,1},{1,0},{2,3},{3,2},{4,5},{5,4},{6,7},{7,6},{8,9},{9,8},{10,11... | collective-permute-start | bytes 196616 | tf_op jit(solution)/shard_map/ppermute | solution.py:301
  45.8 11.8 %all-to-all-start.2 = ((bf16[8,64,256]{2,1,0:T(8,128)(2,1)}), bf16[8,64,256]{2,1,0:T(8,128)(2,1)S(1)}, u32[]{:S(2)}, u32[]{:S(2)}) async-start(bf16[8,64,256]{2,1,0:T(8,128)(2,1)} %get-tuple-element.56), calls=%async_computation.2 | async-start | bytes 524288 | tf_op jit(solution)/shard_map/all_to_all | solution.py:232
  49.4 3.4 %collective-permute-start.8 = (f32[64,256]{1,0:T(8,128)S(1)}, f32[64,256]{1,0:T(8,128)S(1)}, u32[]{:S(2)}, u32[]{:S(2)}) collective-permute-start(f32[64,256]{1,0:T(8,128)S(1)} %get-tuple-element.60), channel_id=1, source_target_pairs={{0,0},{1,2},{2,1},{3,3},{4,4},{5,6},{6,5},{7,7},{8,8},{9,10},{10,9... | collective-permute-start | bytes 196616 | tf_op jit(solution)/shard_map/ppermute | solution.py:223
  58.7 2.5 %collective-permute-start.9 = (bf16[64,256]{1,0:T(8,128)(2,1)S(1)}, bf16[64,256]{1,0:T(8,128)(2,1)S(1)}, u32[]{:S(2)}, u32[]{:S(2)}) collective-permute-start(bf16[64,256]{1,0:T(8,128)(2,1)S(1)} %get-tuple-element.61), channel_id=1, source_target_pairs={{0,0},{1,2},{2,1},{3,3},{4,4},{5,6},{6,5},{7,7},{8,8},{9,10},{10,9... | collective-permute-start | bytes 98312 | tf_op jit(solution)/shard_map/ppermute | solution.py:223
  59.4 3.9 %collective-permute-start.10 = (bf16[64,256]{1,0:T(8,128)(2,1)S(1)}, bf16[64,256]{1,0:T(8,128)(2,1)S(1)}, u32[]{:S(2)}, u32[]{:S(2)}) collective-permute-start(bf16[64,256]{1,0:T(8,128)(2,1)S(1)} %get-tuple-element.62), channel_id=1, source_target_pairs={{0,2},{1,0},{2,3},{3,1},{4,6},{5,4},{6,7},{7,5},{8,10},{9,8},{10,1... | collective-permute-start | bytes 98312 | tf_op jit(solution)/shard_map/ppermute | solution.py:223

commit v19 on v18

--- a/solution.py
+++ b/solution.py
@@ -307,12 +307,12 @@
             )
             finished.append(transpose(solved))
             stores.append(spread(copied))
+    second = over_both(sent, lambda j, k, c: (j, 1 - c, k))
     first = over_both(kept, lambda j, k, c: (j, c, k))
-    second = over_both(sent, lambda j, k, c: (j, 1 - c, k))
     out, = run(
         last_kernel,
         ((jax.ShapeDtypeStruct((level_count, 1, rows, width), jnp.float32), VMEM),),
-        tuple((x, VMEM) for x in (first, second, rhs, inverse, *finished)),
+        tuple((x, VMEM) for x in (second, first, rhs, inverse, *finished)),
         flops=solve_flops,
     )
     return out

time: 64.8 us -> 65.3 us (level)
  the two profiles are of different devices: /device:TPU:0 before, /device:TPU:1 now
where the time goes in v19:
time: 65.3 us; the launch traced here: 64.7 us
  starting transfers between devices  38.5 us (59%)
  Pallas kernels  16 us (25%)
  waiting for transfers between devices  9.46 us (14%)
  local copies, waits for them, and re-layouts  0.67 us (1%)
    ppermute x5, starting transfers between devices, over_both(): return lax.ppermute(x, ('rows', 'cols'), pairs)  18.5 us
    all_to_all x3, starting transfers between devices, spread(): return lax.all_to_all(x, 'rows', 0, 0, axis_index_groups=same_core)  17.8 us
    pallas_call x11, Pallas kernels, run(): pl.pallas_call(kernel, out_shape=out_shape, in_specs=[spec for _, spec in...  16 us
    ppermute x2, waiting for transfers between devices, paired_shards(): arrived = lax.ppermute(sent, 'cols', [(0, 1), (1, 0)])  4.98 us
    ppermute x4, waiting for transfers between devices, swap_core(): return lax.ppermute(x, 'rows', [(i, i ^ 1) for i in range(row_count)])  1.9 us
    ppermute x5, waiting for transfers between devices, over_both(): return lax.ppermute(x, ('rows', 'cols'), pairs)  1.58 us
    ppermute x2, starting transfers between devices, paired_shards(): arrived = lax.ppermute(sent, 'cols', [(0, 1), (1, 0)])  1.38 us
  transfers between devices with their start and end apart: 14, of which 8 were waited for; matrix products, arithmetic and copies ran while one was open for 0% of the time, Pallas kernels for 16%

profile of v19, /device:TPU:1, one launch (start us, length us, event | category | flops | bytes accessed | tf_op | source)
XLA Modules:
  0.0 64.7 jit_solution(16731520021713606087)
XLA Ops:
  0.0 0.1 collective-permute-start
  0.1 0.5 collective-permute-start.1
  0.5 1.6 %shard_map.55 = (s32[3,1,1,8]{3,2,1,0:T(1,128)S(1)}, f32[64,256]{1,0:T(8,128)S(1)}, bf16[256,256]{1,0:T(8,128)(2,1)S(1)}) custom-call(s32[3,1,1,8]{3,2,1,0:T(1,128)} %ids_ref.1, s32[3]{0:T(128)} %bitcast.1, f32[4,1,128,256]{3,2,1,0:T(8,128)} %refs_4_.5, bf16[4,1,256,256]{3,2,1,0:T(8,128)(2,1)} %refs_6_.5), custom_call_target="tpu_custom_call" | custom-call | tf_op jit(solution)/shard_map/pallas_call | solution.py:36
  2.1 0.0 collective-permute-done.other_rhs_ref.refs_5_
  2.1 0.0 copy-start
  2.1 0.7 %collective-permute-done.1.other_inverse_ref.refs_7_ = bf16[4,1,256,256]{3,2,1,0:T(8,128)(2,1)S(1)} collective-permute-done((bf16[4,1,256,256]{3,2,1,0:T(8,128)(2,1)}, bf16[4,1,256,256]{3,2,1,0:T(8,128)(2,1)S(1)}, u32[]{:S(2)}, u32[]{:S(2)}) %collective-permute-start.1) | collective-permute-done | bytes 524320 | tf_op jit(solution)/shard_map/ppermute | solution.py:226
  2.9 0.0 copy-start.1
  2.9 0.1 collective-permute-start.3
  3.0 0.9 %shard_map.56 = (f32[64,256]{1,0:T(8,128)}, bf16[8,64,256]{2,1,0:T(8,128)(2,1)}) custom-call(f32[64,256]{1,0:T(8,128)S(1)} %get-tuple-element.36.rhs_ref, f32[4,1,128,256]{3,2,1,0:T(8,128)S(1)} %collective-permute-done.other_rhs_ref.refs_5_, bf16[256,256]{1,0:T(8,128)(2,1)S(1)} %get-tuple-element.37.inverse_ref, ...), custom_call_target="tpu_custom_call" | custom-call | flops 8388608 | tf_op jit(solution)/shard_map/pallas_call | solution.py:36
  3.9 6.9 %all-to-all-start = ((bf16[8,64,256]{2,1,0:T(8,128)(2,1)}), bf16[8,64,256]{2,1,0:T(8,128)(2,1)S(1)}, u32[]{:S(2)}, u32[]{:S(2)}) async-start(bf16[8,64,256]{2,1,0:T(8,128)(2,1)} %get-tuple-element.40), calls=%async_computation | async-start | bytes 524288 | tf_op jit(solution)/shard_map/all_to_all | solution.py:232
  10.8 3.5 %collective-permute-start.4 = (f32[64,256]{1,0:T(8,128)}, f32[64,256]{1,0:T(8,128)S(1)}, u32[]{:S(2)}, u32[]{:S(2)}) collective-permute-start(f32[64,256]{1,0:T(8,128)} %get-tuple-element.38), channel_id=1, source_target_pairs={{0,0},{1,2},{2,1},{3,3},{4,4},{5,6},{6,5},{7,7},{8,8},{9,10},{10,9... | collective-permute-start | bytes 196616 | tf_op jit(solution)/shard_map/ppermute | solution.py:223
  14.3 0.1 collective-permute-start.2
  14.4 1.1 %collective-permute-done.2.refs_1_ = s32[3,1,1,8]{3,2,1,0:T(1,128)S(1)} collective-permute-done((s32[3,1,1,8]{3,2,1,0:T(1,128)S(1)}, s32[3,1,1,8]{3,2,1,0:T(1,128)S(1)}, u32[]{:S(2)}, u32[]{:S(2)}) %collective-permute-start.2) | collective-permute-done | bytes 128 | tf_op jit(solution)/shard_map/ppermute | solution.py:226
  15.5 0.0 collective-permute-done.3.refs_3_
  15.5 0.0 copy-done
  15.5 0.0 copy-done.1
  15.5 2.3 %shard_map.57 = (bf16[2,8,256,256]{3,2,1,0:T(8,128)(2,1)S(1)}, f32[64,256]{1,0:T(8,128)S(1)}, bf16[256,256]{1,0:T(8,128)(2,1)S(1)}) custom-call(s32[3,1,1,8]{3,2,1,0:T(1,128)S(1)} %get-tuple-element.39.refs_0_, s32[3,1,1,8]{3,2,1,0:T(1,128)S(1)} %collective-permute-done.2.refs_1_, bf16[3,1,1,8,256,256]{5,4,3,2,1,0:T(8,128)(2,1)} %refs_2_.5, ...), custom_call_target="tpu_custom_call" | custom-call | bytes 2097152 | tf_op jit(solution)/shard_map/pallas_call | solution.py:36
  17.8 0.0 copy-start.2
  17.8 0.7 %copy-done.2 = bf16[256,256]{1,0:T(8,128)(2,1)} copy-done((bf16[256,256]{1,0:T(8,128)(2,1)}, bf16[256,256]{1,0:T(8,128)(2,1)S(1)}, u32[]{:S(2)}) %copy-start.2) | copy-done | bytes 131096
  18.5 0.0 collective-permute-done.4.refs_4_.refs_6_.refs_0_
  18.5 0.0 copy-start.3
  18.5 0.4 all-to-all-done.refs_2_.refs_8_
  18.8 1.1 %shard_map.58 = (f32[64,256]{1,0:T(8,128)S(1)}, f32[64,256]{1,0:T(8,128)S(1)}) custom-call(s32[3,1,1,8]{3,2,1,0:T(1,128)S(1)} %get-tuple-element.39.refs_0_, s32[3,1,1,8]{3,2,1,0:T(1,128)S(1)} %collective-permute-done.2.refs_1_, bf16[8,64,256]{2,1,0:T(8,128)(2,1)S(1)} %all-to-all-done.refs_2_.refs_8_, ...), custom_call_target="tpu_custom_call" | custom-call | flops 134217728 | bytes 2097152 | tf_op jit(solution)/shard_map/pallas_call | solution.py:36
  19.9 1.3 %collective-permute-start.5 = (f32[64,256]{1,0:T(8,128)S(1)}, f32[64,256]{1,0:T(8,128)S(1)}, u32[]{:S(2)}, u32[]{:S(2)}) collective-permute-start(f32[64,256]{1,0:T(8,128)S(1)} %get-tuple-element.44), channel_id=1, source_target_pairs={{0,1},{1,0},{2,3},{3,2},{4,5},{5,4},{6,7},{7,6},{8,9},{9,8},{10,11... | collective-permute-start | bytes 196616 | tf_op jit(solution)/shard_map/ppermute | solution.py:301
  21.2 1.9 %collective-permute-done.5.arrived_ref = f32[64,256]{1,0:T(8,128)S(1)} collective-permute-done((f32[64,256]{1,0:T(8,128)S(1)}, f32[64,256]{1,0:T(8,128)S(1)}, u32[]{:S(2)}, u32[]{:S(2)}) %collective-permute-start.5) | collective-permute-done | bytes 65568 | tf_op jit(solution)/shard_map/ppermute | solution.py:301
  23.1 0.0 copy-done.3
  23.1 0.9 %shard_map.59 = (f32[64,256]{1,0:T(8,128)S(1)}, bf16[8,64,256]{2,1,0:T(8,128)(2,1)}) custom-call(f32[64,256]{1,0:T(8,128)S(1)} %get-tuple-element.43.kept_ref.refs_9_, f32[64,256]{1,0:T(8,128)S(1)} %collective-permute-done.5.arrived_ref, f32[64,256]{1,0:T(8,128)S(1)} %get-tuple-element.45.rhs_ref, bf16[256,256]{1,0:T(8,128)(2,1)S(1)} %copy-done.3), custom_call_target="tpu_custom_call" | custom-call | flops 8388608 | tf_op jit(solution)/shard_map/pallas_call | solution.py:36
  23.9 5.8 %all-to-all-start.1 = ((bf16[8,64,256]{2,1,0:T(8,128)(2,1)}), bf16[8,64,256]{2,1,0:T(8,128)(2,1)S(1)}, u32[]{:S(2)}, u32[]{:S(2)}) async-start(bf16[8,64,256]{2,1,0:T(8,128)(2,1)} %get-tuple-element.47), calls=%async_computation.1 | async-start | bytes 524288 | tf_op jit(solution)/shard_map/all_to_all | solution.py:232
  29.7 3.9 %collective-permute-start.6 = (f32[64,256]{1,0:T(8,128)S(1)}, f32[64,256]{1,0:T(8,128)S(1)}, u32[]{:S(2)}, u32[]{:S(2)}) collective-permute-start(f32[64,256]{1,0:T(8,128)S(1)} %get-tuple-element.51), channel_id=1, source_target_pairs={{0,0},{1,2},{2,1},{3,3},{4,4},{5,6},{6,5},{7,7},{8,8},{9,10},{10,9... | collective-permute-start | bytes 196616 | tf_op jit(solution)/shard_map/ppermute | solution.py:223
  33.6 2.7 %shard_map.60 = (bf16[2,8,256,256]{3,2,1,0:T(8,128)(2,1)S(1)}, f32[64,256]{1,0:T(8,128)S(1)}, bf16[256,256]{1,0:T(8,128)(2,1)S(1)}, f32[64,256]{1,0:T(8,128)S(1)}, f32[64,256]{1,0:T(8,128)S(1)}) custom-call(s32[3,1,1,8]{3,2,1,0:T(1,128)S(1)} %get-tuple-element.39.refs_0_, s32[3,1,1,8]{3,2,1,0:T(1,128)S(1)} %collective-permute-done.2.refs_1_, ...), custom_call_target="tpu_custom_call" | custom-call | flops 134217728 | bytes 2097152 | tf_op jit(solution)/shard_map/pallas_call | solution.py:36
  36.3 0.0 collective-permute-done.6.refs_7_.refs_1_
  36.3 0.6 all-to-all-done.1.refs_2_.refs_9_
  36.9 1.1 %shard_map.61 = (f32[64,256]{1,0:T(8,128)S(1)}, f32[64,256]{1,0:T(8,128)S(1)}) custom-call(s32[3,1,1,8]{3,2,1,0:T(1,128)S(1)} %get-tuple-element.39.refs_0_, s32[3,1,1,8]{3,2,1,0:T(1,128)S(1)} %collective-permute-done.2.refs_1_, bf16[8,64,256]{2,1,0:T(8,128)(2,1)S(1)} %all-to-all-done.1.refs_2_.refs_9_, ...), custom_call_target="tpu_custom_call" | custom-call | flops 134217728 | bytes 2097152 | tf_op jit(solution)/shard_map/pallas_call | solution.py:36
  38.0 0.1 collective-permute-start.7
  38.0 3.1 %collective-permute-done.7.arrived_ref = f32[64,256]{1,0:T(8,128)S(1)} collective-permute-done((f32[64,256]{1,0:T(8,128)S(1)}, f32[64,256]{1,0:T(8,128)S(1)}, u32[]{:S(2)}, u32[]{:S(2)}) %collective-permute-start.7) | collective-permute-done | bytes 65568 | tf_op jit(solution)/shard_map/ppermute | solution.py:301
  41.2 0.9 %shard_map.62 = (f32[64,256]{1,0:T(8,128)S(1)}, bf16[8,64,256]{2,1,0:T(8,128)(2,1)}) custom-call(f32[64,256]{1,0:T(8,128)S(1)} %get-tuple-element.52.kept_ref.refs_10_, f32[64,256]{1,0:T(8,128)S(1)} %collective-permute-done.7.arrived_ref, f32[64,256]{1,0:T(8,128)S(1)} %get-tuple-element.54.rhs_ref, bf16[256,256]{1,0:T(8,128)(2,1)S(1)} %get-tuple-element.55.inverse_ref), custom_call_target="tpu_custom_call" | custom-call | flops 8388608 | tf_op jit(solution)/shard_map/pallas_call | solution.py:36
  42.0 5.2 %all-to-all-start.2 = ((bf16[8,64,256]{2,1,0:T(8,128)(2,1)}), bf16[8,64,256]{2,1,0:T(8,128)(2,1)S(1)}, u32[]{:S(2)}, u32[]{:S(2)}) async-start(bf16[8,64,256]{2,1,0:T(8,128)(2,1)} %get-tuple-element.56), calls=%async_computation.2 | async-start | bytes 524288 | tf_op jit(solution)/shard_map/all_to_all | solution.py:232
  47.2 4.3 %collective-permute-start.8 = (f32[64,256]{1,0:T(8,128)S(1)}, f32[64,256]{1,0:T(8,128)S(1)}, u32[]{:S(2)}, u32[]{:S(2)}) collective-permute-start(f32[64,256]{1,0:T(8,128)S(1)} %get-tuple-element.60), channel_id=1, source_target_pairs={{0,0},{1,2},{2,1},{3,3},{4,4},{5,6},{6,5},{7,7},{8,8},{9,10},{10,9... | collective-permute-start | bytes 196616 | tf_op jit(solution)/shard_map/ppermute | solution.py:223
  51.5 2.7 %shard_map.63 = (bf16[2,8,256,256]{3,2,1,0:T(8,128)(2,1)S(1)}, f32[64,256]{1,0:T(8,128)S(1)}, bf16[256,256]{1,0:T(8,128)(2,1)S(1)}, f32[64,256]{1,0:T(8,128)S(1)}, f32[64,256]{1,0:T(8,128)S(1)}) custom-call(s32[3,1,1,8]{3,2,1,0:T(1,128)S(1)} %get-tuple-element.39.refs_0_, s32[3,1,1,8]{3,2,1,0:T(1,128)S(1)} %collective-permute-done.2.refs_1_, ...), custom_call_target="tpu_custom_call" | custom-call | flops 134217728 | bytes 2097152 | tf_op jit(solution)/shard_map/pallas_call | solution.py:36
  54.2 0.0 collective-permute-done.8.refs_8_.refs_2_
  54.2 0.1 all-to-all-done.2.refs_2_
  54.3 1.1 %shard_map.64 = (bf16[64,256]{1,0:T(8,128)(2,1)S(1)}, bf16[64,256]{1,0:T(8,128)(2,1)S(1)}) custom-call(s32[3,1,1,8]{3,2,1,0:T(1,128)S(1)} %get-tuple-element.39.refs_0_, s32[3,1,1,8]{3,2,1,0:T(1,128)S(1)} %collective-permute-done.2.refs_1_, bf16[8,64,256]{2,1,0:T(8,128)(2,1)S(1)} %all-to-all-done.2.refs_2_, ...), custom_call_target="tpu_custom_call" | custom-call | flops 134217728 | bytes 2097152 | tf_op jit(solution)/shard_map/pallas_call | solution.py:36
  55.4 0.0 collective-permute-start.9
  55.4 6.9 %collective-permute-start.10 = (bf16[64,256]{1,0:T(8,128)(2,1)S(1)}, bf16[64,256]{1,0:T(8,128)(2,1)S(1)}, u32[]{:S(2)}, u32[]{:S(2)}) collective-permute-start(bf16[64,256]{1,0:T(8,128)(2,1)S(1)} %get-tuple-element.62), channel_id=1, source_target_pairs={{0,0},{1,2},{2,1},{3,3},{4,4},{5,6},{6,5},{7,7},{8,8},{9,10},{10,9... | collective-permute-start | bytes 98312 | tf_op jit(solution)/shard_map/ppermute | solution.py:223
  62.3 0.0 collective-permute-done.9.first_ref
  62.3 1.6 %collective-permute-done.10.second_ref = bf16[64,256]{1,0:T(8,128)(2,1)S(1)} collective-permute-done((bf16[64,256]{1,0:T(8,128)(2,1)S(1)}, bf16[64,256]{1,0:T(8,128)(2,1)S(1)}, u32[]{:S(2)}, u32[]{:S(2)}) %collective-permute-start.10) | collective-permute-done | bytes 32800 | tf_op jit(solution)/shard_map/ppermute | solution.py:223
  63.9 0.9 %shard_map.65 = f32[4,1,64,256]{3,2,1,0:T(8,128)} custom-call(bf16[64,256]{1,0:T(8,128)(2,1)S(1)} %collective-permute-done.9.first_ref, bf16[64,256]{1,0:T(8,128)(2,1)S(1)} %collective-permute-done.10.second_ref, f32[64,256]{1,0:T(8,128)S(1)} %get-tuple-element.63.rhs_ref, bf16[256,256]{1,0:T(8,128)(2,1)S(1)} %get-tuple-element.64.inverse_ref, ...), custom_call_target="tpu_custom_call" | custom-call | flops 8388608 | tf_op jit(solution)/shard_map/pallas_call | solution.py:36
Async XLA Ops:
  0.0 2.1 %collective-permute-start = (f32[4,1,128,256]{3,2,1,0:T(8,128)}, f32[4,1,128,256]{3,2,1,0:T(8,128)S(1)}, u32[]{:S(2)}, u32[]{:S(2)}) collective-permute-start(f32[4,1,128,256]{3,2,1,0:T(8,128)} %refs_4_.5), channel_id=1, source_target_pairs={{0,2},{2,0},{4,6},{6,4},{8,10},{10,8},{12,14},{14,12},{16,18},{18,... | collective-permute-start | bytes 1572872 | tf_op jit(solution)/shard_map/ppermute | solution.py:226
  0.1 2.8 %collective-permute-start.1 = (bf16[4,1,256,256]{3,2,1,0:T(8,128)(2,1)}, bf16[4,1,256,256]{3,2,1,0:T(8,128)(2,1)S(1)}, u32[]{:S(2)}, u32[]{:S(2)}) collective-permute-start(bf16[4,1,256,256]{3,2,1,0:T(8,128)(2,1)} %refs_6_.5), channel_id=1, source_target_pairs={{0,2},{2,0},{4,6},{6,4},{8,10},{10,8},{12,14},{14,12},{16,18},{18,... | collective-permute-start | bytes 1572872 | tf_op jit(solution)/shard_map/ppermute | solution.py:226
  2.1 13.4 %copy-start = (f32[4,1,128,256]{3,2,1,0:T(8,128)}, f32[4,1,128,256]{3,2,1,0:T(8,128)S(1)}, u32[]{:S(2)}) copy-start(f32[4,1,128,256]{3,2,1,0:T(8,128)S(1)} %collective-permute-done.other_rhs_ref.refs_5_) | copy-start | bytes 1572868
  2.9 12.6 %copy-start.1 = (bf16[4,1,256,256]{3,2,1,0:T(8,128)(2,1)}, bf16[4,1,256,256]{3,2,1,0:T(8,128)(2,1)S(1)}, u32[]{:S(2)}) copy-start(bf16[4,1,256,256]{3,2,1,0:T(8,128)(2,1)S(1)} %collective-permute-done.1.other_inverse_ref.refs_7_) | copy-start | bytes 1572868
  2.9 12.6 %collective-permute-start.3 = (bf16[3,1,1,8,256,256]{5,4,3,2,1,0:T(8,128)(2,1)}, bf16[3,1,1,8,256,256]{5,4,3,2,1,0:T(8,128)(2,1)}, u32[]{:S(2)}, u32[]{:S(2)}) collective-permute-start(bf16[3,1,1,8,256,256]{5,4,3,2,1,0:T(8,128)(2,1)} %refs_2_.5), channel_id=1, source_target_pairs={{0,2},{2,0},{4,6},{6,4},{8,10},{10,8},{12,14},{14,12},{16,18},{18,... | collective-permute-start | bytes 9437192 | tf_op jit(solution)/shard_map/ppermute | solution.py:226
  3.9 14.9 %all-to-all-start = ((bf16[8,64,256]{2,1,0:T(8,128)(2,1)}), bf16[8,64,256]{2,1,0:T(8,128)(2,1)S(1)}, u32[]{:S(2)}, u32[]{:S(2)}) async-start(bf16[8,64,256]{2,1,0:T(8,128)(2,1)} %get-tuple-element.40), calls=%async_computation | async-start | bytes 524288 | tf_op jit(solution)/shard_map/all_to_all | solution.py:232
  10.8 7.6 %collective-permute-start.4 = (f32[64,256]{1,0:T(8,128)}, f32[64,256]{1,0:T(8,128)S(1)}, u32[]{:S(2)}, u32[]{:S(2)}) collective-permute-start(f32[64,256]{1,0:T(8,128)} %get-tuple-element.38), channel_id=1, source_target_pairs={{0,0},{1,2},{2,1},{3,3},{4,4},{5,6},{6,5},{7,7},{8,8},{9,10},{10,9... | collective-permute-start | bytes 196616 | tf_op jit(solution)/shard_map/ppermute | solution.py:223
  14.3 1.2 %collective-permute-start.2 = (s32[3,1,1,8]{3,2,1,0:T(1,128)S(1)}, s32[3,1,1,8]{3,2,1,0:T(1,128)S(1)}, u32[]{:S(2)}, u32[]{:S(2)}) collective-permute-start(s32[3,1,1,8]{3,2,1,0:T(1,128)S(1)} %get-tuple-element.39.refs_0_), channel_id=1, source_target_pairs={{0,2},{2,0},{4,6},{6,4},{8,10},{10,8},{12,14},{14,12},{16,18},{18,... | collective-permute-start | bytes 296 | tf_op jit(solution)/shard_map/ppermute | solution.py:226
  17.8 0.7 %copy-start.2 = (bf16[256,256]{1,0:T(8,128)(2,1)}, bf16[256,256]{1,0:T(8,128)(2,1)S(1)}, u32[]{:S(2)}) copy-start(bf16[256,256]{1,0:T(8,128)(2,1)S(1)} %get-tuple-element.46.inverse_ref) | copy-start | bytes 393220
  18.5 4.6 %copy-start.3 = (bf16[256,256]{1,0:T(8,128)(2,1)S(1)}, bf16[256,256]{1,0:T(8,128)(2,1)}, u32[]{:S(2)}) copy-start(bf16[256,256]{1,0:T(8,128)(2,1)} %copy-done.2) | copy-start | bytes 393220
  19.9 3.2 %collective-permute-start.5 = (f32[64,256]{1,0:T(8,128)S(1)}, f32[64,256]{1,0:T(8,128)S(1)}, u32[]{:S(2)}, u32[]{:S(2)}) collective-permute-start(f32[64,256]{1,0:T(8,128)S(1)} %get-tuple-element.44), channel_id=1, source_target_pairs={{0,1},{1,0},{2,3},{3,2},{4,5},{5,4},{6,7},{7,6},{8,9},{9,8},{10,11... | collective-permute-start | bytes 196616 | tf_op jit(solution)/shard_map/ppermute | solution.py:301
  23.9 13.0 %all-to-all-start.1 = ((bf16[8,64,256]{2,1,0:T(8,128)(2,1)}), bf16[8,64,256]{2,1,0:T(8,128)(2,1)S(1)}, u32[]{:S(2)}, u32[]{:S(2)}) async-start(bf16[8,64,256]{2,1,0:T(8,128)(2,1)} %get-tuple-element.47), calls=%async_computation.1 | async-start | bytes 524288 | tf_op jit(solution)/shard_map/all_to_all | solution.py:232
  29.7 6.6 %collective-permute-start.6 = (f32[64,256]{1,0:T(8,128)S(1)}, f32[64,256]{1,0:T(8,128)S(1)}, u32[]{:S(2)}, u32[]{:S(2)}) collective-permute-start(f32[64,256]{1,0:T(8,128)S(1)} %get-tuple-element.51), channel_id=1, source_target_pairs={{0,0},{1,2},{2,1},{3,3},{4,4},{5,6},{6,5},{7,7},{8,8},{9,10},{10,9... | collective-permute-start | bytes 196616 | tf_op jit(solution)/shard_map/ppermute | solution.py:223
  38.0 3.2 %collective-permute-start.7 = (f32[64,256]{1,0:T(8,128)S(1)}, f32[64,256]{1,0:T(8,128)S(1)}, u32[]{:S(2)}, u32[]{:S(2)}) collective-permute-start(f32[64,256]{1,0:T(8,128)S(1)} %get-tuple-element.53), channel_id=1, source_target_pairs={{0,1},{1,0},{2,3},{3,2},{4,5},{5,4},{6,7},{7,6},{8,9},{9,8},{10,11... | collective-permute-start | bytes 196616 | tf_op jit(solution)/shard_map/ppermute | solution.py:301
  42.0 12.3 %all-to-all-start.2 = ((bf16[8,64,256]{2,1,0:T(8,128)(2,1)}), bf16[8,64,256]{2,1,0:T(8,128)(2,1)S(1)}, u32[]{:S(2)}, u32[]{:S(2)}) async-start(bf16[8,64,256]{2,1,0:T(8,128)(2,1)} %get-tuple-element.56), calls=%async_computation.2 | async-start | bytes 524288 | tf_op jit(solution)/shard_map/all_to_all | solution.py:232
  47.2 7.0 %collective-permute-start.8 = (f32[64,256]{1,0:T(8,128)S(1)}, f32[64,256]{1,0:T(8,128)S(1)}, u32[]{:S(2)}, u32[]{:S(2)}) collective-permute-start(f32[64,256]{1,0:T(8,128)S(1)} %get-tuple-element.60), channel_id=1, source_target_pairs={{0,0},{1,2},{2,1},{3,3},{4,4},{5,6},{6,5},{7,7},{8,8},{9,10},{10,9... | collective-permute-start | bytes 196616 | tf_op jit(solution)/shard_map/ppermute | solution.py:223
  55.4 6.9 %collective-permute-start.9 = (bf16[64,256]{1,0:T(8,128)(2,1)S(1)}, bf16[64,256]{1,0:T(8,128)(2,1)S(1)}, u32[]{:S(2)}, u32[]{:S(2)}) collective-permute-start(bf16[64,256]{1,0:T(8,128)(2,1)S(1)} %get-tuple-element.61), channel_id=1, source_target_pairs={{0,2},{1,0},{2,3},{3,1},{4,6},{5,4},{6,7},{7,5},{8,10},{9,8},{10,1... | collective-permute-start | bytes 98312 | tf_op jit(solution)/shard_map/ppermute | solution.py:223
  55.4 8.5 %collective-permute-start.10 = (bf16[64,256]{1,0:T(8,128)(2,1)S(1)}, bf16[64,256]{1,0:T(8,128)(2,1)S(1)}, u32[]{:S(2)}, u32[]{:S(2)}) collective-permute-start(bf16[64,256]{1,0:T(8,128)(2,1)S(1)} %get-tuple-element.62), channel_id=1, source_target_pairs={{0,0},{1,2},{2,1},{3,3},{4,4},{5,6},{6,5},{7,7},{8,8},{9,10},{10,9... | collective-permute-start | bytes 98312 | tf_op jit(solution)/shard_map/ppermute | solution.py:223

commit v20 on v18

--- a/solution.py
+++ b/solution.py
@@ -159,7 +159,7 @@
         factor_copies[g].wait()
         if level > 1:
             older_refs[g][...] = slot_sum(
-                level, None, chips, slot_refs[g], store, staged_ref.at[g], gathered
+                level, None, chips, slot_refs[g], store, staged_ref.at[g], gathered.at[g]
             )
     for copy in copies:
         copy.wait()
@@ -175,7 +175,7 @@
     core, col = own_place()
     sums = []
     for g in range(2):
-        total = slot_sum(level, level - 1, chips, slot_refs[g], store_ref, staged_ref.at[g], gathered)
+        total = slot_sum(level, level - 1, chips, slot_refs[g], store_ref, staged_ref.at[g], gathered.at[g])
         sums.append(total + older_refs[g][...] if level > 1 else total)
     straight = core == col
     kept_ref[...] = jnp.where(straight, sums[0], sums[1]).astype(kept_ref.dtype)
@@ -268,7 +268,7 @@
         (other_inverses, HBM),
     )
     staged_shape = jax.ShapeDtypeStruct((2, slots, width, width), jnp.bfloat16)
-    gathered = pltpu.VMEM((rows, slots * width), jnp.bfloat16)
+    gathered = pltpu.VMEM((2, rows, slots * width), jnp.bfloat16)
     after = ()
     for l in range(1, level_count):
         staged, rhs, inverse, *older = run(

time: 64.8 us -> 64.8 us (level)
  no operation moved by 1% of the time
where the time goes in v20:
time: 64.8 us; the launch traced here: 64.2 us
  starting transfers between devices  25.2 us (39%)
  waiting for transfers between devices  22.2 us (34%)
  Pallas kernels  16 us (25%)
  local copies, waits for them, and re-layouts  0.67 us (1%)
    pallas_call x11, Pallas kernels, run(): pl.pallas_call(kernel, out_shape=out_shape, in_specs=[spec for _, spec in...  16 us
    all_to_all x3, starting transfers between devices, spread(): return lax.all_to_all(x, 'rows', 0, 0, axis_index_groups=same_core)  14.6 us
    all_to_all x3, waiting for transfers between devices, spread(): return lax.all_to_all(x, 'rows', 0, 0, axis_index_groups=same_core)  12.1 us
    ppermute x2, waiting for transfers between devices, paired_shards(): arrived = lax.ppermute(sent, 'cols', [(0, 1), (1, 0)])  6.31 us
    ppermute x5, starting transfers between devices, over_both(): return lax.ppermute(x, ('rows', 'cols'), pairs)  5.3 us
    ppermute x4, starting transfers between devices, swap_core(): return lax.ppermute(x, 'rows', [(i, i ^ 1) for i in range(row_count)])  3 us
    ppermute x2, starting transfers between devices, paired_shards(): arrived = lax.ppermute(sent, 'cols', [(0, 1), (1, 0)])  2.35 us
    ppermute x5, waiting for transfers between devices, over_both(): return lax.ppermute(x, ('rows', 'cols'), pairs)  2.1 us
  transfers between devices with their start and end apart: 14, of which 9 were waited for; matrix products, arithmetic and copies ran while one was open for 0% of the time, Pallas kernels for 16%

profile of v20, /device:TPU:0, one launch (start us, length us, event | category | flops | bytes accessed | tf_op | source)
XLA Modules:
  0.0 64.2 jit_solution(13719349392634420763)
XLA Ops:
  0.0 0.5 collective-permute-start
  0.5 0.1 collective-permute-start.1
  0.5 1.6 %shard_map.55 = (s32[3,1,1,8]{3,2,1,0:T(1,128)S(1)}, f32[64,256]{1,0:T(8,128)S(1)}, bf16[256,256]{1,0:T(8,128)(2,1)S(1)}) custom-call(s32[3,1,1,8]{3,2,1,0:T(1,128)} %ids_ref.1, s32[3]{0:T(128)} %bitcast.1, f32[4,1,128,256]{3,2,1,0:T(8,128)} %refs_4_.5, bf16[4,1,256,256]{3,2,1,0:T(8,128)(2,1)} %refs_6_.5), custom_call_target="tpu_custom_call" | custom-call | tf_op jit(solution)/shard_map/pallas_call | solution.py:36
  2.1 0.1 collective-permute-done.other_rhs_ref.refs_5_
  2.2 0.0 copy-start
  2.2 0.7 %collective-permute-done.1.other_inverse_ref.refs_7_ = bf16[4,1,256,256]{3,2,1,0:T(8,128)(2,1)S(1)} collective-permute-done((bf16[4,1,256,256]{3,2,1,0:T(8,128)(2,1)}, bf16[4,1,256,256]{3,2,1,0:T(8,128)(2,1)S(1)}, u32[]{:S(2)}, u32[]{:S(2)}) %collective-permute-start.1) | collective-permute-done | bytes 524320 | tf_op jit(solution)/shard_map/ppermute | solution.py:226
  3.0 0.0 copy-start.1
  3.0 0.4 collective-permute-start.3
  3.3 0.9 %shard_map.56 = (f32[64,256]{1,0:T(8,128)}, bf16[8,64,256]{2,1,0:T(8,128)(2,1)}) custom-call(f32[64,256]{1,0:T(8,128)S(1)} %get-tuple-element.36.rhs_ref, f32[4,1,128,256]{3,2,1,0:T(8,128)S(1)} %collective-permute-done.other_rhs_ref.refs_5_, bf16[256,256]{1,0:T(8,128)(2,1)S(1)} %get-tuple-element.37.inverse_ref, ...), custom_call_target="tpu_custom_call" | custom-call | flops 8388608 | tf_op jit(solution)/shard_map/pallas_call | solution.py:36
  4.2 7.0 %all-to-all-start = ((bf16[8,64,256]{2,1,0:T(8,128)(2,1)}), bf16[8,64,256]{2,1,0:T(8,128)(2,1)S(1)}, u32[]{:S(2)}, u32[]{:S(2)}) async-start(bf16[8,64,256]{2,1,0:T(8,128)(2,1)} %get-tuple-element.40), calls=%async_computation | async-start | bytes 524288 | tf_op jit(solution)/shard_map/all_to_all | solution.py:232
  11.2 1.5 %collective-permute-start.4 = (f32[64,256]{1,0:T(8,128)}, f32[64,256]{1,0:T(8,128)S(1)}, u32[]{:S(2)}, u32[]{:S(2)}) collective-permute-start(f32[64,256]{1,0:T(8,128)} %get-tuple-element.38), channel_id=1, source_target_pairs={{0,0},{1,2},{2,1},{3,3},{4,4},{5,6},{6,5},{7,7},{8,8},{9,10},{10,9... | collective-permute-start | bytes 196616 | tf_op jit(solution)/shard_map/ppermute | solution.py:223
  12.7 2.1 %collective-permute-start.2 = (s32[3,1,1,8]{3,2,1,0:T(1,128)S(1)}, s32[3,1,1,8]{3,2,1,0:T(1,128)S(1)}, u32[]{:S(2)}, u32[]{:S(2)}) collective-permute-start(s32[3,1,1,8]{3,2,1,0:T(1,128)S(1)} %get-tuple-element.39.refs_0_), channel_id=1, source_target_pairs={{0,2},{2,0},{4,6},{6,4},{8,10},{10,8},{12,14},{14,12},{16,18},{18,... | collective-permute-start | bytes 296 | tf_op jit(solution)/shard_map/ppermute | solution.py:226
  14.8 0.8 %collective-permute-done.2.refs_1_ = s32[3,1,1,8]{3,2,1,0:T(1,128)S(1)} collective-permute-done((s32[3,1,1,8]{3,2,1,0:T(1,128)S(1)}, s32[3,1,1,8]{3,2,1,0:T(1,128)S(1)}, u32[]{:S(2)}, u32[]{:S(2)}) %collective-permute-start.2) | collective-permute-done | bytes 128 | tf_op jit(solution)/shard_map/ppermute | solution.py:226
  15.6 0.0 collective-permute-done.3.refs_3_
  15.6 0.0 copy-done
  15.6 0.0 copy-done.1
  15.6 2.3 %shard_map.57 = (bf16[2,8,256,256]{3,2,1,0:T(8,128)(2,1)S(1)}, f32[64,256]{1,0:T(8,128)S(1)}, bf16[256,256]{1,0:T(8,128)(2,1)S(1)}) custom-call(s32[3,1,1,8]{3,2,1,0:T(1,128)S(1)} %get-tuple-element.39.refs_0_, s32[3,1,1,8]{3,2,1,0:T(1,128)S(1)} %collective-permute-done.2.refs_1_, bf16[3,1,1,8,256,256]{5,4,3,2,1,0:T(8,128)(2,1)} %refs_2_.5, ...), custom_call_target="tpu_custom_call" | custom-call | bytes 2097152 | tf_op jit(solution)/shard_map/pallas_call | solution.py:36
  17.9 0.0 copy-start.2
  17.9 0.7 %copy-done.2 = bf16[256,256]{1,0:T(8,128)(2,1)} copy-done((bf16[256,256]{1,0:T(8,128)(2,1)}, bf16[256,256]{1,0:T(8,128)(2,1)S(1)}, u32[]{:S(2)}) %copy-start.2) | copy-done | bytes 131096
  18.6 0.0 collective-permute-done.4.refs_4_.refs_6_.refs_0_
  18.6 0.0 copy-start.3
  18.6 2.1 %all-to-all-done.refs_2_.refs_8_ = bf16[8,64,256]{2,1,0:T(8,128)(2,1)S(1)} async-done(((bf16[8,64,256]{2,1,0:T(8,128)(2,1)}), bf16[8,64,256]{2,1,0:T(8,128)(2,1)S(1)}, u32[]{:S(2)}, u32[]{:S(2)}) %all-to-all-start) | async-done | bytes 262176 | tf_op jit(solution)/shard_map/all_to_all | solution.py:232
  20.6 1.1 %shard_map.58 = (f32[64,256]{1,0:T(8,128)S(1)}, f32[64,256]{1,0:T(8,128)S(1)}) custom-call(s32[3,1,1,8]{3,2,1,0:T(1,128)S(1)} %get-tuple-element.39.refs_0_, s32[3,1,1,8]{3,2,1,0:T(1,128)S(1)} %collective-permute-done.2.refs_1_, bf16[8,64,256]{2,1,0:T(8,128)(2,1)S(1)} %all-to-all-done.refs_2_.refs_8_, ...), custom_call_target="tpu_custom_call" | custom-call | flops 134217728 | bytes 2097152 | tf_op jit(solution)/shard_map/pallas_call | solution.py:36
  21.7 1.6 %collective-permute-start.5 = (f32[64,256]{1,0:T(8,128)S(1)}, f32[64,256]{1,0:T(8,128)S(1)}, u32[]{:S(2)}, u32[]{:S(2)}) collective-permute-start(f32[64,256]{1,0:T(8,128)S(1)} %get-tuple-element.44), channel_id=1, source_target_pairs={{0,1},{1,0},{2,3},{3,2},{4,5},{5,4},{6,7},{7,6},{8,9},{9,8},{10,11... | collective-permute-start | bytes 196616 | tf_op jit(solution)/shard_map/ppermute | solution.py:301
  23.3 2.7 %collective-permute-done.5.arrived_ref = f32[64,256]{1,0:T(8,128)S(1)} collective-permute-done((f32[64,256]{1,0:T(8,128)S(1)}, f32[64,256]{1,0:T(8,128)S(1)}, u32[]{:S(2)}, u32[]{:S(2)}) %collective-permute-start.5) | collective-permute-done | bytes 65568 | tf_op jit(solution)/shard_map/ppermute | solution.py:301
  26.0 0.0 copy-done.3
  26.0 0.9 %shard_map.59 = (f32[64,256]{1,0:T(8,128)S(1)}, bf16[8,64,256]{2,1,0:T(8,128)(2,1)}) custom-call(f32[64,256]{1,0:T(8,128)S(1)} %get-tuple-element.43.kept_ref.refs_9_, f32[64,256]{1,0:T(8,128)S(1)} %collective-permute-done.5.arrived_ref, f32[64,256]{1,0:T(8,128)S(1)} %get-tuple-element.45.rhs_ref, bf16[256,256]{1,0:T(8,128)(2,1)S(1)} %copy-done.3), custom_call_target="tpu_custom_call" | custom-call | flops 8388608 | tf_op jit(solution)/shard_map/pallas_call | solution.py:36
  26.9 4.0 %all-to-all-start.1 = ((bf16[8,64,256]{2,1,0:T(8,128)(2,1)}), bf16[8,64,256]{2,1,0:T(8,128)(2,1)S(1)}, u32[]{:S(2)}, u32[]{:S(2)}) async-start(bf16[8,64,256]{2,1,0:T(8,128)(2,1)} %get-tuple-element.47), calls=%async_computation.1 | async-start | bytes 524288 | tf_op jit(solution)/shard_map/all_to_all | solution.py:232
  30.9 0.7 %collective-permute-start.6 = (f32[64,256]{1,0:T(8,128)S(1)}, f32[64,256]{1,0:T(8,128)S(1)}, u32[]{:S(2)}, u32[]{:S(2)}) collective-permute-start(f32[64,256]{1,0:T(8,128)S(1)} %get-tuple-element.51), channel_id=1, source_target_pairs={{0,0},{1,2},{2,1},{3,3},{4,4},{5,6},{6,5},{7,7},{8,8},{9,10},{10,9... | collective-permute-start | bytes 196616 | tf_op jit(solution)/shard_map/ppermute | solution.py:223
  31.6 2.7 %shard_map.60 = (bf16[2,8,256,256]{3,2,1,0:T(8,128)(2,1)S(1)}, f32[64,256]{1,0:T(8,128)S(1)}, bf16[256,256]{1,0:T(8,128)(2,1)S(1)}, f32[64,256]{1,0:T(8,128)S(1)}, f32[64,256]{1,0:T(8,128)S(1)}) custom-call(s32[3,1,1,8]{3,2,1,0:T(1,128)S(1)} %get-tuple-element.39.refs_0_, s32[3,1,1,8]{3,2,1,0:T(1,128)S(1)} %collective-permute-done.2.refs_1_, ...), custom_call_target="tpu_custom_call" | custom-call | flops 134217728 | bytes 2097152 | tf_op jit(solution)/shard_map/pallas_call | solution.py:36
  34.3 0.0 collective-permute-done.6.refs_7_.refs_1_
  34.3 5.2 %all-to-all-done.1.refs_2_.refs_9_ = bf16[8,64,256]{2,1,0:T(8,128)(2,1)S(1)} async-done(((bf16[8,64,256]{2,1,0:T(8,128)(2,1)}), bf16[8,64,256]{2,1,0:T(8,128)(2,1)S(1)}, u32[]{:S(2)}, u32[]{:S(2)}) %all-to-all-start.1) | async-done | bytes 262176 | tf_op jit(solution)/shard_map/all_to_all | solution.py:232
  39.5 1.1 %shard_map.61 = (f32[64,256]{1,0:T(8,128)S(1)}, f32[64,256]{1,0:T(8,128)S(1)}) custom-call(s32[3,1,1,8]{3,2,1,0:T(1,128)S(1)} %get-tuple-element.39.refs_0_, s32[3,1,1,8]{3,2,1,0:T(1,128)S(1)} %collective-permute-done.2.refs_1_, bf16[8,64,256]{2,1,0:T(8,128)(2,1)S(1)} %all-to-all-done.1.refs_2_.refs_9_, ...), custom_call_target="tpu_custom_call" | custom-call | flops 134217728 | bytes 2097152 | tf_op jit(solution)/shard_map/pallas_call | solution.py:36
  40.6 0.8 %collective-permute-start.7 = (f32[64,256]{1,0:T(8,128)S(1)}, f32[64,256]{1,0:T(8,128)S(1)}, u32[]{:S(2)}, u32[]{:S(2)}) collective-permute-start(f32[64,256]{1,0:T(8,128)S(1)} %get-tuple-element.53), channel_id=1, source_target_pairs={{0,1},{1,0},{2,3},{3,2},{4,5},{5,4},{6,7},{7,6},{8,9},{9,8},{10,11... | collective-permute-start | bytes 196616 | tf_op jit(solution)/shard_map/ppermute | solution.py:301
  41.4 3.6 %collective-permute-done.7.arrived_ref = f32[64,256]{1,0:T(8,128)S(1)} collective-permute-done((f32[64,256]{1,0:T(8,128)S(1)}, f32[64,256]{1,0:T(8,128)S(1)}, u32[]{:S(2)}, u32[]{:S(2)}) %collective-permute-start.7) | collective-permute-done | bytes 65568 | tf_op jit(solution)/shard_map/ppermute | solution.py:301
  44.9 0.9 %shard_map.62 = (f32[64,256]{1,0:T(8,128)S(1)}, bf16[8,64,256]{2,1,0:T(8,128)(2,1)}) custom-call(f32[64,256]{1,0:T(8,128)S(1)} %get-tuple-element.52.kept_ref.refs_10_, f32[64,256]{1,0:T(8,128)S(1)} %collective-permute-done.7.arrived_ref, f32[64,256]{1,0:T(8,128)S(1)} %get-tuple-element.54.rhs_ref, bf16[256,256]{1,0:T(8,128)(2,1)S(1)} %get-tuple-element.55.inverse_ref), custom_call_target="tpu_custom_call" | custom-call | flops 8388608 | tf_op jit(solution)/shard_map/pallas_call | solution.py:36
  45.8 3.6 %all-to-all-start.2 = ((bf16[8,64,256]{2,1,0:T(8,128)(2,1)}), bf16[8,64,256]{2,1,0:T(8,128)(2,1)S(1)}, u32[]{:S(2)}, u32[]{:S(2)}) async-start(bf16[8,64,256]{2,1,0:T(8,128)(2,1)} %get-tuple-element.56), calls=%async_computation.2 | async-start | bytes 524288 | tf_op jit(solution)/shard_map/all_to_all | solution.py:232
  49.4 0.7 %collective-permute-start.8 = (f32[64,256]{1,0:T(8,128)S(1)}, f32[64,256]{1,0:T(8,128)S(1)}, u32[]{:S(2)}, u32[]{:S(2)}) collective-permute-start(f32[64,256]{1,0:T(8,128)S(1)} %get-tuple-element.60), channel_id=1, source_target_pairs={{0,0},{1,2},{2,1},{3,3},{4,4},{5,6},{6,5},{7,7},{8,8},{9,10},{10,9... | collective-permute-start | bytes 196616 | tf_op jit(solution)/shard_map/ppermute | solution.py:223
  50.1 2.7 %shard_map.63 = (bf16[2,8,256,256]{3,2,1,0:T(8,128)(2,1)S(1)}, f32[64,256]{1,0:T(8,128)S(1)}, bf16[256,256]{1,0:T(8,128)(2,1)S(1)}, f32[64,256]{1,0:T(8,128)S(1)}, f32[64,256]{1,0:T(8,128)S(1)}) custom-call(s32[3,1,1,8]{3,2,1,0:T(1,128)S(1)} %get-tuple-element.39.refs_0_, s32[3,1,1,8]{3,2,1,0:T(1,128)S(1)} %collective-permute-done.2.refs_1_, ...), custom_call_target="tpu_custom_call" | custom-call | flops 134217728 | bytes 2097152 | tf_op jit(solution)/shard_map/pallas_call | solution.py:36
  52.8 0.0 collective-permute-done.8.refs_8_.refs_2_
  52.8 4.8 %all-to-all-done.2.refs_2_ = bf16[8,64,256]{2,1,0:T(8,128)(2,1)S(1)} async-done(((bf16[8,64,256]{2,1,0:T(8,128)(2,1)}), bf16[8,64,256]{2,1,0:T(8,128)(2,1)S(1)}, u32[]{:S(2)}, u32[]{:S(2)}) %all-to-all-start.2) | async-done | bytes 262176 | tf_op jit(solution)/shard_map/all_to_all | solution.py:232
  57.6 1.1 %shard_map.64 = (bf16[64,256]{1,0:T(8,128)(2,1)S(1)}, bf16[64,256]{1,0:T(8,128)(2,1)S(1)}) custom-call(s32[3,1,1,8]{3,2,1,0:T(1,128)S(1)} %get-tuple-element.39.refs_0_, s32[3,1,1,8]{3,2,1,0:T(1,128)S(1)} %collective-permute-done.2.refs_1_, bf16[8,64,256]{2,1,0:T(8,128)(2,1)S(1)} %all-to-all-done.2.refs_2_, ...), custom_call_target="tpu_custom_call" | custom-call | flops 134217728 | bytes 2097152 | tf_op jit(solution)/shard_map/pallas_call | solution.py:36
  58.7 0.7 %collective-permute-start.9 = (bf16[64,256]{1,0:T(8,128)(2,1)S(1)}, bf16[64,256]{1,0:T(8,128)(2,1)S(1)}, u32[]{:S(2)}, u32[]{:S(2)}) collective-permute-start(bf16[64,256]{1,0:T(8,128)(2,1)S(1)} %get-tuple-element.61), channel_id=1, source_target_pairs={{0,0},{1,2},{2,1},{3,3},{4,4},{5,6},{6,5},{7,7},{8,8},{9,10},{10,9... | collective-permute-start | bytes 98312 | tf_op jit(solution)/shard_map/ppermute | solution.py:223
  59.4 1.8 %collective-permute-start.10 = (bf16[64,256]{1,0:T(8,128)(2,1)S(1)}, bf16[64,256]{1,0:T(8,128)(2,1)S(1)}, u32[]{:S(2)}, u32[]{:S(2)}) collective-permute-start(bf16[64,256]{1,0:T(8,128)(2,1)S(1)} %get-tuple-element.62), channel_id=1, source_target_pairs={{0,2},{1,0},{2,3},{3,1},{4,6},{5,4},{6,7},{7,5},{8,10},{9,8},{10,1... | collective-permute-start | bytes 98312 | tf_op jit(solution)/shard_map/ppermute | solution.py:223
  61.2 0.0 collective-permute-done.9.first_ref
  61.2 2.1 %collective-permute-done.10.second_ref = bf16[64,256]{1,0:T(8,128)(2,1)S(1)} collective-permute-done((bf16[64,256]{1,0:T(8,128)(2,1)S(1)}, bf16[64,256]{1,0:T(8,128)(2,1)S(1)}, u32[]{:S(2)}, u32[]{:S(2)}) %collective-permute-start.10) | collective-permute-done | bytes 32800 | tf_op jit(solution)/shard_map/ppermute | solution.py:223
  63.3 0.9 %shard_map.65 = f32[4,1,64,256]{3,2,1,0:T(8,128)} custom-call(bf16[64,256]{1,0:T(8,128)(2,1)S(1)} %collective-permute-done.9.first_ref, bf16[64,256]{1,0:T(8,128)(2,1)S(1)} %collective-permute-done.10.second_ref, f32[64,256]{1,0:T(8,128)S(1)} %get-tuple-element.63.rhs_ref, bf16[256,256]{1,0:T(8,128)(2,1)S(1)} %get-tuple-element.64.inverse_ref, ...), custom_call_target="tpu_custom_call" | custom-call | flops 8388608 | tf_op jit(solution)/shard_map/pallas_call | solution.py:36
Async XLA Ops:
  0.0 2.2 %collective-permute-start = (f32[4,1,128,256]{3,2,1,0:T(8,128)}, f32[4,1,128,256]{3,2,1,0:T(8,128)S(1)}, u32[]{:S(2)}, u32[]{:S(2)}) collective-permute-start(f32[4,1,128,256]{3,2,1,0:T(8,128)} %refs_4_.5), channel_id=1, source_target_pairs={{0,2},{2,0},{4,6},{6,4},{8,10},{10,8},{12,14},{14,12},{16,18},{18,... | collective-permute-start | bytes 1572872 | tf_op jit(solution)/shard_map/ppermute | solution.py:226
  0.5 2.5 %collective-permute-start.1 = (bf16[4,1,256,256]{3,2,1,0:T(8,128)(2,1)}, bf16[4,1,256,256]{3,2,1,0:T(8,128)(2,1)S(1)}, u32[]{:S(2)}, u32[]{:S(2)}) collective-permute-start(bf16[4,1,256,256]{3,2,1,0:T(8,128)(2,1)} %refs_6_.5), channel_id=1, source_target_pairs={{0,2},{2,0},{4,6},{6,4},{8,10},{10,8},{12,14},{14,12},{16,18},{18,... | collective-permute-start | bytes 1572872 | tf_op jit(solution)/shard_map/ppermute | solution.py:226
  2.2 13.4 %copy-start = (f32[4,1,128,256]{3,2,1,0:T(8,128)}, f32[4,1,128,256]{3,2,1,0:T(8,128)S(1)}, u32[]{:S(2)}) copy-start(f32[4,1,128,256]{3,2,1,0:T(8,128)S(1)} %collective-permute-done.other_rhs_ref.refs_5_) | copy-start | bytes 1572868
  3.0 12.7 %copy-start.1 = (bf16[4,1,256,256]{3,2,1,0:T(8,128)(2,1)}, bf16[4,1,256,256]{3,2,1,0:T(8,128)(2,1)S(1)}, u32[]{:S(2)}) copy-start(bf16[4,1,256,256]{3,2,1,0:T(8,128)(2,1)S(1)} %collective-permute-done.1.other_inverse_ref.refs_7_) | copy-start | bytes 1572868
  3.0 12.7 %collective-permute-start.3 = (bf16[3,1,1,8,256,256]{5,4,3,2,1,0:T(8,128)(2,1)}, bf16[3,1,1,8,256,256]{5,4,3,2,1,0:T(8,128)(2,1)}, u32[]{:S(2)}, u32[]{:S(2)}) collective-permute-start(bf16[3,1,1,8,256,256]{5,4,3,2,1,0:T(8,128)(2,1)} %refs_2_.5), channel_id=1, source_target_pairs={{0,2},{2,0},{4,6},{6,4},{8,10},{10,8},{12,14},{14,12},{16,18},{18,... | collective-permute-start | bytes 9437192 | tf_op jit(solution)/shard_map/ppermute | solution.py:226
  4.2 16.4 %all-to-all-start = ((bf16[8,64,256]{2,1,0:T(8,128)(2,1)}), bf16[8,64,256]{2,1,0:T(8,128)(2,1)S(1)}, u32[]{:S(2)}, u32[]{:S(2)}) async-start(bf16[8,64,256]{2,1,0:T(8,128)(2,1)} %get-tuple-element.40), calls=%async_computation | async-start | bytes 524288 | tf_op jit(solution)/shard_map/all_to_all | solution.py:232
  11.2 7.4 %collective-permute-start.4 = (f32[64,256]{1,0:T(8,128)}, f32[64,256]{1,0:T(8,128)S(1)}, u32[]{:S(2)}, u32[]{:S(2)}) collective-permute-start(f32[64,256]{1,0:T(8,128)} %get-tuple-element.38), channel_id=1, source_target_pairs={{0,0},{1,2},{2,1},{3,3},{4,4},{5,6},{6,5},{7,7},{8,8},{9,10},{10,9... | collective-permute-start | bytes 196616 | tf_op jit(solution)/shard_map/ppermute | solution.py:223
  12.7 2.9 %collective-permute-start.2 = (s32[3,1,1,8]{3,2,1,0:T(1,128)S(1)}, s32[3,1,1,8]{3,2,1,0:T(1,128)S(1)}, u32[]{:S(2)}, u32[]{:S(2)}) collective-permute-start(s32[3,1,1,8]{3,2,1,0:T(1,128)S(1)} %get-tuple-element.39.refs_0_), channel_id=1, source_target_pairs={{0,2},{2,0},{4,6},{6,4},{8,10},{10,8},{12,14},{14,12},{16,18},{18,... | collective-permute-start | bytes 296 | tf_op jit(solution)/shard_map/ppermute | solution.py:226
  17.9 0.7 %copy-start.2 = (bf16[256,256]{1,0:T(8,128)(2,1)}, bf16[256,256]{1,0:T(8,128)(2,1)S(1)}, u32[]{:S(2)}) copy-start(bf16[256,256]{1,0:T(8,128)(2,1)S(1)} %get-tuple-element.46.inverse_ref) | copy-start | bytes 393220
  18.6 7.5 %copy-start.3 = (bf16[256,256]{1,0:T(8,128)(2,1)S(1)}, bf16[256,256]{1,0:T(8,128)(2,1)}, u32[]{:S(2)}) copy-start(bf16[256,256]{1,0:T(8,128)(2,1)} %copy-done.2) | copy-start | bytes 393220
  21.7 4.3 %collective-permute-start.5 = (f32[64,256]{1,0:T(8,128)S(1)}, f32[64,256]{1,0:T(8,128)S(1)}, u32[]{:S(2)}, u32[]{:S(2)}) collective-permute-start(f32[64,256]{1,0:T(8,128)S(1)} %get-tuple-element.44), channel_id=1, source_target_pairs={{0,1},{1,0},{2,3},{3,2},{4,5},{5,4},{6,7},{7,6},{8,9},{9,8},{10,11... | collective-permute-start | bytes 196616 | tf_op jit(solution)/shard_map/ppermute | solution.py:301
  26.9 12.6 %all-to-all-start.1 = ((bf16[8,64,256]{2,1,0:T(8,128)(2,1)}), bf16[8,64,256]{2,1,0:T(8,128)(2,1)S(1)}, u32[]{:S(2)}, u32[]{:S(2)}) async-start(bf16[8,64,256]{2,1,0:T(8,128)(2,1)} %get-tuple-element.47), calls=%async_computation.1 | async-start | bytes 524288 | tf_op jit(solution)/shard_map/all_to_all | solution.py:232
  30.9 3.4 %collective-permute-start.6 = (f32[64,256]{1,0:T(8,128)S(1)}, f32[64,256]{1,0:T(8,128)S(1)}, u32[]{:S(2)}, u32[]{:S(2)}) collective-permute-start(f32[64,256]{1,0:T(8,128)S(1)} %get-tuple-element.51), channel_id=1, source_target_pairs={{0,0},{1,2},{2,1},{3,3},{4,4},{5,6},{6,5},{7,7},{8,8},{9,10},{10,9... | collective-permute-start | bytes 196616 | tf_op jit(solution)/shard_map/ppermute | solution.py:223
  40.6 4.3 %collective-permute-start.7 = (f32[64,256]{1,0:T(8,128)S(1)}, f32[64,256]{1,0:T(8,128)S(1)}, u32[]{:S(2)}, u32[]{:S(2)}) collective-permute-start(f32[64,256]{1,0:T(8,128)S(1)} %get-tuple-element.53), channel_id=1, source_target_pairs={{0,1},{1,0},{2,3},{3,2},{4,5},{5,4},{6,7},{7,6},{8,9},{9,8},{10,11... | collective-permute-start | bytes 196616 | tf_op jit(solution)/shard_map/ppermute | solution.py:301
  45.8 11.8 %all-to-all-start.2 = ((bf16[8,64,256]{2,1,0:T(8,128)(2,1)}), bf16[8,64,256]{2,1,0:T(8,128)(2,1)S(1)}, u32[]{:S(2)}, u32[]{:S(2)}) async-start(bf16[8,64,256]{2,1,0:T(8,128)(2,1)} %get-tuple-element.56), calls=%async_computation.2 | async-start | bytes 524288 | tf_op jit(solution)/shard_map/all_to_all | solution.py:232
  49.4 3.4 %collective-permute-start.8 = (f32[64,256]{1,0:T(8,128)S(1)}, f32[64,256]{1,0:T(8,128)S(1)}, u32[]{:S(2)}, u32[]{:S(2)}) collective-permute-start(f32[64,256]{1,0:T(8,128)S(1)} %get-tuple-element.60), channel_id=1, source_target_pairs={{0,0},{1,2},{2,1},{3,3},{4,4},{5,6},{6,5},{7,7},{8,8},{9,10},{10,9... | collective-permute-start | bytes 196616 | tf_op jit(solution)/shard_map/ppermute | solution.py:223
  58.7 2.5 %collective-permute-start.9 = (bf16[64,256]{1,0:T(8,128)(2,1)S(1)}, bf16[64,256]{1,0:T(8,128)(2,1)S(1)}, u32[]{:S(2)}, u32[]{:S(2)}) collective-permute-start(bf16[64,256]{1,0:T(8,128)(2,1)S(1)} %get-tuple-element.61), channel_id=1, source_target_pairs={{0,0},{1,2},{2,1},{3,3},{4,4},{5,6},{6,5},{7,7},{8,8},{9,10},{10,9... | collective-permute-start | bytes 98312 | tf_op jit(solution)/shard_map/ppermute | solution.py:223
  59.4 3.9 %collective-permute-start.10 = (bf16[64,256]{1,0:T(8,128)(2,1)S(1)}, bf16[64,256]{1,0:T(8,128)(2,1)S(1)}, u32[]{:S(2)}, u32[]{:S(2)}) collective-permute-start(bf16[64,256]{1,0:T(8,128)(2,1)S(1)} %get-tuple-element.62), channel_id=1, source_target_pairs={{0,2},{1,0},{2,3},{3,1},{4,6},{5,4},{6,7},{7,5},{8,10},{9,8},{10,1... | collective-permute-start | bytes 98312 | tf_op jit(solution)/shard_map/ppermute | solution.py:223
